TPU v7x, 32 devices: a whole 2x2x4 slice. The times are simulated.
32 devices in a mesh: groups: 2 (over x), ctx: 16 (over z, y, core).
Axes of the slice: x: 2, y: 2, z: 4, core: 2. Of those that a mesh axis runs over, the one named last changes fastest.
Arguments:
- queries: bfloat16 [4096, 2048], P(('groups', 'ctx')), parts along dimension 0, may hold values from -200 to 200
- rotated_keys: bfloat16 [4096, 256], P(('groups', 'ctx')), parts along dimension 0, may hold values from -6 to 6
- value_matrix: bfloat16 [4096, 256], P(('groups', 'ctx')), parts along dimension 0, may hold values from -6 to 6
- stretch_pos: int32 [32], P(('groups', 'ctx')), parts along dimension 0, may hold values from 0 to 15, each once
- residual: bfloat16 [4096, 2048], P(('groups', 'ctx')), parts along dimension 0, may hold values from -6 to 6
- norm_gain: float32 [2048], replicated, may hold values from 0.1 to 1.9
- routes: int32 [4096, 8], P(('groups', 'ctx')), parts along dimension 0, may hold values from 0 to 15, all different within a row; in each aligned block of 128 rows (0 to 127, 128 to 255, ...) at most 72 rows name the same one
- combine: float32 [4096, 8], P(('groups', 'ctx')), parts along dimension 0, may hold values from 0.05 to 1
- gate_weight: bfloat16 [16, 2048, 384], P('ctx'), may hold values from -0.125 to 0.125
- up_weight: bfloat16 [16, 2048, 384], P('ctx'), may hold values from -0.125 to 0.125
- down_weight: bfloat16 [16, 384, 2048], P('ctx'), may hold values from -0.3125 to 0.3125
Outputs:
- layer_out: bfloat16 [4096, 2048], P(('groups', 'ctx')), parts along dimension 0
There are 2 independent parts, one for each index of `groups`. A program takes and returns all parts, laid end to end along the dimension named above; an argument that names none is the same for every part. Nothing has to cross between parts.
Inputs may be any that keep to these rules, and one draw needn't show every extreme that they name: `routes`: within the rows of one device no expert is named more than 72 times; some device names some expert exactly 72 times. `stretch_pos`: each block place appears once.
All inputs are finite; a program needn't handle non-finite values.
Results may differ from a plain program's by a relative error of at most 0.01.
Values may be sent and summed in bfloat16 or wider, within the bound.
No kernel may reach another device: no remote copies, remote signals or barrier semaphores. Data moves between devices by JAX's collectives and lax.ppermute only.
A program may use at most 128 MiB of HBM per device.

v0:
```python
import math

import jax
import jax.numpy as jnp
from jax import lax
from jax.sharding import PartitionSpec as P

D = 2048
HEAD_SIZE = 128


NEG = -1e30


def on_device(
    queries,
    rotated_keys,
    value_matrix,
    stretch_pos,
    residual,
    norm_gain,
    routes,
    combine,
    gate_weight,
    up_weight,
    down_weight,
):
    tok_rows = queries.shape[0]
    kv_heads = rotated_keys.shape[1] // HEAD_SIZE
    head_group = queries.shape[1] // rotated_keys.shape[1]
    ctx_count = lax.axis_size("ctx")
    positions = stretch_pos[0] * tok_rows + jnp.arange(tok_rows, dtype=jnp.int32)
    latest = jnp.max(positions)
    query_heads = queries.reshape(tok_rows, kv_heads, head_group, HEAD_SIZE)
    scale_factor = 1.0 / math.sqrt(HEAD_SIZE)

    def update(state, key_block, value_block, key_pos):
        best, total, accum = state
        scores = (
            jnp.einsum(
                "tagd,sad->agts",
                query_heads,
                key_block.reshape(-1, kv_heads, HEAD_SIZE),
                preferred_element_type=jnp.float32,
            )
            * scale_factor
        )
        scores = jnp.where(
            key_pos[None, None, None, :] <= positions[None, None, :, None], scores, jnp.float32(NEG)
        )
        fresh = jnp.maximum(best, jnp.max(scores, axis=-1))
        shrink = jnp.exp(best - fresh)
        expo = jnp.exp(scores - fresh[..., None])
        total = total * shrink + jnp.sum(expo, axis=-1)
        weighted = jnp.einsum(
            "agts,sad->agtd",
            expo.astype(jnp.bfloat16),
            value_block.reshape(-1, kv_heads, HEAD_SIZE),
            preferred_element_type=jnp.float32,
        )
        accum = accum * shrink[..., None] + weighted
        return (fresh, total, accum)

    start_state = (
        jnp.full((kv_heads, head_group, tok_rows), NEG, jnp.float32),
        jnp.zeros((kv_heads, head_group, tok_rows), jnp.float32),
        jnp.zeros((kv_heads, head_group, tok_rows, HEAD_SIZE), jnp.float32),
    )
    key_part = lax.all_gather(rotated_keys, "ctx", axis=0, tiled=True)
    value_part = lax.all_gather(value_matrix, "ctx", axis=0, tiled=True)
    pos_part = lax.all_gather(positions, "ctx", axis=0, tiled=True)
    span = key_part.shape[0]
    width = 512
    blocks = span // width
    stacked = (
        key_part.reshape(blocks, width, -1),
        value_part.reshape(blocks, width, -1),
        pos_part.reshape(blocks, width),
    )

    def advance(inner, item):
        key_block, value_block, key_pos = item
        result = lax.cond(
            jnp.min(key_pos) > latest,
            lambda kept: kept,
            lambda kept: update(kept, key_block, value_block, key_pos),
            inner,
        )
        return (result, None)

    final, unused = lax.scan(advance, start_state, stacked)
    best, total, accum = final
    attended = (
        jnp.transpose(accum / total[..., None], (2, 0, 1, 3))
        .reshape(tok_rows, -1)
        .astype(jnp.bfloat16)
    )
    hidden_state = residual.astype(jnp.float32) + attended.astype(jnp.float32)
    meansq = jnp.mean(hidden_state * hidden_state, axis=-1, keepdims=True)
    normed = (hidden_state * lax.rsqrt(meansq + 1e-06) * norm_gain).astype(jnp.bfloat16)
    local_experts = gate_weight.shape[0]
    total_experts = local_experts * ctx_count
    top_count = routes.shape[1]
    capacity = min(
        tok_rows,
        tok_rows * top_count // total_experts + max(1, tok_rows * top_count // (8 * total_experts)),
    )
    flat_routes = routes.reshape(-1)
    onehot = (flat_routes[:, None] == jnp.arange(total_experts, dtype=jnp.int32)[None, :]).astype(
        jnp.int32
    )
    earlier = jnp.cumsum(onehot, axis=0) - onehot
    ranking = jnp.sum(earlier * onehot, axis=1)
    slot_ids = flat_routes * capacity + ranking
    selector = jnp.any(
        slot_ids.reshape(tok_rows, top_count)[:, :, None]
        == jnp.arange(total_experts * capacity, dtype=jnp.int32)[None, None, :],
        axis=1,
    ).astype(jnp.bfloat16)
    outgoing = jnp.einsum("ts,td->sd", selector, normed, preferred_element_type=jnp.float32).astype(
        jnp.bfloat16
    )
    outgoing = outgoing.reshape(ctx_count, local_experts, capacity, D)
    incoming = lax.all_to_all(outgoing, "ctx", split_axis=0, concat_axis=0, tiled=True)
    gate = jnp.einsum("secd,edh->sech", incoming, gate_weight, preferred_element_type=jnp.float32)
    upper = jnp.einsum("secd,edh->sech", incoming, up_weight, preferred_element_type=jnp.float32)
    act = (jax.nn.silu(gate) * upper).astype(jnp.bfloat16)
    returned = lax.all_to_all(
        jnp.einsum("sech,ehd->secd", act, down_weight, preferred_element_type=jnp.float32).astype(
            jnp.bfloat16
        ),
        "ctx",
        split_axis=0,
        concat_axis=0,
        tiled=True,
    )
    flat_back = returned.reshape(total_experts * capacity, D)
    picked = jnp.take(flat_back, slot_ids, axis=0).reshape(tok_rows, top_count, D)
    mixture = jnp.sum(combine[:, :, None] * picked.astype(jnp.float32), axis=1)
    return (hidden_state + mixture).astype(jnp.bfloat16)


def solution(mesh):
    placed = (
        P(("groups", "ctx"), None),
        P(("groups", "ctx"), None),
        P(("groups", "ctx"), None),
        P(("groups", "ctx")),
        P(("groups", "ctx"), None),
        P(),
        P(("groups", "ctx"), None),
        P(("groups", "ctx"), None),
        P("ctx", None, None),
        P("ctx", None, None),
        P("ctx", None, None),
    )
    return jax.shard_map(
        on_device, mesh=mesh, in_specs=placed, out_specs=P(("groups", "ctx"), None), check_vma=False
    )
```

profile of v0, /device:TPU:13, one launch (start us, length us, event | category | flops | bytes accessed | tf_op | source)
XLA Modules:
  0.0 382.9 jit_solution(15610537542623726224)
XLA Ops:
  6.5 0.7 all-gather.4.cloned.1.call-update
  7.3 0.7 all-gather.6.cloned.1.call-update
  8.0 0.8 copy.86
  9.6 0.7 fusion.48
  10.3 15.5 %all-gather = s32[16,1,128]{2,1,0:T(1,128)S(1)} all-gather(s32[1,1,128]{2,1,0:T(1,128)S(1)} %fusion.49), channel_id=1, replica_groups=mesh['groups'=2,'ctx'=16] {'ctx'}, dimensions={0}, use_global_device_ids=true | all-gather | bytes 8704 | tf_op jit(solution)/shard_map/all_gather | solution.py:71
  25.8 0.5 broadcast.132
  26.3 0.6 reduce.4
  26.9 1.3 copy.80
  28.3 0.3 copy.82
  28.6 4.5 %reduce-window.6 = s32[16,8,128]{2,1,0:T(8,128)S(1)} reduce-window(s32[16,8,128]{2,1,0:T(8,128)S(1)} %fusion.47, s32[]{:T(128)} %copy.133), window={size=1x1x128 pad=0_0x0_0x127_0}, to_apply=%region_8.9 | reduce-window | flops 2080768 | bytes 131076 | tf_op jit(solution)/shard_map/reduce-window
  33.7 0.7 compare_and_fusion
  34.5 1.5 fusion.20
  36.0 11.8 %all-gather.4.cloned.1.call-done = bf16[2048,256]{1,0:T(8,128)(2,1)} async-done(((bf16[128,256]{1,0:T(8,128)(2,1)}), bf16[2048,256]{1,0:T(8,128)(2,1)}) %all-gather.4.cloned.1.call-update) | async-done | bytes 1048592 | tf_op jit(solution)/shard_map/all_gather | solution.py:69
  47.8 1.5 copy.81
  49.3 37.6 %all-gather.6.cloned.1.call-done = bf16[2048,256]{1,0:T(8,128)(2,1)} async-done(((bf16[128,256]{1,0:T(8,128)(2,1)}), bf16[2048,256]{1,0:T(8,128)(2,1)}) %all-gather.6.cloned.1.call-update) | async-done | bytes 1048592 | tf_op jit(solution)/shard_map/all_gather | solution.py:70
  86.9 2.3 copy.83
  89.2 1.1 broadcast_in_dim.48
  90.3 18.6 %while.15 = (s32[]{:T(128)}, f32[2,8,128]{2,1,0:T(8,128)S(1)}, f32[2,8,128]{2,1,0:T(8,128)S(1)}, f32[2,8,128,128]{3,2,1,0:T(8,128)}, s32[4,512]{1,0:T(4,128)S(1)...) while((s32[]{:T(128)}, f32[2,8,128]{2,1,0:T(8,128)S(1)}, ...), condition=%wide.region_7.8_spmd.clone, body=%wide.region_1.7_spmd.clone.sunk | while | flops 548999808 | bytes 25567556 | solution.py:91
  90.3 0.6 fusion.59
  92.3 0.6 fusion.59
  94.2 5.5 %conditional.3 = (f32[2,8,128]{2,1,0:T(8,128)S(1)}, f32[2,8,128]{2,1,0:T(8,128)S(1)}, f32[2,8,128,128]{3,2,1,0:T(8,128)}) conditional(s32[]{:T(128)} %convert_element_type.109, (s32[1,512]{1,0:T(1,128)S(1)}, s32[]{:T(128)}, bf16[4,512,256]{1,2,0:T(8,128)(2,1)S(1)}, s32[]{:T(128)}, bf16[128,2,8,128]{3,0,2,1:T(8,128)(2,1)S(1)}, ...), branch_computations={%region_3.5_spmd, %region_6.6_spmd} | conditional | flops 548999296 | bytes 25546328 | solution.py:83
  94.2 0.1 broadcast_compare_fusion
  94.3 1.0 constant_dynamic-slice_fusion
  95.3 0.8 fusion.4
  96.2 0.9 fusion.3
  97.1 1.5 fusion.11
  98.6 1.0 copy-done.4
  99.7 0.6 fusion.59
  101.5 5.5 %conditional.3 = (f32[2,8,128]{2,1,0:T(8,128)S(1)}, f32[2,8,128]{2,1,0:T(8,128)S(1)}, f32[2,8,128,128]{3,2,1,0:T(8,128)}) conditional(s32[]{:T(128)} %convert_element_type.109, (s32[1,512]{1,0:T(1,128)S(1)}, s32[]{:T(128)}, bf16[4,512,256]{1,2,0:T(8,128)(2,1)S(1)}, s32[]{:T(128)}, bf16[128,2,8,128]{3,0,2,1:T(8,128)(2,1)S(1)}, ...), branch_computations={%region_3.5_spmd, %region_6.6_spmd} | conditional | flops 548999296 | bytes 25546328 | solution.py:83
  101.7 1.0 constant_dynamic-slice_fusion
  102.7 0.8 fusion.4
  103.6 0.9 fusion.3
  104.5 1.5 fusion.11
  106.0 1.0 copy-done.4
  107.0 0.6 fusion.59
  109.0 1.6 convert_bitcast_fusion.1
  110.6 0.6 copy.84
  111.3 0.6 multiply_reduce_fusion.1
  111.8 1.6 convolution_convert_fusion
  113.4 119.5 %all_to_all.10 = bf16[16,1,72,2048]{3,2,1,0:T(8,128)(2,1)S(1)} all-to-all(bf16[16,1,72,2048]{3,2,1,0:T(8,128)(2,1)S(1)} %bitcast.147), channel_id=1, replica_groups=mesh['groups'=2,'ctx'=16] {'ctx'}, dimensions={0} | all-to-all | bytes 9437184 | tf_op jit(solution)/shard_map/all_to_all | solution.py:124
  232.9 2.2 copy-done.1
  235.1 3.8 %fusion.16 = f32[16,72,384]{2,1,0:T(8,128)} fusion(bf16[16,1,72,2048]{3,2,1,0:T(8,128)(2,1)S(1)} %all_to_all.10, bf16[1,2048,384]{2,1,0:T(8,128)(2,1)S(1)} %copy-done.8), kind=kOutput, calls=%fused_computation.24 | convolution fusion | flops 1811939328 | bytes 8060928 | tf_op jit(solution)/shard_map/secd,edh->sech/dot_general | solution.py:126
  238.9 9.2 %convert_bitcast_fusion = bf16[16,1,72,2048]{3,2,1,0:T(8,128)(2,1)} fusion(bf16[1,384,2048]{2,1,0:T(8,128)(2,1)S(1)} %copy-done, f32[16,72,384]{2,1,0:T(8,128)} %fusion.16, bf16[1,2048,384]{2,1,0:T(8,128)(2,1)} %param.23, bf16[16,1,72,2048]{3,2,1,0:T(8,128)(2,1)} %copy-done.1), kind=kOutput, calls=%fused_computation.28 | convolution fusion | flops 3628892160 | bytes 14352384 | tf_op jit(solution)/shard_map/sech,ehd->secd/dot_general | solution.py:129
  248.1 5.5 %all-to-all-start.1 = ((bf16[16,1,72,2048]{3,2,1,0:T(8,128)(2,1)}), bf16[16,1,72,2048]{3,2,1,0:T(8,128)(2,1)}, u32[]{:S(2)}, u32[]{:S(2)}) async-start(bf16[16,1,72,2048]{3,2,1,0:T(8,128)(2,1)} %convert_bitcast_fusion), calls=%async_computation.1 | async-start | bytes 9437184 | tf_op jit(solution)/shard_map/all_to_all | solution.py:128
  254.1 103.2 %all-to-all-done.1 = bf16[16,1,72,2048]{3,2,1,0:T(8,128)(2,1)} async-done(((bf16[16,1,72,2048]{3,2,1,0:T(8,128)(2,1)}), bf16[16,1,72,2048]{3,2,1,0:T(8,128)(2,1)}, u32[]{:S(2)}, u32[]{:S(2)}) %all-to-all-start.1) | async-done | bytes 4718624 | tf_op jit(solution)/shard_map/all_to_all | solution.py:128
  357.3 11.8 %gather_fusion = bf16[1024,2048]{1,0:T(8,128)(2,1)} fusion(bf16[1152,2048]{1,0:T(8,128)(2,1)} %bitcast.36, s32[1024]{0:T(1024)S(1)} %broadcast_clamp_fusion), kind=kCustom, calls=%fused_computation | custom fusion | bytes 8392704 | tf_op jit(solution)/shard_map/jit(_take)/gather | solution.py:138
  369.1 5.6 %multiply_reduce_fusion = f32[128,2048]{1,0:T(8,128)S(1)} fusion(bf16[1024,2048]{1,0:T(8,128)(2,1)} %gather_fusion, f32[128,8]{1,0:T(8,128)S(1)} %copy.85, pred[128,8]{1,0:T(8,128)(4,1)S(1)} %copy.91), kind=kLoop, calls=%fused_computation.22 | loop fusion | flops 8126464 | bytes 5248000 | tf_op jit(solution)/shard_map/reduce_sum | solution.py:139
  374.7 1.3 add_convert_fusion
  (65 shorter events, 1.7 us)
Async XLA Ops:
  6.5 232.4 %copy-start = (bf16[1,384,2048]{2,1,0:T(8,128)(2,1)S(1)}, bf16[1,384,2048]{2,1,0:T(8,128)(2,1)}, u32[]{:S(2)}) copy-start(bf16[1,384,2048]{2,1,0:T(8,128)(2,1)} %param.25) | copy-start | bytes 4718596
  6.5 41.3 %all-gather.4.cloned.1.call-start = ((), (), s32[]{:S(2)}) async-start(), calls=%async_computation.2 | async-start | bytes 1114112 | tf_op jit(solution)/shard_map/all_gather | solution.py:69
  7.3 79.6 %all-gather.6.cloned.1.call-start = ((), (), s32[]{:S(2)}) async-start(), calls=%async_computation.3 | async-start | bytes 1114112 | tf_op jit(solution)/shard_map/all_gather | solution.py:70
  95.3 1.8 copy-start.3
  98.6 1.0 copy-start.4
  102.7 1.8 copy-start.3
  106.0 1.0 copy-start.4
  109.0 2.3 copy-start.2
  109.0 2.8 copy-start.6
  113.4 121.7 %copy-start.8 = (bf16[1,2048,384]{2,1,0:T(8,128)(2,1)S(1)}, bf16[1,2048,384]{2,1,0:T(8,128)(2,1)}, u32[]{:S(2)}) copy-start(bf16[1,2048,384]{2,1,0:T(8,128)(2,1)} %param.24) | copy-start | bytes 4718596
  232.9 2.2 copy-start.1
  248.1 5.5 %copy-start.5 = (s32[128,8]{0,1:T(8,128)S(1)}, s32[128,8]{0,1:T(8,128)}, u32[]{:S(2)}) copy-start(s32[128,8]{0,1:T(8,128)} %param.21) | copy-start | bytes 12292
  248.1 5.8 %copy-start.7 = (f32[128,8]{0,1:T(8,128)S(1)}, f32[128,8]{0,1:T(8,128)}, u32[]{:S(2)}) copy-start(f32[128,8]{0,1:T(8,128)} %param.22) | copy-start | bytes 12292
  248.1 109.2 %all-to-all-start.1 = ((bf16[16,1,72,2048]{3,2,1,0:T(8,128)(2,1)}), bf16[16,1,72,2048]{3,2,1,0:T(8,128)(2,1)}, u32[]{:S(2)}, u32[]{:S(2)}) async-start(bf16[16,1,72,2048]{3,2,1,0:T(8,128)(2,1)} %convert_bitcast_fusion), calls=%async_computation.1 | async-start | bytes 9437184 | tf_op jit(solution)/shard_map/all_to_all | solution.py:128
Sparse Core Ops, SparseCore 0:
  9.5 38.2 all-gather.3
  50.0 36.8 all-gather.5
where the time goes:
time: 384 us; the launch traced here: 383 us
  waiting for transfers between devices  154 us (40%)
  blocking collectives  135 us (35%)
  local copies, waits for them, and re-layouts  27.6 us (7%)
  other arithmetic  21.9 us (6%)
  matrix products  19.4 us (5%)
  between operations  14.2 us (4%)
  starting transfers between devices  5.53 us (1%)
  loops' own time  5.21 us (1%)
    all_to_all x1, blocking collectives, on_device(): lax.all_to_all(outgoing, 'ctx', split_axis=0, concat_axis=0, tiled=True)  119 us
    all_to_all x1, waiting for transfers between devices, on_device(): lax.all_to_all(jnp.einsum('sech,ehd->secd', act, down_weight, preferred_e...  103 us
    all_gather x1, waiting for transfers between devices, on_device(): value_part = lax.all_gather(value_matrix, 'ctx', axis=0, tiled=True)  37.6 us
    all_gather x1, blocking collectives, on_device(): pos_part = lax.all_gather(positions, 'ctx', axis=0, tiled=True)  15.5 us
    all_gather x1, waiting for transfers between devices, on_device(): key_part = lax.all_gather(rotated_keys, 'ctx', axis=0, tiled=True)  11.8 us
    gather x1, local copies, waits for them, and re-layouts, on_device(): jnp.take(flat_back, slot_ids, axis=0).reshape(tok_rows, top_count, D)  11.8 us
    dot_general x1, matrix products, on_device(): jnp.einsum('sech,ehd->secd', act, down_weight, preferred_element_type=jnp...  9.23 us
    unnamed x20, local copies, waits for them, and re-layouts  8.46 us
  transfers between devices with their start and end apart: 3, of which 3 were waited for; matrix products, arithmetic and copies ran while one was open for 4% of the time, Pallas kernels for 0%

commit v1 on v0

--- a/solution.py
+++ b/solution.py
@@ -1,18 +1,331 @@
+import functools
 import math
 
 import jax
 import jax.numpy as jnp
 from jax import lax
+from jax.experimental import pallas as pl
+from jax.experimental.pallas import tpu as pltpu
 from jax.sharding import PartitionSpec as P
 
 D = 2048
 HEAD_SIZE = 128
+CORES = 2
+EXTRA = 16
 
 
 NEG = -1e30
 
 
-def on_device(
+def ring_pairs(chips):
+    order = list(range(0, chips, 2)) + list(range(chips - 1, 0, -2))
+    onward = [
+        (order[i] * CORES + core, order[(i + 1) % chips] * CORES + core)
+        for i in range(chips)
+        for core in range(CORES)
+    ]
+    back = [(b, a) for a, b in onward]
+    swap = [(i, i ^ 1) for i in range(chips * CORES)]
+    return onward, back, swap
+
+
+def pack_kernel(pos_ref, key_ref, value_ref, routes_ref, combine_ref, out_ref):
+    rows, width = key_ref.shape
+    top = routes_ref.shape[1]
+    out_ref[0:rows, 0:width] = key_ref[...]
+    out_ref[0:rows, width : 2 * width] = value_ref[...]
+    weight = combine_ref[...]
+    high = weight.astype(jnp.bfloat16)
+    low = (weight - high.astype(jnp.float32)).astype(jnp.bfloat16)
+    lane = lax.broadcasted_iota(jnp.int32, (top, HEAD_SIZE), 1)
+    row = lax.broadcasted_iota(jnp.int32, (top, HEAD_SIZE), 0)
+
+    def put(part, shift):
+        spread = jnp.where(lane == row + shift, 1.0, 0.0).astype(jnp.bfloat16)
+        return jnp.dot(part, spread, preferred_element_type=jnp.float32)
+
+    names = routes_ref[...].astype(jnp.float32).astype(jnp.bfloat16)
+    turned = (put(names, 0) + put(high, top) + put(low, 2 * top)).T
+    out_ref[rows : rows + EXTRA, 0:128] = turned[0:EXTRA].astype(jnp.bfloat16)
+    out_ref[rows : rows + EXTRA, 128:256] = turned[EXTRA : 2 * EXTRA].astype(jnp.bfloat16)
+    place = jnp.full((EXTRA, 2 * width - 256), pos_ref[0].astype(jnp.float32), jnp.float32)
+    out_ref[rows : rows + EXTRA, 256 : 2 * width] = place.astype(jnp.bfloat16)
+
+
+def pack_message(stretch_pos, keys, values, routes, combine):
+    rows, width = keys.shape
+    vmem = pl.BlockSpec(memory_space=pltpu.VMEM)
+    return pl.pallas_call(
+        pack_kernel,
+        out_shape=jax.ShapeDtypeStruct((rows + EXTRA, 2 * width), jnp.bfloat16),
+        in_specs=[pl.BlockSpec(memory_space=pltpu.SMEM), vmem, vmem, vmem, vmem],
+        out_specs=vmem,
+        name="pack_message",
+    )(stretch_pos, keys, values, routes, combine)
+
+
+def attend_kernel(count, *refs):
+    query_ref, residual_ref, gain_ref = refs[:3]
+    messages = refs[3 : 3 + count]
+    hidden_ref, normed_ref, key_ext, value_ext = refs[3 + count :]
+    rows = query_ref.shape[0]
+    kv_heads = key_ext.shape[0]
+    heads = query_ref.shape[1] // HEAD_SIZE
+    group = heads // kv_heads
+    span = count * rows
+    width = kv_heads * HEAD_SIZE
+    sub = lax.broadcasted_iota(jnp.int32, (rows, rows), 0)
+    lane = lax.broadcasted_iota(jnp.int32, (rows, rows), 1)
+    ahead = (sub - lane).astype(jnp.float32)
+    own_pos = messages[0][rows : rows + EXTRA, 256 : 256 + rows][0:1].astype(jnp.float32)
+    ones = jnp.ones((rows, HEAD_SIZE), jnp.bfloat16)
+    for block in range(count):
+        ref = messages[block]
+        at = slice(block * rows, (block + 1) * rows)
+        pos = ref[rows : rows + EXTRA, 256 : 256 + rows][0:1].astype(jnp.float32)
+        later = (pos - own_pos) * float(rows) + ahead
+        bias = jnp.where(later > 0.0, NEG, 0.0).astype(jnp.bfloat16)
+        for a in range(kv_heads):
+            key_ext[a, at, 0:HEAD_SIZE] = ref[0:rows, a * HEAD_SIZE : (a + 1) * HEAD_SIZE]
+            key_ext[a, at, HEAD_SIZE : HEAD_SIZE + rows] = bias
+            value_ext[a, at, 0:HEAD_SIZE] = ref[
+                0:rows, width + a * HEAD_SIZE : width + (a + 1) * HEAD_SIZE
+            ]
+            value_ext[a, at, HEAD_SIZE : 2 * HEAD_SIZE] = ones
+    eye = jnp.where(sub == lane, 1.0, 0.0).astype(jnp.bfloat16)
+    rate = math.log2(math.e) / math.sqrt(HEAD_SIZE)
+    step = min(512, span)
+    pair = 2
+    squares = jnp.zeros((rows, HEAD_SIZE), jnp.float32)
+    for first in range(0, heads, pair):
+        a = first // group
+        stacked = jnp.concatenate(
+            [
+                jnp.concatenate([query_ref[:, h * HEAD_SIZE : (h + 1) * HEAD_SIZE], eye], axis=1)
+                for h in range(first, first + pair)
+            ],
+            axis=0,
+        )
+        scores = [
+            lax.dot_general(
+                stacked,
+                key_ext[a, at : at + step, :],
+                (((1,), (1,)), ((), ())),
+                preferred_element_type=jnp.float32,
+            )
+            for at in range(0, span, step)
+        ]
+        best = functools.reduce(jnp.maximum, scores)
+        best = jnp.max(best, axis=1, keepdims=True)
+        total = None
+        for i, part in enumerate(scores):
+            probs = jnp.exp2((part - best) * rate).astype(jnp.bfloat16)
+            term = jnp.dot(
+                probs,
+                value_ext[a, i * step : (i + 1) * step, :],
+                preferred_element_type=jnp.float32,
+            )
+            total = term if total is None else total + term
+        attended = (total[:, 0:HEAD_SIZE] / total[:, HEAD_SIZE:]).astype(jnp.bfloat16)
+        for j in range(pair):
+            cols = slice((first + j) * HEAD_SIZE, (first + j + 1) * HEAD_SIZE)
+            state = residual_ref[:, cols].astype(jnp.float32) + attended[
+                j * rows : (j + 1) * rows
+            ].astype(jnp.float32)
+            hidden_ref[:, cols] = state
+            squares = squares + state * state
+    meansq = jnp.sum(squares, axis=1, keepdims=True) / float(heads * HEAD_SIZE)
+    inverse = lax.rsqrt(meansq + 1e-06)
+    for h in range(heads):
+        cols = slice(h * HEAD_SIZE, (h + 1) * HEAD_SIZE)
+        normed_ref[:, cols] = (hidden_ref[:, cols] * inverse * gain_ref[:, cols]).astype(
+            jnp.bfloat16
+        )
+
+
+def attend(queries, residual, gain, messages):
+    rows, features = queries.shape
+    count = len(messages)
+    kv_heads = messages[0].shape[1] // (2 * HEAD_SIZE)
+    vmem = pl.BlockSpec(memory_space=pltpu.VMEM)
+    span = count * rows
+    return pl.pallas_call(
+        functools.partial(attend_kernel, count),
+        out_shape=(
+            jax.ShapeDtypeStruct((rows, features), jnp.float32),
+            jax.ShapeDtypeStruct((rows, features), jnp.bfloat16),
+        ),
+        in_specs=[vmem] * (3 + count),
+        out_specs=(vmem, vmem),
+        scratch_shapes=[
+            pltpu.VMEM((kv_heads, span, 2 * HEAD_SIZE), jnp.bfloat16),
+            pltpu.VMEM((kv_heads, span, 2 * HEAD_SIZE), jnp.bfloat16),
+        ],
+        compiler_params=pltpu.CompilerParams(vmem_limit_bytes=40 * 1024 * 1024),
+        cost_estimate=pl.CostEstimate(
+            flops=8 * rows * span * features, bytes_accessed=8 * 1024 * 1024, transcendentals=0
+        ),
+        name="attend",
+    )(queries, residual, gain.reshape(1, features), *messages)
+
+
+def expert_kernel(blocks, *refs):
+    own_ref = refs[0]
+    tokens = refs[1 : 1 + blocks]
+    messages = refs[1 + blocks : 1 + 2 * blocks]
+    weights = refs[1 + 2 * blocks : 1 + 2 * blocks + 3 * CORES]
+    outs = refs[1 + 2 * blocks + 3 * CORES : 1 + 3 * blocks + 3 * CORES]
+    rows, features = tokens[0].shape
+    top = 8
+    if blocks == 1:
+        normed = tokens[0][...]
+    else:
+        normed = jnp.concatenate([ref[...] for ref in tokens], axis=0)
+    shares, acts = [], []
+    for e in range(CORES):
+        gate_ref, up_ref = weights[3 * e], weights[3 * e + 1]
+        gate = jnp.dot(normed, gate_ref[0], preferred_element_type=jnp.float32)
+        upper = jnp.dot(normed, up_ref[0], preferred_element_type=jnp.float32)
+        acts.append((gate / (1.0 + jnp.exp(-gate)) * upper).astype(jnp.bfloat16))
+        columns = []
+        for ref in messages:
+            extra = ref[...].astype(jnp.float32)
+            named = extra[0:top, 0:128]
+            value = extra[top : 2 * top, 0:128] + extra[0:top, 128:256]
+            hit = jnp.where(named == own_ref[e].astype(jnp.float32), value, 0.0)
+            line = jnp.sum(hit, axis=0, keepdims=True)
+            columns.append(jnp.broadcast_to(line, (rows, rows)).T)
+        shares.append(columns)
+    step = 512
+    for at in range(0, features, step):
+        parts = [
+            jnp.dot(acts[e], weights[3 * e + 2][0, :, at : at + step], preferred_element_type=jnp.float32)
+            .astype(jnp.bfloat16)
+            .astype(jnp.float32)
+            for e in range(CORES)
+        ]
+        for b in range(blocks):
+            for c in range(0, step, HEAD_SIZE):
+                mixed = sum(
+                    shares[e][b] * parts[e][b * rows : (b + 1) * rows, c : c + HEAD_SIZE]
+                    for e in range(CORES)
+                )
+                outs[b][:, at + c : at + c + HEAD_SIZE] = mixed.astype(jnp.bfloat16)
+
+
+def run_experts(own, tokens, messages, weights):
+    rows, features = tokens[0].shape
+    blocks = len(tokens)
+    hidden = weights[0].shape[2]
+    vmem = pl.BlockSpec(memory_space=pltpu.VMEM)
+    tail = pl.BlockSpec((EXTRA, messages[0].shape[1]), lambda i: (rows // EXTRA, 0))
+
+    def whole(shape):
+        return pl.BlockSpec(shape, lambda i: (0,) * len(shape))
+
+    return pl.pallas_call(
+        functools.partial(expert_kernel, blocks),
+        grid=(1,),
+        out_shape=[jax.ShapeDtypeStruct((rows, features), jnp.bfloat16)] * blocks,
+        in_specs=[pl.BlockSpec(memory_space=pltpu.SMEM)]
+        + [whole((rows, features))] * blocks
+        + [tail] * blocks
+        + [whole(w.shape) for w in weights],
+        out_specs=[whole((rows, features))] * blocks,
+        compiler_params=pltpu.CompilerParams(vmem_limit_bytes=48 * 1024 * 1024),
+        cost_estimate=pl.CostEstimate(
+            flops=12 * blocks * rows * features * hidden,
+            bytes_accessed=12 * features * hidden,
+            transcendentals=0,
+        ),
+        name="experts",
+    )(own, *tokens, *messages, *weights)
+
+
+def add_parts(*parts):
+    total = parts[0].astype(jnp.float32)
+    for part in parts[1:]:
+        total = total + part.astype(jnp.float32)
+    return total.astype(jnp.bfloat16)
+
+
+def ring_device(
+    queries,
+    rotated_keys,
+    value_matrix,
+    stretch_pos,
+    residual,
+    norm_gain,
+    routes,
+    combine,
+    gate_weight,
+    up_weight,
+    down_weight,
+):
+    chips = lax.axis_size("ctx") // CORES
+    far = chips // 2
+    onward, back, swap = ring_pairs(chips)
+
+    def send(array, pairs):
+        return lax.ppermute(array, "ctx", pairs)
+
+    message = pack_message(stretch_pos, rotated_keys, value_matrix, routes, combine)
+    twins = tuple(send(w, swap) for w in (gate_weight, up_weight, down_weight))
+    weights = (gate_weight, up_weight, down_weight) + twins
+    me = lax.axis_index("ctx").astype(jnp.int32)
+    own = jnp.stack([me, me ^ 1])
+
+    left, right = {0: message}, {0: message}
+    for hop in range(1, far + 1):
+        left[hop] = send(left[hop - 1], onward)
+        if hop < far:
+            right[hop] = send(right[hop - 1], back)
+    plane = [message] + [left[h] for h in range(1, far + 1)] + [right[h] for h in range(1, far)]
+    everything = plane + [send(m, swap) for m in plane]
+    hidden_state, normed = attend(queries, residual, norm_gain, everything)
+
+    half = normed.shape[0] // 2
+    from_left, from_right = {0: normed}, {0: normed}
+    for hop in range(1, far):
+        from_left[hop] = send(from_left[hop - 1], onward)
+        from_right[hop] = send(from_right[hop - 1], back)
+    upper_half = send(from_left[far - 1][:half], onward)
+    lower_half = send(from_right[far - 1][half:], back)
+
+    out_left, out_right = {}, {}
+    (own_out,) = run_experts(own, [normed], [message], weights)
+    for hop in range(1, far):
+        out_left[hop], out_right[hop] = run_experts(
+            own, [from_left[hop], from_right[hop]], [left[hop], right[hop]], weights
+        )
+    (out_far,) = run_experts(
+        own, [jnp.concatenate([upper_half, lower_half], axis=0)], [left[far]], weights
+    )
+
+    moving_on = send(out_far[:half], onward)
+    moving_back = send(out_far[half:], back)
+    for hop in range(far - 1, 0, -1):
+        if hop == far - 1:
+            ready_on = jnp.concatenate(
+                [add_parts(moving_on, out_right[hop][:half]), out_right[hop][half:]], axis=0
+            )
+            ready_back = jnp.concatenate(
+                [out_left[hop][:half], add_parts(moving_back, out_left[hop][half:])], axis=0
+            )
+        else:
+            ready_on = add_parts(moving_on, out_right[hop])
+            ready_back = add_parts(moving_back, out_left[hop])
+        moving_on = send(ready_on, onward)
+        moving_back = send(ready_back, back)
+    mixture = (
+        own_out.astype(jnp.float32)
+        + moving_on.astype(jnp.float32)
+        + moving_back.astype(jnp.float32)
+    )
+    return (hidden_state + mixture).astype(jnp.bfloat16)
+
+
+def exchange_device(
     queries,
     rotated_keys,
     value_matrix,
@@ -154,6 +467,14 @@
         P("ctx", None, None),
         P("ctx", None, None),
     )
+    ctx_count = mesh.shape["ctx"]
+
+    def on_device(*arguments):
+        routes, gate_weight = arguments[6], arguments[8]
+        dense = 4 * routes.shape[1] >= gate_weight.shape[0] * ctx_count
+        ringed = gate_weight.shape[0] == 1 and ctx_count % (2 * CORES) == 0
+        return (ring_device if dense and ringed else exchange_device)(*arguments)
+
     return jax.shard_map(
         on_device, mesh=mesh, in_specs=placed, out_specs=P(("groups", "ctx"), None), check_vma=False
     )

time: 384 us -> 152 us (0.40)
  the two profiles are of different devices: /device:TPU:13 before, /device:TPU:0 now
where the time goes in v1:
time: 152 us
  waiting for transfers between devices  69.1 us (45%)
  Pallas kernels  36.2 us (24%)
  starting transfers between devices  27.4 us (18%)
  local copies, waits for them, and re-layouts  15 us (10%)
  other arithmetic  2.94 us (2%)
    ppermute x34, waiting for transfers between devices, send(): return lax.ppermute(array, 'ctx', pairs)  69.1 us
    pallas_call x5, Pallas kernels, run_experts(): pl.pallas_call(functools.partial(expert_kernel, blocks), grid=(1,), out_s...  28.3 us
    ppermute x34, starting transfers between devices, send(): return lax.ppermute(array, 'ctx', pairs)  27.4 us
    unnamed x68, local copies, waits for them, and re-layouts  13.4 us
    pallas_call x1, Pallas kernels, attend(): pl.pallas_call(functools.partial(attend_kernel, count), out_shape=(jax.Sh...  6.09 us
  transfers between devices with their start and end apart: 34, of which 16 were waited for; matrix products, arithmetic and copies ran while one was open for 2% of the time, Pallas kernels for 16%

profile of v1, /device:TPU:0, one launch (start us, length us, event | category | flops | bytes accessed | tf_op | source)
XLA Modules:
  0.0 151.7 jit_solution(6141802829328778631)
XLA Ops:
  0.7 1.4 copy.12.routes_ref
  2.1 1.4 copy.13.combine_ref
  3.5 1.8 %pack_message.1.refs_3_.refs_2_ = bf16[144,512]{1,0:T(8,128)(2,1)} custom-call(s32[1]{0:T(128)S(6)} %copy.14.pos_ref, bf16[128,256]{1,0:T(8,128)(2,1)} %key_ref.1, bf16[128,256]{1,0:T(8,128)(2,1)} %value_ref.1, s32[128,8]{1,0:T(8,128)} %copy.12.routes_ref, f32[128,8]{1,0:T(8,128)} %copy.13.combine_ref), custom_call_target="tpu_custom_call" | custom-call | tf_op jit(solution)/shard_map/pack_message/pallas_call | solution.py:58
  5.3 3.0 %collective-permute-start = (bf16[144,512]{1,0:T(8,128)(2,1)}, bf16[144,512]{1,0:T(8,128)(2,1)S(1)}, u32[]{:S(2)}, u32[]{:S(2)}) collective-permute-start(bf16[144,512]{1,0:T(8,128)(2,1)} %pack_message.1.refs_3_.refs_2_), channel_id=1, source_target_pairs={{0,4},{1,5},{4,8},{5,9},{8,12},{9,13},{12,14},{13,15},{14,10},{15,... | collective-permute-start | bytes 442376 | tf_op jit(solution)/shard_map/ppermute | solution.py:270
  8.3 4.0 %collective-permute-done.refs_4_.refs_3_ = bf16[144,512]{1,0:T(8,128)(2,1)S(1)} collective-permute-done((bf16[144,512]{1,0:T(8,128)(2,1)}, bf16[144,512]{1,0:T(8,128)(2,1)S(1)}, u32[]{:S(2)}, u32[]{:S(2)}) %collective-permute-start) | collective-permute-done | bytes 147488 | tf_op jit(solution)/shard_map/ppermute | solution.py:270
  12.3 1.8 %collective-permute-start.1 = (bf16[144,512]{1,0:T(8,128)(2,1)S(1)}, bf16[144,512]{1,0:T(8,128)(2,1)S(1)}, u32[]{:S(2)}, u32[]{:S(2)}) collective-permute-start(bf16[144,512]{1,0:T(8,128)(2,1)S(1)} %collective-permute-done.refs_4_.refs_3_), channel_id=1, source_target_pairs={{0,4},{1,5},{4,8},{5,9},{8,12},{9,13},{12,14},{13,15},{14,10},{15,... | collective-permute-start | bytes 442376 | tf_op jit(solution)/shard_map/ppermute | solution.py:270
  14.3 3.1 %collective-permute-done.1.refs_5_.refs_3_ = bf16[144,512]{1,0:T(8,128)(2,1)S(1)} collective-permute-done((bf16[144,512]{1,0:T(8,128)(2,1)S(1)}, bf16[144,512]{1,0:T(8,128)(2,1)S(1)}, u32[]{:S(2)}, u32[]{:S(2)}) %collective-permute-start.1) | collective-permute-done | bytes 147488 | tf_op jit(solution)/shard_map/ppermute | solution.py:270
  17.5 1.8 %collective-permute-start.2 = (bf16[144,512]{1,0:T(8,128)(2,1)S(1)}, bf16[144,512]{1,0:T(8,128)(2,1)S(1)}, u32[]{:S(2)}, u32[]{:S(2)}) collective-permute-start(bf16[144,512]{1,0:T(8,128)(2,1)S(1)} %collective-permute-done.1.refs_5_.refs_3_), channel_id=1, source_target_pairs={{0,4},{1,5},{4,8},{5,9},{8,12},{9,13},{12,14},{13,15},{14,10},{15,... | collective-permute-start | bytes 442376 | tf_op jit(solution)/shard_map/ppermute | solution.py:270
  20.1 2.5 %collective-permute-done.2.refs_6_.refs_3_ = bf16[144,512]{1,0:T(8,128)(2,1)S(1)} collective-permute-done((bf16[144,512]{1,0:T(8,128)(2,1)S(1)}, bf16[144,512]{1,0:T(8,128)(2,1)S(1)}, u32[]{:S(2)}, u32[]{:S(2)}) %collective-permute-start.2) | collective-permute-done | bytes 147488 | tf_op jit(solution)/shard_map/ppermute | solution.py:270
  22.6 1.8 %collective-permute-start.3 = (bf16[144,512]{1,0:T(8,128)(2,1)S(1)}, bf16[144,512]{1,0:T(8,128)(2,1)S(1)}, u32[]{:S(2)}, u32[]{:S(2)}) collective-permute-start(bf16[144,512]{1,0:T(8,128)(2,1)S(1)} %collective-permute-done.2.refs_6_.refs_3_), channel_id=1, source_target_pairs={{0,4},{1,5},{4,8},{5,9},{8,12},{9,13},{12,14},{13,15},{14,10},{15,... | collective-permute-start | bytes 442376 | tf_op jit(solution)/shard_map/ppermute | solution.py:270
  25.0 1.0 collective-permute-done.6.refs_10_.refs_4_
  26.0 1.7 %collective-permute-done.3.refs_7_.refs_2_ = bf16[144,512]{1,0:T(8,128)(2,1)S(1)} collective-permute-done((bf16[144,512]{1,0:T(8,128)(2,1)S(1)}, bf16[144,512]{1,0:T(8,128)(2,1)S(1)}, u32[]{:S(2)}, u32[]{:S(2)}) %collective-permute-start.3) | collective-permute-done | bytes 147488 | tf_op jit(solution)/shard_map/ppermute | solution.py:270
  27.8 1.3 collective-permute-done.11.refs_15_
  29.1 0.9 copy-done.8
  30.0 1.0 copy-done.30
  31.1 1.0 copy-done.31
  32.8 6.1 %attend.1 = (f32[128,2048]{1,0:T(8,128)S(1)}, bf16[128,2048]{1,0:T(8,128)(2,1)S(1)}) custom-call(bf16[128,2048]{1,0:T(8,128)(2,1)S(1)} %copy-done.30, bf16[128,2048]{1,0:T(8,128)(2,1)S(1)} %copy-done.31, f32[1,2048]{1,0:T(1,128)S(1)} %bitcast.3, bf16[144,512]{1,0:T(8,128)(2,1)S(1)} %copy-done.8, bf16[144,512]{1,0:T(8,128)(2,1)S(1)} %collective-permute-done.refs_4_.refs_3_, ...), custom_call_target="tpu_custom_call" | custom-call | flops 4294967296 | bytes 8388608 | tf_op jit(solution)/shard_map/attend/pallas_call | solution.py:152
  39.0 1.0 copy-done.6
  40.0 1.7 %collective-permute-start.22 = (bf16[128,2048]{1,0:T(8,128)(2,1)S(1)}, bf16[128,2048]{1,0:T(8,128)(2,1)S(1)}, u32[]{:S(2)}, u32[]{:S(2)}) collective-permute-start(bf16[128,2048]{1,0:T(8,128)(2,1)S(1)} %get-tuple-element.14.refs_1_), channel_id=1, source_target_pairs={{4,0},{5,1},{8,4},{9,5},{12,8},{13,9},{14,12},{15,13},{10,14},{11,... | collective-permute-start | bytes 1572872 | tf_op jit(solution)/shard_map/ppermute | solution.py:270
  42.6 11.4 %collective-permute-done.22.refs_2_ = bf16[128,2048]{1,0:T(8,128)(2,1)S(1)} collective-permute-done((bf16[128,2048]{1,0:T(8,128)(2,1)S(1)}, bf16[128,2048]{1,0:T(8,128)(2,1)S(1)}, u32[]{:S(2)}, u32[]{:S(2)}) %collective-permute-start.22) | collective-permute-done | bytes 524320 | tf_op jit(solution)/shard_map/ppermute | solution.py:270
  54.0 1.7 %collective-permute-start.23 = (bf16[128,2048]{1,0:T(8,128)(2,1)S(1)}, bf16[128,2048]{1,0:T(8,128)(2,1)S(1)}, u32[]{:S(2)}, u32[]{:S(2)}) collective-permute-start(bf16[128,2048]{1,0:T(8,128)(2,1)S(1)} %collective-permute-done.22.refs_2_), channel_id=1, source_target_pairs={{4,0},{5,1},{8,4},{9,5},{12,8},{13,9},{14,12},{15,13},{10,14},{11,... | collective-permute-start | bytes 1572872 | tf_op jit(solution)/shard_map/ppermute | solution.py:270
  56.8 0.8 copy-done.14
  57.6 9.6 %collective-permute-done.23.refs_2_ = bf16[128,2048]{1,0:T(8,128)(2,1)S(1)} collective-permute-done((bf16[128,2048]{1,0:T(8,128)(2,1)S(1)}, bf16[128,2048]{1,0:T(8,128)(2,1)S(1)}, u32[]{:S(2)}, u32[]{:S(2)}) %collective-permute-start.23) | collective-permute-done | bytes 524320 | tf_op jit(solution)/shard_map/ppermute | solution.py:270
  67.2 1.6 %collective-permute-start.24 = (bf16[128,2048]{1,0:T(8,128)(2,1)S(1)}, bf16[128,2048]{1,0:T(8,128)(2,1)S(1)}, u32[]{:S(2)}, u32[]{:S(2)}) collective-permute-start(bf16[128,2048]{1,0:T(8,128)(2,1)S(1)} %collective-permute-done.23.refs_2_), channel_id=1, source_target_pairs={{4,0},{5,1},{8,4},{9,5},{12,8},{13,9},{14,12},{15,13},{10,14},{11,... | collective-permute-start | bytes 1572872 | tf_op jit(solution)/shard_map/ppermute | solution.py:270
  68.8 0.8 copy-done.16
  70.1 0.8 copy-done.18
  70.9 8.6 %collective-permute-done.24.refs_2_ = bf16[128,2048]{1,0:T(8,128)(2,1)S(1)} collective-permute-done((bf16[128,2048]{1,0:T(8,128)(2,1)S(1)}, bf16[128,2048]{1,0:T(8,128)(2,1)S(1)}, u32[]{:S(2)}, u32[]{:S(2)}) %collective-permute-start.24) | collective-permute-done | bytes 524320 | tf_op jit(solution)/shard_map/ppermute | solution.py:270
  80.2 0.8 copy-done.2
  81.0 1.6 %collective-permute-start.25 = (bf16[64,2048]{1,0:T(8,128)(2,1)}, bf16[64,2048]{1,0:T(8,128)(2,1)}, u32[]{:S(2)}, u32[]{:S(2)}) collective-permute-start(bf16[64,2048]{1,0:T(8,128)(2,1)} %slice.33), channel_id=1, source_target_pairs={{4,0},{5,1},{8,4},{9,5},{12,8},{13,9},{14,12},{15,13},{10,14},{11,... | collective-permute-start | bytes 786440 | tf_op jit(solution)/shard_map/ppermute | solution.py:270
  83.3 0.8 copy-done.4
  84.7 3.1 %collective-permute-done.25 = bf16[64,2048]{1,0:T(8,128)(2,1)} collective-permute-done((bf16[64,2048]{1,0:T(8,128)(2,1)}, bf16[64,2048]{1,0:T(8,128)(2,1)}, u32[]{:S(2)}, u32[]{:S(2)}) %collective-permute-start.25) | collective-permute-done | bytes 262176 | tf_op jit(solution)/shard_map/ppermute | solution.py:270
  87.7 3.1 %collective-permute-done.21 = bf16[64,2048]{1,0:T(8,128)(2,1)} collective-permute-done((bf16[64,2048]{1,0:T(8,128)(2,1)}, bf16[64,2048]{1,0:T(8,128)(2,1)}, u32[]{:S(2)}, u32[]{:S(2)}) %collective-permute-start.21) | collective-permute-done | bytes 262176 | tf_op jit(solution)/shard_map/ppermute | solution.py:270
  90.8 1.1 pad_maximum_fusion.refs_1_
  92.0 1.0 copy-done.29
  93.0 4.7 %experts.6 = bf16[128,2048]{1,0:T(8,128)(2,1)S(1)} custom-call(s32[2]{0:T(128)S(1)} %pad_add_fusion.refs_0_, bf16[128,2048]{1,0:T(8,128)(2,1)S(1)} %pad_maximum_fusion.refs_1_, bf16[144,512]{1,0:T(8,128)(2,1)S(1)} %copy-done.29, bf16[1,2048,384]{2,1,0:T(8,128)(2,1)S(1)} %copy-done, bf16[1,2048,384]{2,1,0:T(8,128)(2,1)S(1)} %copy-done.1, ...), custom_call_target="tpu_custom_call" | custom-call | flops 1207959552 | bytes 9437184 | tf_op jit(solution)/shard_map/experts/pallas_call | solution.py:226
  97.7 1.8 %collective-permute-start.30 = (bf16[64,2048]{1,0:T(8,128)(2,1)S(1)}, bf16[64,2048]{1,0:T(8,128)(2,1)S(1)}, u32[]{:S(2)}, u32[]{:S(2)}) collective-permute-start(bf16[64,2048]{1,0:T(8,128)(2,1)S(1)} %get-tuple-element.22), channel_id=1, source_target_pairs={{4,0},{5,1},{8,4},{9,5},{12,8},{13,9},{14,12},{15,13},{10,14},{11,... | collective-permute-start | bytes 786440 | tf_op jit(solution)/shard_map/ppermute | solution.py:270
  99.5 6.3 %experts.7 = (bf16[128,2048]{1,0:T(8,128)(2,1)S(1)}, bf16[128,2048]{1,0:T(8,128)(2,1)S(1)}) custom-call(s32[2]{0:T(128)S(1)} %pad_add_fusion.refs_0_, bf16[128,2048]{1,0:T(8,128)(2,1)S(1)} %copy-done.5, bf16[128,2048]{1,0:T(8,128)(2,1)S(1)} %copy-done.3, bf16[144,512]{1,0:T(8,128)(2,1)S(1)} %copy-done.25, bf16[144,512]{1,0:T(8,128)(2,1)S(1)} %copy-done.27, ...), custom_call_target="tpu_custom_call" | custom-call | flops 2415919104 | bytes 9437184 | tf_op jit(solution)/shard_map/experts/pallas_call | solution.py:226
  106.6 1.6 %collective-permute-start.31 = (bf16[128,2048]{1,0:T(8,128)(2,1)S(1)}, bf16[128,2048]{1,0:T(8,128)(2,1)S(1)}, u32[]{:S(2)}, u32[]{:S(2)}) collective-permute-start(bf16[128,2048]{1,0:T(8,128)(2,1)S(1)} %pad_maximum_fusion.2), channel_id=1, source_target_pairs={{4,0},{5,1},{8,4},{9,5},{12,8},{13,9},{14,12},{15,13},{10,14},{11,... | collective-permute-start | bytes 1572872 | tf_op jit(solution)/shard_map/ppermute | solution.py:270
  108.2 6.5 %collective-permute-done.26 = bf16[64,2048]{1,0:T(8,128)(2,1)S(1)} collective-permute-done((bf16[64,2048]{1,0:T(8,128)(2,1)S(1)}, bf16[64,2048]{1,0:T(8,128)(2,1)S(1)}, u32[]{:S(2)}, u32[]{:S(2)}) %collective-permute-start.26) | collective-permute-done | bytes 262176 | tf_op jit(solution)/shard_map/ppermute | solution.py:270
  115.4 6.3 %experts.8 = (bf16[128,2048]{1,0:T(8,128)(2,1)S(1)}, bf16[128,2048]{1,0:T(8,128)(2,1)S(1)}) custom-call(s32[2]{0:T(128)S(1)} %pad_add_fusion.refs_0_, bf16[128,2048]{1,0:T(8,128)(2,1)S(1)} %copy-done.19, bf16[128,2048]{1,0:T(8,128)(2,1)S(1)} %copy-done.17, bf16[144,512]{1,0:T(8,128)(2,1)S(1)} %copy-done.21, bf16[144,512]{1,0:T(8,128)(2,1)S(1)} %copy-done.23, ...), custom_call_target="tpu_custom_call" | custom-call | flops 2415919104 | bytes 9437184 | tf_op jit(solution)/shard_map/experts/pallas_call | solution.py:226
  121.9 1.6 %collective-permute-start.32 = (bf16[128,2048]{1,0:T(8,128)(2,1)S(1)}, bf16[128,2048]{1,0:T(8,128)(2,1)S(1)}, u32[]{:S(2)}, u32[]{:S(2)}) collective-permute-start(bf16[128,2048]{1,0:T(8,128)(2,1)S(1)} %add_convert_fusion.2), channel_id=1, source_target_pairs={{4,0},{5,1},{8,4},{9,5},{12,8},{13,9},{14,12},{15,13},{10,14},{11,... | collective-permute-start | bytes 1572872 | tf_op jit(solution)/shard_map/ppermute | solution.py:270
  123.5 4.1 %collective-permute-done.27 = bf16[128,2048]{1,0:T(8,128)(2,1)S(1)} collective-permute-done((bf16[128,2048]{1,0:T(8,128)(2,1)S(1)}, bf16[128,2048]{1,0:T(8,128)(2,1)S(1)}, u32[]{:S(2)}, u32[]{:S(2)}) %collective-permute-start.27) | collective-permute-done | bytes 524320 | tf_op jit(solution)/shard_map/ppermute | solution.py:270
  128.2 6.3 %experts.9 = (bf16[128,2048]{1,0:T(8,128)(2,1)S(1)}, bf16[128,2048]{1,0:T(8,128)(2,1)S(1)}) custom-call(s32[2]{0:T(128)S(1)} %pad_add_fusion.refs_0_, bf16[128,2048]{1,0:T(8,128)(2,1)S(1)} %copy-done.15, bf16[128,2048]{1,0:T(8,128)(2,1)S(1)} %copy-done.13, bf16[144,512]{1,0:T(8,128)(2,1)S(1)} %collective-permute-done.refs_4_.refs_3_, ...), custom_call_target="tpu_custom_call" | custom-call | flops 2415919104 | bytes 9437184 | tf_op jit(solution)/shard_map/experts/pallas_call | solution.py:226
  135.0 1.6 %collective-permute-start.33 = (bf16[128,2048]{1,0:T(8,128)(2,1)S(1)}, bf16[128,2048]{1,0:T(8,128)(2,1)S(1)}, u32[]{:S(2)}, u32[]{:S(2)}) collective-permute-start(bf16[128,2048]{1,0:T(8,128)(2,1)S(1)} %add_convert_fusion.1), channel_id=1, source_target_pairs={{4,0},{5,1},{8,4},{9,5},{12,8},{13,9},{14,12},{15,13},{10,14},{11,... | collective-permute-start | bytes 1572872 | tf_op jit(solution)/shard_map/ppermute | solution.py:270
  136.6 4.6 %collective-permute-done.28 = bf16[128,2048]{1,0:T(8,128)(2,1)S(1)} collective-permute-done((bf16[128,2048]{1,0:T(8,128)(2,1)S(1)}, bf16[128,2048]{1,0:T(8,128)(2,1)S(1)}, u32[]{:S(2)}, u32[]{:S(2)}) %collective-permute-start.28) | collective-permute-done | bytes 524320 | tf_op jit(solution)/shard_map/ppermute | solution.py:270
  141.8 4.7 %experts.5 = bf16[128,2048]{1,0:T(8,128)(2,1)S(1)} custom-call(s32[2]{0:T(128)S(1)} %pad_add_fusion.refs_0_, bf16[128,2048]{1,0:T(8,128)(2,1)S(1)} %copy-done.11, bf16[144,512]{1,0:T(8,128)(2,1)S(1)} %copy-done.9, bf16[1,2048,384]{2,1,0:T(8,128)(2,1)S(1)} %copy-done, bf16[1,2048,384]{2,1,0:T(8,128)(2,1)S(1)} %copy-done.1, bf16[1,384,2048]{2,1,0:T(8,128)(2,1)} %refs_7_.5, ...), custom_call_target="tpu_custom_call" | custom-call | flops 1207959552 | bytes 9437184 | tf_op jit(solution)/shard_map/experts/pallas_call | solution.py:226
  146.5 4.0 %collective-permute-done.29 = bf16[128,2048]{1,0:T(8,128)(2,1)S(1)} collective-permute-done((bf16[128,2048]{1,0:T(8,128)(2,1)S(1)}, bf16[128,2048]{1,0:T(8,128)(2,1)S(1)}, u32[]{:S(2)}, u32[]{:S(2)}) %collective-permute-start.29) | collective-permute-done | bytes 524320 | tf_op jit(solution)/shard_map/ppermute | solution.py:270
  150.6 1.1 add_convert_fusion
  (111 shorter events, 9.9 us)
Async XLA Ops:
  5.3 7.0 %collective-permute-start = (bf16[144,512]{1,0:T(8,128)(2,1)}, bf16[144,512]{1,0:T(8,128)(2,1)S(1)}, u32[]{:S(2)}, u32[]{:S(2)}) collective-permute-start(bf16[144,512]{1,0:T(8,128)(2,1)} %pack_message.1.refs_3_.refs_2_), channel_id=1, source_target_pairs={{0,4},{1,5},{4,8},{5,9},{8,12},{9,13},{12,14},{13,15},{14,10},{15,... | collective-permute-start | bytes 442376 | tf_op jit(solution)/shard_map/ppermute | solution.py:270
  8.3 5.8 %collective-permute-start.4 = (bf16[144,512]{1,0:T(8,128)(2,1)}, bf16[144,512]{1,0:T(8,128)(2,1)S(1)}, u32[]{:S(2)}, u32[]{:S(2)}) collective-permute-start(bf16[144,512]{1,0:T(8,128)(2,1)} %pack_message.1.refs_3_.refs_2_), channel_id=1, source_target_pairs={{4,0},{5,1},{8,4},{9,5},{12,8},{13,9},{14,12},{15,13},{10,14},{11,... | collective-permute-start | bytes 442376 | tf_op jit(solution)/shard_map/ppermute | solution.py:270
  12.3 5.1 %collective-permute-start.1 = (bf16[144,512]{1,0:T(8,128)(2,1)S(1)}, bf16[144,512]{1,0:T(8,128)(2,1)S(1)}, u32[]{:S(2)}, u32[]{:S(2)}) collective-permute-start(bf16[144,512]{1,0:T(8,128)(2,1)S(1)} %collective-permute-done.refs_4_.refs_3_), channel_id=1, source_target_pairs={{0,4},{1,5},{4,8},{5,9},{8,12},{9,13},{12,14},{13,15},{14,10},{15,... | collective-permute-start | bytes 442376 | tf_op jit(solution)/shard_map/ppermute | solution.py:270
  14.1 5.7 %collective-permute-start.5 = (bf16[144,512]{1,0:T(8,128)(2,1)S(1)}, bf16[144,512]{1,0:T(8,128)(2,1)S(1)}, u32[]{:S(2)}, u32[]{:S(2)}) collective-permute-start(bf16[144,512]{1,0:T(8,128)(2,1)S(1)} %collective-permute-done.4.refs_8_.refs_4_), channel_id=1, source_target_pairs={{4,0},{5,1},{8,4},{9,5},{12,8},{13,9},{14,12},{15,13},{10,14},{11,... | collective-permute-start | bytes 442376 | tf_op jit(solution)/shard_map/ppermute | solution.py:270
  17.5 21.5 %copy-start.20 = (bf16[144,512]{1,0:T(8,128)(2,1)}, bf16[144,512]{1,0:T(8,128)(2,1)S(1)}, u32[]{:S(2)}) copy-start(bf16[144,512]{1,0:T(8,128)(2,1)S(1)} %collective-permute-done.1.refs_5_.refs_3_) | copy-start | bytes 442372
  17.5 5.1 %collective-permute-start.2 = (bf16[144,512]{1,0:T(8,128)(2,1)S(1)}, bf16[144,512]{1,0:T(8,128)(2,1)S(1)}, u32[]{:S(2)}, u32[]{:S(2)}) collective-permute-start(bf16[144,512]{1,0:T(8,128)(2,1)S(1)} %collective-permute-done.1.refs_5_.refs_3_), channel_id=1, source_target_pairs={{0,4},{1,5},{4,8},{5,9},{8,12},{9,13},{12,14},{13,15},{14,10},{15,... | collective-permute-start | bytes 442376 | tf_op jit(solution)/shard_map/ppermute | solution.py:270
  19.3 5.1 %collective-permute-start.7 = (bf16[144,512]{1,0:T(8,128)(2,1)}, bf16[144,512]{1,0:T(8,128)(2,1)S(1)}, u32[]{:S(2)}, u32[]{:S(2)}) collective-permute-start(bf16[144,512]{1,0:T(8,128)(2,1)} %pack_message.1.refs_3_.refs_2_), channel_id=1, source_target_pairs={{0,1},{1,0},{2,3},{3,2},{4,5},{5,4},{6,7},{7,6},{8,9},{9,8},{10,11... | collective-permute-start | bytes 442376 | tf_op jit(solution)/shard_map/ppermute | solution.py:270
  19.3 5.2 %collective-permute-start.8 = (bf16[144,512]{1,0:T(8,128)(2,1)S(1)}, bf16[144,512]{1,0:T(8,128)(2,1)S(1)}, u32[]{:S(2)}, u32[]{:S(2)}) collective-permute-start(bf16[144,512]{1,0:T(8,128)(2,1)S(1)} %collective-permute-done.refs_4_.refs_3_), channel_id=1, source_target_pairs={{0,1},{1,0},{2,3},{3,2},{4,5},{5,4},{6,7},{7,6},{8,9},{9,8},{10,11... | collective-permute-start | bytes 442376 | tf_op jit(solution)/shard_map/ppermute | solution.py:270
  19.8 5.2 %collective-permute-start.12 = (bf16[144,512]{1,0:T(8,128)(2,1)S(1)}, bf16[144,512]{1,0:T(8,128)(2,1)S(1)}, u32[]{:S(2)}, u32[]{:S(2)}) collective-permute-start(bf16[144,512]{1,0:T(8,128)(2,1)S(1)} %collective-permute-done.4.refs_8_.refs_4_), channel_id=1, source_target_pairs={{0,1},{1,0},{2,3},{3,2},{4,5},{5,4},{6,7},{7,6},{8,9},{9,8},{10,11... | collective-permute-start | bytes 442376 | tf_op jit(solution)/shard_map/ppermute | solution.py:270
  19.8 19.2 %copy-start.22 = (bf16[144,512]{1,0:T(8,128)(2,1)}, bf16[144,512]{1,0:T(8,128)(2,1)S(1)}, u32[]{:S(2)}) copy-start(bf16[144,512]{1,0:T(8,128)(2,1)S(1)} %collective-permute-done.5.refs_9_.refs_4_) | copy-start | bytes 442372
  19.8 6.3 %collective-permute-start.6 = (bf16[144,512]{1,0:T(8,128)(2,1)S(1)}, bf16[144,512]{1,0:T(8,128)(2,1)S(1)}, u32[]{:S(2)}, u32[]{:S(2)}) collective-permute-start(bf16[144,512]{1,0:T(8,128)(2,1)S(1)} %collective-permute-done.5.refs_9_.refs_4_), channel_id=1, source_target_pairs={{4,0},{5,1},{8,4},{9,5},{12,8},{13,9},{14,12},{15,13},{10,14},{11,... | collective-permute-start | bytes 442376 | tf_op jit(solution)/shard_map/ppermute | solution.py:270
  22.6 16.3 %copy-start.24 = (bf16[144,512]{1,0:T(8,128)(2,1)}, bf16[144,512]{1,0:T(8,128)(2,1)S(1)}, u32[]{:S(2)}) copy-start(bf16[144,512]{1,0:T(8,128)(2,1)S(1)} %collective-permute-done.2.refs_6_.refs_3_) | copy-start | bytes 442372
  22.6 5.1 %collective-permute-start.3 = (bf16[144,512]{1,0:T(8,128)(2,1)S(1)}, bf16[144,512]{1,0:T(8,128)(2,1)S(1)}, u32[]{:S(2)}, u32[]{:S(2)}) collective-permute-start(bf16[144,512]{1,0:T(8,128)(2,1)S(1)} %collective-permute-done.2.refs_6_.refs_3_), channel_id=1, source_target_pairs={{0,4},{1,5},{4,8},{5,9},{8,12},{9,13},{12,14},{13,15},{14,10},{15,... | collective-permute-start | bytes 442376 | tf_op jit(solution)/shard_map/ppermute | solution.py:270
  24.4 3.3 %collective-permute-start.9 = (bf16[144,512]{1,0:T(8,128)(2,1)S(1)}, bf16[144,512]{1,0:T(8,128)(2,1)S(1)}, u32[]{:S(2)}, u32[]{:S(2)}) collective-permute-start(bf16[144,512]{1,0:T(8,128)(2,1)S(1)} %collective-permute-done.1.refs_5_.refs_3_), channel_id=1, source_target_pairs={{0,1},{1,0},{2,3},{3,2},{4,5},{5,4},{6,7},{7,6},{8,9},{9,8},{10,11... | collective-permute-start | bytes 442376 | tf_op jit(solution)/shard_map/ppermute | solution.py:270
  24.4 3.3 %collective-permute-start.13 = (bf16[144,512]{1,0:T(8,128)(2,1)S(1)}, bf16[144,512]{1,0:T(8,128)(2,1)S(1)}, u32[]{:S(2)}, u32[]{:S(2)}) collective-permute-start(bf16[144,512]{1,0:T(8,128)(2,1)S(1)} %collective-permute-done.5.refs_9_.refs_4_), channel_id=1, source_target_pairs={{0,1},{1,0},{2,3},{3,2},{4,5},{5,4},{6,7},{7,6},{8,9},{9,8},{10,11... | collective-permute-start | bytes 442376 | tf_op jit(solution)/shard_map/ppermute | solution.py:270
  24.9 2.8 %collective-permute-start.10 = (bf16[144,512]{1,0:T(8,128)(2,1)S(1)}, bf16[144,512]{1,0:T(8,128)(2,1)S(1)}, u32[]{:S(2)}, u32[]{:S(2)}) collective-permute-start(bf16[144,512]{1,0:T(8,128)(2,1)S(1)} %collective-permute-done.2.refs_6_.refs_3_), channel_id=1, source_target_pairs={{0,1},{1,0},{2,3},{3,2},{4,5},{5,4},{6,7},{7,6},{8,9},{9,8},{10,11... | collective-permute-start | bytes 442376 | tf_op jit(solution)/shard_map/ppermute | solution.py:270
  26.0 12.9 %copy-start.26 = (bf16[144,512]{1,0:T(8,128)(2,1)}, bf16[144,512]{1,0:T(8,128)(2,1)S(1)}, u32[]{:S(2)}) copy-start(bf16[144,512]{1,0:T(8,128)(2,1)S(1)} %collective-permute-done.6.refs_10_.refs_4_) | copy-start | bytes 442372
  26.0 1.7 %collective-permute-start.14 = (bf16[144,512]{1,0:T(8,128)(2,1)S(1)}, bf16[144,512]{1,0:T(8,128)(2,1)S(1)}, u32[]{:S(2)}, u32[]{:S(2)}) collective-permute-start(bf16[144,512]{1,0:T(8,128)(2,1)S(1)} %collective-permute-done.6.refs_10_.refs_4_), channel_id=1, source_target_pairs={{0,1},{1,0},{2,3},{3,2},{4,5},{5,4},{6,7},{7,6},{8,9},{9,8},{10,11... | collective-permute-start | bytes 442376 | tf_op jit(solution)/shard_map/ppermute | solution.py:270
  27.7 11.2 %copy-start.28 = (bf16[144,512]{1,0:T(8,128)(2,1)}, bf16[144,512]{1,0:T(8,128)(2,1)S(1)}, u32[]{:S(2)}) copy-start(bf16[144,512]{1,0:T(8,128)(2,1)S(1)} %collective-permute-done.3.refs_7_.refs_2_) | copy-start | bytes 442372
  27.7 1.4 collective-permute-start.11
  32.8 9.2 %copy-start = (bf16[1,2048,384]{2,1,0:T(8,128)(2,1)S(1)}, bf16[1,2048,384]{2,1,0:T(8,128)(2,1)}, u32[]{:S(2)}) copy-start(bf16[1,2048,384]{2,1,0:T(8,128)(2,1)} %refs_5_.9) | copy-start | bytes 4718596
  32.8 9.2 %copy-start.1 = (bf16[1,2048,384]{2,1,0:T(8,128)(2,1)S(1)}, bf16[1,2048,384]{2,1,0:T(8,128)(2,1)}, u32[]{:S(2)}) copy-start(bf16[1,2048,384]{2,1,0:T(8,128)(2,1)} %refs_6_.5) | copy-start | bytes 4718596
  40.0 43.4 %copy-start.10 = (bf16[128,2048]{1,0:T(8,128)(2,1)}, bf16[128,2048]{1,0:T(8,128)(2,1)S(1)}, u32[]{:S(2)}) copy-start(bf16[128,2048]{1,0:T(8,128)(2,1)S(1)} %get-tuple-element.14.refs_1_) | copy-start | bytes 1572868
  40.0 14.0 %collective-permute-start.22 = (bf16[128,2048]{1,0:T(8,128)(2,1)S(1)}, bf16[128,2048]{1,0:T(8,128)(2,1)S(1)}, u32[]{:S(2)}, u32[]{:S(2)}) collective-permute-start(bf16[128,2048]{1,0:T(8,128)(2,1)S(1)} %get-tuple-element.14.refs_1_), channel_id=1, source_target_pairs={{4,0},{5,1},{8,4},{9,5},{12,8},{13,9},{14,12},{15,13},{10,14},{11,... | collective-permute-start | bytes 1572872 | tf_op jit(solution)/shard_map/ppermute | solution.py:270
  41.7 14.8 %collective-permute-start.18 = (bf16[128,2048]{1,0:T(8,128)(2,1)S(1)}, bf16[128,2048]{1,0:T(8,128)(2,1)S(1)}, u32[]{:S(2)}, u32[]{:S(2)}) collective-permute-start(bf16[128,2048]{1,0:T(8,128)(2,1)S(1)} %get-tuple-element.14.refs_1_), channel_id=1, source_target_pairs={{0,4},{1,5},{4,8},{5,9},{8,12},{9,13},{12,14},{13,15},{14,10},{15,... | collective-permute-start | bytes 1572872 | tf_op jit(solution)/shard_map/ppermute | solution.py:270
  42.0 49.9 %collective-permute-start.15 = (bf16[1,2048,384]{2,1,0:T(8,128)(2,1)S(1)}, bf16[1,2048,384]{2,1,0:T(8,128)(2,1)}, u32[]{:S(2)}, u32[]{:S(2)}) collective-permute-start(bf16[1,2048,384]{2,1,0:T(8,128)(2,1)S(1)} %copy-done), channel_id=1, source_target_pairs={{0,1},{1,0},{2,3},{3,2},{4,5},{5,4},{6,7},{7,6},{8,9},{9,8},{10,11... | collective-permute-start | bytes 4718600 | tf_op jit(solution)/shard_map/ppermute | solution.py:270
  42.0 49.9 %collective-permute-start.16 = (bf16[1,2048,384]{2,1,0:T(8,128)(2,1)S(1)}, bf16[1,2048,384]{2,1,0:T(8,128)(2,1)}, u32[]{:S(2)}, u32[]{:S(2)}) collective-permute-start(bf16[1,2048,384]{2,1,0:T(8,128)(2,1)S(1)} %copy-done.1), channel_id=1, source_target_pairs={{0,1},{1,0},{2,3},{3,2},{4,5},{5,4},{6,7},{7,6},{8,9},{9,8},{10,11... | collective-permute-start | bytes 4718600 | tf_op jit(solution)/shard_map/ppermute | solution.py:270
  42.5 49.4 %collective-permute-start.17 = (bf16[1,384,2048]{2,1,0:T(8,128)(2,1)}, bf16[1,384,2048]{2,1,0:T(8,128)(2,1)}, u32[]{:S(2)}, u32[]{:S(2)}) collective-permute-start(bf16[1,384,2048]{2,1,0:T(8,128)(2,1)} %refs_7_.5), channel_id=1, source_target_pairs={{0,1},{1,0},{2,3},{3,2},{4,5},{5,4},{6,7},{7,6},{8,9},{9,8},{10,11... | collective-permute-start | bytes 4718600 | tf_op jit(solution)/shard_map/ppermute | solution.py:270
  54.0 13.2 %collective-permute-start.23 = (bf16[128,2048]{1,0:T(8,128)(2,1)S(1)}, bf16[128,2048]{1,0:T(8,128)(2,1)S(1)}, u32[]{:S(2)}, u32[]{:S(2)}) collective-permute-start(bf16[128,2048]{1,0:T(8,128)(2,1)S(1)} %collective-permute-done.22.refs_2_), channel_id=1, source_target_pairs={{4,0},{5,1},{8,4},{9,5},{12,8},{13,9},{14,12},{15,13},{10,14},{11,... | collective-permute-start | bytes 1572872 | tf_op jit(solution)/shard_map/ppermute | solution.py:270
  56.5 13.2 %collective-permute-start.19 = (bf16[128,2048]{1,0:T(8,128)(2,1)S(1)}, bf16[128,2048]{1,0:T(8,128)(2,1)S(1)}, u32[]{:S(2)}, u32[]{:S(2)}) collective-permute-start(bf16[128,2048]{1,0:T(8,128)(2,1)S(1)} %collective-permute-done.18.refs_1_), channel_id=1, source_target_pairs={{0,4},{1,5},{4,8},{5,9},{8,12},{9,13},{12,14},{13,15},{14,10},{15,... | collective-permute-start | bytes 1572872 | tf_op jit(solution)/shard_map/ppermute | solution.py:270
  67.2 12.3 %collective-permute-start.24 = (bf16[128,2048]{1,0:T(8,128)(2,1)S(1)}, bf16[128,2048]{1,0:T(8,128)(2,1)S(1)}, u32[]{:S(2)}, u32[]{:S(2)}) collective-permute-start(bf16[128,2048]{1,0:T(8,128)(2,1)S(1)} %collective-permute-done.23.refs_2_), channel_id=1, source_target_pairs={{4,0},{5,1},{8,4},{9,5},{12,8},{13,9},{14,12},{15,13},{10,14},{11,... | collective-permute-start | bytes 1572872 | tf_op jit(solution)/shard_map/ppermute | solution.py:270
  69.7 12.9 %collective-permute-start.20 = (bf16[128,2048]{1,0:T(8,128)(2,1)S(1)}, bf16[128,2048]{1,0:T(8,128)(2,1)S(1)}, u32[]{:S(2)}, u32[]{:S(2)}) collective-permute-start(bf16[128,2048]{1,0:T(8,128)(2,1)S(1)} %collective-permute-done.19.refs_1_), channel_id=1, source_target_pairs={{0,4},{1,5},{4,8},{5,9},{8,12},{9,13},{12,14},{13,15},{14,10},{15,... | collective-permute-start | bytes 1572872 | tf_op jit(solution)/shard_map/ppermute | solution.py:270
  81.0 6.7 %collective-permute-start.25 = (bf16[64,2048]{1,0:T(8,128)(2,1)}, bf16[64,2048]{1,0:T(8,128)(2,1)}, u32[]{:S(2)}, u32[]{:S(2)}) collective-permute-start(bf16[64,2048]{1,0:T(8,128)(2,1)} %slice.33), channel_id=1, source_target_pairs={{4,0},{5,1},{8,4},{9,5},{12,8},{13,9},{14,12},{15,13},{10,14},{11,... | collective-permute-start | bytes 786440 | tf_op jit(solution)/shard_map/ppermute | solution.py:270
  84.1 6.7 %collective-permute-start.21 = (bf16[64,2048]{1,0:T(8,128)(2,1)}, bf16[64,2048]{1,0:T(8,128)(2,1)}, u32[]{:S(2)}, u32[]{:S(2)}) collective-permute-start(bf16[64,2048]{1,0:T(8,128)(2,1)} %slice.32), channel_id=1, source_target_pairs={{0,4},{1,5},{4,8},{5,9},{8,12},{9,13},{12,14},{13,15},{14,10},{15,... | collective-permute-start | bytes 786440 | tf_op jit(solution)/shard_map/ppermute | solution.py:270
  91.9 7.6 %copy-start.3 = (bf16[128,2048]{1,0:T(8,128)(2,1)S(1)}, bf16[128,2048]{1,0:T(8,128)(2,1)}, u32[]{:S(2)}) copy-start(bf16[128,2048]{1,0:T(8,128)(2,1)} %copy-done.2) | copy-start | bytes 1572868
  97.7 8.7 %collective-permute-start.30 = (bf16[64,2048]{1,0:T(8,128)(2,1)S(1)}, bf16[64,2048]{1,0:T(8,128)(2,1)S(1)}, u32[]{:S(2)}, u32[]{:S(2)}) collective-permute-start(bf16[64,2048]{1,0:T(8,128)(2,1)S(1)} %get-tuple-element.22), channel_id=1, source_target_pairs={{4,0},{5,1},{8,4},{9,5},{12,8},{13,9},{14,12},{15,13},{10,14},{11,... | collective-permute-start | bytes 786440 | tf_op jit(solution)/shard_map/ppermute | solution.py:270
  105.9 8.8 %collective-permute-start.26 = (bf16[64,2048]{1,0:T(8,128)(2,1)S(1)}, bf16[64,2048]{1,0:T(8,128)(2,1)S(1)}, u32[]{:S(2)}, u32[]{:S(2)}) collective-permute-start(bf16[64,2048]{1,0:T(8,128)(2,1)S(1)} %get-tuple-element.21), channel_id=1, source_target_pairs={{0,4},{1,5},{4,8},{5,9},{8,12},{9,13},{12,14},{13,15},{14,10},{15,... | collective-permute-start | bytes 786440 | tf_op jit(solution)/shard_map/ppermute | solution.py:270
  106.5 8.9 %copy-start.17 = (bf16[128,2048]{1,0:T(8,128)(2,1)S(1)}, bf16[128,2048]{1,0:T(8,128)(2,1)}, u32[]{:S(2)}) copy-start(bf16[128,2048]{1,0:T(8,128)(2,1)} %copy-done.16) | copy-start | bytes 1572868
  106.5 8.9 %copy-start.19 = (bf16[128,2048]{1,0:T(8,128)(2,1)S(1)}, bf16[128,2048]{1,0:T(8,128)(2,1)}, u32[]{:S(2)}) copy-start(bf16[128,2048]{1,0:T(8,128)(2,1)} %copy-done.18) | copy-start | bytes 1572868
  106.5 8.9 %copy-start.21 = (bf16[144,512]{1,0:T(8,128)(2,1)S(1)}, bf16[144,512]{1,0:T(8,128)(2,1)}, u32[]{:S(2)}) copy-start(bf16[144,512]{1,0:T(8,128)(2,1)} %copy-done.20) | copy-start | bytes 442372
  106.5 8.9 %copy-start.23 = (bf16[144,512]{1,0:T(8,128)(2,1)S(1)}, bf16[144,512]{1,0:T(8,128)(2,1)}, u32[]{:S(2)}) copy-start(bf16[144,512]{1,0:T(8,128)(2,1)} %copy-done.22) | copy-start | bytes 442372
  106.6 15.1 %collective-permute-start.31 = (bf16[128,2048]{1,0:T(8,128)(2,1)S(1)}, bf16[128,2048]{1,0:T(8,128)(2,1)S(1)}, u32[]{:S(2)}, u32[]{:S(2)}) collective-permute-start(bf16[128,2048]{1,0:T(8,128)(2,1)S(1)} %pad_maximum_fusion.2), channel_id=1, source_target_pairs={{4,0},{5,1},{8,4},{9,5},{12,8},{13,9},{14,12},{15,13},{10,14},{11,... | collective-permute-start | bytes 1572872 | tf_op jit(solution)/shard_map/ppermute | solution.py:270
  114.8 12.7 %collective-permute-start.27 = (bf16[128,2048]{1,0:T(8,128)(2,1)S(1)}, bf16[128,2048]{1,0:T(8,128)(2,1)S(1)}, u32[]{:S(2)}, u32[]{:S(2)}) collective-permute-start(bf16[128,2048]{1,0:T(8,128)(2,1)S(1)} %pad_maximum_fusion.1), channel_id=1, source_target_pairs={{0,4},{1,5},{4,8},{5,9},{8,12},{9,13},{12,14},{13,15},{14,10},{15,... | collective-permute-start | bytes 1572872 | tf_op jit(solution)/shard_map/ppermute | solution.py:270
  121.9 13.0 %collective-permute-start.32 = (bf16[128,2048]{1,0:T(8,128)(2,1)S(1)}, bf16[128,2048]{1,0:T(8,128)(2,1)S(1)}, u32[]{:S(2)}, u32[]{:S(2)}) collective-permute-start(bf16[128,2048]{1,0:T(8,128)(2,1)S(1)} %add_convert_fusion.2), channel_id=1, source_target_pairs={{4,0},{5,1},{8,4},{9,5},{12,8},{13,9},{14,12},{15,13},{10,14},{11,... | collective-permute-start | bytes 1572872 | tf_op jit(solution)/shard_map/ppermute | solution.py:270
  127.7 13.5 %collective-permute-start.28 = (bf16[128,2048]{1,0:T(8,128)(2,1)S(1)}, bf16[128,2048]{1,0:T(8,128)(2,1)S(1)}, u32[]{:S(2)}, u32[]{:S(2)}) collective-permute-start(bf16[128,2048]{1,0:T(8,128)(2,1)S(1)} %add_convert_fusion.4), channel_id=1, source_target_pairs={{0,4},{1,5},{4,8},{5,9},{8,12},{9,13},{12,14},{13,15},{14,10},{15,... | collective-permute-start | bytes 1572872 | tf_op jit(solution)/shard_map/ppermute | solution.py:270
  135.0 11.5 %collective-permute-start.33 = (bf16[128,2048]{1,0:T(8,128)(2,1)S(1)}, bf16[128,2048]{1,0:T(8,128)(2,1)S(1)}, u32[]{:S(2)}, u32[]{:S(2)}) collective-permute-start(bf16[128,2048]{1,0:T(8,128)(2,1)S(1)} %add_convert_fusion.1), channel_id=1, source_target_pairs={{4,0},{5,1},{8,4},{9,5},{12,8},{13,9},{14,12},{15,13},{10,14},{11,... | collective-permute-start | bytes 1572872 | tf_op jit(solution)/shard_map/ppermute | solution.py:270
  141.3 9.2 %copy-start.7 = (f32[128,2048]{1,0:T(8,128)S(1)}, f32[128,2048]{1,0:T(8,128)}, u32[]{:S(2)}) copy-start(f32[128,2048]{1,0:T(8,128)} %copy-done.6) | copy-start | bytes 3145732
  141.3 9.2 %collective-permute-start.29 = (bf16[128,2048]{1,0:T(8,128)(2,1)S(1)}, bf16[128,2048]{1,0:T(8,128)(2,1)S(1)}, u32[]{:S(2)}, u32[]{:S(2)}) collective-permute-start(bf16[128,2048]{1,0:T(8,128)(2,1)S(1)} %add_convert_fusion.3), channel_id=1, source_target_pairs={{0,4},{1,5},{4,8},{5,9},{8,12},{9,13},{12,14},{13,15},{14,10},{15,... | collective-permute-start | bytes 1572872 | tf_op jit(solution)/shard_map/ppermute | solution.py:270
  (19 other events, 60.3 us)

commit v2 on v1

--- a/solution.py
+++ b/solution.py
@@ -31,25 +31,20 @@
 
 def pack_kernel(pos_ref, key_ref, value_ref, routes_ref, combine_ref, out_ref):
     rows, width = key_ref.shape
-    top = routes_ref.shape[1]
+    top = routes_ref.shape[0]
     out_ref[0:rows, 0:width] = key_ref[...]
     out_ref[0:rows, width : 2 * width] = value_ref[...]
     weight = combine_ref[...]
-    high = weight.astype(jnp.bfloat16)
-    low = (weight - high.astype(jnp.float32)).astype(jnp.bfloat16)
-    lane = lax.broadcasted_iota(jnp.int32, (top, HEAD_SIZE), 1)
-    row = lax.broadcasted_iota(jnp.int32, (top, HEAD_SIZE), 0)
-
-    def put(part, shift):
-        spread = jnp.where(lane == row + shift, 1.0, 0.0).astype(jnp.bfloat16)
-        return jnp.dot(part, spread, preferred_element_type=jnp.float32)
-
-    names = routes_ref[...].astype(jnp.float32).astype(jnp.bfloat16)
-    turned = (put(names, 0) + put(high, top) + put(low, 2 * top)).T
-    out_ref[rows : rows + EXTRA, 0:128] = turned[0:EXTRA].astype(jnp.bfloat16)
-    out_ref[rows : rows + EXTRA, 128:256] = turned[EXTRA : 2 * EXTRA].astype(jnp.bfloat16)
-    place = jnp.full((EXTRA, 2 * width - 256), pos_ref[0].astype(jnp.float32), jnp.float32)
-    out_ref[rows : rows + EXTRA, 256 : 2 * width] = place.astype(jnp.bfloat16)
+    high = weight.astype(jnp.bfloat16).astype(jnp.float32)
+    low = weight - high
+    names = routes_ref[...].astype(jnp.float32)
+    place = jnp.full((EXTRA, 2 * width - 2 * rows), pos_ref[0].astype(jnp.float32), jnp.float32)
+    tail = slice(rows, rows + EXTRA)
+    out_ref[tail, 0:rows] = jnp.concatenate([names, high], axis=0).astype(jnp.bfloat16)
+    out_ref[tail, rows : 2 * rows] = jnp.concatenate([low, jnp.zeros_like(low)], axis=0).astype(
+        jnp.bfloat16
+    )
+    out_ref[tail, 2 * rows : 2 * width] = place.astype(jnp.bfloat16)
 
 
 def pack_message(stretch_pos, keys, values, routes, combine):
@@ -61,13 +56,22 @@
         in_specs=[pl.BlockSpec(memory_space=pltpu.SMEM), vmem, vmem, vmem, vmem],
         out_specs=vmem,
         name="pack_message",
-    )(stretch_pos, keys, values, routes, combine)
+    )(stretch_pos, keys, values, routes.T, combine.T)
 
 
 def attend_kernel(count, *refs):
-    query_ref, residual_ref, gain_ref = refs[:3]
+    query_hbm, residual_hbm, gain_hbm = refs[:3]
     messages = refs[3 : 3 + count]
-    hidden_ref, normed_ref, key_ext, value_ext = refs[3 + count :]
+    hidden_ref, upper_ref, lower_ref, key_ext, value_ext = refs[3 + count : 8 + count]
+    query_ref, residual_ref, gain_ref, arrived = refs[8 + count :]
+    fetches = [
+        pltpu.make_async_copy(source, target, arrived.at[i])
+        for i, (source, target) in enumerate(
+            [(query_hbm, query_ref), (residual_hbm, residual_ref), (gain_hbm, gain_ref)]
+        )
+    ]
+    for fetch in fetches:
+        fetch.start()
     rows = query_ref.shape[0]
     kv_heads = key_ext.shape[0]
     heads = query_ref.shape[1] // HEAD_SIZE
@@ -93,6 +97,8 @@
             ]
             value_ext[a, at, HEAD_SIZE : 2 * HEAD_SIZE] = ones
     eye = jnp.where(sub == lane, 1.0, 0.0).astype(jnp.bfloat16)
+    for fetch in fetches:
+        fetch.wait()
     rate = math.log2(math.e) / math.sqrt(HEAD_SIZE)
     step = min(512, span)
     pair = 2
@@ -138,9 +144,9 @@
     inverse = lax.rsqrt(meansq + 1e-06)
     for h in range(heads):
         cols = slice(h * HEAD_SIZE, (h + 1) * HEAD_SIZE)
-        normed_ref[:, cols] = (hidden_ref[:, cols] * inverse * gain_ref[:, cols]).astype(
-            jnp.bfloat16
-        )
+        normed = (hidden_ref[:, cols] * inverse * gain_ref[:, cols]).astype(jnp.bfloat16)
+        upper_ref[:, cols] = normed[: rows // 2]
+        lower_ref[:, cols] = normed[rows // 2 :]
 
 
 def attend(queries, residual, gain, messages):
@@ -153,15 +159,20 @@
         functools.partial(attend_kernel, count),
         out_shape=(
             jax.ShapeDtypeStruct((rows, features), jnp.float32),
-            jax.ShapeDtypeStruct((rows, features), jnp.bfloat16),
+            jax.ShapeDtypeStruct((rows // 2, features), jnp.bfloat16),
+            jax.ShapeDtypeStruct((rows // 2, features), jnp.bfloat16),
         ),
-        in_specs=[vmem] * (3 + count),
-        out_specs=(vmem, vmem),
+        in_specs=[pl.BlockSpec(memory_space=pl.ANY)] * 3 + [vmem] * count,
+        out_specs=(vmem, vmem, vmem),
         scratch_shapes=[
             pltpu.VMEM((kv_heads, span, 2 * HEAD_SIZE), jnp.bfloat16),
             pltpu.VMEM((kv_heads, span, 2 * HEAD_SIZE), jnp.bfloat16),
+            pltpu.VMEM((rows, features), jnp.bfloat16),
+            pltpu.VMEM((rows, features), jnp.bfloat16),
+            pltpu.VMEM((1, features), jnp.float32),
+            pltpu.SemaphoreType.DMA((3,)),
         ],
-        compiler_params=pltpu.CompilerParams(vmem_limit_bytes=40 * 1024 * 1024),
+        compiler_params=pltpu.CompilerParams(vmem_limit_bytes=28 * 1024 * 1024),
         cost_estimate=pl.CostEstimate(
             flops=8 * rows * span * features, bytes_accessed=8 * 1024 * 1024, transcendentals=0
         ),
@@ -169,33 +180,32 @@
     )(queries, residual, gain.reshape(1, features), *messages)
 
 
-def expert_kernel(blocks, *refs):
-    own_ref = refs[0]
-    tokens = refs[1 : 1 + blocks]
-    messages = refs[1 + blocks : 1 + 2 * blocks]
-    weights = refs[1 + 2 * blocks : 1 + 2 * blocks + 3 * CORES]
-    outs = refs[1 + 2 * blocks + 3 * CORES : 1 + 3 * blocks + 3 * CORES]
+def expert_kernel(places, count, *refs):
+    pieces = len(places)
+    tokens = refs[:pieces]
+    messages = refs[pieces : pieces + count]
+    weights = refs[pieces + count : pieces + count + 3 * CORES]
+    outs = refs[pieces + count + 3 * CORES :]
     rows, features = tokens[0].shape
-    top = 8
-    if blocks == 1:
-        normed = tokens[0][...]
-    else:
-        normed = jnp.concatenate([ref[...] for ref in tokens], axis=0)
+    whole = messages[0].shape[0] - EXTRA
+    top = EXTRA // 2
+    me = lax.axis_index("ctx")
+    normed = jnp.concatenate([ref[...] for ref in tokens], axis=0)
     shares, acts = [], []
     for e in range(CORES):
         gate_ref, up_ref = weights[3 * e], weights[3 * e + 1]
         gate = jnp.dot(normed, gate_ref[0], preferred_element_type=jnp.float32)
         upper = jnp.dot(normed, up_ref[0], preferred_element_type=jnp.float32)
         acts.append((gate / (1.0 + jnp.exp(-gate)) * upper).astype(jnp.bfloat16))
+        name = jnp.bitwise_xor(me, e).astype(jnp.float32)
         columns = []
         for ref in messages:
-            extra = ref[...].astype(jnp.float32)
-            named = extra[0:top, 0:128]
-            value = extra[top : 2 * top, 0:128] + extra[0:top, 128:256]
-            hit = jnp.where(named == own_ref[e].astype(jnp.float32), value, 0.0)
+            extra = ref[whole : whole + EXTRA, 0 : 2 * whole].astype(jnp.float32)
+            value = extra[top : 2 * top, 0:whole] + extra[0:top, whole : 2 * whole]
+            hit = jnp.where(extra[0:top, 0:whole] == name, value, 0.0)
             line = jnp.sum(hit, axis=0, keepdims=True)
-            columns.append(jnp.broadcast_to(line, (rows, rows)).T)
-        shares.append(columns)
+            columns.append(jnp.broadcast_to(line, (whole, whole)).T)
+        shares.append([columns[m][half * rows : (half + 1) * rows] for m, half in places])
     step = 512
     for at in range(0, features, step):
         parts = [
@@ -204,42 +214,33 @@
             .astype(jnp.float32)
             for e in range(CORES)
         ]
-        for b in range(blocks):
-            for c in range(0, step, HEAD_SIZE):
+        for b in range(pieces):
+            for c in range(0, step, whole):
                 mixed = sum(
-                    shares[e][b] * parts[e][b * rows : (b + 1) * rows, c : c + HEAD_SIZE]
+                    shares[e][b] * parts[e][b * rows : (b + 1) * rows, c : c + whole]
                     for e in range(CORES)
                 )
-                outs[b][:, at + c : at + c + HEAD_SIZE] = mixed.astype(jnp.bfloat16)
-
-
-def run_experts(own, tokens, messages, weights):
+                outs[b][:, at + c : at + c + whole] = mixed.astype(jnp.bfloat16)
+
+
+def run_experts(pieces, messages, weights):
+    tokens = [piece[0] for piece in pieces]
     rows, features = tokens[0].shape
-    blocks = len(tokens)
     hidden = weights[0].shape[2]
     vmem = pl.BlockSpec(memory_space=pltpu.VMEM)
-    tail = pl.BlockSpec((EXTRA, messages[0].shape[1]), lambda i: (rows // EXTRA, 0))
-
-    def whole(shape):
-        return pl.BlockSpec(shape, lambda i: (0,) * len(shape))
-
     return pl.pallas_call(
-        functools.partial(expert_kernel, blocks),
-        grid=(1,),
-        out_shape=[jax.ShapeDtypeStruct((rows, features), jnp.bfloat16)] * blocks,
-        in_specs=[pl.BlockSpec(memory_space=pltpu.SMEM)]
-        + [whole((rows, features))] * blocks
-        + [tail] * blocks
-        + [whole(w.shape) for w in weights],
-        out_specs=[whole((rows, features))] * blocks,
-        compiler_params=pltpu.CompilerParams(vmem_limit_bytes=48 * 1024 * 1024),
+        functools.partial(expert_kernel, [piece[1:] for piece in pieces], len(messages)),
+        out_shape=[jax.ShapeDtypeStruct((rows, features), jnp.bfloat16)] * len(pieces),
+        in_specs=[vmem] * (len(pieces) + len(messages) + len(weights)),
+        out_specs=[vmem] * len(pieces),
+        compiler_params=pltpu.CompilerParams(vmem_limit_bytes=24 * 1024 * 1024),
         cost_estimate=pl.CostEstimate(
-            flops=12 * blocks * rows * features * hidden,
+            flops=12 * len(pieces) * rows * features * hidden,
             bytes_accessed=12 * features * hidden,
             transcendentals=0,
         ),
         name="experts",
-    )(own, *tokens, *messages, *weights)
+    )(*tokens, *messages, *weights)
 
 
 def add_parts(*parts):
@@ -271,9 +272,6 @@
 
     message = pack_message(stretch_pos, rotated_keys, value_matrix, routes, combine)
     twins = tuple(send(w, swap) for w in (gate_weight, up_weight, down_weight))
-    weights = (gate_weight, up_weight, down_weight) + twins
-    me = lax.axis_index("ctx").astype(jnp.int32)
-    own = jnp.stack([me, me ^ 1])
 
     left, right = {0: message}, {0: message}
     for hop in range(1, far + 1):
@@ -282,45 +280,62 @@
             right[hop] = send(right[hop - 1], back)
     plane = [message] + [left[h] for h in range(1, far + 1)] + [right[h] for h in range(1, far)]
     everything = plane + [send(m, swap) for m in plane]
-    hidden_state, normed = attend(queries, residual, norm_gain, everything)
-
-    half = normed.shape[0] // 2
-    from_left, from_right = {0: normed}, {0: normed}
-    for hop in range(1, far):
-        from_left[hop] = send(from_left[hop - 1], onward)
-        from_right[hop] = send(from_right[hop - 1], back)
-    upper_half = send(from_left[far - 1][:half], onward)
-    lower_half = send(from_right[far - 1][half:], back)
-
+    norm_gain, twins = lax.optimization_barrier((norm_gain, twins))
+    weights = (gate_weight, up_weight, down_weight) + twins
+    hidden_state, upper, lower = attend(queries, residual, norm_gain, everything)
+
+    from_left = {(0, 0): upper, (0, 1): lower}
+    from_right = {(0, 0): upper, (0, 1): lower}
     out_left, out_right = {}, {}
-    (own_out,) = run_experts(own, [normed], [message], weights)
-    for hop in range(1, far):
-        out_left[hop], out_right[hop] = run_experts(
-            own, [from_left[hop], from_right[hop]], [left[hop], right[hop]], weights
-        )
-    (out_far,) = run_experts(
-        own, [jnp.concatenate([upper_half, lower_half], axis=0)], [left[far]], weights
-    )
-
-    moving_on = send(out_far[:half], onward)
-    moving_back = send(out_far[half:], back)
+
+    def pieces_of(hop):
+        return [
+            (from_left[hop, 0], 0, 0),
+            (from_left[hop, 1], 0, 1),
+            (from_right[hop, 0], 1, 0),
+            (from_right[hop, 1], 1, 1),
+        ]
+
+    for hop in range(1, far + 1):
+        first_left, first_right = from_left[hop - 1, 0], from_right[hop - 1, 1]
+        if hop == 2:
+            own_out = run_experts([(upper, 0, 0), (lower, 0, 1)], [message], weights)
+            first_left, first_right, own_out = lax.optimization_barrier(
+                (first_left, first_right, own_out)
+            )
+        if hop > 2:
+            outs = run_experts(pieces_of(hop - 2), [left[hop - 2], right[hop - 2]], weights)
+            first_left, first_right, outs = lax.optimization_barrier((first_left, first_right, outs))
+            out_left[hop - 2], out_right[hop - 2] = outs[:2], outs[2:]
+        from_left[hop, 0] = send(first_left, onward)
+        from_right[hop, 1] = send(first_right, back)
+        if hop < far:
+            from_left[hop, 1] = send(from_left[hop - 1, 1], onward)
+            from_right[hop, 0] = send(from_right[hop - 1, 0], back)
+    outs = run_experts(pieces_of(far - 1), [left[far - 1], right[far - 1]], weights)
+    out_left[far - 1], out_right[far - 1] = outs[:2], outs[2:]
+    far_upper, far_lower = run_experts(
+        [(from_left[far, 0], 0, 0), (from_right[far, 1], 0, 1)], [left[far]], weights
+    )
+
+    sums_on = {1: send(out_right[far - 1][1], onward)}
+    sums_back = {0: send(out_left[far - 1][0], back)}
+    sums_on[0] = send(far_upper, onward)
+    sums_back[1] = send(far_lower, back)
     for hop in range(far - 1, 0, -1):
-        if hop == far - 1:
-            ready_on = jnp.concatenate(
-                [add_parts(moving_on, out_right[hop][:half]), out_right[hop][half:]], axis=0
-            )
-            ready_back = jnp.concatenate(
-                [out_left[hop][:half], add_parts(moving_back, out_left[hop][half:])], axis=0
-            )
-        else:
-            ready_on = add_parts(moving_on, out_right[hop])
-            ready_back = add_parts(moving_back, out_left[hop])
-        moving_on = send(ready_on, onward)
-        moving_back = send(ready_back, back)
-    mixture = (
-        own_out.astype(jnp.float32)
-        + moving_on.astype(jnp.float32)
-        + moving_back.astype(jnp.float32)
+        if hop < far - 1:
+            sums_on[1] = send(add_parts(sums_on[1], out_right[hop][1]), onward)
+            sums_back[0] = send(add_parts(sums_back[0], out_left[hop][0]), back)
+        sums_on[0] = send(add_parts(sums_on[0], out_right[hop][0]), onward)
+        sums_back[1] = send(add_parts(sums_back[1], out_left[hop][1]), back)
+    mixture = jnp.concatenate(
+        [
+            own_out[half].astype(jnp.float32)
+            + sums_on[half].astype(jnp.float32)
+            + sums_back[half].astype(jnp.float32)
+            for half in range(2)
+        ],
+        axis=0,
     )
     return (hidden_state + mixture).astype(jnp.bfloat16)
 
@@ -473,6 +488,7 @@
         routes, gate_weight = arguments[6], arguments[8]
         dense = 4 * routes.shape[1] >= gate_weight.shape[0] * ctx_count
         ringed = gate_weight.shape[0] == 1 and ctx_count % (2 * CORES) == 0
+        ringed = ringed and ctx_count >= 4 * CORES and 2 * routes.shape[1] == EXTRA
         return (ring_device if dense and ringed else exchange_device)(*arguments)
 
     return jax.shard_map(

time: 152 us -> 149 us (0.980)
  starting transfers between devices: 27.4 us -> 42.8 us
  local copies, waits for them, and re-layouts: 15 us -> 3.7 us
  Pallas kernels: 36.2 us -> 29.3 us
    ppermute x34 -> x46, starting transfers between devices: 27.4 us -> 42.8 us  [send(): return lax.ppermute(array, 'ctx', pairs)]
    unnamed x68 -> x14, local copies, waits for them, and re-layouts: 13.4 us -> 3.7 us
    pallas_call x5, Pallas kernels: 28.3 us -> 21.1 us  [run_experts(): pl.pallas_call(functools.partial(expert_kernel, [piece[1:] for piece in p...]
    ppermute x34 -> x46, waiting for transfers between devices: 69.1 us -> 70.5 us  [send(): return lax.ppermute(array, 'ctx', pairs)]
  transfers between devices with their start and end apart: 34 -> 46, of which waited for: 16 -> 24; matrix products, arithmetic and copies ran while one was open for 2% -> 0% of each run, Pallas kernels for 16% -> 12%
where the time goes in v2:
time: 149 us
  waiting for transfers between devices  70.5 us (47%)
  starting transfers between devices  42.8 us (29%)
  Pallas kernels  29.3 us (20%)
  local copies, waits for them, and re-layouts  3.7 us (2%)
  other arithmetic  1.73 us (1%)
    ppermute x46, waiting for transfers between devices, send(): return lax.ppermute(array, 'ctx', pairs)  70.5 us
    ppermute x46, starting transfers between devices, send(): return lax.ppermute(array, 'ctx', pairs)  42.8 us
    pallas_call x5, Pallas kernels, run_experts(): pl.pallas_call(functools.partial(expert_kernel, [piece[1:] for piece in p...  21.1 us
    pallas_call x1, Pallas kernels, attend(): pl.pallas_call(functools.partial(attend_kernel, count), out_shape=(jax.Sh...  6.6 us
    unnamed x14, local copies, waits for them, and re-layouts  3.7 us
  transfers between devices with their start and end apart: 46, of which 24 were waited for; matrix products, arithmetic and copies ran while one was open for 0% of the time, Pallas kernels for 12%

profile of v2, /device:TPU:0, one launch (start us, length us, event | category | flops | bytes accessed | tf_op | source)
XLA Modules:
  0.0 148.8 jit_solution(1309378977263357679)
XLA Ops:
  1.6 1.6 %pack_message.1.refs_3_.refs_2_ = bf16[144,512]{1,0:T(8,128)(2,1)} custom-call(s32[1]{0:T(128)S(6)} %copy.12.pos_ref, bf16[128,256]{1,0:T(8,128)(2,1)} %key_ref.1, bf16[128,256]{1,0:T(8,128)(2,1)} %value_ref.1, s32[8,128]{1,0:T(8,128)} %bitcast.4, f32[8,128]{1,0:T(8,128)} %bitcast.5), custom_call_target="tpu_custom_call" | custom-call | tf_op jit(solution)/shard_map/pack_message/pallas_call | solution.py:53
  3.2 3.0 %collective-permute-start.7 = (bf16[144,512]{1,0:T(8,128)(2,1)}, bf16[144,512]{1,0:T(8,128)(2,1)S(1)}, u32[]{:S(2)}, u32[]{:S(2)}) collective-permute-start(bf16[144,512]{1,0:T(8,128)(2,1)} %pack_message.1.refs_3_.refs_2_), channel_id=1, source_target_pairs={{4,0},{5,1},{8,4},{9,5},{12,8},{13,9},{14,12},{15,13},{10,14},{11,... | collective-permute-start | bytes 442376 | tf_op jit(solution)/shard_map/ppermute | solution.py:271
  6.2 2.2 %collective-permute-done.10.refs_11_ = bf16[144,512]{1,0:T(8,128)(2,1)S(1)} collective-permute-done((bf16[144,512]{1,0:T(8,128)(2,1)}, bf16[144,512]{1,0:T(8,128)(2,1)S(1)}, u32[]{:S(2)}, u32[]{:S(2)}) %collective-permute-start.10) | collective-permute-done | bytes 147488 | tf_op jit(solution)/shard_map/ppermute | solution.py:271
  8.4 2.9 %collective-permute-start.3 = (bf16[144,512]{1,0:T(8,128)(2,1)}, bf16[144,512]{1,0:T(8,128)(2,1)S(1)}, u32[]{:S(2)}, u32[]{:S(2)}) collective-permute-start(bf16[144,512]{1,0:T(8,128)(2,1)} %pack_message.1.refs_3_.refs_2_), channel_id=1, source_target_pairs={{0,4},{1,5},{4,8},{5,9},{8,12},{9,13},{12,14},{13,15},{14,10},{15,... | collective-permute-start | bytes 442376 | tf_op jit(solution)/shard_map/ppermute | solution.py:271
  11.4 4.3 %collective-permute-done.3.refs_4_ = bf16[144,512]{1,0:T(8,128)(2,1)S(1)} collective-permute-done((bf16[144,512]{1,0:T(8,128)(2,1)}, bf16[144,512]{1,0:T(8,128)(2,1)S(1)}, u32[]{:S(2)}, u32[]{:S(2)}) %collective-permute-start.3) | collective-permute-done | bytes 147488 | tf_op jit(solution)/shard_map/ppermute | solution.py:271
  15.7 1.7 %collective-permute-start.8 = (bf16[144,512]{1,0:T(8,128)(2,1)S(1)}, bf16[144,512]{1,0:T(8,128)(2,1)S(1)}, u32[]{:S(2)}, u32[]{:S(2)}) collective-permute-start(bf16[144,512]{1,0:T(8,128)(2,1)S(1)} %collective-permute-done.7.refs_8_.refs_5_), channel_id=1, source_target_pairs={{4,0},{5,1},{8,4},{9,5},{12,8},{13,9},{14,12},{15,13},{10,14},{11,... | collective-permute-start | bytes 442376 | tf_op jit(solution)/shard_map/ppermute | solution.py:271
  17.7 3.4 %collective-permute-done.8.refs_9_.refs_5_ = bf16[144,512]{1,0:T(8,128)(2,1)S(1)} collective-permute-done((bf16[144,512]{1,0:T(8,128)(2,1)S(1)}, bf16[144,512]{1,0:T(8,128)(2,1)S(1)}, u32[]{:S(2)}, u32[]{:S(2)}) %collective-permute-start.8) | collective-permute-done | bytes 147488 | tf_op jit(solution)/shard_map/ppermute | solution.py:271
  21.0 1.5 %collective-permute-done.4.refs_5_.refs_4_ = bf16[144,512]{1,0:T(8,128)(2,1)S(1)} collective-permute-done((bf16[144,512]{1,0:T(8,128)(2,1)S(1)}, bf16[144,512]{1,0:T(8,128)(2,1)S(1)}, u32[]{:S(2)}, u32[]{:S(2)}) %collective-permute-start.4) | collective-permute-done | bytes 147488 | tf_op jit(solution)/shard_map/ppermute | solution.py:271
  22.8 1.7 %collective-permute-start.9 = (bf16[144,512]{1,0:T(8,128)(2,1)S(1)}, bf16[144,512]{1,0:T(8,128)(2,1)S(1)}, u32[]{:S(2)}, u32[]{:S(2)}) collective-permute-start(bf16[144,512]{1,0:T(8,128)(2,1)S(1)} %collective-permute-done.8.refs_9_.refs_5_), channel_id=1, source_target_pairs={{4,0},{5,1},{8,4},{9,5},{12,8},{13,9},{14,12},{15,13},{10,14},{11,... | collective-permute-start | bytes 442376 | tf_op jit(solution)/shard_map/ppermute | solution.py:271
  24.6 3.1 %collective-permute-done.5.refs_6_.refs_4_ = bf16[144,512]{1,0:T(8,128)(2,1)S(1)} collective-permute-done((bf16[144,512]{1,0:T(8,128)(2,1)S(1)}, bf16[144,512]{1,0:T(8,128)(2,1)S(1)}, u32[]{:S(2)}, u32[]{:S(2)}) %collective-permute-start.5) | collective-permute-done | bytes 147488 | tf_op jit(solution)/shard_map/ppermute | solution.py:271
  27.7 1.2 collective-permute-start.6
  28.9 4.0 %collective-permute-done.6.refs_7_.refs_2_ = bf16[144,512]{1,0:T(8,128)(2,1)S(1)} collective-permute-done((bf16[144,512]{1,0:T(8,128)(2,1)S(1)}, bf16[144,512]{1,0:T(8,128)(2,1)S(1)}, u32[]{:S(2)}, u32[]{:S(2)}) %collective-permute-start.6) | collective-permute-done | bytes 147488 | tf_op jit(solution)/shard_map/ppermute | solution.py:271
  35.8 1.0 copy-done.4
  36.9 1.0 copy-done.5
  38.6 6.6 %attend.1 = (f32[128,2048]{1,0:T(8,128)S(1)}, bf16[64,2048]{1,0:T(8,128)(2,1)S(1)}, bf16[64,2048]{1,0:T(8,128)(2,1)S(1)}) custom-call(bf16[128,2048]{1,0:T(8,128)(2,1)S(1)} %copy-done.4, bf16[128,2048]{1,0:T(8,128)(2,1)S(1)} %copy-done.5, f32[1,2048]{1,0:T(1,128)S(1)} %bitcast.3, bf16[144,512]{1,0:T(8,128)(2,1)S(1)} %copy-done.3, ...), custom_call_target="tpu_custom_call" | custom-call | flops 4294967296 | bytes 8388608 | tf_op jit(solution)/shard_map/attend/pallas_call | solution.py:158
  45.2 1.3 collective-permute-start.18
  47.3 1.6 %collective-permute-start.23 = (bf16[64,2048]{1,0:T(8,128)(2,1)S(1)}, bf16[64,2048]{1,0:T(8,128)(2,1)S(1)}, u32[]{:S(2)}, u32[]{:S(2)}) collective-permute-start(bf16[64,2048]{1,0:T(8,128)(2,1)S(1)} %get-tuple-element.46.refs_0_), channel_id=1, source_target_pairs={{4,0},{5,1},{8,4},{9,5},{12,8},{13,9},{14,12},{15,13},{10,14},{11,... | collective-permute-start | bytes 786440 | tf_op jit(solution)/shard_map/ppermute | solution.py:271
  49.4 3.2 %experts.5 = (bf16[64,2048]{1,0:T(8,128)(2,1)S(1)}, bf16[64,2048]{1,0:T(8,128)(2,1)S(1)}) custom-call(bf16[64,2048]{1,0:T(8,128)(2,1)S(1)} %get-tuple-element.46.refs_0_, bf16[64,2048]{1,0:T(8,128)(2,1)S(1)} %get-tuple-element.47.refs_1_, bf16[144,512]{1,0:T(8,128)(2,1)S(1)} %copy-done.3, bf16[1,2048,384]{2,1,0:T(8,128)(2,1)S(1)} %copy-done, ...), custom_call_target="tpu_custom_call" | custom-call | flops 1207959552 | bytes 9437184 | tf_op jit(solution)/shard_map/experts/pallas_call | solution.py:231
  52.6 1.8 %collective-permute-done.18.refs_0_ = bf16[64,2048]{1,0:T(8,128)(2,1)S(1)} collective-permute-done((bf16[64,2048]{1,0:T(8,128)(2,1)S(1)}, bf16[64,2048]{1,0:T(8,128)(2,1)S(1)}, u32[]{:S(2)}, u32[]{:S(2)}) %collective-permute-start.18) | collective-permute-done | bytes 262176 | tf_op jit(solution)/shard_map/ppermute | solution.py:271
  54.4 1.3 collective-permute-done.19.refs_3_
  55.7 1.5 %collective-permute-start.20 = (bf16[64,2048]{1,0:T(8,128)(2,1)S(1)}, bf16[64,2048]{1,0:T(8,128)(2,1)S(1)}, u32[]{:S(2)}, u32[]{:S(2)}) collective-permute-start(bf16[64,2048]{1,0:T(8,128)(2,1)S(1)} %collective-permute-done.18.refs_0_), channel_id=1, source_target_pairs={{0,4},{1,5},{4,8},{5,9},{8,12},{9,13},{12,14},{13,15},{14,10},{15,... | collective-permute-start | bytes 786440 | tf_op jit(solution)/shard_map/ppermute | solution.py:271
  57.7 3.6 %collective-permute-done.23.refs_2_ = bf16[64,2048]{1,0:T(8,128)(2,1)S(1)} collective-permute-done((bf16[64,2048]{1,0:T(8,128)(2,1)S(1)}, bf16[64,2048]{1,0:T(8,128)(2,1)S(1)}, u32[]{:S(2)}, u32[]{:S(2)}) %collective-permute-start.23) | collective-permute-done | bytes 262176 | tf_op jit(solution)/shard_map/ppermute | solution.py:271
  62.1 1.3 collective-permute-start.26
  63.4 4.9 %experts.6 = (bf16[64,2048]{1,0:T(8,128)(2,1)S(1)}, bf16[64,2048]{1,0:T(8,128)(2,1)S(1)}, bf16[64,2048]{1,0:T(8,128)(2,1)S(1)}, bf16[64,2048]{1,0:T(8,128)(2,1)S(1)}) custom-call(bf16[64,2048]{1,0:T(8,128)(2,1)S(1)} %collective-permute-done.18.refs_0_, bf16[64,2048]{1,0:T(8,128)(2,1)S(1)} %collective-permute-done.22.refs_1_, ...), custom_call_target="tpu_custom_call" | custom-call | flops 2415919104 | bytes 9437184 | tf_op jit(solution)/shard_map/experts/pallas_call | solution.py:231
  68.3 1.6 %collective-permute-start.24 = (bf16[64,2048]{1,0:T(8,128)(2,1)S(1)}, bf16[64,2048]{1,0:T(8,128)(2,1)S(1)}, u32[]{:S(2)}, u32[]{:S(2)}) collective-permute-start(bf16[64,2048]{1,0:T(8,128)(2,1)S(1)} %collective-permute-done.20.refs_0_), channel_id=1, source_target_pairs={{0,4},{1,5},{4,8},{5,9},{8,12},{9,13},{12,14},{13,15},{14,10},{15,... | collective-permute-start | bytes 786440 | tf_op jit(solution)/shard_map/ppermute | solution.py:271
  69.8 1.8 %collective-permute-done.27.refs_2_ = bf16[64,2048]{1,0:T(8,128)(2,1)S(1)} collective-permute-done((bf16[64,2048]{1,0:T(8,128)(2,1)S(1)}, bf16[64,2048]{1,0:T(8,128)(2,1)S(1)}, u32[]{:S(2)}, u32[]{:S(2)}) %collective-permute-start.27) | collective-permute-done | bytes 262176 | tf_op jit(solution)/shard_map/ppermute | solution.py:271
  72.4 1.3 collective-permute-start.31
  74.4 6.4 %collective-permute-done.32.refs_2_ = bf16[64,2048]{1,0:T(8,128)(2,1)S(1)} collective-permute-done((bf16[64,2048]{1,0:T(8,128)(2,1)S(1)}, bf16[64,2048]{1,0:T(8,128)(2,1)S(1)}, u32[]{:S(2)}, u32[]{:S(2)}) %collective-permute-start.32) | collective-permute-done | bytes 262176 | tf_op jit(solution)/shard_map/ppermute | solution.py:271
  80.9 1.0 collective-permute-done.31.refs_1_
  81.9 2.7 %collective-permute-done.25.refs_3_ = bf16[64,2048]{1,0:T(8,128)(2,1)S(1)} collective-permute-done((bf16[64,2048]{1,0:T(8,128)(2,1)S(1)}, bf16[64,2048]{1,0:T(8,128)(2,1)S(1)}, u32[]{:S(2)}, u32[]{:S(2)}) %collective-permute-start.25) | collective-permute-done | bytes 262176 | tf_op jit(solution)/shard_map/ppermute | solution.py:271
  84.6 4.9 %experts.9 = (bf16[64,2048]{1,0:T(8,128)(2,1)S(1)}, bf16[64,2048]{1,0:T(8,128)(2,1)S(1)}, bf16[64,2048]{1,0:T(8,128)(2,1)S(1)}, bf16[64,2048]{1,0:T(8,128)(2,1)S(1)}) custom-call(bf16[64,2048]{1,0:T(8,128)(2,1)S(1)} %collective-permute-done.24.refs_0_, bf16[64,2048]{1,0:T(8,128)(2,1)S(1)} %collective-permute-done.31.refs_1_, ...), custom_call_target="tpu_custom_call" | custom-call | flops 2415919104 | bytes 9437184 | tf_op jit(solution)/shard_map/experts/pallas_call | solution.py:231
  90.4 4.9 %experts.7 = (bf16[64,2048]{1,0:T(8,128)(2,1)S(1)}, bf16[64,2048]{1,0:T(8,128)(2,1)S(1)}, bf16[64,2048]{1,0:T(8,128)(2,1)S(1)}, bf16[64,2048]{1,0:T(8,128)(2,1)S(1)}) custom-call(bf16[64,2048]{1,0:T(8,128)(2,1)S(1)} %collective-permute-done.20.refs_0_, bf16[64,2048]{1,0:T(8,128)(2,1)S(1)} %collective-permute-done.26.refs_1_, ...), custom_call_target="tpu_custom_call" | custom-call | flops 2415919104 | bytes 9437184 | tf_op jit(solution)/shard_map/experts/pallas_call | solution.py:231
  95.3 1.3 collective-permute-start.39
  96.6 1.5 %collective-permute-start.28 = (bf16[64,2048]{1,0:T(8,128)(2,1)S(1)}, bf16[64,2048]{1,0:T(8,128)(2,1)S(1)}, u32[]{:S(2)}, u32[]{:S(2)}) collective-permute-start(bf16[64,2048]{1,0:T(8,128)(2,1)S(1)} %collective-permute-done.24.refs_0_), channel_id=1, source_target_pairs={{0,4},{1,5},{4,8},{5,9},{8,12},{9,13},{12,14},{13,15},{14,10},{15,... | collective-permute-start | bytes 786440 | tf_op jit(solution)/shard_map/ppermute | solution.py:271
  99.5 5.1 %collective-permute-done.39 = bf16[64,2048]{1,0:T(8,128)(2,1)S(1)} collective-permute-done((bf16[64,2048]{1,0:T(8,128)(2,1)S(1)}, bf16[64,2048]{1,0:T(8,128)(2,1)S(1)}, u32[]{:S(2)}, u32[]{:S(2)}) %collective-permute-start.39) | collective-permute-done | bytes 262176 | tf_op jit(solution)/shard_map/ppermute | solution.py:271
  104.6 1.5 %collective-permute-start.40 = (bf16[64,2048]{1,0:T(8,128)(2,1)S(1)}, bf16[64,2048]{1,0:T(8,128)(2,1)S(1)}, u32[]{:S(2)}, u32[]{:S(2)}) collective-permute-start(bf16[64,2048]{1,0:T(8,128)(2,1)S(1)} %add_convert_fusion.4), channel_id=1, source_target_pairs={{0,4},{1,5},{4,8},{5,9},{8,12},{9,13},{12,14},{13,15},{14,10},{15,... | collective-permute-start | bytes 786440 | tf_op jit(solution)/shard_map/ppermute | solution.py:271
  106.1 3.8 %collective-permute-done.28.refs_0_ = bf16[64,2048]{1,0:T(8,128)(2,1)S(1)} collective-permute-done((bf16[64,2048]{1,0:T(8,128)(2,1)S(1)}, bf16[64,2048]{1,0:T(8,128)(2,1)S(1)}, u32[]{:S(2)}, u32[]{:S(2)}) %collective-permute-start.28) | collective-permute-done | bytes 262176 | tf_op jit(solution)/shard_map/ppermute | solution.py:271
  109.9 3.2 %experts.8 = (bf16[64,2048]{1,0:T(8,128)(2,1)S(1)}, bf16[64,2048]{1,0:T(8,128)(2,1)S(1)}) custom-call(bf16[64,2048]{1,0:T(8,128)(2,1)S(1)} %collective-permute-done.28.refs_0_, bf16[64,2048]{1,0:T(8,128)(2,1)S(1)} %collective-permute-done.29.refs_1_, bf16[144,512]{1,0:T(8,128)(2,1)S(1)} %collective-permute-done.6.refs_7_.refs_2_, ...), custom_call_target="tpu_custom_call" | custom-call | flops 1207959552 | bytes 9437184 | tf_op jit(solution)/shard_map/experts/pallas_call | solution.py:231
  113.2 1.3 collective-permute-start.30
  115.3 1.6 %collective-permute-start.38 = (bf16[64,2048]{1,0:T(8,128)(2,1)S(1)}, bf16[64,2048]{1,0:T(8,128)(2,1)S(1)}, u32[]{:S(2)}, u32[]{:S(2)}) collective-permute-start(bf16[64,2048]{1,0:T(8,128)(2,1)S(1)} %add_convert_fusion.5), channel_id=1, source_target_pairs={{4,0},{5,1},{8,4},{9,5},{12,8},{13,9},{14,12},{15,13},{10,14},{11,... | collective-permute-start | bytes 786440 | tf_op jit(solution)/shard_map/ppermute | solution.py:271
  117.5 4.9 %collective-permute-done.30 = bf16[64,2048]{1,0:T(8,128)(2,1)S(1)} collective-permute-done((bf16[64,2048]{1,0:T(8,128)(2,1)S(1)}, bf16[64,2048]{1,0:T(8,128)(2,1)S(1)}, u32[]{:S(2)}, u32[]{:S(2)}) %collective-permute-start.30) | collective-permute-done | bytes 262176 | tf_op jit(solution)/shard_map/ppermute | solution.py:271
  122.5 1.3 collective-permute-start.33
  124.7 6.1 %collective-permute-done.33 = bf16[64,2048]{1,0:T(8,128)(2,1)S(1)} collective-permute-done((bf16[64,2048]{1,0:T(8,128)(2,1)S(1)}, bf16[64,2048]{1,0:T(8,128)(2,1)S(1)}, u32[]{:S(2)}, u32[]{:S(2)}) %collective-permute-start.33) | collective-permute-done | bytes 262176 | tf_op jit(solution)/shard_map/ppermute | solution.py:271
  130.9 1.3 collective-permute-start.34
  133.1 6.7 %collective-permute-done.34 = bf16[64,2048]{1,0:T(8,128)(2,1)S(1)} collective-permute-done((bf16[64,2048]{1,0:T(8,128)(2,1)S(1)}, bf16[64,2048]{1,0:T(8,128)(2,1)S(1)}, u32[]{:S(2)}, u32[]{:S(2)}) %collective-permute-start.34) | collective-permute-done | bytes 262176 | tf_op jit(solution)/shard_map/ppermute | solution.py:271
  139.8 1.3 collective-permute-start.35
  142.2 4.0 %collective-permute-done.35 = bf16[64,2048]{1,0:T(8,128)(2,1)S(1)} collective-permute-done((bf16[64,2048]{1,0:T(8,128)(2,1)S(1)}, bf16[64,2048]{1,0:T(8,128)(2,1)S(1)}, u32[]{:S(2)}, u32[]{:S(2)}) %collective-permute-start.35) | collective-permute-done | bytes 262176 | tf_op jit(solution)/shard_map/ppermute | solution.py:271
  146.4 1.5 collective-permute-done.45
  (78 shorter events, 17.2 us)
Async XLA Ops:
  0.0 32.8 %collective-permute-start = (bf16[1,2048,384]{2,1,0:T(8,128)(2,1)}, bf16[1,2048,384]{2,1,0:T(8,128)(2,1)S(1)}, u32[]{:S(2)}, u32[]{:S(2)}) collective-permute-start(bf16[1,2048,384]{2,1,0:T(8,128)(2,1)} %refs_6_.5), channel_id=1, source_target_pairs={{0,1},{1,0},{2,3},{3,2},{4,5},{5,4},{6,7},{7,6},{8,9},{9,8},{10,11... | collective-permute-start | bytes 4718600 | tf_op jit(solution)/shard_map/ppermute | solution.py:271
  0.5 32.9 %collective-permute-start.1 = (bf16[1,2048,384]{2,1,0:T(8,128)(2,1)}, bf16[1,2048,384]{2,1,0:T(8,128)(2,1)S(1)}, u32[]{:S(2)}, u32[]{:S(2)}) collective-permute-start(bf16[1,2048,384]{2,1,0:T(8,128)(2,1)} %refs_7_.5), channel_id=1, source_target_pairs={{0,1},{1,0},{2,3},{3,2},{4,5},{5,4},{6,7},{7,6},{8,9},{9,8},{10,11... | collective-permute-start | bytes 4718600 | tf_op jit(solution)/shard_map/ppermute | solution.py:271
  0.5 32.9 %collective-permute-start.2 = (bf16[1,384,2048]{2,1,0:T(8,128)(2,1)}, bf16[1,384,2048]{2,1,0:T(8,128)(2,1)}, u32[]{:S(2)}, u32[]{:S(2)}) collective-permute-start(bf16[1,384,2048]{2,1,0:T(8,128)(2,1)} %refs_8_.5), channel_id=1, source_target_pairs={{0,1},{1,0},{2,3},{3,2},{4,5},{5,4},{6,7},{7,6},{8,9},{9,8},{10,11... | collective-permute-start | bytes 4718600 | tf_op jit(solution)/shard_map/ppermute | solution.py:271
  3.2 5.2 %collective-permute-start.10 = (bf16[144,512]{1,0:T(8,128)(2,1)}, bf16[144,512]{1,0:T(8,128)(2,1)S(1)}, u32[]{:S(2)}, u32[]{:S(2)}) collective-permute-start(bf16[144,512]{1,0:T(8,128)(2,1)} %pack_message.1.refs_3_.refs_2_), channel_id=1, source_target_pairs={{0,1},{1,0},{2,3},{3,2},{4,5},{5,4},{6,7},{7,6},{8,9},{9,8},{10,11... | collective-permute-start | bytes 442376 | tf_op jit(solution)/shard_map/ppermute | solution.py:271
  3.2 8.1 %collective-permute-start.7 = (bf16[144,512]{1,0:T(8,128)(2,1)}, bf16[144,512]{1,0:T(8,128)(2,1)S(1)}, u32[]{:S(2)}, u32[]{:S(2)}) collective-permute-start(bf16[144,512]{1,0:T(8,128)(2,1)} %pack_message.1.refs_3_.refs_2_), channel_id=1, source_target_pairs={{4,0},{5,1},{8,4},{9,5},{12,8},{13,9},{14,12},{15,13},{10,14},{11,... | collective-permute-start | bytes 442376 | tf_op jit(solution)/shard_map/ppermute | solution.py:271
  8.4 7.2 %collective-permute-start.3 = (bf16[144,512]{1,0:T(8,128)(2,1)}, bf16[144,512]{1,0:T(8,128)(2,1)S(1)}, u32[]{:S(2)}, u32[]{:S(2)}) collective-permute-start(bf16[144,512]{1,0:T(8,128)(2,1)} %pack_message.1.refs_3_.refs_2_), channel_id=1, source_target_pairs={{0,4},{1,5},{4,8},{5,9},{8,12},{9,13},{12,14},{13,15},{14,10},{15,... | collective-permute-start | bytes 442376 | tf_op jit(solution)/shard_map/ppermute | solution.py:271
  11.4 6.0 %collective-permute-start.15 = (bf16[144,512]{1,0:T(8,128)(2,1)S(1)}, bf16[144,512]{1,0:T(8,128)(2,1)S(1)}, u32[]{:S(2)}, u32[]{:S(2)}) collective-permute-start(bf16[144,512]{1,0:T(8,128)(2,1)S(1)} %collective-permute-done.7.refs_8_.refs_5_), channel_id=1, source_target_pairs={{0,1},{1,0},{2,3},{3,2},{4,5},{5,4},{6,7},{7,6},{8,9},{9,8},{10,11... | collective-permute-start | bytes 442376 | tf_op jit(solution)/shard_map/ppermute | solution.py:271
  15.7 5.4 %collective-permute-start.8 = (bf16[144,512]{1,0:T(8,128)(2,1)S(1)}, bf16[144,512]{1,0:T(8,128)(2,1)S(1)}, u32[]{:S(2)}, u32[]{:S(2)}) collective-permute-start(bf16[144,512]{1,0:T(8,128)(2,1)S(1)} %collective-permute-done.7.refs_8_.refs_5_), channel_id=1, source_target_pairs={{4,0},{5,1},{8,4},{9,5},{12,8},{13,9},{14,12},{15,13},{10,14},{11,... | collective-permute-start | bytes 442376 | tf_op jit(solution)/shard_map/ppermute | solution.py:271
  17.4 5.1 %collective-permute-start.4 = (bf16[144,512]{1,0:T(8,128)(2,1)S(1)}, bf16[144,512]{1,0:T(8,128)(2,1)S(1)}, u32[]{:S(2)}, u32[]{:S(2)}) collective-permute-start(bf16[144,512]{1,0:T(8,128)(2,1)S(1)} %collective-permute-done.3.refs_4_), channel_id=1, source_target_pairs={{0,4},{1,5},{4,8},{5,9},{8,12},{9,13},{12,14},{13,15},{14,10},{15,... | collective-permute-start | bytes 442376 | tf_op jit(solution)/shard_map/ppermute | solution.py:271
  21.0 1.8 %collective-permute-start.11 = (bf16[144,512]{1,0:T(8,128)(2,1)S(1)}, bf16[144,512]{1,0:T(8,128)(2,1)S(1)}, u32[]{:S(2)}, u32[]{:S(2)}) collective-permute-start(bf16[144,512]{1,0:T(8,128)(2,1)S(1)} %collective-permute-done.3.refs_4_), channel_id=1, source_target_pairs={{0,1},{1,0},{2,3},{3,2},{4,5},{5,4},{6,7},{7,6},{8,9},{9,8},{10,11... | collective-permute-start | bytes 442376 | tf_op jit(solution)/shard_map/ppermute | solution.py:271
  22.5 5.1 %collective-permute-start.5 = (bf16[144,512]{1,0:T(8,128)(2,1)S(1)}, bf16[144,512]{1,0:T(8,128)(2,1)S(1)}, u32[]{:S(2)}, u32[]{:S(2)}) collective-permute-start(bf16[144,512]{1,0:T(8,128)(2,1)S(1)} %collective-permute-done.4.refs_5_.refs_4_), channel_id=1, source_target_pairs={{0,4},{1,5},{4,8},{5,9},{8,12},{9,13},{12,14},{13,15},{14,10},{15,... | collective-permute-start | bytes 442376 | tf_op jit(solution)/shard_map/ppermute | solution.py:271
  22.8 6.0 %collective-permute-start.9 = (bf16[144,512]{1,0:T(8,128)(2,1)S(1)}, bf16[144,512]{1,0:T(8,128)(2,1)S(1)}, u32[]{:S(2)}, u32[]{:S(2)}) collective-permute-start(bf16[144,512]{1,0:T(8,128)(2,1)S(1)} %collective-permute-done.8.refs_9_.refs_5_), channel_id=1, source_target_pairs={{4,0},{5,1},{8,4},{9,5},{12,8},{13,9},{14,12},{15,13},{10,14},{11,... | collective-permute-start | bytes 442376 | tf_op jit(solution)/shard_map/ppermute | solution.py:271
  27.7 5.1 %collective-permute-start.6 = (bf16[144,512]{1,0:T(8,128)(2,1)S(1)}, bf16[144,512]{1,0:T(8,128)(2,1)S(1)}, u32[]{:S(2)}, u32[]{:S(2)}) collective-permute-start(bf16[144,512]{1,0:T(8,128)(2,1)S(1)} %collective-permute-done.5.refs_6_.refs_4_), channel_id=1, source_target_pairs={{0,4},{1,5},{4,8},{5,9},{8,12},{9,13},{12,14},{13,15},{14,10},{15,... | collective-permute-start | bytes 442376 | tf_op jit(solution)/shard_map/ppermute | solution.py:271
  28.9 5.0 %collective-permute-start.16 = (bf16[144,512]{1,0:T(8,128)(2,1)S(1)}, bf16[144,512]{1,0:T(8,128)(2,1)S(1)}, u32[]{:S(2)}, u32[]{:S(2)}) collective-permute-start(bf16[144,512]{1,0:T(8,128)(2,1)S(1)} %collective-permute-done.8.refs_9_.refs_5_), channel_id=1, source_target_pairs={{0,1},{1,0},{2,3},{3,2},{4,5},{5,4},{6,7},{7,6},{8,9},{9,8},{10,11... | collective-permute-start | bytes 442376 | tf_op jit(solution)/shard_map/ppermute | solution.py:271
  32.8 1.4 collective-permute-start.12
  32.8 1.9 %collective-permute-start.13 = (bf16[144,512]{1,0:T(8,128)(2,1)S(1)}, bf16[144,512]{1,0:T(8,128)(2,1)S(1)}, u32[]{:S(2)}, u32[]{:S(2)}) collective-permute-start(bf16[144,512]{1,0:T(8,128)(2,1)S(1)} %collective-permute-done.5.refs_6_.refs_4_), channel_id=1, source_target_pairs={{0,1},{1,0},{2,3},{3,2},{4,5},{5,4},{6,7},{7,6},{8,9},{9,8},{10,11... | collective-permute-start | bytes 442376 | tf_op jit(solution)/shard_map/ppermute | solution.py:271
  33.4 1.4 collective-permute-start.17
  33.4 1.5 %collective-permute-start.14 = (bf16[144,512]{1,0:T(8,128)(2,1)S(1)}, bf16[144,512]{1,0:T(8,128)(2,1)S(1)}, u32[]{:S(2)}, u32[]{:S(2)}) collective-permute-start(bf16[144,512]{1,0:T(8,128)(2,1)S(1)} %collective-permute-done.6.refs_7_.refs_2_), channel_id=1, source_target_pairs={{0,1},{1,0},{2,3},{3,2},{4,5},{5,4},{6,7},{7,6},{8,9},{9,8},{10,11... | collective-permute-start | bytes 442376 | tf_op jit(solution)/shard_map/ppermute | solution.py:271
  38.6 10.7 %copy-start.1 = (bf16[1,2048,384]{2,1,0:T(8,128)(2,1)S(1)}, bf16[1,2048,384]{2,1,0:T(8,128)(2,1)}, u32[]{:S(2)}) copy-start(bf16[1,2048,384]{2,1,0:T(8,128)(2,1)} %refs_7_.5) | copy-start | bytes 4718596
  38.6 10.7 %copy-start.2 = (bf16[1,384,2048]{2,1,0:T(8,128)(2,1)S(1)}, bf16[1,384,2048]{2,1,0:T(8,128)(2,1)}, u32[]{:S(2)}) copy-start(bf16[1,384,2048]{2,1,0:T(8,128)(2,1)} %refs_8_.5) | copy-start | bytes 4718596
  45.2 9.2 %collective-permute-start.18 = (bf16[64,2048]{1,0:T(8,128)(2,1)S(1)}, bf16[64,2048]{1,0:T(8,128)(2,1)S(1)}, u32[]{:S(2)}, u32[]{:S(2)}) collective-permute-start(bf16[64,2048]{1,0:T(8,128)(2,1)S(1)} %get-tuple-element.46.refs_0_), channel_id=1, source_target_pairs={{0,4},{1,5},{4,8},{5,9},{8,12},{9,13},{12,14},{13,15},{14,10},{15,... | collective-permute-start | bytes 786440 | tf_op jit(solution)/shard_map/ppermute | solution.py:271
  46.5 9.2 %collective-permute-start.19 = (bf16[64,2048]{1,0:T(8,128)(2,1)S(1)}, bf16[64,2048]{1,0:T(8,128)(2,1)S(1)}, u32[]{:S(2)}, u32[]{:S(2)}) collective-permute-start(bf16[64,2048]{1,0:T(8,128)(2,1)S(1)} %get-tuple-element.47.refs_1_), channel_id=1, source_target_pairs={{4,0},{5,1},{8,4},{9,5},{12,8},{13,9},{14,12},{15,13},{10,14},{11,... | collective-permute-start | bytes 786440 | tf_op jit(solution)/shard_map/ppermute | solution.py:271
  47.3 14.0 %collective-permute-start.23 = (bf16[64,2048]{1,0:T(8,128)(2,1)S(1)}, bf16[64,2048]{1,0:T(8,128)(2,1)S(1)}, u32[]{:S(2)}, u32[]{:S(2)}) collective-permute-start(bf16[64,2048]{1,0:T(8,128)(2,1)S(1)} %get-tuple-element.46.refs_0_), channel_id=1, source_target_pairs={{4,0},{5,1},{8,4},{9,5},{12,8},{13,9},{14,12},{15,13},{10,14},{11,... | collective-permute-start | bytes 786440 | tf_op jit(solution)/shard_map/ppermute | solution.py:271
  48.9 13.2 %collective-permute-start.22 = (bf16[64,2048]{1,0:T(8,128)(2,1)S(1)}, bf16[64,2048]{1,0:T(8,128)(2,1)S(1)}, u32[]{:S(2)}, u32[]{:S(2)}) collective-permute-start(bf16[64,2048]{1,0:T(8,128)(2,1)S(1)} %get-tuple-element.47.refs_1_), channel_id=1, source_target_pairs={{0,4},{1,5},{4,8},{5,9},{8,12},{9,13},{12,14},{13,15},{14,10},{15,... | collective-permute-start | bytes 786440 | tf_op jit(solution)/shard_map/ppermute | solution.py:271
  55.7 12.5 %collective-permute-start.20 = (bf16[64,2048]{1,0:T(8,128)(2,1)S(1)}, bf16[64,2048]{1,0:T(8,128)(2,1)S(1)}, u32[]{:S(2)}, u32[]{:S(2)}) collective-permute-start(bf16[64,2048]{1,0:T(8,128)(2,1)S(1)} %collective-permute-done.18.refs_0_), channel_id=1, source_target_pairs={{0,4},{1,5},{4,8},{5,9},{8,12},{9,13},{12,14},{13,15},{14,10},{15,... | collective-permute-start | bytes 786440 | tf_op jit(solution)/shard_map/ppermute | solution.py:271
  57.2 11.1 %collective-permute-start.21 = (bf16[64,2048]{1,0:T(8,128)(2,1)S(1)}, bf16[64,2048]{1,0:T(8,128)(2,1)S(1)}, u32[]{:S(2)}, u32[]{:S(2)}) collective-permute-start(bf16[64,2048]{1,0:T(8,128)(2,1)S(1)} %collective-permute-done.19.refs_3_), channel_id=1, source_target_pairs={{4,0},{5,1},{8,4},{9,5},{12,8},{13,9},{14,12},{15,13},{10,14},{11,... | collective-permute-start | bytes 786440 | tf_op jit(solution)/shard_map/ppermute | solution.py:271
  61.3 10.3 %collective-permute-start.27 = (bf16[64,2048]{1,0:T(8,128)(2,1)S(1)}, bf16[64,2048]{1,0:T(8,128)(2,1)S(1)}, u32[]{:S(2)}, u32[]{:S(2)}) collective-permute-start(bf16[64,2048]{1,0:T(8,128)(2,1)S(1)} %collective-permute-done.23.refs_2_), channel_id=1, source_target_pairs={{4,0},{5,1},{8,4},{9,5},{12,8},{13,9},{14,12},{15,13},{10,14},{11,... | collective-permute-start | bytes 786440 | tf_op jit(solution)/shard_map/ppermute | solution.py:271
  62.1 10.3 %collective-permute-start.26 = (bf16[64,2048]{1,0:T(8,128)(2,1)S(1)}, bf16[64,2048]{1,0:T(8,128)(2,1)S(1)}, u32[]{:S(2)}, u32[]{:S(2)}) collective-permute-start(bf16[64,2048]{1,0:T(8,128)(2,1)S(1)} %collective-permute-done.22.refs_1_), channel_id=1, source_target_pairs={{0,4},{1,5},{4,8},{5,9},{8,12},{9,13},{12,14},{13,15},{14,10},{15,... | collective-permute-start | bytes 786440 | tf_op jit(solution)/shard_map/ppermute | solution.py:271
  68.3 13.6 %collective-permute-start.24 = (bf16[64,2048]{1,0:T(8,128)(2,1)S(1)}, bf16[64,2048]{1,0:T(8,128)(2,1)S(1)}, u32[]{:S(2)}, u32[]{:S(2)}) collective-permute-start(bf16[64,2048]{1,0:T(8,128)(2,1)S(1)} %collective-permute-done.20.refs_0_), channel_id=1, source_target_pairs={{0,4},{1,5},{4,8},{5,9},{8,12},{9,13},{12,14},{13,15},{14,10},{15,... | collective-permute-start | bytes 786440 | tf_op jit(solution)/shard_map/ppermute | solution.py:271
  71.6 9.2 %collective-permute-start.32 = (bf16[64,2048]{1,0:T(8,128)(2,1)S(1)}, bf16[64,2048]{1,0:T(8,128)(2,1)S(1)}, u32[]{:S(2)}, u32[]{:S(2)}) collective-permute-start(bf16[64,2048]{1,0:T(8,128)(2,1)S(1)} %collective-permute-done.27.refs_2_), channel_id=1, source_target_pairs={{4,0},{5,1},{8,4},{9,5},{12,8},{13,9},{14,12},{15,13},{10,14},{11,... | collective-permute-start | bytes 786440 | tf_op jit(solution)/shard_map/ppermute | solution.py:271
  72.4 9.5 %collective-permute-start.31 = (bf16[64,2048]{1,0:T(8,128)(2,1)S(1)}, bf16[64,2048]{1,0:T(8,128)(2,1)S(1)}, u32[]{:S(2)}, u32[]{:S(2)}) collective-permute-start(bf16[64,2048]{1,0:T(8,128)(2,1)S(1)} %collective-permute-done.26.refs_1_), channel_id=1, source_target_pairs={{0,4},{1,5},{4,8},{5,9},{8,12},{9,13},{12,14},{13,15},{14,10},{15,... | collective-permute-start | bytes 786440 | tf_op jit(solution)/shard_map/ppermute | solution.py:271
  73.7 11.0 %collective-permute-start.25 = (bf16[64,2048]{1,0:T(8,128)(2,1)S(1)}, bf16[64,2048]{1,0:T(8,128)(2,1)S(1)}, u32[]{:S(2)}, u32[]{:S(2)}) collective-permute-start(bf16[64,2048]{1,0:T(8,128)(2,1)S(1)} %collective-permute-done.21.refs_3_), channel_id=1, source_target_pairs={{4,0},{5,1},{8,4},{9,5},{12,8},{13,9},{14,12},{15,13},{10,14},{11,... | collective-permute-start | bytes 786440 | tf_op jit(solution)/shard_map/ppermute | solution.py:271
  89.5 9.1 %collective-permute-start.36 = (bf16[64,2048]{1,0:T(8,128)(2,1)S(1)}, bf16[64,2048]{1,0:T(8,128)(2,1)S(1)}, u32[]{:S(2)}, u32[]{:S(2)}) collective-permute-start(bf16[64,2048]{1,0:T(8,128)(2,1)S(1)} %get-tuple-element.72), channel_id=1, source_target_pairs={{4,0},{5,1},{8,4},{9,5},{12,8},{13,9},{14,12},{15,13},{10,14},{11,... | collective-permute-start | bytes 786440 | tf_op jit(solution)/shard_map/ppermute | solution.py:271
  95.3 9.3 %collective-permute-start.39 = (bf16[64,2048]{1,0:T(8,128)(2,1)S(1)}, bf16[64,2048]{1,0:T(8,128)(2,1)S(1)}, u32[]{:S(2)}, u32[]{:S(2)}) collective-permute-start(bf16[64,2048]{1,0:T(8,128)(2,1)S(1)} %get-tuple-element.76), channel_id=1, source_target_pairs={{0,4},{1,5},{4,8},{5,9},{8,12},{9,13},{12,14},{13,15},{14,10},{15,... | collective-permute-start | bytes 786440 | tf_op jit(solution)/shard_map/ppermute | solution.py:271
  96.6 13.4 %collective-permute-start.28 = (bf16[64,2048]{1,0:T(8,128)(2,1)S(1)}, bf16[64,2048]{1,0:T(8,128)(2,1)S(1)}, u32[]{:S(2)}, u32[]{:S(2)}) collective-permute-start(bf16[64,2048]{1,0:T(8,128)(2,1)S(1)} %collective-permute-done.24.refs_0_), channel_id=1, source_target_pairs={{0,4},{1,5},{4,8},{5,9},{8,12},{9,13},{12,14},{13,15},{14,10},{15,... | collective-permute-start | bytes 786440 | tf_op jit(solution)/shard_map/ppermute | solution.py:271
  98.1 11.9 %collective-permute-start.29 = (bf16[64,2048]{1,0:T(8,128)(2,1)S(1)}, bf16[64,2048]{1,0:T(8,128)(2,1)S(1)}, u32[]{:S(2)}, u32[]{:S(2)}) collective-permute-start(bf16[64,2048]{1,0:T(8,128)(2,1)S(1)} %collective-permute-done.25.refs_3_), channel_id=1, source_target_pairs={{4,0},{5,1},{8,4},{9,5},{12,8},{13,9},{14,12},{15,13},{10,14},{11,... | collective-permute-start | bytes 786440 | tf_op jit(solution)/shard_map/ppermute | solution.py:271
  98.7 16.6 %collective-permute-start.37 = (bf16[64,2048]{1,0:T(8,128)(2,1)S(1)}, bf16[64,2048]{1,0:T(8,128)(2,1)S(1)}, u32[]{:S(2)}, u32[]{:S(2)}) collective-permute-start(bf16[64,2048]{1,0:T(8,128)(2,1)S(1)} %add_convert_fusion.6), channel_id=1, source_target_pairs={{4,0},{5,1},{8,4},{9,5},{12,8},{13,9},{14,12},{15,13},{10,14},{11,... | collective-permute-start | bytes 786440 | tf_op jit(solution)/shard_map/ppermute | solution.py:271
  104.6 12.3 %collective-permute-start.40 = (bf16[64,2048]{1,0:T(8,128)(2,1)S(1)}, bf16[64,2048]{1,0:T(8,128)(2,1)S(1)}, u32[]{:S(2)}, u32[]{:S(2)}) collective-permute-start(bf16[64,2048]{1,0:T(8,128)(2,1)S(1)} %add_convert_fusion.4), channel_id=1, source_target_pairs={{0,4},{1,5},{4,8},{5,9},{8,12},{9,13},{12,14},{13,15},{14,10},{15,... | collective-permute-start | bytes 786440 | tf_op jit(solution)/shard_map/ppermute | solution.py:271
  113.2 9.3 %collective-permute-start.30 = (bf16[64,2048]{1,0:T(8,128)(2,1)S(1)}, bf16[64,2048]{1,0:T(8,128)(2,1)S(1)}, u32[]{:S(2)}, u32[]{:S(2)}) collective-permute-start(bf16[64,2048]{1,0:T(8,128)(2,1)S(1)} %get-tuple-element.68), channel_id=1, source_target_pairs={{0,4},{1,5},{4,8},{5,9},{8,12},{9,13},{12,14},{13,15},{14,10},{15,... | collective-permute-start | bytes 786440 | tf_op jit(solution)/shard_map/ppermute | solution.py:271
  114.5 9.4 %collective-permute-start.42 = (bf16[64,2048]{1,0:T(8,128)(2,1)S(1)}, bf16[64,2048]{1,0:T(8,128)(2,1)S(1)}, u32[]{:S(2)}, u32[]{:S(2)}) collective-permute-start(bf16[64,2048]{1,0:T(8,128)(2,1)S(1)} %get-tuple-element.79), channel_id=1, source_target_pairs={{4,0},{5,1},{8,4},{9,5},{12,8},{13,9},{14,12},{15,13},{10,14},{11,... | collective-permute-start | bytes 786440 | tf_op jit(solution)/shard_map/ppermute | solution.py:271
  115.3 26.9 %collective-permute-start.38 = (bf16[64,2048]{1,0:T(8,128)(2,1)S(1)}, bf16[64,2048]{1,0:T(8,128)(2,1)S(1)}, u32[]{:S(2)}, u32[]{:S(2)}) collective-permute-start(bf16[64,2048]{1,0:T(8,128)(2,1)S(1)} %add_convert_fusion.5), channel_id=1, source_target_pairs={{4,0},{5,1},{8,4},{9,5},{12,8},{13,9},{14,12},{15,13},{10,14},{11,... | collective-permute-start | bytes 786440 | tf_op jit(solution)/shard_map/ppermute | solution.py:271
  117.0 29.3 %collective-permute-start.41 = (bf16[64,2048]{1,0:T(8,128)(2,1)S(1)}, bf16[64,2048]{1,0:T(8,128)(2,1)S(1)}, u32[]{:S(2)}, u32[]{:S(2)}) collective-permute-start(bf16[64,2048]{1,0:T(8,128)(2,1)S(1)} %add_convert_fusion.3), channel_id=1, source_target_pairs={{0,4},{1,5},{4,8},{5,9},{8,12},{9,13},{12,14},{13,15},{14,10},{15,... | collective-permute-start | bytes 786440 | tf_op jit(solution)/shard_map/ppermute | solution.py:271
  122.5 8.3 %collective-permute-start.33 = (bf16[64,2048]{1,0:T(8,128)(2,1)S(1)}, bf16[64,2048]{1,0:T(8,128)(2,1)S(1)}, u32[]{:S(2)}, u32[]{:S(2)}) collective-permute-start(bf16[64,2048]{1,0:T(8,128)(2,1)S(1)} %add_convert_fusion.9), channel_id=1, source_target_pairs={{0,4},{1,5},{4,8},{5,9},{8,12},{9,13},{12,14},{13,15},{14,10},{15,... | collective-permute-start | bytes 786440 | tf_op jit(solution)/shard_map/ppermute | solution.py:271
  123.9 8.3 %collective-permute-start.43 = (bf16[64,2048]{1,0:T(8,128)(2,1)S(1)}, bf16[64,2048]{1,0:T(8,128)(2,1)S(1)}, u32[]{:S(2)}, u32[]{:S(2)}) collective-permute-start(bf16[64,2048]{1,0:T(8,128)(2,1)S(1)} %add_convert_fusion.2), channel_id=1, source_target_pairs={{4,0},{5,1},{8,4},{9,5},{12,8},{13,9},{14,12},{15,13},{10,14},{11,... | collective-permute-start | bytes 786440 | tf_op jit(solution)/shard_map/ppermute | solution.py:271
  130.9 8.9 %collective-permute-start.34 = (bf16[64,2048]{1,0:T(8,128)(2,1)S(1)}, bf16[64,2048]{1,0:T(8,128)(2,1)S(1)}, u32[]{:S(2)}, u32[]{:S(2)}) collective-permute-start(bf16[64,2048]{1,0:T(8,128)(2,1)S(1)} %add_convert_fusion.8), channel_id=1, source_target_pairs={{0,4},{1,5},{4,8},{5,9},{8,12},{9,13},{12,14},{13,15},{14,10},{15,... | collective-permute-start | bytes 786440 | tf_op jit(solution)/shard_map/ppermute | solution.py:271
  132.3 9.1 %collective-permute-start.44 = (bf16[64,2048]{1,0:T(8,128)(2,1)S(1)}, bf16[64,2048]{1,0:T(8,128)(2,1)S(1)}, u32[]{:S(2)}, u32[]{:S(2)}) collective-permute-start(bf16[64,2048]{1,0:T(8,128)(2,1)S(1)} %add_convert_fusion.1), channel_id=1, source_target_pairs={{4,0},{5,1},{8,4},{9,5},{12,8},{13,9},{14,12},{15,13},{10,14},{11,... | collective-permute-start | bytes 786440 | tf_op jit(solution)/shard_map/ppermute | solution.py:271
  139.8 6.4 %collective-permute-start.35 = (bf16[64,2048]{1,0:T(8,128)(2,1)S(1)}, bf16[64,2048]{1,0:T(8,128)(2,1)S(1)}, u32[]{:S(2)}, u32[]{:S(2)}) collective-permute-start(bf16[64,2048]{1,0:T(8,128)(2,1)S(1)} %add_convert_fusion.7), channel_id=1, source_target_pairs={{0,4},{1,5},{4,8},{5,9},{8,12},{9,13},{12,14},{13,15},{14,10},{15,... | collective-permute-start | bytes 786440 | tf_op jit(solution)/shard_map/ppermute | solution.py:271
  141.4 6.4 %collective-permute-start.45 = (bf16[64,2048]{1,0:T(8,128)(2,1)S(1)}, bf16[64,2048]{1,0:T(8,128)(2,1)S(1)}, u32[]{:S(2)}, u32[]{:S(2)}) collective-permute-start(bf16[64,2048]{1,0:T(8,128)(2,1)S(1)} %add_convert_fusion), channel_id=1, source_target_pairs={{4,0},{5,1},{8,4},{9,5},{12,8},{13,9},{14,12},{15,13},{10,14},{11,... | collective-permute-start | bytes 786440 | tf_op jit(solution)/shard_map/ppermute | solution.py:271
  (5 other events, 14.4 us)

commit v3 on v2

--- a/solution.py
+++ b/solution.py
@@ -59,22 +59,51 @@
     )(stretch_pos, keys, values, routes.T, combine.T)
 
 
-def attend_kernel(count, *refs):
-    query_hbm, residual_hbm, gain_hbm = refs[:3]
+def stage_kernel(query_ref, residual_ref, gain_ref, stacked_ref, residual_out, gain_out):
+    rows = query_ref.shape[0]
+    halves = stacked_ref.shape[0]
+    some = rows // halves
+    sub = lax.broadcasted_iota(jnp.int32, (rows, rows), 0)
+    lane = lax.broadcasted_iota(jnp.int32, (rows, rows), 1)
+    eye = jnp.where(sub == lane, 1.0, 0.0).astype(jnp.bfloat16)
+    for half in range(halves):
+        mine = slice(half * some, (half + 1) * some)
+        for h in range(query_ref.shape[1] // HEAD_SIZE):
+            at = slice(h * some, (h + 1) * some)
+            stacked_ref[half, at, 0:HEAD_SIZE] = query_ref[mine, h * HEAD_SIZE : (h + 1) * HEAD_SIZE]
+            stacked_ref[half, at, HEAD_SIZE : HEAD_SIZE + rows] = eye[mine]
+        residual_out[half] = residual_ref[mine, :]
+    gain_out[...] = gain_ref[...]
+
+
+def stage(queries, residual, gain):
+    rows, features = queries.shape
+    heads = features // HEAD_SIZE
+    vmem = pl.BlockSpec(memory_space=pltpu.VMEM)
+    return pl.pallas_call(
+        stage_kernel,
+        out_shape=(
+            jax.ShapeDtypeStruct((2, heads * rows // 2, HEAD_SIZE + rows), jnp.bfloat16),
+            jax.ShapeDtypeStruct((2, rows // 2, features), jnp.bfloat16),
+            jax.ShapeDtypeStruct((1, features), jnp.float32),
+        ),
+        in_specs=[vmem] * 3,
+        out_specs=(vmem,) * 3,
+        cost_estimate=pl.CostEstimate(
+            flops=0, bytes_accessed=10 * rows * features, transcendentals=0
+        ),
+        name="stage",
+    )(queries, residual, gain.reshape(1, features))
+
+
+def attend_kernel(count, half, *refs):
+    stacked_ref, residual_ref, gain_ref = refs[:3]
     messages = refs[3 : 3 + count]
-    hidden_ref, upper_ref, lower_ref, key_ext, value_ext = refs[3 + count : 8 + count]
-    query_ref, residual_ref, gain_ref, arrived = refs[8 + count :]
-    fetches = [
-        pltpu.make_async_copy(source, target, arrived.at[i])
-        for i, (source, target) in enumerate(
-            [(query_hbm, query_ref), (residual_hbm, residual_ref), (gain_hbm, gain_ref)]
-        )
-    ]
-    for fetch in fetches:
-        fetch.start()
-    rows = query_ref.shape[0]
+    hidden_ref, normed_ref, key_ext, value_ext = refs[3 + count :]
+    some, features = residual_ref.shape[1:]
+    rows = messages[0].shape[0] - EXTRA
     kv_heads = key_ext.shape[0]
-    heads = query_ref.shape[1] // HEAD_SIZE
+    heads = features // HEAD_SIZE
     group = heads // kv_heads
     span = count * rows
     width = kv_heads * HEAD_SIZE
@@ -96,22 +125,13 @@
                 0:rows, width + a * HEAD_SIZE : width + (a + 1) * HEAD_SIZE
             ]
             value_ext[a, at, HEAD_SIZE : 2 * HEAD_SIZE] = ones
-    eye = jnp.where(sub == lane, 1.0, 0.0).astype(jnp.bfloat16)
-    for fetch in fetches:
-        fetch.wait()
     rate = math.log2(math.e) / math.sqrt(HEAD_SIZE)
     step = min(512, span)
-    pair = 2
-    squares = jnp.zeros((rows, HEAD_SIZE), jnp.float32)
+    pair = 4
+    squares = jnp.zeros((some, HEAD_SIZE), jnp.float32)
     for first in range(0, heads, pair):
         a = first // group
-        stacked = jnp.concatenate(
-            [
-                jnp.concatenate([query_ref[:, h * HEAD_SIZE : (h + 1) * HEAD_SIZE], eye], axis=1)
-                for h in range(first, first + pair)
-            ],
-            axis=0,
-        )
+        stacked = stacked_ref[half, first * some : (first + pair) * some, :]
         scores = [
             lax.dot_general(
                 stacked,
@@ -135,8 +155,8 @@
         attended = (total[:, 0:HEAD_SIZE] / total[:, HEAD_SIZE:]).astype(jnp.bfloat16)
         for j in range(pair):
             cols = slice((first + j) * HEAD_SIZE, (first + j + 1) * HEAD_SIZE)
-            state = residual_ref[:, cols].astype(jnp.float32) + attended[
-                j * rows : (j + 1) * rows
+            state = residual_ref[half, :, cols].astype(jnp.float32) + attended[
+                j * some : (j + 1) * some
             ].astype(jnp.float32)
             hidden_ref[:, cols] = state
             squares = squares + state * state
@@ -144,40 +164,36 @@
     inverse = lax.rsqrt(meansq + 1e-06)
     for h in range(heads):
         cols = slice(h * HEAD_SIZE, (h + 1) * HEAD_SIZE)
-        normed = (hidden_ref[:, cols] * inverse * gain_ref[:, cols]).astype(jnp.bfloat16)
-        upper_ref[:, cols] = normed[: rows // 2]
-        lower_ref[:, cols] = normed[rows // 2 :]
-
-
-def attend(queries, residual, gain, messages):
-    rows, features = queries.shape
+        normed_ref[:, cols] = (hidden_ref[:, cols] * inverse * gain_ref[:, cols]).astype(
+            jnp.bfloat16
+        )
+
+
+def attend(half, staged, messages):
+    some, features = staged[1].shape[1:]
+    rows = messages[0].shape[0] - EXTRA
     count = len(messages)
     kv_heads = messages[0].shape[1] // (2 * HEAD_SIZE)
     vmem = pl.BlockSpec(memory_space=pltpu.VMEM)
     span = count * rows
     return pl.pallas_call(
-        functools.partial(attend_kernel, count),
+        functools.partial(attend_kernel, count, half),
         out_shape=(
-            jax.ShapeDtypeStruct((rows, features), jnp.float32),
-            jax.ShapeDtypeStruct((rows // 2, features), jnp.bfloat16),
-            jax.ShapeDtypeStruct((rows // 2, features), jnp.bfloat16),
+            jax.ShapeDtypeStruct((some, features), jnp.float32),
+            jax.ShapeDtypeStruct((some, features), jnp.bfloat16),
         ),
-        in_specs=[pl.BlockSpec(memory_space=pl.ANY)] * 3 + [vmem] * count,
-        out_specs=(vmem, vmem, vmem),
+        in_specs=[vmem] * (3 + count),
+        out_specs=(vmem, vmem),
         scratch_shapes=[
             pltpu.VMEM((kv_heads, span, 2 * HEAD_SIZE), jnp.bfloat16),
             pltpu.VMEM((kv_heads, span, 2 * HEAD_SIZE), jnp.bfloat16),
-            pltpu.VMEM((rows, features), jnp.bfloat16),
-            pltpu.VMEM((rows, features), jnp.bfloat16),
-            pltpu.VMEM((1, features), jnp.float32),
-            pltpu.SemaphoreType.DMA((3,)),
         ],
         compiler_params=pltpu.CompilerParams(vmem_limit_bytes=28 * 1024 * 1024),
         cost_estimate=pl.CostEstimate(
-            flops=8 * rows * span * features, bytes_accessed=8 * 1024 * 1024, transcendentals=0
+            flops=4 * rows * span * features, bytes_accessed=4 * 1024 * 1024, transcendentals=0
         ),
         name="attend",
-    )(queries, residual, gain.reshape(1, features), *messages)
+    )(*staged, *messages)
 
 
 def expert_kernel(places, count, *refs):
@@ -271,52 +287,64 @@
         return lax.ppermute(array, "ctx", pairs)
 
     message = pack_message(stretch_pos, rotated_keys, value_matrix, routes, combine)
-    twins = tuple(send(w, swap) for w in (gate_weight, up_weight, down_weight))
 
     left, right = {0: message}, {0: message}
     for hop in range(1, far + 1):
+        if hop == 3:
+            inputs, unused = lax.optimization_barrier(
+                ((queries, residual, norm_gain), (left[1], right[1]))
+            )
+            staged = stage(*inputs)
+            left[2], staged = lax.optimization_barrier((left[2], staged))
         left[hop] = send(left[hop - 1], onward)
         if hop < far:
             right[hop] = send(right[hop - 1], back)
     plane = [message] + [left[h] for h in range(1, far + 1)] + [right[h] for h in range(1, far)]
     everything = plane + [send(m, swap) for m in plane]
-    norm_gain, twins = lax.optimization_barrier((norm_gain, twins))
-    weights = (gate_weight, up_weight, down_weight) + twins
-    hidden_state, upper, lower = attend(queries, residual, norm_gain, everything)
-
-    from_left = {(0, 0): upper, (0, 1): lower}
-    from_right = {(0, 0): upper, (0, 1): lower}
-    out_left, out_right = {}, {}
-
-    def pieces_of(hop):
-        return [
-            (from_left[hop, 0], 0, 0),
-            (from_left[hop, 1], 0, 1),
-            (from_right[hop, 0], 1, 0),
-            (from_right[hop, 1], 1, 1),
-        ]
+    everything, to_swap = lax.optimization_barrier(
+        (everything, (gate_weight, up_weight, down_weight))
+    )
+    weights = (gate_weight, up_weight, down_weight) + tuple(send(w, swap) for w in to_swap)
+    hidden_upper, upper = attend(0, staged, everything)
+    everything, upper = lax.optimization_barrier((everything, upper))
+    hidden_lower, lower = attend(1, staged, everything)
+
+    from_left, from_right = {(0, 0): upper, (0, 1): lower}, {(0, 0): upper, (0, 1): lower}
+    outs = {}
+
+    def experts_of(hop, after):
+        if hop == 0:
+            pieces, used = [(upper, 0, 0), (lower, 0, 1)], [message]
+        elif hop == far:
+            pieces, used = [(from_left[far, 0], 0, 0), (from_right[far, 1], 0, 1)], [left[far]]
+        else:
+            pieces = [(from_left[hop, 0], 0, 0), (from_left[hop, 1], 0, 1)]
+            pieces += [(from_right[hop, 0], 1, 0), (from_right[hop, 1], 1, 1)]
+            used = [left[hop], right[hop]]
+        used, after = lax.optimization_barrier((used, after))
+        return run_experts(pieces, used, weights), after
 
     for hop in range(1, far + 1):
-        first_left, first_right = from_left[hop - 1, 0], from_right[hop - 1, 1]
+        onto, backto = from_left[hop - 1, 0], from_right[hop - 1, 0]
+        if hop > 2:
+            outs[hop - 2], outs[hop - 3] = experts_of(hop - 2, outs[hop - 3])
+            onto, backto, outs[hop - 2] = lax.optimization_barrier((onto, backto, outs[hop - 2]))
+        from_left[hop, 0] = send(onto, onward)
+        if hop < far:
+            from_right[hop, 0] = send(backto, back)
+        onto, backto = from_left[hop - 1, 1], from_right[hop - 1, 1]
         if hop == 2:
-            own_out = run_experts([(upper, 0, 0), (lower, 0, 1)], [message], weights)
-            first_left, first_right, own_out = lax.optimization_barrier(
-                (first_left, first_right, own_out)
-            )
-        if hop > 2:
-            outs = run_experts(pieces_of(hop - 2), [left[hop - 2], right[hop - 2]], weights)
-            first_left, first_right, outs = lax.optimization_barrier((first_left, first_right, outs))
-            out_left[hop - 2], out_right[hop - 2] = outs[:2], outs[2:]
-        from_left[hop, 0] = send(first_left, onward)
-        from_right[hop, 1] = send(first_right, back)
+            outs[0], unused = experts_of(0, from_left[1, 0])
+            onto, backto, outs[0] = lax.optimization_barrier((onto, backto, outs[0]))
         if hop < far:
-            from_left[hop, 1] = send(from_left[hop - 1, 1], onward)
-            from_right[hop, 0] = send(from_right[hop - 1, 0], back)
-    outs = run_experts(pieces_of(far - 1), [left[far - 1], right[far - 1]], weights)
-    out_left[far - 1], out_right[far - 1] = outs[:2], outs[2:]
-    far_upper, far_lower = run_experts(
-        [(from_left[far, 0], 0, 0), (from_right[far, 1], 0, 1)], [left[far]], weights
-    )
+            from_left[hop, 1] = send(onto, onward)
+        from_right[hop, 1] = send(backto, back)
+    outs[far - 1], outs[far - 2] = experts_of(far - 1, outs[far - 2])
+    outs[far], outs[far - 1] = experts_of(far, outs[far - 1])
+    out_left = {hop: outs[hop][:2] for hop in range(1, far)}
+    out_right = {hop: outs[hop][2:] for hop in range(1, far)}
+    far_upper, far_lower = outs[far]
+    own_out = outs[0]
 
     sums_on = {1: send(out_right[far - 1][1], onward)}
     sums_back = {0: send(out_left[far - 1][0], back)}
@@ -328,16 +356,19 @@
             sums_back[0] = send(add_parts(sums_back[0], out_left[hop][0]), back)
         sums_on[0] = send(add_parts(sums_on[0], out_right[hop][0]), onward)
         sums_back[1] = send(add_parts(sums_back[1], out_left[hop][1]), back)
-    mixture = jnp.concatenate(
+    hidden_state = (hidden_upper, hidden_lower)
+    return jnp.concatenate(
         [
-            own_out[half].astype(jnp.float32)
-            + sums_on[half].astype(jnp.float32)
-            + sums_back[half].astype(jnp.float32)
+            (
+                hidden_state[half]
+                + own_out[half].astype(jnp.float32)
+                + sums_on[half].astype(jnp.float32)
+                + sums_back[half].astype(jnp.float32)
+            ).astype(jnp.bfloat16)
             for half in range(2)
         ],
         axis=0,
     )
-    return (hidden_state + mixture).astype(jnp.bfloat16)
 
 
 def exchange_device(
@@ -488,7 +519,7 @@
         routes, gate_weight = arguments[6], arguments[8]
         dense = 4 * routes.shape[1] >= gate_weight.shape[0] * ctx_count
         ringed = gate_weight.shape[0] == 1 and ctx_count % (2 * CORES) == 0
-        ringed = ringed and ctx_count >= 4 * CORES and 2 * routes.shape[1] == EXTRA
+        ringed = ringed and ctx_count >= 6 * CORES and 2 * routes.shape[1] == EXTRA
         return (ring_device if dense and ringed else exchange_device)(*arguments)
 
     return jax.shard_map(

time: 149 us -> 125 us (0.84)
  waiting for transfers between devices: 70.5 us -> 55.3 us
  starting transfers between devices: 42.8 us -> 37.1 us
  Pallas kernels: 29.3 us -> 26 us
    ppermute x46, waiting for transfers between devices: 70.5 us -> 55.3 us  [send(): return lax.ppermute(array, 'ctx', pairs)]
    pallas_call x5, Pallas kernels: 21.1 us -> 14.1 us  [run_experts(): pl.pallas_call(functools.partial(expert_kernel, [piece[1:] for piece in p...]
    ppermute x46, starting transfers between devices: 42.8 us -> 37.1 us  [send(): return lax.ppermute(array, 'ctx', pairs)]
    pallas_call x1 -> x3, Pallas kernels: 6.6 us -> 10.3 us  [the longest x2 7.6 us: attend(): pl.pallas_call(functools.partial(attend_kernel, count, half), out_shape=(...]
    unnamed x14 -> x20, local copies, waits for them, and re-layouts: 3.7 us -> 3.9 us
  transfers between devices with their start and end apart: 46 -> 46, of which waited for: 24 -> 28; matrix products, arithmetic and copies ran while one was open for 0% -> 1% of each run, Pallas kernels for 12% -> 20%
where the time goes in v3:
time: 125 us
  waiting for transfers between devices  55.3 us (44%)
  starting transfers between devices  37.1 us (30%)
  Pallas kernels  26 us (21%)
  local copies, waits for them, and re-layouts  3.9 us (3%)
  other arithmetic  1.73 us (1%)
    ppermute x46, waiting for transfers between devices, send(): return lax.ppermute(array, 'ctx', pairs)  55.3 us
    ppermute x46, starting transfers between devices, send(): return lax.ppermute(array, 'ctx', pairs)  37.1 us
    pallas_call x5, Pallas kernels, run_experts(): pl.pallas_call(functools.partial(expert_kernel, [piece[1:] for piece in p...  14.1 us
    pallas_call x2, Pallas kernels, attend(): pl.pallas_call(functools.partial(attend_kernel, count, half), out_shape=(...  7.6 us
    unnamed x20, local copies, waits for them, and re-layouts  3.9 us
    pallas_call x1, Pallas kernels, stage(): pl.pallas_call(stage_kernel, out_shape=(jax.ShapeDtypeStruct((2, heads *...  2.67 us
  transfers between devices with their start and end apart: 46, of which 28 were waited for; matrix products, arithmetic and copies ran while one was open for 1% of the time, Pallas kernels for 20%

profile of v3, /device:TPU:0, one launch (start us, length us, event | category | flops | bytes accessed | tf_op | source)
XLA Modules:
  0.0 124.9 jit_solution(13390924824416437271)
XLA Ops:
  0.7 1.6 %pack_message.1.refs_3_.refs_2_ = bf16[144,512]{1,0:T(8,128)(2,1)} custom-call(s32[1]{0:T(128)S(6)} %copy.12.pos_ref, bf16[128,256]{1,0:T(8,128)(2,1)} %key_ref.1, bf16[128,256]{1,0:T(8,128)(2,1)} %value_ref.1, s32[8,128]{1,0:T(8,128)} %bitcast.4, f32[8,128]{1,0:T(8,128)} %bitcast.5), custom_call_target="tpu_custom_call" | custom-call | tf_op jit(solution)/shard_map/pack_message/pallas_call | solution.py:53
  2.2 3.0 %collective-permute-start = (bf16[144,512]{1,0:T(8,128)(2,1)}, bf16[144,512]{1,0:T(8,128)(2,1)S(1)}, u32[]{:S(2)}, u32[]{:S(2)}) collective-permute-start(bf16[144,512]{1,0:T(8,128)(2,1)} %pack_message.1.refs_3_.refs_2_), channel_id=1, source_target_pairs={{0,4},{1,5},{4,8},{5,9},{8,12},{9,13},{12,14},{13,15},{14,10},{15,... | collective-permute-start | bytes 442376 | tf_op jit(solution)/shard_map/ppermute | solution.py:287
  5.2 4.0 %collective-permute-done.refs_4_ = bf16[144,512]{1,0:T(8,128)(2,1)S(1)} collective-permute-done((bf16[144,512]{1,0:T(8,128)(2,1)}, bf16[144,512]{1,0:T(8,128)(2,1)S(1)}, u32[]{:S(2)}, u32[]{:S(2)}) %collective-permute-start) | collective-permute-done | bytes 147488 | tf_op jit(solution)/shard_map/ppermute | solution.py:287
  9.2 1.8 %collective-permute-start.1 = (bf16[144,512]{1,0:T(8,128)(2,1)S(1)}, bf16[144,512]{1,0:T(8,128)(2,1)S(1)}, u32[]{:S(2)}, u32[]{:S(2)}) collective-permute-start(bf16[144,512]{1,0:T(8,128)(2,1)S(1)} %collective-permute-done.refs_4_), channel_id=1, source_target_pairs={{0,4},{1,5},{4,8},{5,9},{8,12},{9,13},{12,14},{13,15},{14,10},{15,... | collective-permute-start | bytes 442376 | tf_op jit(solution)/shard_map/ppermute | solution.py:287
  11.0 2.7 %stage.1 = (bf16[2,1024,256]{2,1,0:T(8,128)(2,1)}, bf16[2,64,2048]{2,1,0:T(8,128)(2,1)}, f32[1,2048]{1,0:T(1,128)}) custom-call(bf16[128,2048]{1,0:T(8,128)(2,1)} %query_ref, bf16[128,2048]{1,0:T(8,128)(2,1)} %residual_ref, f32[1,2048]{1,0:T(1,128)} %bitcast.3), custom_call_target="tpu_custom_call" | custom-call | bytes 2621440 | tf_op jit(solution)/shard_map/stage/pallas_call | solution.py:83
  14.4 1.8 %collective-permute-start.3 = (bf16[144,512]{1,0:T(8,128)(2,1)S(1)}, bf16[144,512]{1,0:T(8,128)(2,1)S(1)}, u32[]{:S(2)}, u32[]{:S(2)}) collective-permute-start(bf16[144,512]{1,0:T(8,128)(2,1)S(1)} %collective-permute-done.1.refs_5_.refs_4_), channel_id=1, source_target_pairs={{0,4},{1,5},{4,8},{5,9},{8,12},{9,13},{12,14},{13,15},{14,10},{15,... | collective-permute-start | bytes 442376 | tf_op jit(solution)/shard_map/ppermute | solution.py:287
  16.7 2.2 %collective-permute-done.5.refs_9_.refs_5_ = bf16[144,512]{1,0:T(8,128)(2,1)S(1)} collective-permute-done((bf16[144,512]{1,0:T(8,128)(2,1)S(1)}, bf16[144,512]{1,0:T(8,128)(2,1)S(1)}, u32[]{:S(2)}, u32[]{:S(2)}) %collective-permute-start.5) | collective-permute-done | bytes 147488 | tf_op jit(solution)/shard_map/ppermute | solution.py:287
  19.5 1.8 %collective-permute-start.4 = (bf16[144,512]{1,0:T(8,128)(2,1)S(1)}, bf16[144,512]{1,0:T(8,128)(2,1)S(1)}, u32[]{:S(2)}, u32[]{:S(2)}) collective-permute-start(bf16[144,512]{1,0:T(8,128)(2,1)S(1)} %collective-permute-done.3.refs_6_.refs_4_), channel_id=1, source_target_pairs={{0,4},{1,5},{4,8},{5,9},{8,12},{9,13},{12,14},{13,15},{14,10},{15,... | collective-permute-start | bytes 442376 | tf_op jit(solution)/shard_map/ppermute | solution.py:287
  21.9 2.1 %collective-permute-done.6.refs_10_.refs_5_ = bf16[144,512]{1,0:T(8,128)(2,1)S(1)} collective-permute-done((bf16[144,512]{1,0:T(8,128)(2,1)S(1)}, bf16[144,512]{1,0:T(8,128)(2,1)S(1)}, u32[]{:S(2)}, u32[]{:S(2)}) %collective-permute-start.6) | collective-permute-done | bytes 147488 | tf_op jit(solution)/shard_map/ppermute | solution.py:287
  26.7 0.9 copy-done.3
  27.6 1.2 copy-done.5
  28.8 1.0 copy-done.7
  30.6 3.7 %attend.2 = (f32[64,2048]{1,0:T(8,128)S(1)}, bf16[64,2048]{1,0:T(8,128)(2,1)S(1)}) custom-call(bf16[2,1024,256]{2,1,0:T(8,128)(2,1)S(1)} %copy-done.5, bf16[2,64,2048]{2,1,0:T(8,128)(2,1)S(1)} %copy-done.7, f32[1,2048]{1,0:T(1,128)S(1)} %copy-done.9, bf16[144,512]{1,0:T(8,128)(2,1)S(1)} %copy-done.3, bf16[144,512]{1,0:T(8,128)(2,1)S(1)} %collective-permute-done.refs_4_, ...), custom_call_target="tpu_custom_call" | custom-call | flops 2147483648 | bytes 4194304 | tf_op jit(solution)/shard_map/attend/pallas_call | solution.py:179
  34.3 1.9 %collective-permute-start.17 = (bf16[64,2048]{1,0:T(8,128)(2,1)S(1)}, bf16[64,2048]{1,0:T(8,128)(2,1)S(1)}, u32[]{:S(2)}, u32[]{:S(2)}) collective-permute-start(bf16[64,2048]{1,0:T(8,128)(2,1)S(1)} %get-tuple-element.153.refs_0_), channel_id=1, source_target_pairs={{0,4},{1,5},{4,8},{5,9},{8,12},{9,13},{12,14},{13,15},{14,10},{15,... | collective-permute-start | bytes 786440 | tf_op jit(solution)/shard_map/ppermute | solution.py:287
  36.4 3.9 %attend.3 = (f32[64,2048]{1,0:T(8,128)S(1)}, bf16[64,2048]{1,0:T(8,128)(2,1)S(1)}) custom-call(bf16[2,1024,256]{2,1,0:T(8,128)(2,1)S(1)} %copy-done.6, bf16[2,64,2048]{2,1,0:T(8,128)(2,1)S(1)} %copy-done.8, f32[1,2048]{1,0:T(1,128)S(1)} %copy-done.9, bf16[144,512]{1,0:T(8,128)(2,1)S(1)} %copy-done.4, bf16[144,512]{1,0:T(8,128)(2,1)S(1)} %collective-permute-done.refs_4_, ...), custom_call_target="tpu_custom_call" | custom-call | flops 2147483648 | bytes 4194304 | tf_op jit(solution)/shard_map/attend/pallas_call | solution.py:179
  40.3 2.6 %collective-permute-done.17.refs_0_ = bf16[64,2048]{1,0:T(8,128)(2,1)S(1)} collective-permute-done((bf16[64,2048]{1,0:T(8,128)(2,1)S(1)}, bf16[64,2048]{1,0:T(8,128)(2,1)S(1)}, u32[]{:S(2)}, u32[]{:S(2)}) %collective-permute-start.17) | collective-permute-done | bytes 262176 | tf_op jit(solution)/shard_map/ppermute | solution.py:287
  43.0 1.8 %collective-permute-start.15 = (bf16[64,2048]{1,0:T(8,128)(2,1)S(1)}, bf16[64,2048]{1,0:T(8,128)(2,1)S(1)}, u32[]{:S(2)}, u32[]{:S(2)}) collective-permute-start(bf16[64,2048]{1,0:T(8,128)(2,1)S(1)} %get-tuple-element.152.refs_1_), channel_id=1, source_target_pairs={{0,4},{1,5},{4,8},{5,9},{8,12},{9,13},{12,14},{13,15},{14,10},{15,... | collective-permute-start | bytes 786440 | tf_op jit(solution)/shard_map/ppermute | solution.py:287
  45.0 1.8 %collective-permute-start.21 = (bf16[64,2048]{1,0:T(8,128)(2,1)S(1)}, bf16[64,2048]{1,0:T(8,128)(2,1)S(1)}, u32[]{:S(2)}, u32[]{:S(2)}) collective-permute-start(bf16[64,2048]{1,0:T(8,128)(2,1)S(1)} %collective-permute-done.17.refs_0_), channel_id=1, source_target_pairs={{0,4},{1,5},{4,8},{5,9},{8,12},{9,13},{12,14},{13,15},{14,10},{15,... | collective-permute-start | bytes 786440 | tf_op jit(solution)/shard_map/ppermute | solution.py:287
  47.1 1.9 %experts.5 = (bf16[64,2048]{1,0:T(8,128)(2,1)S(1)}, bf16[64,2048]{1,0:T(8,128)(2,1)S(1)}) custom-call(bf16[64,2048]{1,0:T(8,128)(2,1)S(1)} %get-tuple-element.153.refs_0_, bf16[64,2048]{1,0:T(8,128)(2,1)S(1)} %get-tuple-element.152.refs_1_, bf16[144,512]{1,0:T(8,128)(2,1)S(1)} %copy-done.4, bf16[1,2048,384]{2,1,0:T(8,128)(2,1)S(1)} %copy-done, ...), custom_call_target="tpu_custom_call" | custom-call | flops 1207959552 | bytes 9437184 | tf_op jit(solution)/shard_map/experts/pallas_call | solution.py:247
  48.9 3.3 %collective-permute-done.15.refs_1_ = bf16[64,2048]{1,0:T(8,128)(2,1)S(1)} collective-permute-done((bf16[64,2048]{1,0:T(8,128)(2,1)S(1)}, bf16[64,2048]{1,0:T(8,128)(2,1)S(1)}, u32[]{:S(2)}, u32[]{:S(2)}) %collective-permute-start.15) | collective-permute-done | bytes 262176 | tf_op jit(solution)/shard_map/ppermute | solution.py:287
  52.2 1.8 %collective-permute-done.16.refs_3_ = bf16[64,2048]{1,0:T(8,128)(2,1)S(1)} collective-permute-done((bf16[64,2048]{1,0:T(8,128)(2,1)S(1)}, bf16[64,2048]{1,0:T(8,128)(2,1)S(1)}, u32[]{:S(2)}, u32[]{:S(2)}) %collective-permute-start.16) | collective-permute-done | bytes 262176 | tf_op jit(solution)/shard_map/ppermute | solution.py:287
  54.2 1.8 %collective-permute-start.26 = (bf16[64,2048]{1,0:T(8,128)(2,1)S(1)}, bf16[64,2048]{1,0:T(8,128)(2,1)S(1)}, u32[]{:S(2)}, u32[]{:S(2)}) collective-permute-start(bf16[64,2048]{1,0:T(8,128)(2,1)S(1)} %collective-permute-done.15.refs_1_), channel_id=1, source_target_pairs={{0,4},{1,5},{4,8},{5,9},{8,12},{9,13},{12,14},{13,15},{14,10},{15,... | collective-permute-start | bytes 786440 | tf_op jit(solution)/shard_map/ppermute | solution.py:287
  56.0 3.5 %experts.6 = (bf16[64,2048]{1,0:T(8,128)(2,1)S(1)}, bf16[64,2048]{1,0:T(8,128)(2,1)S(1)}, bf16[64,2048]{1,0:T(8,128)(2,1)S(1)}, bf16[64,2048]{1,0:T(8,128)(2,1)S(1)}) custom-call(bf16[64,2048]{1,0:T(8,128)(2,1)S(1)} %collective-permute-done.17.refs_0_, bf16[64,2048]{1,0:T(8,128)(2,1)S(1)} %collective-permute-done.15.refs_1_, ...), custom_call_target="tpu_custom_call" | custom-call | flops 2415919104 | bytes 9437184 | tf_op jit(solution)/shard_map/experts/pallas_call | solution.py:247
  59.6 1.6 %collective-permute-start.24 = (bf16[64,2048]{1,0:T(8,128)(2,1)S(1)}, bf16[64,2048]{1,0:T(8,128)(2,1)S(1)}, u32[]{:S(2)}, u32[]{:S(2)}) collective-permute-start(bf16[64,2048]{1,0:T(8,128)(2,1)S(1)} %collective-permute-done.21.refs_0_), channel_id=1, source_target_pairs={{0,4},{1,5},{4,8},{5,9},{8,12},{9,13},{12,14},{13,15},{14,10},{15,... | collective-permute-start | bytes 786440 | tf_op jit(solution)/shard_map/ppermute | solution.py:287
  61.7 3.6 %collective-permute-done.27.refs_3_ = bf16[64,2048]{1,0:T(8,128)(2,1)S(1)} collective-permute-done((bf16[64,2048]{1,0:T(8,128)(2,1)S(1)}, bf16[64,2048]{1,0:T(8,128)(2,1)S(1)}, u32[]{:S(2)}, u32[]{:S(2)}) %collective-permute-start.27) | collective-permute-done | bytes 262176 | tf_op jit(solution)/shard_map/ppermute | solution.py:287
  65.5 1.8 %collective-permute-start.31 = (bf16[64,2048]{1,0:T(8,128)(2,1)S(1)}, bf16[64,2048]{1,0:T(8,128)(2,1)S(1)}, u32[]{:S(2)}, u32[]{:S(2)}) collective-permute-start(bf16[64,2048]{1,0:T(8,128)(2,1)S(1)} %collective-permute-done.26.refs_1_), channel_id=1, source_target_pairs={{0,4},{1,5},{4,8},{5,9},{8,12},{9,13},{12,14},{13,15},{14,10},{15,... | collective-permute-start | bytes 786440 | tf_op jit(solution)/shard_map/ppermute | solution.py:287
  67.3 3.5 %experts.7 = (bf16[64,2048]{1,0:T(8,128)(2,1)S(1)}, bf16[64,2048]{1,0:T(8,128)(2,1)S(1)}, bf16[64,2048]{1,0:T(8,128)(2,1)S(1)}, bf16[64,2048]{1,0:T(8,128)(2,1)S(1)}) custom-call(bf16[64,2048]{1,0:T(8,128)(2,1)S(1)} %collective-permute-done.21.refs_0_, bf16[64,2048]{1,0:T(8,128)(2,1)S(1)} %collective-permute-done.26.refs_1_, ...), custom_call_target="tpu_custom_call" | custom-call | flops 2415919104 | bytes 9437184 | tf_op jit(solution)/shard_map/experts/pallas_call | solution.py:247
  70.9 1.6 %collective-permute-start.28 = (bf16[64,2048]{1,0:T(8,128)(2,1)S(1)}, bf16[64,2048]{1,0:T(8,128)(2,1)S(1)}, u32[]{:S(2)}, u32[]{:S(2)}) collective-permute-start(bf16[64,2048]{1,0:T(8,128)(2,1)S(1)} %collective-permute-done.24.refs_0_), channel_id=1, source_target_pairs={{0,4},{1,5},{4,8},{5,9},{8,12},{9,13},{12,14},{13,15},{14,10},{15,... | collective-permute-start | bytes 786440 | tf_op jit(solution)/shard_map/ppermute | solution.py:287
  72.4 2.3 %collective-permute-done.29.refs_3_ = bf16[64,2048]{1,0:T(8,128)(2,1)S(1)} collective-permute-done((bf16[64,2048]{1,0:T(8,128)(2,1)S(1)}, bf16[64,2048]{1,0:T(8,128)(2,1)S(1)}, u32[]{:S(2)}, u32[]{:S(2)}) %collective-permute-start.29) | collective-permute-done | bytes 262176 | tf_op jit(solution)/shard_map/ppermute | solution.py:287
  75.0 3.5 %experts.8 = (bf16[64,2048]{1,0:T(8,128)(2,1)S(1)}, bf16[64,2048]{1,0:T(8,128)(2,1)S(1)}, bf16[64,2048]{1,0:T(8,128)(2,1)S(1)}, bf16[64,2048]{1,0:T(8,128)(2,1)S(1)}) custom-call(bf16[64,2048]{1,0:T(8,128)(2,1)S(1)} %collective-permute-done.24.refs_0_, bf16[64,2048]{1,0:T(8,128)(2,1)S(1)} %collective-permute-done.31.refs_1_, ...), custom_call_target="tpu_custom_call" | custom-call | flops 2415919104 | bytes 9437184 | tf_op jit(solution)/shard_map/experts/pallas_call | solution.py:247
  78.5 1.7 %collective-permute-start.36 = (bf16[64,2048]{1,0:T(8,128)(2,1)S(1)}, bf16[64,2048]{1,0:T(8,128)(2,1)S(1)}, u32[]{:S(2)}, u32[]{:S(2)}) collective-permute-start(bf16[64,2048]{1,0:T(8,128)(2,1)S(1)} %get-tuple-element.199), channel_id=1, source_target_pairs={{4,0},{5,1},{8,4},{9,5},{12,8},{13,9},{14,12},{15,13},{10,14},{11,... | collective-permute-start | bytes 786440 | tf_op jit(solution)/shard_map/ppermute | solution.py:287
  80.6 2.7 %collective-permute-done.30.refs_1_ = bf16[64,2048]{1,0:T(8,128)(2,1)S(1)} collective-permute-done((bf16[64,2048]{1,0:T(8,128)(2,1)S(1)}, bf16[64,2048]{1,0:T(8,128)(2,1)S(1)}, u32[]{:S(2)}, u32[]{:S(2)}) %collective-permute-start.30) | collective-permute-done | bytes 262176 | tf_op jit(solution)/shard_map/ppermute | solution.py:287
  83.3 1.8 %experts.9 = (bf16[64,2048]{1,0:T(8,128)(2,1)S(1)}, bf16[64,2048]{1,0:T(8,128)(2,1)S(1)}) custom-call(bf16[64,2048]{1,0:T(8,128)(2,1)S(1)} %collective-permute-done.28.refs_0_, bf16[64,2048]{1,0:T(8,128)(2,1)S(1)} %collective-permute-done.30.refs_1_, bf16[144,512]{1,0:T(8,128)(2,1)S(1)} %collective-permute-done.4.refs_7_.refs_2_, ...), custom_call_target="tpu_custom_call" | custom-call | flops 1207959552 | bytes 9437184 | tf_op jit(solution)/shard_map/experts/pallas_call | solution.py:247
  85.1 1.5 %collective-permute-start.32 = (bf16[64,2048]{1,0:T(8,128)(2,1)S(1)}, bf16[64,2048]{1,0:T(8,128)(2,1)S(1)}, u32[]{:S(2)}, u32[]{:S(2)}) collective-permute-start(bf16[64,2048]{1,0:T(8,128)(2,1)S(1)} %get-tuple-element.195), channel_id=1, source_target_pairs={{0,4},{1,5},{4,8},{5,9},{8,12},{9,13},{12,14},{13,15},{14,10},{15,... | collective-permute-start | bytes 786440 | tf_op jit(solution)/shard_map/ppermute | solution.py:287
  87.3 2.1 %collective-permute-done.39 = bf16[64,2048]{1,0:T(8,128)(2,1)S(1)} collective-permute-done((bf16[64,2048]{1,0:T(8,128)(2,1)S(1)}, bf16[64,2048]{1,0:T(8,128)(2,1)S(1)}, u32[]{:S(2)}, u32[]{:S(2)}) %collective-permute-start.39) | collective-permute-done | bytes 262176 | tf_op jit(solution)/shard_map/ppermute | solution.py:287
  89.6 2.0 %collective-permute-start.42 = (bf16[64,2048]{1,0:T(8,128)(2,1)S(1)}, bf16[64,2048]{1,0:T(8,128)(2,1)S(1)}, u32[]{:S(2)}, u32[]{:S(2)}) collective-permute-start(bf16[64,2048]{1,0:T(8,128)(2,1)S(1)} %get-tuple-element.207), channel_id=1, source_target_pairs={{4,0},{5,1},{8,4},{9,5},{12,8},{13,9},{14,12},{15,13},{10,14},{11,... | collective-permute-start | bytes 786440 | tf_op jit(solution)/shard_map/ppermute | solution.py:287
  91.6 3.5 %collective-permute-done.32 = bf16[64,2048]{1,0:T(8,128)(2,1)S(1)} collective-permute-done((bf16[64,2048]{1,0:T(8,128)(2,1)S(1)}, bf16[64,2048]{1,0:T(8,128)(2,1)S(1)}, u32[]{:S(2)}, u32[]{:S(2)}) %collective-permute-start.32) | collective-permute-done | bytes 262176 | tf_op jit(solution)/shard_map/ppermute | solution.py:287
  95.2 0.8 collective-permute-start.33
  96.3 1.1 collective-permute-start.38
  97.4 3.3 %collective-permute-done.40 = bf16[64,2048]{1,0:T(8,128)(2,1)S(1)} collective-permute-done((bf16[64,2048]{1,0:T(8,128)(2,1)S(1)}, bf16[64,2048]{1,0:T(8,128)(2,1)S(1)}, u32[]{:S(2)}, u32[]{:S(2)}) %collective-permute-start.40) | collective-permute-done | bytes 262176 | tf_op jit(solution)/shard_map/ppermute | solution.py:287
  100.8 0.8 collective-permute-start.41
  101.9 1.1 collective-permute-start.43
  103.0 3.3 %collective-permute-done.33 = bf16[64,2048]{1,0:T(8,128)(2,1)S(1)} collective-permute-done((bf16[64,2048]{1,0:T(8,128)(2,1)S(1)}, bf16[64,2048]{1,0:T(8,128)(2,1)S(1)}, u32[]{:S(2)}, u32[]{:S(2)}) %collective-permute-start.33) | collective-permute-done | bytes 262176 | tf_op jit(solution)/shard_map/ppermute | solution.py:287
  107.3 2.9 %collective-permute-done.43 = bf16[64,2048]{1,0:T(8,128)(2,1)S(1)} collective-permute-done((bf16[64,2048]{1,0:T(8,128)(2,1)S(1)}, bf16[64,2048]{1,0:T(8,128)(2,1)S(1)}, u32[]{:S(2)}, u32[]{:S(2)}) %collective-permute-start.43) | collective-permute-done | bytes 262176 | tf_op jit(solution)/shard_map/ppermute | solution.py:287
  110.6 4.1 %collective-permute-done.34 = bf16[64,2048]{1,0:T(8,128)(2,1)S(1)} collective-permute-done((bf16[64,2048]{1,0:T(8,128)(2,1)S(1)}, bf16[64,2048]{1,0:T(8,128)(2,1)S(1)}, u32[]{:S(2)}, u32[]{:S(2)}) %collective-permute-start.34) | collective-permute-done | bytes 262176 | tf_op jit(solution)/shard_map/ppermute | solution.py:287
  115.6 1.8 %collective-permute-done.44 = bf16[64,2048]{1,0:T(8,128)(2,1)S(1)} collective-permute-done((bf16[64,2048]{1,0:T(8,128)(2,1)S(1)}, bf16[64,2048]{1,0:T(8,128)(2,1)S(1)}, u32[]{:S(2)}, u32[]{:S(2)}) %collective-permute-start.44) | collective-permute-done | bytes 262176 | tf_op jit(solution)/shard_map/ppermute | solution.py:287
  118.0 3.2 %collective-permute-done.35 = bf16[64,2048]{1,0:T(8,128)(2,1)S(1)} collective-permute-done((bf16[64,2048]{1,0:T(8,128)(2,1)S(1)}, bf16[64,2048]{1,0:T(8,128)(2,1)S(1)}, u32[]{:S(2)}, u32[]{:S(2)}) %collective-permute-start.35) | collective-permute-done | bytes 262176 | tf_op jit(solution)/shard_map/ppermute | solution.py:287
  121.3 2.6 %collective-permute-done.45 = bf16[64,2048]{1,0:T(8,128)(2,1)S(1)} collective-permute-done((bf16[64,2048]{1,0:T(8,128)(2,1)S(1)}, bf16[64,2048]{1,0:T(8,128)(2,1)S(1)}, u32[]{:S(2)}, u32[]{:S(2)}) %collective-permute-start.45) | collective-permute-done | bytes 262176 | tf_op jit(solution)/shard_map/ppermute | solution.py:287
  (86 shorter events, 13.7 us)
Async XLA Ops:
  2.2 7.0 %collective-permute-start = (bf16[144,512]{1,0:T(8,128)(2,1)}, bf16[144,512]{1,0:T(8,128)(2,1)S(1)}, u32[]{:S(2)}, u32[]{:S(2)}) collective-permute-start(bf16[144,512]{1,0:T(8,128)(2,1)} %pack_message.1.refs_3_.refs_2_), channel_id=1, source_target_pairs={{0,4},{1,5},{4,8},{5,9},{8,12},{9,13},{12,14},{13,15},{14,10},{15,... | collective-permute-start | bytes 442376 | tf_op jit(solution)/shard_map/ppermute | solution.py:287
  5.2 5.8 %collective-permute-start.2 = (bf16[144,512]{1,0:T(8,128)(2,1)}, bf16[144,512]{1,0:T(8,128)(2,1)S(1)}, u32[]{:S(2)}, u32[]{:S(2)}) collective-permute-start(bf16[144,512]{1,0:T(8,128)(2,1)} %pack_message.1.refs_3_.refs_2_), channel_id=1, source_target_pairs={{4,0},{5,1},{8,4},{9,5},{12,8},{13,9},{14,12},{15,13},{10,14},{11,... | collective-permute-start | bytes 442376 | tf_op jit(solution)/shard_map/ppermute | solution.py:287
  9.2 5.1 %collective-permute-start.1 = (bf16[144,512]{1,0:T(8,128)(2,1)S(1)}, bf16[144,512]{1,0:T(8,128)(2,1)S(1)}, u32[]{:S(2)}, u32[]{:S(2)}) collective-permute-start(bf16[144,512]{1,0:T(8,128)(2,1)S(1)} %collective-permute-done.refs_4_), channel_id=1, source_target_pairs={{0,4},{1,5},{4,8},{5,9},{8,12},{9,13},{12,14},{13,15},{14,10},{15,... | collective-permute-start | bytes 442376 | tf_op jit(solution)/shard_map/ppermute | solution.py:287
  11.0 25.4 %copy-start.4 = (bf16[144,512]{1,0:T(8,128)(2,1)S(1)}, bf16[144,512]{1,0:T(8,128)(2,1)}, u32[]{:S(2)}) copy-start(bf16[144,512]{1,0:T(8,128)(2,1)} %pack_message.1.refs_3_.refs_2_) | copy-start | bytes 442372
  13.7 5.1 %collective-permute-start.5 = (bf16[144,512]{1,0:T(8,128)(2,1)S(1)}, bf16[144,512]{1,0:T(8,128)(2,1)S(1)}, u32[]{:S(2)}, u32[]{:S(2)}) collective-permute-start(bf16[144,512]{1,0:T(8,128)(2,1)S(1)} %collective-permute-done.2.refs_8_.refs_5_), channel_id=1, source_target_pairs={{4,0},{5,1},{8,4},{9,5},{12,8},{13,9},{14,12},{15,13},{10,14},{11,... | collective-permute-start | bytes 442376 | tf_op jit(solution)/shard_map/ppermute | solution.py:287
  14.4 5.1 %collective-permute-start.3 = (bf16[144,512]{1,0:T(8,128)(2,1)S(1)}, bf16[144,512]{1,0:T(8,128)(2,1)S(1)}, u32[]{:S(2)}, u32[]{:S(2)}) collective-permute-start(bf16[144,512]{1,0:T(8,128)(2,1)S(1)} %collective-permute-done.1.refs_5_.refs_4_), channel_id=1, source_target_pairs={{0,4},{1,5},{4,8},{5,9},{8,12},{9,13},{12,14},{13,15},{14,10},{15,... | collective-permute-start | bytes 442376 | tf_op jit(solution)/shard_map/ppermute | solution.py:287
  16.2 5.1 %collective-permute-start.7 = (bf16[144,512]{1,0:T(8,128)(2,1)}, bf16[144,512]{1,0:T(8,128)(2,1)S(1)}, u32[]{:S(2)}, u32[]{:S(2)}) collective-permute-start(bf16[144,512]{1,0:T(8,128)(2,1)} %pack_message.1.refs_3_.refs_2_), channel_id=1, source_target_pairs={{0,1},{1,0},{2,3},{3,2},{4,5},{5,4},{6,7},{7,6},{8,9},{9,8},{10,11... | collective-permute-start | bytes 442376 | tf_op jit(solution)/shard_map/ppermute | solution.py:287
  16.2 5.1 %collective-permute-start.12 = (bf16[144,512]{1,0:T(8,128)(2,1)S(1)}, bf16[144,512]{1,0:T(8,128)(2,1)S(1)}, u32[]{:S(2)}, u32[]{:S(2)}) collective-permute-start(bf16[144,512]{1,0:T(8,128)(2,1)S(1)} %collective-permute-done.2.refs_8_.refs_5_), channel_id=1, source_target_pairs={{0,1},{1,0},{2,3},{3,2},{4,5},{5,4},{6,7},{7,6},{8,9},{9,8},{10,11... | collective-permute-start | bytes 442376 | tf_op jit(solution)/shard_map/ppermute | solution.py:287
  16.7 5.2 %collective-permute-start.8 = (bf16[144,512]{1,0:T(8,128)(2,1)S(1)}, bf16[144,512]{1,0:T(8,128)(2,1)S(1)}, u32[]{:S(2)}, u32[]{:S(2)}) collective-permute-start(bf16[144,512]{1,0:T(8,128)(2,1)S(1)} %collective-permute-done.refs_4_), channel_id=1, source_target_pairs={{0,1},{1,0},{2,3},{3,2},{4,5},{5,4},{6,7},{7,6},{8,9},{9,8},{10,11... | collective-permute-start | bytes 442376 | tf_op jit(solution)/shard_map/ppermute | solution.py:287
  18.9 5.1 %collective-permute-start.6 = (bf16[144,512]{1,0:T(8,128)(2,1)S(1)}, bf16[144,512]{1,0:T(8,128)(2,1)S(1)}, u32[]{:S(2)}, u32[]{:S(2)}) collective-permute-start(bf16[144,512]{1,0:T(8,128)(2,1)S(1)} %collective-permute-done.5.refs_9_.refs_5_), channel_id=1, source_target_pairs={{4,0},{5,1},{8,4},{9,5},{12,8},{13,9},{14,12},{15,13},{10,14},{11,... | collective-permute-start | bytes 442376 | tf_op jit(solution)/shard_map/ppermute | solution.py:287
  19.5 5.1 %collective-permute-start.4 = (bf16[144,512]{1,0:T(8,128)(2,1)S(1)}, bf16[144,512]{1,0:T(8,128)(2,1)S(1)}, u32[]{:S(2)}, u32[]{:S(2)}) collective-permute-start(bf16[144,512]{1,0:T(8,128)(2,1)S(1)} %collective-permute-done.3.refs_6_.refs_4_), channel_id=1, source_target_pairs={{0,4},{1,5},{4,8},{5,9},{8,12},{9,13},{12,14},{13,15},{14,10},{15,... | collective-permute-start | bytes 442376 | tf_op jit(solution)/shard_map/ppermute | solution.py:287
  21.3 3.3 %collective-permute-start.9 = (bf16[144,512]{1,0:T(8,128)(2,1)S(1)}, bf16[144,512]{1,0:T(8,128)(2,1)S(1)}, u32[]{:S(2)}, u32[]{:S(2)}) collective-permute-start(bf16[144,512]{1,0:T(8,128)(2,1)S(1)} %collective-permute-done.1.refs_5_.refs_4_), channel_id=1, source_target_pairs={{0,1},{1,0},{2,3},{3,2},{4,5},{5,4},{6,7},{7,6},{8,9},{9,8},{10,11... | collective-permute-start | bytes 442376 | tf_op jit(solution)/shard_map/ppermute | solution.py:287
  21.3 3.3 %collective-permute-start.13 = (bf16[144,512]{1,0:T(8,128)(2,1)S(1)}, bf16[144,512]{1,0:T(8,128)(2,1)S(1)}, u32[]{:S(2)}, u32[]{:S(2)}) collective-permute-start(bf16[144,512]{1,0:T(8,128)(2,1)S(1)} %collective-permute-done.5.refs_9_.refs_5_), channel_id=1, source_target_pairs={{0,1},{1,0},{2,3},{3,2},{4,5},{5,4},{6,7},{7,6},{8,9},{9,8},{10,11... | collective-permute-start | bytes 442376 | tf_op jit(solution)/shard_map/ppermute | solution.py:287
  21.8 2.8 %collective-permute-start.10 = (bf16[144,512]{1,0:T(8,128)(2,1)S(1)}, bf16[144,512]{1,0:T(8,128)(2,1)S(1)}, u32[]{:S(2)}, u32[]{:S(2)}) collective-permute-start(bf16[144,512]{1,0:T(8,128)(2,1)S(1)} %collective-permute-done.3.refs_6_.refs_4_), channel_id=1, source_target_pairs={{0,1},{1,0},{2,3},{3,2},{4,5},{5,4},{6,7},{7,6},{8,9},{9,8},{10,11... | collective-permute-start | bytes 442376 | tf_op jit(solution)/shard_map/ppermute | solution.py:287
  24.0 1.4 %collective-permute-start.14 = (bf16[144,512]{1,0:T(8,128)(2,1)S(1)}, bf16[144,512]{1,0:T(8,128)(2,1)S(1)}, u32[]{:S(2)}, u32[]{:S(2)}) collective-permute-start(bf16[144,512]{1,0:T(8,128)(2,1)S(1)} %collective-permute-done.6.refs_10_.refs_5_), channel_id=1, source_target_pairs={{0,1},{1,0},{2,3},{3,2},{4,5},{5,4},{6,7},{7,6},{8,9},{9,8},{10,11... | collective-permute-start | bytes 442376 | tf_op jit(solution)/shard_map/ppermute | solution.py:287
  24.7 1.4 %collective-permute-start.11 = (bf16[144,512]{1,0:T(8,128)(2,1)S(1)}, bf16[144,512]{1,0:T(8,128)(2,1)S(1)}, u32[]{:S(2)}, u32[]{:S(2)}) collective-permute-start(bf16[144,512]{1,0:T(8,128)(2,1)S(1)} %collective-permute-done.4.refs_7_.refs_2_), channel_id=1, source_target_pairs={{0,1},{1,0},{2,3},{3,2},{4,5},{5,4},{6,7},{7,6},{8,9},{9,8},{10,11... | collective-permute-start | bytes 442376 | tf_op jit(solution)/shard_map/ppermute | solution.py:287
  26.0 19.0 %collective-permute-start.18 = (bf16[1,2048,384]{2,1,0:T(8,128)(2,1)}, bf16[1,2048,384]{2,1,0:T(8,128)(2,1)S(1)}, u32[]{:S(2)}, u32[]{:S(2)}) collective-permute-start(bf16[1,2048,384]{2,1,0:T(8,128)(2,1)} %refs_3_.3), channel_id=1, source_target_pairs={{0,1},{1,0},{2,3},{3,2},{4,5},{5,4},{6,7},{7,6},{8,9},{9,8},{10,11... | collective-permute-start | bytes 4718600 | tf_op jit(solution)/shard_map/ppermute | solution.py:287
  26.2 20.6 %collective-permute-start.19 = (bf16[1,2048,384]{2,1,0:T(8,128)(2,1)}, bf16[1,2048,384]{2,1,0:T(8,128)(2,1)S(1)}, u32[]{:S(2)}, u32[]{:S(2)}) collective-permute-start(bf16[1,2048,384]{2,1,0:T(8,128)(2,1)} %refs_4_.3), channel_id=1, source_target_pairs={{0,1},{1,0},{2,3},{3,2},{4,5},{5,4},{6,7},{7,6},{8,9},{9,8},{10,11... | collective-permute-start | bytes 4718600 | tf_op jit(solution)/shard_map/ppermute | solution.py:287
  26.5 20.5 %collective-permute-start.20 = (bf16[1,384,2048]{2,1,0:T(8,128)(2,1)}, bf16[1,384,2048]{2,1,0:T(8,128)(2,1)S(1)}, u32[]{:S(2)}, u32[]{:S(2)}) collective-permute-start(bf16[1,384,2048]{2,1,0:T(8,128)(2,1)} %refs_5_.3), channel_id=1, source_target_pairs={{0,1},{1,0},{2,3},{3,2},{4,5},{5,4},{6,7},{7,6},{8,9},{9,8},{10,11... | collective-permute-start | bytes 4718600 | tf_op jit(solution)/shard_map/ppermute | solution.py:287
  34.3 12.7 %copy-start = (bf16[1,2048,384]{2,1,0:T(8,128)(2,1)S(1)}, bf16[1,2048,384]{2,1,0:T(8,128)(2,1)}, u32[]{:S(2)}) copy-start(bf16[1,2048,384]{2,1,0:T(8,128)(2,1)} %refs_3_.3) | copy-start | bytes 4718596
  34.3 8.6 %collective-permute-start.17 = (bf16[64,2048]{1,0:T(8,128)(2,1)S(1)}, bf16[64,2048]{1,0:T(8,128)(2,1)S(1)}, u32[]{:S(2)}, u32[]{:S(2)}) collective-permute-start(bf16[64,2048]{1,0:T(8,128)(2,1)S(1)} %get-tuple-element.153.refs_0_), channel_id=1, source_target_pairs={{0,4},{1,5},{4,8},{5,9},{8,12},{9,13},{12,14},{13,15},{14,10},{15,... | collective-permute-start | bytes 786440 | tf_op jit(solution)/shard_map/ppermute | solution.py:287
  36.2 8.6 %collective-permute-start.22 = (bf16[64,2048]{1,0:T(8,128)(2,1)S(1)}, bf16[64,2048]{1,0:T(8,128)(2,1)S(1)}, u32[]{:S(2)}, u32[]{:S(2)}) collective-permute-start(bf16[64,2048]{1,0:T(8,128)(2,1)S(1)} %get-tuple-element.153.refs_0_), channel_id=1, source_target_pairs={{4,0},{5,1},{8,4},{9,5},{12,8},{13,9},{14,12},{15,13},{10,14},{11,... | collective-permute-start | bytes 786440 | tf_op jit(solution)/shard_map/ppermute | solution.py:287
  43.0 9.2 %collective-permute-start.15 = (bf16[64,2048]{1,0:T(8,128)(2,1)S(1)}, bf16[64,2048]{1,0:T(8,128)(2,1)S(1)}, u32[]{:S(2)}, u32[]{:S(2)}) collective-permute-start(bf16[64,2048]{1,0:T(8,128)(2,1)S(1)} %get-tuple-element.152.refs_1_), channel_id=1, source_target_pairs={{0,4},{1,5},{4,8},{5,9},{8,12},{9,13},{12,14},{13,15},{14,10},{15,... | collective-permute-start | bytes 786440 | tf_op jit(solution)/shard_map/ppermute | solution.py:287
  44.8 9.2 %collective-permute-start.16 = (bf16[64,2048]{1,0:T(8,128)(2,1)S(1)}, bf16[64,2048]{1,0:T(8,128)(2,1)S(1)}, u32[]{:S(2)}, u32[]{:S(2)}) collective-permute-start(bf16[64,2048]{1,0:T(8,128)(2,1)S(1)} %get-tuple-element.152.refs_1_), channel_id=1, source_target_pairs={{4,0},{5,1},{8,4},{9,5},{12,8},{13,9},{14,12},{15,13},{10,14},{11,... | collective-permute-start | bytes 786440 | tf_op jit(solution)/shard_map/ppermute | solution.py:287
  45.0 14.5 %collective-permute-start.21 = (bf16[64,2048]{1,0:T(8,128)(2,1)S(1)}, bf16[64,2048]{1,0:T(8,128)(2,1)S(1)}, u32[]{:S(2)}, u32[]{:S(2)}) collective-permute-start(bf16[64,2048]{1,0:T(8,128)(2,1)S(1)} %collective-permute-done.17.refs_0_), channel_id=1, source_target_pairs={{0,4},{1,5},{4,8},{5,9},{8,12},{9,13},{12,14},{13,15},{14,10},{15,... | collective-permute-start | bytes 786440 | tf_op jit(solution)/shard_map/ppermute | solution.py:287
  46.8 12.8 %collective-permute-start.23 = (bf16[64,2048]{1,0:T(8,128)(2,1)S(1)}, bf16[64,2048]{1,0:T(8,128)(2,1)S(1)}, u32[]{:S(2)}, u32[]{:S(2)}) collective-permute-start(bf16[64,2048]{1,0:T(8,128)(2,1)S(1)} %collective-permute-done.22.refs_2_), channel_id=1, source_target_pairs={{4,0},{5,1},{8,4},{9,5},{12,8},{13,9},{14,12},{15,13},{10,14},{11,... | collective-permute-start | bytes 786440 | tf_op jit(solution)/shard_map/ppermute | solution.py:287
  54.0 11.2 %collective-permute-start.27 = (bf16[64,2048]{1,0:T(8,128)(2,1)S(1)}, bf16[64,2048]{1,0:T(8,128)(2,1)S(1)}, u32[]{:S(2)}, u32[]{:S(2)}) collective-permute-start(bf16[64,2048]{1,0:T(8,128)(2,1)S(1)} %collective-permute-done.16.refs_3_), channel_id=1, source_target_pairs={{4,0},{5,1},{8,4},{9,5},{12,8},{13,9},{14,12},{15,13},{10,14},{11,... | collective-permute-start | bytes 786440 | tf_op jit(solution)/shard_map/ppermute | solution.py:287
  54.2 11.2 %collective-permute-start.26 = (bf16[64,2048]{1,0:T(8,128)(2,1)S(1)}, bf16[64,2048]{1,0:T(8,128)(2,1)S(1)}, u32[]{:S(2)}, u32[]{:S(2)}) collective-permute-start(bf16[64,2048]{1,0:T(8,128)(2,1)S(1)} %collective-permute-done.15.refs_1_), channel_id=1, source_target_pairs={{0,4},{1,5},{4,8},{5,9},{8,12},{9,13},{12,14},{13,15},{14,10},{15,... | collective-permute-start | bytes 786440 | tf_op jit(solution)/shard_map/ppermute | solution.py:287
  59.6 11.1 %collective-permute-start.24 = (bf16[64,2048]{1,0:T(8,128)(2,1)S(1)}, bf16[64,2048]{1,0:T(8,128)(2,1)S(1)}, u32[]{:S(2)}, u32[]{:S(2)}) collective-permute-start(bf16[64,2048]{1,0:T(8,128)(2,1)S(1)} %collective-permute-done.21.refs_0_), channel_id=1, source_target_pairs={{0,4},{1,5},{4,8},{5,9},{8,12},{9,13},{12,14},{13,15},{14,10},{15,... | collective-permute-start | bytes 786440 | tf_op jit(solution)/shard_map/ppermute | solution.py:287
  61.2 9.7 %collective-permute-start.25 = (bf16[64,2048]{1,0:T(8,128)(2,1)S(1)}, bf16[64,2048]{1,0:T(8,128)(2,1)S(1)}, u32[]{:S(2)}, u32[]{:S(2)}) collective-permute-start(bf16[64,2048]{1,0:T(8,128)(2,1)S(1)} %collective-permute-done.23.refs_2_), channel_id=1, source_target_pairs={{4,0},{5,1},{8,4},{9,5},{12,8},{13,9},{14,12},{15,13},{10,14},{11,... | collective-permute-start | bytes 786440 | tf_op jit(solution)/shard_map/ppermute | solution.py:287
  65.2 9.5 %collective-permute-start.29 = (bf16[64,2048]{1,0:T(8,128)(2,1)S(1)}, bf16[64,2048]{1,0:T(8,128)(2,1)S(1)}, u32[]{:S(2)}, u32[]{:S(2)}) collective-permute-start(bf16[64,2048]{1,0:T(8,128)(2,1)S(1)} %collective-permute-done.27.refs_3_), channel_id=1, source_target_pairs={{4,0},{5,1},{8,4},{9,5},{12,8},{13,9},{14,12},{15,13},{10,14},{11,... | collective-permute-start | bytes 786440 | tf_op jit(solution)/shard_map/ppermute | solution.py:287
  65.5 9.5 %collective-permute-start.31 = (bf16[64,2048]{1,0:T(8,128)(2,1)S(1)}, bf16[64,2048]{1,0:T(8,128)(2,1)S(1)}, u32[]{:S(2)}, u32[]{:S(2)}) collective-permute-start(bf16[64,2048]{1,0:T(8,128)(2,1)S(1)} %collective-permute-done.26.refs_1_), channel_id=1, source_target_pairs={{0,4},{1,5},{4,8},{5,9},{8,12},{9,13},{12,14},{13,15},{14,10},{15,... | collective-permute-start | bytes 786440 | tf_op jit(solution)/shard_map/ppermute | solution.py:287
  70.9 9.7 %collective-permute-start.28 = (bf16[64,2048]{1,0:T(8,128)(2,1)S(1)}, bf16[64,2048]{1,0:T(8,128)(2,1)S(1)}, u32[]{:S(2)}, u32[]{:S(2)}) collective-permute-start(bf16[64,2048]{1,0:T(8,128)(2,1)S(1)} %collective-permute-done.24.refs_0_), channel_id=1, source_target_pairs={{0,4},{1,5},{4,8},{5,9},{8,12},{9,13},{12,14},{13,15},{14,10},{15,... | collective-permute-start | bytes 786440 | tf_op jit(solution)/shard_map/ppermute | solution.py:287
  74.7 8.6 %collective-permute-start.30 = (bf16[64,2048]{1,0:T(8,128)(2,1)S(1)}, bf16[64,2048]{1,0:T(8,128)(2,1)S(1)}, u32[]{:S(2)}, u32[]{:S(2)}) collective-permute-start(bf16[64,2048]{1,0:T(8,128)(2,1)S(1)} %collective-permute-done.29.refs_3_), channel_id=1, source_target_pairs={{4,0},{5,1},{8,4},{9,5},{12,8},{13,9},{14,12},{15,13},{10,14},{11,... | collective-permute-start | bytes 786440 | tf_op jit(solution)/shard_map/ppermute | solution.py:287
  78.5 8.4 %collective-permute-start.36 = (bf16[64,2048]{1,0:T(8,128)(2,1)S(1)}, bf16[64,2048]{1,0:T(8,128)(2,1)S(1)}, u32[]{:S(2)}, u32[]{:S(2)}) collective-permute-start(bf16[64,2048]{1,0:T(8,128)(2,1)S(1)} %get-tuple-element.199), channel_id=1, source_target_pairs={{4,0},{5,1},{8,4},{9,5},{12,8},{13,9},{14,12},{15,13},{10,14},{11,... | collective-permute-start | bytes 786440 | tf_op jit(solution)/shard_map/ppermute | solution.py:287
  80.2 9.3 %collective-permute-start.39 = (bf16[64,2048]{1,0:T(8,128)(2,1)S(1)}, bf16[64,2048]{1,0:T(8,128)(2,1)S(1)}, u32[]{:S(2)}, u32[]{:S(2)}) collective-permute-start(bf16[64,2048]{1,0:T(8,128)(2,1)S(1)} %get-tuple-element.204), channel_id=1, source_target_pairs={{0,4},{1,5},{4,8},{5,9},{8,12},{9,13},{12,14},{13,15},{14,10},{15,... | collective-permute-start | bytes 786440 | tf_op jit(solution)/shard_map/ppermute | solution.py:287
  85.1 10.0 %collective-permute-start.32 = (bf16[64,2048]{1,0:T(8,128)(2,1)S(1)}, bf16[64,2048]{1,0:T(8,128)(2,1)S(1)}, u32[]{:S(2)}, u32[]{:S(2)}) collective-permute-start(bf16[64,2048]{1,0:T(8,128)(2,1)S(1)} %get-tuple-element.195), channel_id=1, source_target_pairs={{0,4},{1,5},{4,8},{5,9},{8,12},{9,13},{12,14},{13,15},{14,10},{15,... | collective-permute-start | bytes 786440 | tf_op jit(solution)/shard_map/ppermute | solution.py:287
  87.0 9.3 %collective-permute-start.37 = (bf16[64,2048]{1,0:T(8,128)(2,1)S(1)}, bf16[64,2048]{1,0:T(8,128)(2,1)S(1)}, u32[]{:S(2)}, u32[]{:S(2)}) collective-permute-start(bf16[64,2048]{1,0:T(8,128)(2,1)S(1)} %add_convert_fusion.8), channel_id=1, source_target_pairs={{4,0},{5,1},{8,4},{9,5},{12,8},{13,9},{14,12},{15,13},{10,14},{11,... | collective-permute-start | bytes 786440 | tf_op jit(solution)/shard_map/ppermute | solution.py:287
  89.6 11.2 %collective-permute-start.40 = (bf16[64,2048]{1,0:T(8,128)(2,1)S(1)}, bf16[64,2048]{1,0:T(8,128)(2,1)S(1)}, u32[]{:S(2)}, u32[]{:S(2)}) collective-permute-start(bf16[64,2048]{1,0:T(8,128)(2,1)S(1)} %add_convert_fusion.5), channel_id=1, source_target_pairs={{0,4},{1,5},{4,8},{5,9},{8,12},{9,13},{12,14},{13,15},{14,10},{15,... | collective-permute-start | bytes 786440 | tf_op jit(solution)/shard_map/ppermute | solution.py:287
  89.6 12.2 %collective-permute-start.42 = (bf16[64,2048]{1,0:T(8,128)(2,1)S(1)}, bf16[64,2048]{1,0:T(8,128)(2,1)S(1)}, u32[]{:S(2)}, u32[]{:S(2)}) collective-permute-start(bf16[64,2048]{1,0:T(8,128)(2,1)S(1)} %get-tuple-element.207), channel_id=1, source_target_pairs={{4,0},{5,1},{8,4},{9,5},{12,8},{13,9},{14,12},{15,13},{10,14},{11,... | collective-permute-start | bytes 786440 | tf_op jit(solution)/shard_map/ppermute | solution.py:287
  95.2 11.2 %collective-permute-start.33 = (bf16[64,2048]{1,0:T(8,128)(2,1)S(1)}, bf16[64,2048]{1,0:T(8,128)(2,1)S(1)}, u32[]{:S(2)}, u32[]{:S(2)}) collective-permute-start(bf16[64,2048]{1,0:T(8,128)(2,1)S(1)} %add_convert_fusion.11), channel_id=1, source_target_pairs={{0,4},{1,5},{4,8},{5,9},{8,12},{9,13},{12,14},{13,15},{14,10},{15,... | collective-permute-start | bytes 786440 | tf_op jit(solution)/shard_map/ppermute | solution.py:287
  96.3 21.6 %collective-permute-start.38 = (bf16[64,2048]{1,0:T(8,128)(2,1)S(1)}, bf16[64,2048]{1,0:T(8,128)(2,1)S(1)}, u32[]{:S(2)}, u32[]{:S(2)}) collective-permute-start(bf16[64,2048]{1,0:T(8,128)(2,1)S(1)} %add_convert_fusion.7), channel_id=1, source_target_pairs={{4,0},{5,1},{8,4},{9,5},{12,8},{13,9},{14,12},{15,13},{10,14},{11,... | collective-permute-start | bytes 786440 | tf_op jit(solution)/shard_map/ppermute | solution.py:287
  100.8 20.5 %collective-permute-start.41 = (bf16[64,2048]{1,0:T(8,128)(2,1)S(1)}, bf16[64,2048]{1,0:T(8,128)(2,1)S(1)}, u32[]{:S(2)}, u32[]{:S(2)}) collective-permute-start(bf16[64,2048]{1,0:T(8,128)(2,1)S(1)} %add_convert_fusion.4), channel_id=1, source_target_pairs={{0,4},{1,5},{4,8},{5,9},{8,12},{9,13},{12,14},{13,15},{14,10},{15,... | collective-permute-start | bytes 786440 | tf_op jit(solution)/shard_map/ppermute | solution.py:287
  101.9 8.2 %collective-permute-start.43 = (bf16[64,2048]{1,0:T(8,128)(2,1)S(1)}, bf16[64,2048]{1,0:T(8,128)(2,1)S(1)}, u32[]{:S(2)}, u32[]{:S(2)}) collective-permute-start(bf16[64,2048]{1,0:T(8,128)(2,1)S(1)} %add_convert_fusion.3), channel_id=1, source_target_pairs={{4,0},{5,1},{8,4},{9,5},{12,8},{13,9},{14,12},{15,13},{10,14},{11,... | collective-permute-start | bytes 786440 | tf_op jit(solution)/shard_map/ppermute | solution.py:287
  106.4 8.3 %collective-permute-start.34 = (bf16[64,2048]{1,0:T(8,128)(2,1)S(1)}, bf16[64,2048]{1,0:T(8,128)(2,1)S(1)}, u32[]{:S(2)}, u32[]{:S(2)}) collective-permute-start(bf16[64,2048]{1,0:T(8,128)(2,1)S(1)} %add_convert_fusion.10), channel_id=1, source_target_pairs={{0,4},{1,5},{4,8},{5,9},{8,12},{9,13},{12,14},{13,15},{14,10},{15,... | collective-permute-start | bytes 786440 | tf_op jit(solution)/shard_map/ppermute | solution.py:287
  110.2 7.2 %collective-permute-start.44 = (bf16[64,2048]{1,0:T(8,128)(2,1)S(1)}, bf16[64,2048]{1,0:T(8,128)(2,1)S(1)}, u32[]{:S(2)}, u32[]{:S(2)}) collective-permute-start(bf16[64,2048]{1,0:T(8,128)(2,1)S(1)} %add_convert_fusion.2), channel_id=1, source_target_pairs={{4,0},{5,1},{8,4},{9,5},{12,8},{13,9},{14,12},{15,13},{10,14},{11,... | collective-permute-start | bytes 786440 | tf_op jit(solution)/shard_map/ppermute | solution.py:287
  114.8 6.4 %collective-permute-start.35 = (bf16[64,2048]{1,0:T(8,128)(2,1)S(1)}, bf16[64,2048]{1,0:T(8,128)(2,1)S(1)}, u32[]{:S(2)}, u32[]{:S(2)}) collective-permute-start(bf16[64,2048]{1,0:T(8,128)(2,1)S(1)} %add_convert_fusion.9), channel_id=1, source_target_pairs={{0,4},{1,5},{4,8},{5,9},{8,12},{9,13},{12,14},{13,15},{14,10},{15,... | collective-permute-start | bytes 786440 | tf_op jit(solution)/shard_map/ppermute | solution.py:287
  117.5 6.4 %collective-permute-start.45 = (bf16[64,2048]{1,0:T(8,128)(2,1)S(1)}, bf16[64,2048]{1,0:T(8,128)(2,1)S(1)}, u32[]{:S(2)}, u32[]{:S(2)}) collective-permute-start(bf16[64,2048]{1,0:T(8,128)(2,1)S(1)} %add_convert_fusion.1), channel_id=1, source_target_pairs={{4,0},{5,1},{8,4},{9,5},{12,8},{13,9},{14,12},{15,13},{10,14},{11,... | collective-permute-start | bytes 786440 | tf_op jit(solution)/shard_map/ppermute | solution.py:287
  (8 other events, 41.0 us)

commit v4 on v3

--- a/solution.py
+++ b/solution.py
@@ -12,6 +12,7 @@
 HEAD_SIZE = 128
 CORES = 2
 EXTRA = 16
+QUERY_SCALE = 0.125
 
 
 NEG = -1e30
@@ -59,48 +60,13 @@
     )(stretch_pos, keys, values, routes.T, combine.T)
 
 
-def stage_kernel(query_ref, residual_ref, gain_ref, stacked_ref, residual_out, gain_out):
-    rows = query_ref.shape[0]
-    halves = stacked_ref.shape[0]
-    some = rows // halves
-    sub = lax.broadcasted_iota(jnp.int32, (rows, rows), 0)
-    lane = lax.broadcasted_iota(jnp.int32, (rows, rows), 1)
-    eye = jnp.where(sub == lane, 1.0, 0.0).astype(jnp.bfloat16)
-    for half in range(halves):
-        mine = slice(half * some, (half + 1) * some)
-        for h in range(query_ref.shape[1] // HEAD_SIZE):
-            at = slice(h * some, (h + 1) * some)
-            stacked_ref[half, at, 0:HEAD_SIZE] = query_ref[mine, h * HEAD_SIZE : (h + 1) * HEAD_SIZE]
-            stacked_ref[half, at, HEAD_SIZE : HEAD_SIZE + rows] = eye[mine]
-        residual_out[half] = residual_ref[mine, :]
-    gain_out[...] = gain_ref[...]
-
-
-def stage(queries, residual, gain):
-    rows, features = queries.shape
-    heads = features // HEAD_SIZE
-    vmem = pl.BlockSpec(memory_space=pltpu.VMEM)
-    return pl.pallas_call(
-        stage_kernel,
-        out_shape=(
-            jax.ShapeDtypeStruct((2, heads * rows // 2, HEAD_SIZE + rows), jnp.bfloat16),
-            jax.ShapeDtypeStruct((2, rows // 2, features), jnp.bfloat16),
-            jax.ShapeDtypeStruct((1, features), jnp.float32),
-        ),
-        in_specs=[vmem] * 3,
-        out_specs=(vmem,) * 3,
-        cost_estimate=pl.CostEstimate(
-            flops=0, bytes_accessed=10 * rows * features, transcendentals=0
-        ),
-        name="stage",
-    )(queries, residual, gain.reshape(1, features))
-
-
 def attend_kernel(count, half, *refs):
-    stacked_ref, residual_ref, gain_ref = refs[:3]
+    query_ref, residual_ref, gain_ref = refs[:3]
     messages = refs[3 : 3 + count]
     hidden_ref, normed_ref, key_ext, value_ext = refs[3 + count :]
-    some, features = residual_ref.shape[1:]
+    features = query_ref.shape[1]
+    some = query_ref.shape[0] // 2
+    mine = slice(half * some, (half + 1) * some)
     rows = messages[0].shape[0] - EXTRA
     kv_heads = key_ext.shape[0]
     heads = features // HEAD_SIZE
@@ -125,13 +91,20 @@
                 0:rows, width + a * HEAD_SIZE : width + (a + 1) * HEAD_SIZE
             ]
             value_ext[a, at, HEAD_SIZE : 2 * HEAD_SIZE] = ones
-    rate = math.log2(math.e) / math.sqrt(HEAD_SIZE)
+    eye = jnp.where(sub == lane, 1.0, 0.0).astype(jnp.bfloat16)[mine]
+    rate = math.log2(math.e) / math.sqrt(HEAD_SIZE) / QUERY_SCALE
     step = min(512, span)
     pair = 4
     squares = jnp.zeros((some, HEAD_SIZE), jnp.float32)
     for first in range(0, heads, pair):
         a = first // group
-        stacked = stacked_ref[half, first * some : (first + pair) * some, :]
+        stacked = jnp.concatenate(
+            [
+                jnp.concatenate([query_ref[mine, h * HEAD_SIZE : (h + 1) * HEAD_SIZE], eye], axis=1)
+                for h in range(first, first + pair)
+            ],
+            axis=0,
+        )
         scores = [
             lax.dot_general(
                 stacked,
@@ -155,7 +128,7 @@
         attended = (total[:, 0:HEAD_SIZE] / total[:, HEAD_SIZE:]).astype(jnp.bfloat16)
         for j in range(pair):
             cols = slice((first + j) * HEAD_SIZE, (first + j + 1) * HEAD_SIZE)
-            state = residual_ref[half, :, cols].astype(jnp.float32) + attended[
+            state = residual_ref[mine, cols] + attended[
                 j * some : (j + 1) * some
             ].astype(jnp.float32)
             hidden_ref[:, cols] = state
@@ -164,14 +137,14 @@
     inverse = lax.rsqrt(meansq + 1e-06)
     for h in range(heads):
         cols = slice(h * HEAD_SIZE, (h + 1) * HEAD_SIZE)
-        normed_ref[:, cols] = (hidden_ref[:, cols] * inverse * gain_ref[:, cols]).astype(
+        normed_ref[:, cols] = (hidden_ref[:, cols] * inverse * gain_ref[0:1, cols]).astype(
             jnp.bfloat16
         )
 
 
 def attend(half, staged, messages):
-    some, features = staged[1].shape[1:]
-    rows = messages[0].shape[0] - EXTRA
+    rows, features = staged[0].shape
+    some = rows // 2
     count = len(messages)
     kv_heads = messages[0].shape[1] // (2 * HEAD_SIZE)
     vmem = pl.BlockSpec(memory_space=pltpu.VMEM)
@@ -288,74 +261,80 @@
 
     message = pack_message(stretch_pos, rotated_keys, value_matrix, routes, combine)
 
+    tie = lax.optimization_barrier
     left, right = {0: message}, {0: message}
+    gate_from, unused = tie((gate_weight, message))
+    twin_gate = send(gate_from, swap)
     for hop in range(1, far + 1):
         if hop == 3:
-            inputs, unused = lax.optimization_barrier(
-                ((queries, residual, norm_gain), (left[1], right[1]))
+            inputs, unused = tie(((queries, residual, norm_gain), (left[1], right[1])))
+            staged = (
+                inputs[0] * jnp.bfloat16(QUERY_SCALE),
+                inputs[1].astype(jnp.float32),
+                jnp.broadcast_to(inputs[2][None, :], (8, inputs[2].shape[0])),
             )
-            staged = stage(*inputs)
-            left[2], staged = lax.optimization_barrier((left[2], staged))
+            left[2], staged, twin_gate = tie((left[2], staged, twin_gate))
+            up_from, unused = tie((up_weight, left[2]))
+            twin_up = send(up_from, swap)
         left[hop] = send(left[hop - 1], onward)
         if hop < far:
             right[hop] = send(right[hop - 1], back)
     plane = [message] + [left[h] for h in range(1, far + 1)] + [right[h] for h in range(1, far)]
     everything = plane + [send(m, swap) for m in plane]
-    everything, to_swap = lax.optimization_barrier(
-        (everything, (gate_weight, up_weight, down_weight))
-    )
-    weights = (gate_weight, up_weight, down_weight) + tuple(send(w, swap) for w in to_swap)
+    everything, down_from, twin_up = tie((everything, down_weight, twin_up))
+    weights = (gate_weight, up_weight, down_weight, twin_gate, twin_up, send(down_from, swap))
     hidden_upper, upper = attend(0, staged, everything)
-    everything, upper = lax.optimization_barrier((everything, upper))
+    everything, upper = tie((everything, upper))
     hidden_lower, lower = attend(1, staged, everything)
 
     from_left, from_right = {(0, 0): upper, (0, 1): lower}, {(0, 0): upper, (0, 1): lower}
     outs = {}
 
-    def experts_of(hop, after):
-        if hop == 0:
-            pieces, used = [(upper, 0, 0), (lower, 0, 1)], [message]
-        elif hop == far:
-            pieces, used = [(from_left[far, 0], 0, 0), (from_right[far, 1], 0, 1)], [left[far]]
-        else:
-            pieces = [(from_left[hop, 0], 0, 0), (from_left[hop, 1], 0, 1)]
-            pieces += [(from_right[hop, 0], 1, 0), (from_right[hop, 1], 1, 1)]
-            used = [left[hop], right[hop]]
-        used, after = lax.optimization_barrier((used, after))
-        return run_experts(pieces, used, weights), after
-
+    def experts_on(tokens, used, after):
+        used, after = tie((used, after))
+        return run_experts(tokens, used, weights), after
+
+    def experts_of(hop, half, after):
+        tokens = [(from_left[hop, half], 0, half), (from_right[hop, half], 1, half)]
+        return experts_on(tokens, [left[hop], right[hop]], after)
+
+    last = (upper, lower)
     for hop in range(1, far + 1):
-        onto, backto = from_left[hop - 1, 0], from_right[hop - 1, 0]
-        if hop > 2:
-            outs[hop - 2], outs[hop - 3] = experts_of(hop - 2, outs[hop - 3])
-            onto, backto, outs[hop - 2] = lax.optimization_barrier((onto, backto, outs[hop - 2]))
-        from_left[hop, 0] = send(onto, onward)
-        if hop < far:
-            from_right[hop, 0] = send(backto, back)
-        onto, backto = from_left[hop - 1, 1], from_right[hop - 1, 1]
-        if hop == 2:
-            outs[0], unused = experts_of(0, from_left[1, 0])
-            onto, backto, outs[0] = lax.optimization_barrier((onto, backto, outs[0]))
-        if hop < far:
-            from_left[hop, 1] = send(onto, onward)
-        from_right[hop, 1] = send(backto, back)
-    outs[far - 1], outs[far - 2] = experts_of(far - 1, outs[far - 2])
-    outs[far], outs[far - 1] = experts_of(far, outs[far - 1])
-    out_left = {hop: outs[hop][:2] for hop in range(1, far)}
-    out_right = {hop: outs[hop][2:] for hop in range(1, far)}
-    far_upper, far_lower = outs[far]
-    own_out = outs[0]
-
-    sums_on = {1: send(out_right[far - 1][1], onward)}
-    sums_back = {0: send(out_left[far - 1][0], back)}
+        for half in range(2):
+            onto, backto = from_left[hop - 1, half], from_right[hop - 1, half]
+            if hop > 1:
+                before = (hop - 1, 1 - half) if half == 1 else (hop - 2, 1)
+                if before[0] > 0:
+                    outs[before], unused = experts_of(*before, last)
+                    last = outs[before]
+                    onto, backto, last = tie((onto, backto, last))
+                    outs[before] = last
+            if hop < far or half == 0:
+                from_left[hop, half] = send(onto, onward)
+            if hop < far or half == 1:
+                from_right[hop, half] = send(backto, back)
+    outs[far - 1, 1], unused = experts_of(far - 1, 1, last)
+    outs[far - 1, 0], outs[far - 1, 1] = tie((outs[far - 1, 0], outs[far - 1, 1]))
+    out_left = {key: pair[0] for key, pair in outs.items()}
+    out_right = {key: pair[1] for key, pair in outs.items()}
+
+    sums_on = {1: send(out_right[far - 1, 1], onward)}
+    sums_back = {0: send(out_left[far - 1, 0], back)}
+    (far_upper, far_lower), unused = experts_on(
+        [(from_left[far, 0], 0, 0), (from_right[far, 1], 0, 1)], [left[far]], outs[far - 1, 1]
+    )
     sums_on[0] = send(far_upper, onward)
     sums_back[1] = send(far_lower, back)
+    own_out, unused = experts_on([(upper, 0, 0), (lower, 0, 1)], [message], (far_upper, far_lower))
     for hop in range(far - 1, 0, -1):
         if hop < far - 1:
-            sums_on[1] = send(add_parts(sums_on[1], out_right[hop][1]), onward)
-            sums_back[0] = send(add_parts(sums_back[0], out_left[hop][0]), back)
-        sums_on[0] = send(add_parts(sums_on[0], out_right[hop][0]), onward)
-        sums_back[1] = send(add_parts(sums_back[1], out_left[hop][1]), back)
+            sums_on[1] = send(add_parts(sums_on[1], out_right[hop, 1]), onward)
+            sums_back[0] = send(add_parts(sums_back[0], out_left[hop, 0]), back)
+        onto, backto = sums_on[0], sums_back[1]
+        if hop == far - 1:
+            onto, backto, own_out = tie((onto, backto, own_out))
+        sums_on[0] = send(add_parts(onto, out_right[hop, 0]), onward)
+        sums_back[1] = send(add_parts(backto, out_left[hop, 1]), back)
     hidden_state = (hidden_upper, hidden_lower)
     return jnp.concatenate(
         [

time: 125 us -> 130 us (1.040)
  waiting for transfers between devices: 55.3 us -> 63.5 us
  local copies, waits for them, and re-layouts: 3.9 us -> 0.03 us
  Pallas kernels: 26 us -> 23.6 us
  starting transfers between devices: 37.1 us -> 38.7 us
    ppermute x46, waiting for transfers between devices: 55.3 us -> 63.5 us  [send(): return lax.ppermute(array, 'ctx', pairs)]
    unnamed x20 -> x12, local copies, waits for them, and re-layouts: 3.9 us -> 0.03 us
    pallas_call x1 -> x0, Pallas kernels: 2.67 us -> none  [stage(): pl.pallas_call(stage_kernel, out_shape=(jax.ShapeDtypeStruct((2, heads *...]
    ppermute x46, starting transfers between devices: 37.1 us -> 38.7 us  [send(): return lax.ppermute(array, 'ctx', pairs)]
    pallas_call x5 -> x8, Pallas kernels: 14.1 us -> 14.7 us  [run_experts(): pl.pallas_call(functools.partial(expert_kernel, [piece[1:] for piece in p...]
  transfers between devices with their start and end apart: 46 -> 46, of which waited for: 28 -> 22; matrix products, arithmetic and copies ran while one was open for 1% -> 1% of each run, Pallas kernels for 20% -> 17%
where the time goes in v4:
time: 130 us
  waiting for transfers between devices  63.5 us (49%)
  starting transfers between devices  38.7 us (30%)
  Pallas kernels  23.6 us (18%)
  other arithmetic  2.89 us (2%)
    ppermute x46, waiting for transfers between devices, send(): return lax.ppermute(array, 'ctx', pairs)  63.5 us
    ppermute x46, starting transfers between devices, send(): return lax.ppermute(array, 'ctx', pairs)  38.7 us
    pallas_call x8, Pallas kernels, run_experts(): pl.pallas_call(functools.partial(expert_kernel, [piece[1:] for piece in p...  14.7 us
    pallas_call x2, Pallas kernels, attend(): pl.pallas_call(functools.partial(attend_kernel, count, half), out_shape=(...  7.3 us
  transfers between devices with their start and end apart: 46, of which 22 were waited for; matrix products, arithmetic and copies ran while one was open for 1% of the time, Pallas kernels for 17%

profile of v4, /device:TPU:0, one launch (start us, length us, event | category | flops | bytes accessed | tf_op | source)
XLA Modules:
  0.0 129.8 jit_solution(59295796951108576)
XLA Ops:
  0.8 1.6 %pack_message.1.refs_3_.refs_2_ = bf16[144,512]{1,0:T(8,128)(2,1)} custom-call(s32[1]{0:T(128)S(6)} %copy.12.pos_ref, bf16[128,256]{1,0:T(8,128)(2,1)} %key_ref.1, bf16[128,256]{1,0:T(8,128)(2,1)} %value_ref.1, s32[8,128]{1,0:T(8,128)} %bitcast.2, f32[8,128]{1,0:T(8,128)} %bitcast.3), custom_call_target="tpu_custom_call" | custom-call | tf_op jit(solution)/shard_map/pack_message/pallas_call | solution.py:54
  2.8 2.5 %collective-permute-start.2 = (bf16[144,512]{1,0:T(8,128)(2,1)}, bf16[144,512]{1,0:T(8,128)(2,1)S(1)}, u32[]{:S(2)}, u32[]{:S(2)}) collective-permute-start(bf16[144,512]{1,0:T(8,128)(2,1)} %pack_message.1.refs_3_.refs_2_), channel_id=1, source_target_pairs={{4,0},{5,1},{8,4},{9,5},{12,8},{13,9},{14,12},{15,13},{10,14},{11,... | collective-permute-start | bytes 442376 | tf_op jit(solution)/shard_map/ppermute | solution.py:260
  5.4 4.7 %collective-permute-done.2.refs_8_.refs_3_ = bf16[144,512]{1,0:T(8,128)(2,1)S(1)} collective-permute-done((bf16[144,512]{1,0:T(8,128)(2,1)}, bf16[144,512]{1,0:T(8,128)(2,1)S(1)}, u32[]{:S(2)}, u32[]{:S(2)}) %collective-permute-start.2) | collective-permute-done | bytes 147488 | tf_op jit(solution)/shard_map/ppermute | solution.py:260
  10.1 1.4 %collective-permute-done.refs_4_.refs_2_ = bf16[144,512]{1,0:T(8,128)(2,1)S(1)} collective-permute-done((bf16[144,512]{1,0:T(8,128)(2,1)}, bf16[144,512]{1,0:T(8,128)(2,1)S(1)}, u32[]{:S(2)}, u32[]{:S(2)}) %collective-permute-start) | collective-permute-done | bytes 147488 | tf_op jit(solution)/shard_map/ppermute | solution.py:260
  13.1 3.6 %collective-permute-done.1.refs_5_.refs_2_ = bf16[144,512]{1,0:T(8,128)(2,1)S(1)} collective-permute-done((bf16[144,512]{1,0:T(8,128)(2,1)S(1)}, bf16[144,512]{1,0:T(8,128)(2,1)S(1)}, u32[]{:S(2)}, u32[]{:S(2)}) %collective-permute-start.1) | collective-permute-done | bytes 147488 | tf_op jit(solution)/shard_map/ppermute | solution.py:260
  16.8 1.6 %collective-permute-start.6 = (bf16[144,512]{1,0:T(8,128)(2,1)S(1)}, bf16[144,512]{1,0:T(8,128)(2,1)S(1)}, u32[]{:S(2)}, u32[]{:S(2)}) collective-permute-start(bf16[144,512]{1,0:T(8,128)(2,1)S(1)} %collective-permute-done.2.refs_8_.refs_3_), channel_id=1, source_target_pairs={{4,0},{5,1},{8,4},{9,5},{12,8},{13,9},{14,12},{15,13},{10,14},{11,... | collective-permute-start | bytes 442376 | tf_op jit(solution)/shard_map/ppermute | solution.py:260
  19.4 3.7 %collective-permute-done.6.refs_9_.refs_3_ = bf16[144,512]{1,0:T(8,128)(2,1)S(1)} collective-permute-done((bf16[144,512]{1,0:T(8,128)(2,1)S(1)}, bf16[144,512]{1,0:T(8,128)(2,1)S(1)}, u32[]{:S(2)}, u32[]{:S(2)}) %collective-permute-start.6) | collective-permute-done | bytes 147488 | tf_op jit(solution)/shard_map/ppermute | solution.py:260
  23.0 1.6 %collective-permute-start.7 = (bf16[144,512]{1,0:T(8,128)(2,1)S(1)}, bf16[144,512]{1,0:T(8,128)(2,1)S(1)}, u32[]{:S(2)}, u32[]{:S(2)}) collective-permute-start(bf16[144,512]{1,0:T(8,128)(2,1)S(1)} %collective-permute-done.6.refs_9_.refs_3_), channel_id=1, source_target_pairs={{4,0},{5,1},{8,4},{9,5},{12,8},{13,9},{14,12},{15,13},{10,14},{11,... | collective-permute-start | bytes 442376 | tf_op jit(solution)/shard_map/ppermute | solution.py:260
  25.6 2.9 %collective-permute-done.7.refs_10_.refs_3_ = bf16[144,512]{1,0:T(8,128)(2,1)S(1)} collective-permute-done((bf16[144,512]{1,0:T(8,128)(2,1)S(1)}, bf16[144,512]{1,0:T(8,128)(2,1)S(1)}, u32[]{:S(2)}, u32[]{:S(2)}) %collective-permute-start.7) | collective-permute-done | bytes 147488 | tf_op jit(solution)/shard_map/ppermute | solution.py:260
  29.0 1.9 %collective-permute-done.5.refs_7_.refs_2_ = bf16[144,512]{1,0:T(8,128)(2,1)S(1)} collective-permute-done((bf16[144,512]{1,0:T(8,128)(2,1)S(1)}, bf16[144,512]{1,0:T(8,128)(2,1)S(1)}, u32[]{:S(2)}, u32[]{:S(2)}) %collective-permute-start.5) | collective-permute-done | bytes 147488 | tf_op jit(solution)/shard_map/ppermute | solution.py:260
  31.0 1.3 %collective-permute-done.12.refs_15_ = bf16[144,512]{1,0:T(8,128)(2,1)S(1)} collective-permute-done((bf16[144,512]{1,0:T(8,128)(2,1)S(1)}, bf16[144,512]{1,0:T(8,128)(2,1)S(1)}, u32[]{:S(2)}, u32[]{:S(2)}) %collective-permute-start.12) | collective-permute-done | bytes 147488 | tf_op jit(solution)/shard_map/ppermute | solution.py:260
  32.5 3.6 %attend.2 = (f32[64,2048]{1,0:T(8,128)S(1)}, bf16[64,2048]{1,0:T(8,128)(2,1)S(1)}) custom-call(bf16[128,2048]{1,0:T(8,128)(2,1)S(1)} %broadcast_multiply_fusion.refs_0_, f32[128,2048]{1,0:T(8,128)S(1)} %convert_element_type.117.refs_1_, f32[8,2048]{1,0:T(8,128)S(1)} %broadcast_in_dim.2.refs_2_, bf16[144,512]{1,0:T(8,128)(2,1)S(1)} %copy-done.3, ...), custom_call_target="tpu_custom_call" | custom-call | flops 2147483648 | bytes 4194304 | tf_op jit(solution)/shard_map/attend/pallas_call | solution.py:152
  36.2 1.6 %collective-permute-start.19 = (bf16[64,2048]{1,0:T(8,128)(2,1)S(1)}, bf16[64,2048]{1,0:T(8,128)(2,1)S(1)}, u32[]{:S(2)}, u32[]{:S(2)}) collective-permute-start(bf16[64,2048]{1,0:T(8,128)(2,1)S(1)} %get-tuple-element.137.refs_0_), channel_id=1, source_target_pairs={{4,0},{5,1},{8,4},{9,5},{12,8},{13,9},{14,12},{15,13},{10,14},{11,... | collective-permute-start | bytes 786440 | tf_op jit(solution)/shard_map/ppermute | solution.py:260
  38.3 3.6 %attend.3 = (f32[64,2048]{1,0:T(8,128)S(1)}, bf16[64,2048]{1,0:T(8,128)(2,1)S(1)}) custom-call(bf16[128,2048]{1,0:T(8,128)(2,1)S(1)} %broadcast_multiply_fusion.refs_0_, f32[128,2048]{1,0:T(8,128)S(1)} %convert_element_type.117.refs_1_, f32[8,2048]{1,0:T(8,128)S(1)} %broadcast_in_dim.2.refs_2_, bf16[144,512]{1,0:T(8,128)(2,1)S(1)} %copy-done.3, ...), custom_call_target="tpu_custom_call" | custom-call | flops 2147483648 | bytes 4194304 | tf_op jit(solution)/shard_map/attend/pallas_call | solution.py:152
  41.9 1.6 %collective-permute-start.22 = (bf16[64,2048]{1,0:T(8,128)(2,1)S(1)}, bf16[64,2048]{1,0:T(8,128)(2,1)S(1)}, u32[]{:S(2)}, u32[]{:S(2)}) collective-permute-start(bf16[64,2048]{1,0:T(8,128)(2,1)S(1)} %get-tuple-element.154.refs_1_), channel_id=1, source_target_pairs={{4,0},{5,1},{8,4},{9,5},{12,8},{13,9},{14,12},{15,13},{10,14},{11,... | collective-permute-start | bytes 786440 | tf_op jit(solution)/shard_map/ppermute | solution.py:260
  44.0 1.2 collective-permute-done.19.refs_1_
  45.2 1.6 %collective-permute-start.20 = (bf16[64,2048]{1,0:T(8,128)(2,1)S(1)}, bf16[64,2048]{1,0:T(8,128)(2,1)S(1)}, u32[]{:S(2)}, u32[]{:S(2)}) collective-permute-start(bf16[64,2048]{1,0:T(8,128)(2,1)S(1)} %collective-permute-done.19.refs_1_), channel_id=1, source_target_pairs={{4,0},{5,1},{8,4},{9,5},{12,8},{13,9},{14,12},{15,13},{10,14},{11,... | collective-permute-start | bytes 786440 | tf_op jit(solution)/shard_map/ppermute | solution.py:260
  47.2 1.8 %experts.8 = (bf16[64,2048]{1,0:T(8,128)(2,1)S(1)}, bf16[64,2048]{1,0:T(8,128)(2,1)S(1)}) custom-call(bf16[64,2048]{1,0:T(8,128)(2,1)S(1)} %collective-permute-done.17.refs_0_, bf16[64,2048]{1,0:T(8,128)(2,1)S(1)} %collective-permute-done.19.refs_1_, bf16[144,512]{1,0:T(8,128)(2,1)S(1)} %collective-permute-done.refs_4_.refs_2_, ...), custom_call_target="tpu_custom_call" | custom-call | flops 1207959552 | bytes 9437184 | tf_op jit(solution)/shard_map/experts/pallas_call | solution.py:220
  49.1 2.1 %collective-permute-done.22.refs_1_ = bf16[64,2048]{1,0:T(8,128)(2,1)S(1)} collective-permute-done((bf16[64,2048]{1,0:T(8,128)(2,1)S(1)}, bf16[64,2048]{1,0:T(8,128)(2,1)S(1)}, u32[]{:S(2)}, u32[]{:S(2)}) %collective-permute-start.22) | collective-permute-done | bytes 262176 | tf_op jit(solution)/shard_map/ppermute | solution.py:260
  51.2 1.6 %collective-permute-done.21.refs_0_ = bf16[64,2048]{1,0:T(8,128)(2,1)S(1)} collective-permute-done((bf16[64,2048]{1,0:T(8,128)(2,1)S(1)}, bf16[64,2048]{1,0:T(8,128)(2,1)S(1)}, u32[]{:S(2)}, u32[]{:S(2)}) %collective-permute-start.21) | collective-permute-done | bytes 262176 | tf_op jit(solution)/shard_map/ppermute | solution.py:260
  53.2 1.6 %collective-permute-start.27 = (bf16[64,2048]{1,0:T(8,128)(2,1)S(1)}, bf16[64,2048]{1,0:T(8,128)(2,1)S(1)}, u32[]{:S(2)}, u32[]{:S(2)}) collective-permute-start(bf16[64,2048]{1,0:T(8,128)(2,1)S(1)} %collective-permute-done.22.refs_1_), channel_id=1, source_target_pairs={{4,0},{5,1},{8,4},{9,5},{12,8},{13,9},{14,12},{15,13},{10,14},{11,... | collective-permute-start | bytes 786440 | tf_op jit(solution)/shard_map/ppermute | solution.py:260
  54.8 1.8 %experts.9 = (bf16[64,2048]{1,0:T(8,128)(2,1)S(1)}, bf16[64,2048]{1,0:T(8,128)(2,1)S(1)}) custom-call(bf16[64,2048]{1,0:T(8,128)(2,1)S(1)} %collective-permute-done.21.refs_0_, bf16[64,2048]{1,0:T(8,128)(2,1)S(1)} %collective-permute-done.22.refs_1_, bf16[144,512]{1,0:T(8,128)(2,1)S(1)} %collective-permute-done.refs_4_.refs_2_, ...), custom_call_target="tpu_custom_call" | custom-call | flops 1207959552 | bytes 9437184 | tf_op jit(solution)/shard_map/experts/pallas_call | solution.py:220
  56.8 1.6 %collective-permute-done.18.refs_0_ = bf16[64,2048]{1,0:T(8,128)(2,1)S(1)} collective-permute-done((bf16[64,2048]{1,0:T(8,128)(2,1)S(1)}, bf16[64,2048]{1,0:T(8,128)(2,1)S(1)}, u32[]{:S(2)}, u32[]{:S(2)}) %collective-permute-start.18) | collective-permute-done | bytes 262176 | tf_op jit(solution)/shard_map/ppermute | solution.py:260
  58.8 1.6 %collective-permute-start.25 = (bf16[64,2048]{1,0:T(8,128)(2,1)S(1)}, bf16[64,2048]{1,0:T(8,128)(2,1)S(1)}, u32[]{:S(2)}, u32[]{:S(2)}) collective-permute-start(bf16[64,2048]{1,0:T(8,128)(2,1)S(1)} %collective-permute-done.20.refs_1_), channel_id=1, source_target_pairs={{4,0},{5,1},{8,4},{9,5},{12,8},{13,9},{14,12},{15,13},{10,14},{11,... | collective-permute-start | bytes 786440 | tf_op jit(solution)/shard_map/ppermute | solution.py:260
  60.4 1.8 %experts.10 = (bf16[64,2048]{1,0:T(8,128)(2,1)S(1)}, bf16[64,2048]{1,0:T(8,128)(2,1)S(1)}) custom-call(bf16[64,2048]{1,0:T(8,128)(2,1)S(1)} %collective-permute-done.18.refs_0_, bf16[64,2048]{1,0:T(8,128)(2,1)S(1)} %collective-permute-done.20.refs_1_, bf16[144,512]{1,0:T(8,128)(2,1)S(1)} %collective-permute-done.1.refs_5_.refs_2_, ...), custom_call_target="tpu_custom_call" | custom-call | flops 1207959552 | bytes 9437184 | tf_op jit(solution)/shard_map/experts/pallas_call | solution.py:220
  62.3 1.7 %collective-permute-done.26.refs_0_ = bf16[64,2048]{1,0:T(8,128)(2,1)S(1)} collective-permute-done((bf16[64,2048]{1,0:T(8,128)(2,1)S(1)}, bf16[64,2048]{1,0:T(8,128)(2,1)S(1)}, u32[]{:S(2)}, u32[]{:S(2)}) %collective-permute-start.26) | collective-permute-done | bytes 262176 | tf_op jit(solution)/shard_map/ppermute | solution.py:260
  64.5 1.6 %collective-permute-start.30 = (bf16[64,2048]{1,0:T(8,128)(2,1)S(1)}, bf16[64,2048]{1,0:T(8,128)(2,1)S(1)}, u32[]{:S(2)}, u32[]{:S(2)}) collective-permute-start(bf16[64,2048]{1,0:T(8,128)(2,1)S(1)} %collective-permute-done.27.refs_1_), channel_id=1, source_target_pairs={{4,0},{5,1},{8,4},{9,5},{12,8},{13,9},{14,12},{15,13},{10,14},{11,... | collective-permute-start | bytes 786440 | tf_op jit(solution)/shard_map/ppermute | solution.py:260
  66.0 1.8 %experts.11 = (bf16[64,2048]{1,0:T(8,128)(2,1)S(1)}, bf16[64,2048]{1,0:T(8,128)(2,1)S(1)}) custom-call(bf16[64,2048]{1,0:T(8,128)(2,1)S(1)} %collective-permute-done.26.refs_0_, bf16[64,2048]{1,0:T(8,128)(2,1)S(1)} %collective-permute-done.27.refs_1_, bf16[144,512]{1,0:T(8,128)(2,1)S(1)} %collective-permute-done.1.refs_5_.refs_2_, ...), custom_call_target="tpu_custom_call" | custom-call | flops 1207959552 | bytes 9437184 | tf_op jit(solution)/shard_map/experts/pallas_call | solution.py:220
  67.9 1.7 %collective-permute-done.24.refs_0_ = bf16[64,2048]{1,0:T(8,128)(2,1)S(1)} collective-permute-done((bf16[64,2048]{1,0:T(8,128)(2,1)S(1)}, bf16[64,2048]{1,0:T(8,128)(2,1)S(1)}, u32[]{:S(2)}, u32[]{:S(2)}) %collective-permute-start.24) | collective-permute-done | bytes 262176 | tf_op jit(solution)/shard_map/ppermute | solution.py:260
  70.1 1.8 %experts.12 = (bf16[64,2048]{1,0:T(8,128)(2,1)S(1)}, bf16[64,2048]{1,0:T(8,128)(2,1)S(1)}) custom-call(bf16[64,2048]{1,0:T(8,128)(2,1)S(1)} %collective-permute-done.24.refs_0_, bf16[64,2048]{1,0:T(8,128)(2,1)S(1)} %collective-permute-done.25.refs_1_, bf16[144,512]{1,0:T(8,128)(2,1)S(1)} %collective-permute-done.4.refs_6_.refs_2_, ...), custom_call_target="tpu_custom_call" | custom-call | flops 1207959552 | bytes 9437184 | tf_op jit(solution)/shard_map/experts/pallas_call | solution.py:220
  71.9 3.3 %collective-permute-done.29.refs_0_ = bf16[64,2048]{1,0:T(8,128)(2,1)S(1)} collective-permute-done((bf16[64,2048]{1,0:T(8,128)(2,1)S(1)}, bf16[64,2048]{1,0:T(8,128)(2,1)S(1)}, u32[]{:S(2)}, u32[]{:S(2)}) %collective-permute-start.29) | collective-permute-done | bytes 262176 | tf_op jit(solution)/shard_map/ppermute | solution.py:260
  75.3 1.6 %collective-permute-start.31 = (bf16[64,2048]{1,0:T(8,128)(2,1)S(1)}, bf16[64,2048]{1,0:T(8,128)(2,1)S(1)}, u32[]{:S(2)}, u32[]{:S(2)}) collective-permute-start(bf16[64,2048]{1,0:T(8,128)(2,1)S(1)} %collective-permute-done.30.refs_1_), channel_id=1, source_target_pairs={{4,0},{5,1},{8,4},{9,5},{12,8},{13,9},{14,12},{15,13},{10,14},{11,... | collective-permute-start | bytes 786440 | tf_op jit(solution)/shard_map/ppermute | solution.py:260
  76.8 1.8 %experts.13 = (bf16[64,2048]{1,0:T(8,128)(2,1)S(1)}, bf16[64,2048]{1,0:T(8,128)(2,1)S(1)}) custom-call(bf16[64,2048]{1,0:T(8,128)(2,1)S(1)} %collective-permute-done.29.refs_0_, bf16[64,2048]{1,0:T(8,128)(2,1)S(1)} %collective-permute-done.30.refs_1_, bf16[144,512]{1,0:T(8,128)(2,1)S(1)} %collective-permute-done.4.refs_6_.refs_2_, ...), custom_call_target="tpu_custom_call" | custom-call | flops 1207959552 | bytes 9437184 | tf_op jit(solution)/shard_map/experts/pallas_call | solution.py:220
  79.3 1.4 %collective-permute-start.40 = (bf16[64,2048]{1,0:T(8,128)(2,1)S(1)}, bf16[64,2048]{1,0:T(8,128)(2,1)S(1)}, u32[]{:S(2)}, u32[]{:S(2)}) collective-permute-start(bf16[64,2048]{1,0:T(8,128)(2,1)S(1)} %get-tuple-element.201), channel_id=1, source_target_pairs={{0,4},{1,5},{4,8},{5,9},{8,12},{9,13},{12,14},{13,15},{14,10},{15,... | collective-permute-start | bytes 786440 | tf_op jit(solution)/shard_map/ppermute | solution.py:260
  80.8 3.5 %collective-permute-done.31.refs_1_ = bf16[64,2048]{1,0:T(8,128)(2,1)S(1)} collective-permute-done((bf16[64,2048]{1,0:T(8,128)(2,1)S(1)}, bf16[64,2048]{1,0:T(8,128)(2,1)S(1)}, u32[]{:S(2)}, u32[]{:S(2)}) %collective-permute-start.31) | collective-permute-done | bytes 262176 | tf_op jit(solution)/shard_map/ppermute | solution.py:260
  84.3 1.8 %experts.14 = (bf16[64,2048]{1,0:T(8,128)(2,1)S(1)}, bf16[64,2048]{1,0:T(8,128)(2,1)S(1)}) custom-call(bf16[64,2048]{1,0:T(8,128)(2,1)S(1)} %collective-permute-done.28.refs_0_, bf16[64,2048]{1,0:T(8,128)(2,1)S(1)} %collective-permute-done.31.refs_1_, bf16[144,512]{1,0:T(8,128)(2,1)S(1)} %collective-permute-done.5.refs_7_.refs_2_, ...), custom_call_target="tpu_custom_call" | custom-call | flops 1207959552 | bytes 9437184 | tf_op jit(solution)/shard_map/experts/pallas_call | solution.py:220
  86.8 1.6 %collective-permute-start.33 = (bf16[64,2048]{1,0:T(8,128)(2,1)S(1)}, bf16[64,2048]{1,0:T(8,128)(2,1)S(1)}, u32[]{:S(2)}, u32[]{:S(2)}) collective-permute-start(bf16[64,2048]{1,0:T(8,128)(2,1)S(1)} %get-tuple-element.204), channel_id=1, source_target_pairs={{4,0},{5,1},{8,4},{9,5},{12,8},{13,9},{14,12},{15,13},{10,14},{11,... | collective-permute-start | bytes 786440 | tf_op jit(solution)/shard_map/ppermute | solution.py:260
  88.4 1.5 %collective-permute-done.37 = bf16[64,2048]{1,0:T(8,128)(2,1)S(1)} collective-permute-done((bf16[64,2048]{1,0:T(8,128)(2,1)S(1)}, bf16[64,2048]{1,0:T(8,128)(2,1)S(1)}, u32[]{:S(2)}, u32[]{:S(2)}) %collective-permute-start.37) | collective-permute-done | bytes 262176 | tf_op jit(solution)/shard_map/ppermute | solution.py:260
  89.9 1.9 %collective-permute-start.38 = (bf16[64,2048]{1,0:T(8,128)(2,1)S(1)}, bf16[64,2048]{1,0:T(8,128)(2,1)S(1)}, u32[]{:S(2)}, u32[]{:S(2)}) collective-permute-start(bf16[64,2048]{1,0:T(8,128)(2,1)S(1)} %add_convert_fusion.8), channel_id=1, source_target_pairs={{4,0},{5,1},{8,4},{9,5},{12,8},{13,9},{14,12},{15,13},{10,14},{11,... | collective-permute-start | bytes 786440 | tf_op jit(solution)/shard_map/ppermute | solution.py:260
  92.1 1.8 %experts.15 = (bf16[64,2048]{1,0:T(8,128)(2,1)S(1)}, bf16[64,2048]{1,0:T(8,128)(2,1)S(1)}) custom-call(bf16[64,2048]{1,0:T(8,128)(2,1)S(1)} %get-tuple-element.137.refs_0_, bf16[64,2048]{1,0:T(8,128)(2,1)S(1)} %get-tuple-element.154.refs_1_, bf16[144,512]{1,0:T(8,128)(2,1)S(1)} %copy-done.3, bf16[1,2048,384]{2,1,0:T(8,128)(2,1)S(1)} %copy-done, ...), custom_call_target="tpu_custom_call" | custom-call | flops 1207959552 | bytes 9437184 | tf_op jit(solution)/shard_map/experts/pallas_call | solution.py:220
  94.0 4.8 %collective-permute-done.38 = bf16[64,2048]{1,0:T(8,128)(2,1)S(1)} collective-permute-done((bf16[64,2048]{1,0:T(8,128)(2,1)S(1)}, bf16[64,2048]{1,0:T(8,128)(2,1)S(1)}, u32[]{:S(2)}, u32[]{:S(2)}) %collective-permute-start.38) | collective-permute-done | bytes 262176 | tf_op jit(solution)/shard_map/ppermute | solution.py:260
  98.9 1.6 %collective-permute-start.39 = (bf16[64,2048]{1,0:T(8,128)(2,1)S(1)}, bf16[64,2048]{1,0:T(8,128)(2,1)S(1)}, u32[]{:S(2)}, u32[]{:S(2)}) collective-permute-start(bf16[64,2048]{1,0:T(8,128)(2,1)S(1)} %add_convert_fusion.7), channel_id=1, source_target_pairs={{4,0},{5,1},{8,4},{9,5},{12,8},{13,9},{14,12},{15,13},{10,14},{11,... | collective-permute-start | bytes 786440 | tf_op jit(solution)/shard_map/ppermute | solution.py:260
  101.7 1.6 %collective-permute-start.43 = (bf16[64,2048]{1,0:T(8,128)(2,1)S(1)}, bf16[64,2048]{1,0:T(8,128)(2,1)S(1)}, u32[]{:S(2)}, u32[]{:S(2)}) collective-permute-start(bf16[64,2048]{1,0:T(8,128)(2,1)S(1)} %add_convert_fusion.3), channel_id=1, source_target_pairs={{4,0},{5,1},{8,4},{9,5},{12,8},{13,9},{14,12},{15,13},{10,14},{11,... | collective-permute-start | bytes 786440 | tf_op jit(solution)/shard_map/ppermute | solution.py:260
  103.3 9.2 %collective-permute-done.34 = bf16[64,2048]{1,0:T(8,128)(2,1)S(1)} collective-permute-done((bf16[64,2048]{1,0:T(8,128)(2,1)S(1)}, bf16[64,2048]{1,0:T(8,128)(2,1)S(1)}, u32[]{:S(2)}, u32[]{:S(2)}) %collective-permute-start.34) | collective-permute-done | bytes 262176 | tf_op jit(solution)/shard_map/ppermute | solution.py:260
  113.2 1.6 %collective-permute-start.44 = (bf16[64,2048]{1,0:T(8,128)(2,1)S(1)}, bf16[64,2048]{1,0:T(8,128)(2,1)S(1)}, u32[]{:S(2)}, u32[]{:S(2)}) collective-permute-start(bf16[64,2048]{1,0:T(8,128)(2,1)S(1)} %add_convert_fusion.2), channel_id=1, source_target_pairs={{4,0},{5,1},{8,4},{9,5},{12,8},{13,9},{14,12},{15,13},{10,14},{11,... | collective-permute-start | bytes 786440 | tf_op jit(solution)/shard_map/ppermute | solution.py:260
  114.8 6.5 %collective-permute-done.35 = bf16[64,2048]{1,0:T(8,128)(2,1)S(1)} collective-permute-done((bf16[64,2048]{1,0:T(8,128)(2,1)S(1)}, bf16[64,2048]{1,0:T(8,128)(2,1)S(1)}, u32[]{:S(2)}, u32[]{:S(2)}) %collective-permute-start.35) | collective-permute-done | bytes 262176 | tf_op jit(solution)/shard_map/ppermute | solution.py:260
  122.4 1.2 collective-permute-start.45
  123.6 4.2 %collective-permute-done.36 = bf16[64,2048]{1,0:T(8,128)(2,1)S(1)} collective-permute-done((bf16[64,2048]{1,0:T(8,128)(2,1)S(1)}, bf16[64,2048]{1,0:T(8,128)(2,1)S(1)}, u32[]{:S(2)}, u32[]{:S(2)}) %collective-permute-start.36) | collective-permute-done | bytes 262176 | tf_op jit(solution)/shard_map/ppermute | solution.py:260
  (83 shorter events, 14.7 us)
Async XLA Ops:
  0.0 16.7 %copy-start.5 = (f32[2048]{0:T(1024)S(1)}, f32[2048]{0:T(1024)}, u32[]{:S(2)}) copy-start(f32[2048]{0:T(1024)} %param.16) | copy-start | bytes 24580
  0.0 16.7 %copy-start.1 = (bf16[1,2048,384]{2,1,0:T(8,128)(2,1)S(1)}, bf16[1,2048,384]{2,1,0:T(8,128)(2,1)}, u32[]{:S(2)}) copy-start(bf16[1,2048,384]{2,1,0:T(8,128)(2,1)} %refs_4_.15) | copy-start | bytes 4718596
  2.4 14.3 %collective-permute-start.3 = (bf16[1,2048,384]{2,1,0:T(8,128)(2,1)}, bf16[1,2048,384]{2,1,0:T(8,128)(2,1)S(1)}, u32[]{:S(2)}, u32[]{:S(2)}) collective-permute-start(bf16[1,2048,384]{2,1,0:T(8,128)(2,1)} %refs_3_.3), channel_id=1, source_target_pairs={{0,1},{1,0},{2,3},{3,2},{4,5},{5,4},{6,7},{7,6},{8,9},{9,8},{10,11... | collective-permute-start | bytes 4718600 | tf_op jit(solution)/shard_map/ppermute | solution.py:260
  2.8 7.3 %collective-permute-start.2 = (bf16[144,512]{1,0:T(8,128)(2,1)}, bf16[144,512]{1,0:T(8,128)(2,1)S(1)}, u32[]{:S(2)}, u32[]{:S(2)}) collective-permute-start(bf16[144,512]{1,0:T(8,128)(2,1)} %pack_message.1.refs_3_.refs_2_), channel_id=1, source_target_pairs={{4,0},{5,1},{8,4},{9,5},{12,8},{13,9},{14,12},{15,13},{10,14},{11,... | collective-permute-start | bytes 442376 | tf_op jit(solution)/shard_map/ppermute | solution.py:260
  5.3 6.2 %collective-permute-start = (bf16[144,512]{1,0:T(8,128)(2,1)}, bf16[144,512]{1,0:T(8,128)(2,1)S(1)}, u32[]{:S(2)}, u32[]{:S(2)}) collective-permute-start(bf16[144,512]{1,0:T(8,128)(2,1)} %pack_message.1.refs_3_.refs_2_), channel_id=1, source_target_pairs={{0,4},{1,5},{4,8},{5,9},{8,12},{9,13},{12,14},{13,15},{14,10},{15,... | collective-permute-start | bytes 442376 | tf_op jit(solution)/shard_map/ppermute | solution.py:260
  11.5 5.2 %collective-permute-start.1 = (bf16[144,512]{1,0:T(8,128)(2,1)S(1)}, bf16[144,512]{1,0:T(8,128)(2,1)S(1)}, u32[]{:S(2)}, u32[]{:S(2)}) collective-permute-start(bf16[144,512]{1,0:T(8,128)(2,1)S(1)} %collective-permute-done.refs_4_.refs_2_), channel_id=1, source_target_pairs={{0,4},{1,5},{4,8},{5,9},{8,12},{9,13},{12,14},{13,15},{14,10},{15,... | collective-permute-start | bytes 442376 | tf_op jit(solution)/shard_map/ppermute | solution.py:260
  16.7 15.6 %collective-permute-start.16 = (bf16[1,2048,384]{2,1,0:T(8,128)(2,1)S(1)}, bf16[1,2048,384]{2,1,0:T(8,128)(2,1)S(1)}, u32[]{:S(2)}, u32[]{:S(2)}) collective-permute-start(bf16[1,2048,384]{2,1,0:T(8,128)(2,1)S(1)} %copy-done.1), channel_id=1, source_target_pairs={{0,1},{1,0},{2,3},{3,2},{4,5},{5,4},{6,7},{7,6},{8,9},{9,8},{10,11... | collective-permute-start | bytes 4718600 | tf_op jit(solution)/shard_map/ppermute | solution.py:260
  16.8 6.2 %collective-permute-start.6 = (bf16[144,512]{1,0:T(8,128)(2,1)S(1)}, bf16[144,512]{1,0:T(8,128)(2,1)S(1)}, u32[]{:S(2)}, u32[]{:S(2)}) collective-permute-start(bf16[144,512]{1,0:T(8,128)(2,1)S(1)} %collective-permute-done.2.refs_8_.refs_3_), channel_id=1, source_target_pairs={{4,0},{5,1},{8,4},{9,5},{12,8},{13,9},{14,12},{15,13},{10,14},{11,... | collective-permute-start | bytes 442376 | tf_op jit(solution)/shard_map/ppermute | solution.py:260
  18.4 6.2 %collective-permute-start.8 = (bf16[144,512]{1,0:T(8,128)(2,1)S(1)}, bf16[144,512]{1,0:T(8,128)(2,1)S(1)}, u32[]{:S(2)}, u32[]{:S(2)}) collective-permute-start(bf16[144,512]{1,0:T(8,128)(2,1)S(1)} %copy-done.3), channel_id=1, source_target_pairs={{0,1},{1,0},{2,3},{3,2},{4,5},{5,4},{6,7},{7,6},{8,9},{9,8},{10,11... | collective-permute-start | bytes 442376 | tf_op jit(solution)/shard_map/ppermute | solution.py:260
  18.6 6.0 %collective-permute-start.13 = (bf16[144,512]{1,0:T(8,128)(2,1)S(1)}, bf16[144,512]{1,0:T(8,128)(2,1)S(1)}, u32[]{:S(2)}, u32[]{:S(2)}) collective-permute-start(bf16[144,512]{1,0:T(8,128)(2,1)S(1)} %collective-permute-done.2.refs_8_.refs_3_), channel_id=1, source_target_pairs={{0,1},{1,0},{2,3},{3,2},{4,5},{5,4},{6,7},{7,6},{8,9},{9,8},{10,11... | collective-permute-start | bytes 442376 | tf_op jit(solution)/shard_map/ppermute | solution.py:260
  18.9 6.2 %collective-permute-start.4 = (bf16[144,512]{1,0:T(8,128)(2,1)S(1)}, bf16[144,512]{1,0:T(8,128)(2,1)S(1)}, u32[]{:S(2)}, u32[]{:S(2)}) collective-permute-start(bf16[144,512]{1,0:T(8,128)(2,1)S(1)} %collective-permute-done.1.refs_5_.refs_2_), channel_id=1, source_target_pairs={{0,4},{1,5},{4,8},{5,9},{8,12},{9,13},{12,14},{13,15},{14,10},{15,... | collective-permute-start | bytes 442376 | tf_op jit(solution)/shard_map/ppermute | solution.py:260
  23.0 5.4 %collective-permute-start.7 = (bf16[144,512]{1,0:T(8,128)(2,1)S(1)}, bf16[144,512]{1,0:T(8,128)(2,1)S(1)}, u32[]{:S(2)}, u32[]{:S(2)}) collective-permute-start(bf16[144,512]{1,0:T(8,128)(2,1)S(1)} %collective-permute-done.6.refs_9_.refs_3_), channel_id=1, source_target_pairs={{4,0},{5,1},{8,4},{9,5},{12,8},{13,9},{14,12},{15,13},{10,14},{11,... | collective-permute-start | bytes 442376 | tf_op jit(solution)/shard_map/ppermute | solution.py:260
  24.6 3.8 %collective-permute-start.9 = (bf16[144,512]{1,0:T(8,128)(2,1)S(1)}, bf16[144,512]{1,0:T(8,128)(2,1)S(1)}, u32[]{:S(2)}, u32[]{:S(2)}) collective-permute-start(bf16[144,512]{1,0:T(8,128)(2,1)S(1)} %collective-permute-done.refs_4_.refs_2_), channel_id=1, source_target_pairs={{0,1},{1,0},{2,3},{3,2},{4,5},{5,4},{6,7},{7,6},{8,9},{9,8},{10,11... | collective-permute-start | bytes 442376 | tf_op jit(solution)/shard_map/ppermute | solution.py:260
  24.6 4.3 %collective-permute-start.14 = (bf16[144,512]{1,0:T(8,128)(2,1)S(1)}, bf16[144,512]{1,0:T(8,128)(2,1)S(1)}, u32[]{:S(2)}, u32[]{:S(2)}) collective-permute-start(bf16[144,512]{1,0:T(8,128)(2,1)S(1)} %collective-permute-done.6.refs_9_.refs_3_), channel_id=1, source_target_pairs={{0,1},{1,0},{2,3},{3,2},{4,5},{5,4},{6,7},{7,6},{8,9},{9,8},{10,11... | collective-permute-start | bytes 442376 | tf_op jit(solution)/shard_map/ppermute | solution.py:260
  25.1 5.8 %collective-permute-start.5 = (bf16[144,512]{1,0:T(8,128)(2,1)S(1)}, bf16[144,512]{1,0:T(8,128)(2,1)S(1)}, u32[]{:S(2)}, u32[]{:S(2)}) collective-permute-start(bf16[144,512]{1,0:T(8,128)(2,1)S(1)} %collective-permute-done.4.refs_6_.refs_2_), channel_id=1, source_target_pairs={{0,4},{1,5},{4,8},{5,9},{8,12},{9,13},{12,14},{13,15},{14,10},{15,... | collective-permute-start | bytes 442376 | tf_op jit(solution)/shard_map/ppermute | solution.py:260
  28.5 2.5 %collective-permute-start.15 = (bf16[144,512]{1,0:T(8,128)(2,1)S(1)}, bf16[144,512]{1,0:T(8,128)(2,1)S(1)}, u32[]{:S(2)}, u32[]{:S(2)}) collective-permute-start(bf16[144,512]{1,0:T(8,128)(2,1)S(1)} %collective-permute-done.7.refs_10_.refs_3_), channel_id=1, source_target_pairs={{0,1},{1,0},{2,3},{3,2},{4,5},{5,4},{6,7},{7,6},{8,9},{9,8},{10,11... | collective-permute-start | bytes 442376 | tf_op jit(solution)/shard_map/ppermute | solution.py:260
  28.5 2.5 %collective-permute-start.10 = (bf16[144,512]{1,0:T(8,128)(2,1)S(1)}, bf16[144,512]{1,0:T(8,128)(2,1)S(1)}, u32[]{:S(2)}, u32[]{:S(2)}) collective-permute-start(bf16[144,512]{1,0:T(8,128)(2,1)S(1)} %collective-permute-done.1.refs_5_.refs_2_), channel_id=1, source_target_pairs={{0,1},{1,0},{2,3},{3,2},{4,5},{5,4},{6,7},{7,6},{8,9},{9,8},{10,11... | collective-permute-start | bytes 442376 | tf_op jit(solution)/shard_map/ppermute | solution.py:260
  29.0 2.0 %collective-permute-start.11 = (bf16[144,512]{1,0:T(8,128)(2,1)S(1)}, bf16[144,512]{1,0:T(8,128)(2,1)S(1)}, u32[]{:S(2)}, u32[]{:S(2)}) collective-permute-start(bf16[144,512]{1,0:T(8,128)(2,1)S(1)} %collective-permute-done.4.refs_6_.refs_2_), channel_id=1, source_target_pairs={{0,1},{1,0},{2,3},{3,2},{4,5},{5,4},{6,7},{7,6},{8,9},{9,8},{10,11... | collective-permute-start | bytes 442376 | tf_op jit(solution)/shard_map/ppermute | solution.py:260
  31.0 1.4 %collective-permute-start.12 = (bf16[144,512]{1,0:T(8,128)(2,1)S(1)}, bf16[144,512]{1,0:T(8,128)(2,1)S(1)}, u32[]{:S(2)}, u32[]{:S(2)}) collective-permute-start(bf16[144,512]{1,0:T(8,128)(2,1)S(1)} %collective-permute-done.5.refs_7_.refs_2_), channel_id=1, source_target_pairs={{0,1},{1,0},{2,3},{3,2},{4,5},{5,4},{6,7},{7,6},{8,9},{9,8},{10,11... | collective-permute-start | bytes 442376 | tf_op jit(solution)/shard_map/ppermute | solution.py:260
  32.3 14.9 %collective-permute-start.23 = (bf16[1,384,2048]{2,1,0:T(8,128)(2,1)}, bf16[1,384,2048]{2,1,0:T(8,128)(2,1)S(1)}, u32[]{:S(2)}, u32[]{:S(2)}) collective-permute-start(bf16[1,384,2048]{2,1,0:T(8,128)(2,1)} %refs_5_.15), channel_id=1, source_target_pairs={{0,1},{1,0},{2,3},{3,2},{4,5},{5,4},{6,7},{7,6},{8,9},{9,8},{10,11... | collective-permute-start | bytes 4718600 | tf_op jit(solution)/shard_map/ppermute | solution.py:260
  36.2 9.0 %collective-permute-start.19 = (bf16[64,2048]{1,0:T(8,128)(2,1)S(1)}, bf16[64,2048]{1,0:T(8,128)(2,1)S(1)}, u32[]{:S(2)}, u32[]{:S(2)}) collective-permute-start(bf16[64,2048]{1,0:T(8,128)(2,1)S(1)} %get-tuple-element.137.refs_0_), channel_id=1, source_target_pairs={{4,0},{5,1},{8,4},{9,5},{12,8},{13,9},{14,12},{15,13},{10,14},{11,... | collective-permute-start | bytes 786440 | tf_op jit(solution)/shard_map/ppermute | solution.py:260
  37.8 8.9 %collective-permute-start.17 = (bf16[64,2048]{1,0:T(8,128)(2,1)S(1)}, bf16[64,2048]{1,0:T(8,128)(2,1)S(1)}, u32[]{:S(2)}, u32[]{:S(2)}) collective-permute-start(bf16[64,2048]{1,0:T(8,128)(2,1)S(1)} %get-tuple-element.137.refs_0_), channel_id=1, source_target_pairs={{0,4},{1,5},{4,8},{5,9},{8,12},{9,13},{12,14},{13,15},{14,10},{15,... | collective-permute-start | bytes 786440 | tf_op jit(solution)/shard_map/ppermute | solution.py:260
  41.9 9.3 %collective-permute-start.22 = (bf16[64,2048]{1,0:T(8,128)(2,1)S(1)}, bf16[64,2048]{1,0:T(8,128)(2,1)S(1)}, u32[]{:S(2)}, u32[]{:S(2)}) collective-permute-start(bf16[64,2048]{1,0:T(8,128)(2,1)S(1)} %get-tuple-element.154.refs_1_), channel_id=1, source_target_pairs={{4,0},{5,1},{8,4},{9,5},{12,8},{13,9},{14,12},{15,13},{10,14},{11,... | collective-permute-start | bytes 786440 | tf_op jit(solution)/shard_map/ppermute | solution.py:260
  43.5 9.2 %collective-permute-start.21 = (bf16[64,2048]{1,0:T(8,128)(2,1)S(1)}, bf16[64,2048]{1,0:T(8,128)(2,1)S(1)}, u32[]{:S(2)}, u32[]{:S(2)}) collective-permute-start(bf16[64,2048]{1,0:T(8,128)(2,1)S(1)} %get-tuple-element.154.refs_1_), channel_id=1, source_target_pairs={{0,4},{1,5},{4,8},{5,9},{8,12},{9,13},{12,14},{13,15},{14,10},{15,... | collective-permute-start | bytes 786440 | tf_op jit(solution)/shard_map/ppermute | solution.py:260
  45.2 11.6 %collective-permute-start.20 = (bf16[64,2048]{1,0:T(8,128)(2,1)S(1)}, bf16[64,2048]{1,0:T(8,128)(2,1)S(1)}, u32[]{:S(2)}, u32[]{:S(2)}) collective-permute-start(bf16[64,2048]{1,0:T(8,128)(2,1)S(1)} %collective-permute-done.19.refs_1_), channel_id=1, source_target_pairs={{4,0},{5,1},{8,4},{9,5},{12,8},{13,9},{14,12},{15,13},{10,14},{11,... | collective-permute-start | bytes 786440 | tf_op jit(solution)/shard_map/ppermute | solution.py:260
  46.7 11.7 %collective-permute-start.18 = (bf16[64,2048]{1,0:T(8,128)(2,1)S(1)}, bf16[64,2048]{1,0:T(8,128)(2,1)S(1)}, u32[]{:S(2)}, u32[]{:S(2)}) collective-permute-start(bf16[64,2048]{1,0:T(8,128)(2,1)S(1)} %collective-permute-done.17.refs_0_), channel_id=1, source_target_pairs={{0,4},{1,5},{4,8},{5,9},{8,12},{9,13},{12,14},{13,15},{14,10},{15,... | collective-permute-start | bytes 786440 | tf_op jit(solution)/shard_map/ppermute | solution.py:260
  52.8 11.2 %collective-permute-start.26 = (bf16[64,2048]{1,0:T(8,128)(2,1)S(1)}, bf16[64,2048]{1,0:T(8,128)(2,1)S(1)}, u32[]{:S(2)}, u32[]{:S(2)}) collective-permute-start(bf16[64,2048]{1,0:T(8,128)(2,1)S(1)} %collective-permute-done.21.refs_0_), channel_id=1, source_target_pairs={{0,4},{1,5},{4,8},{5,9},{8,12},{9,13},{12,14},{13,15},{14,10},{15,... | collective-permute-start | bytes 786440 | tf_op jit(solution)/shard_map/ppermute | solution.py:260
  53.2 10.8 %collective-permute-start.27 = (bf16[64,2048]{1,0:T(8,128)(2,1)S(1)}, bf16[64,2048]{1,0:T(8,128)(2,1)S(1)}, u32[]{:S(2)}, u32[]{:S(2)}) collective-permute-start(bf16[64,2048]{1,0:T(8,128)(2,1)S(1)} %collective-permute-done.22.refs_1_), channel_id=1, source_target_pairs={{4,0},{5,1},{8,4},{9,5},{12,8},{13,9},{14,12},{15,13},{10,14},{11,... | collective-permute-start | bytes 786440 | tf_op jit(solution)/shard_map/ppermute | solution.py:260
  58.4 11.2 %collective-permute-start.24 = (bf16[64,2048]{1,0:T(8,128)(2,1)S(1)}, bf16[64,2048]{1,0:T(8,128)(2,1)S(1)}, u32[]{:S(2)}, u32[]{:S(2)}) collective-permute-start(bf16[64,2048]{1,0:T(8,128)(2,1)S(1)} %collective-permute-done.18.refs_0_), channel_id=1, source_target_pairs={{0,4},{1,5},{4,8},{5,9},{8,12},{9,13},{12,14},{13,15},{14,10},{15,... | collective-permute-start | bytes 786440 | tf_op jit(solution)/shard_map/ppermute | solution.py:260
  58.8 10.8 %collective-permute-start.25 = (bf16[64,2048]{1,0:T(8,128)(2,1)S(1)}, bf16[64,2048]{1,0:T(8,128)(2,1)S(1)}, u32[]{:S(2)}, u32[]{:S(2)}) collective-permute-start(bf16[64,2048]{1,0:T(8,128)(2,1)S(1)} %collective-permute-done.20.refs_1_), channel_id=1, source_target_pairs={{4,0},{5,1},{8,4},{9,5},{12,8},{13,9},{14,12},{15,13},{10,14},{11,... | collective-permute-start | bytes 786440 | tf_op jit(solution)/shard_map/ppermute | solution.py:260
  64.0 11.2 %collective-permute-start.29 = (bf16[64,2048]{1,0:T(8,128)(2,1)S(1)}, bf16[64,2048]{1,0:T(8,128)(2,1)S(1)}, u32[]{:S(2)}, u32[]{:S(2)}) collective-permute-start(bf16[64,2048]{1,0:T(8,128)(2,1)S(1)} %collective-permute-done.26.refs_0_), channel_id=1, source_target_pairs={{0,4},{1,5},{4,8},{5,9},{8,12},{9,13},{12,14},{13,15},{14,10},{15,... | collective-permute-start | bytes 786440 | tf_op jit(solution)/shard_map/ppermute | solution.py:260
  64.5 10.8 %collective-permute-start.30 = (bf16[64,2048]{1,0:T(8,128)(2,1)S(1)}, bf16[64,2048]{1,0:T(8,128)(2,1)S(1)}, u32[]{:S(2)}, u32[]{:S(2)}) collective-permute-start(bf16[64,2048]{1,0:T(8,128)(2,1)S(1)} %collective-permute-done.27.refs_1_), channel_id=1, source_target_pairs={{4,0},{5,1},{8,4},{9,5},{12,8},{13,9},{14,12},{15,13},{10,14},{11,... | collective-permute-start | bytes 786440 | tf_op jit(solution)/shard_map/ppermute | solution.py:260
  69.6 11.1 %collective-permute-start.28 = (bf16[64,2048]{1,0:T(8,128)(2,1)S(1)}, bf16[64,2048]{1,0:T(8,128)(2,1)S(1)}, u32[]{:S(2)}, u32[]{:S(2)}) collective-permute-start(bf16[64,2048]{1,0:T(8,128)(2,1)S(1)} %collective-permute-done.24.refs_0_), channel_id=1, source_target_pairs={{0,4},{1,5},{4,8},{5,9},{8,12},{9,13},{12,14},{13,15},{14,10},{15,... | collective-permute-start | bytes 786440 | tf_op jit(solution)/shard_map/ppermute | solution.py:260
  75.3 9.0 %collective-permute-start.31 = (bf16[64,2048]{1,0:T(8,128)(2,1)S(1)}, bf16[64,2048]{1,0:T(8,128)(2,1)S(1)}, u32[]{:S(2)}, u32[]{:S(2)}) collective-permute-start(bf16[64,2048]{1,0:T(8,128)(2,1)S(1)} %collective-permute-done.30.refs_1_), channel_id=1, source_target_pairs={{4,0},{5,1},{8,4},{9,5},{12,8},{13,9},{14,12},{15,13},{10,14},{11,... | collective-permute-start | bytes 786440 | tf_op jit(solution)/shard_map/ppermute | solution.py:260
  78.7 11.2 %collective-permute-start.37 = (bf16[64,2048]{1,0:T(8,128)(2,1)S(1)}, bf16[64,2048]{1,0:T(8,128)(2,1)S(1)}, u32[]{:S(2)}, u32[]{:S(2)}) collective-permute-start(bf16[64,2048]{1,0:T(8,128)(2,1)S(1)} %get-tuple-element.211), channel_id=1, source_target_pairs={{4,0},{5,1},{8,4},{9,5},{12,8},{13,9},{14,12},{15,13},{10,14},{11,... | collective-permute-start | bytes 786440 | tf_op jit(solution)/shard_map/ppermute | solution.py:260
  79.3 12.5 %collective-permute-start.40 = (bf16[64,2048]{1,0:T(8,128)(2,1)S(1)}, bf16[64,2048]{1,0:T(8,128)(2,1)S(1)}, u32[]{:S(2)}, u32[]{:S(2)}) collective-permute-start(bf16[64,2048]{1,0:T(8,128)(2,1)S(1)} %get-tuple-element.201), channel_id=1, source_target_pairs={{0,4},{1,5},{4,8},{5,9},{8,12},{9,13},{12,14},{13,15},{14,10},{15,... | collective-permute-start | bytes 786440 | tf_op jit(solution)/shard_map/ppermute | solution.py:260
  86.1 15.0 %collective-permute-start.32 = (bf16[64,2048]{1,0:T(8,128)(2,1)S(1)}, bf16[64,2048]{1,0:T(8,128)(2,1)S(1)}, u32[]{:S(2)}, u32[]{:S(2)}) collective-permute-start(bf16[64,2048]{1,0:T(8,128)(2,1)S(1)} %get-tuple-element.203), channel_id=1, source_target_pairs={{0,4},{1,5},{4,8},{5,9},{8,12},{9,13},{12,14},{13,15},{14,10},{15,... | collective-permute-start | bytes 786440 | tf_op jit(solution)/shard_map/ppermute | solution.py:260
  86.8 14.2 %collective-permute-start.33 = (bf16[64,2048]{1,0:T(8,128)(2,1)S(1)}, bf16[64,2048]{1,0:T(8,128)(2,1)S(1)}, u32[]{:S(2)}, u32[]{:S(2)}) collective-permute-start(bf16[64,2048]{1,0:T(8,128)(2,1)S(1)} %get-tuple-element.204), channel_id=1, source_target_pairs={{4,0},{5,1},{8,4},{9,5},{12,8},{13,9},{14,12},{15,13},{10,14},{11,... | collective-permute-start | bytes 786440 | tf_op jit(solution)/shard_map/ppermute | solution.py:260
  89.9 8.9 %collective-permute-start.38 = (bf16[64,2048]{1,0:T(8,128)(2,1)S(1)}, bf16[64,2048]{1,0:T(8,128)(2,1)S(1)}, u32[]{:S(2)}, u32[]{:S(2)}) collective-permute-start(bf16[64,2048]{1,0:T(8,128)(2,1)S(1)} %add_convert_fusion.8), channel_id=1, source_target_pairs={{4,0},{5,1},{8,4},{9,5},{12,8},{13,9},{14,12},{15,13},{10,14},{11,... | collective-permute-start | bytes 786440 | tf_op jit(solution)/shard_map/ppermute | solution.py:260
  91.9 8.6 %collective-permute-start.41 = (bf16[64,2048]{1,0:T(8,128)(2,1)S(1)}, bf16[64,2048]{1,0:T(8,128)(2,1)S(1)}, u32[]{:S(2)}, u32[]{:S(2)}) collective-permute-start(bf16[64,2048]{1,0:T(8,128)(2,1)S(1)} %add_convert_fusion.5), channel_id=1, source_target_pairs={{0,4},{1,5},{4,8},{5,9},{8,12},{9,13},{12,14},{13,15},{14,10},{15,... | collective-permute-start | bytes 786440 | tf_op jit(solution)/shard_map/ppermute | solution.py:260
  98.9 24.8 %collective-permute-start.39 = (bf16[64,2048]{1,0:T(8,128)(2,1)S(1)}, bf16[64,2048]{1,0:T(8,128)(2,1)S(1)}, u32[]{:S(2)}, u32[]{:S(2)}) collective-permute-start(bf16[64,2048]{1,0:T(8,128)(2,1)S(1)} %add_convert_fusion.7), channel_id=1, source_target_pairs={{4,0},{5,1},{8,4},{9,5},{12,8},{13,9},{14,12},{15,13},{10,14},{11,... | collective-permute-start | bytes 786440 | tf_op jit(solution)/shard_map/ppermute | solution.py:260
  100.6 27.4 %collective-permute-start.42 = (bf16[64,2048]{1,0:T(8,128)(2,1)S(1)}, bf16[64,2048]{1,0:T(8,128)(2,1)S(1)}, u32[]{:S(2)}, u32[]{:S(2)}) collective-permute-start(bf16[64,2048]{1,0:T(8,128)(2,1)S(1)} %add_convert_fusion.4), channel_id=1, source_target_pairs={{0,4},{1,5},{4,8},{5,9},{8,12},{9,13},{12,14},{13,15},{14,10},{15,... | collective-permute-start | bytes 786440 | tf_op jit(solution)/shard_map/ppermute | solution.py:260
  101.1 11.4 %collective-permute-start.34 = (bf16[64,2048]{1,0:T(8,128)(2,1)S(1)}, bf16[64,2048]{1,0:T(8,128)(2,1)S(1)}, u32[]{:S(2)}, u32[]{:S(2)}) collective-permute-start(bf16[64,2048]{1,0:T(8,128)(2,1)S(1)} %add_convert_fusion.11), channel_id=1, source_target_pairs={{0,4},{1,5},{4,8},{5,9},{8,12},{9,13},{12,14},{13,15},{14,10},{15,... | collective-permute-start | bytes 786440 | tf_op jit(solution)/shard_map/ppermute | solution.py:260
  101.7 11.4 %collective-permute-start.43 = (bf16[64,2048]{1,0:T(8,128)(2,1)S(1)}, bf16[64,2048]{1,0:T(8,128)(2,1)S(1)}, u32[]{:S(2)}, u32[]{:S(2)}) collective-permute-start(bf16[64,2048]{1,0:T(8,128)(2,1)S(1)} %add_convert_fusion.3), channel_id=1, source_target_pairs={{4,0},{5,1},{8,4},{9,5},{12,8},{13,9},{14,12},{15,13},{10,14},{11,... | collective-permute-start | bytes 786440 | tf_op jit(solution)/shard_map/ppermute | solution.py:260
  112.6 8.7 %collective-permute-start.35 = (bf16[64,2048]{1,0:T(8,128)(2,1)S(1)}, bf16[64,2048]{1,0:T(8,128)(2,1)S(1)}, u32[]{:S(2)}, u32[]{:S(2)}) collective-permute-start(bf16[64,2048]{1,0:T(8,128)(2,1)S(1)} %add_convert_fusion.10), channel_id=1, source_target_pairs={{0,4},{1,5},{4,8},{5,9},{8,12},{9,13},{12,14},{13,15},{14,10},{15,... | collective-permute-start | bytes 786440 | tf_op jit(solution)/shard_map/ppermute | solution.py:260
  113.2 9.1 %collective-permute-start.44 = (bf16[64,2048]{1,0:T(8,128)(2,1)S(1)}, bf16[64,2048]{1,0:T(8,128)(2,1)S(1)}, u32[]{:S(2)}, u32[]{:S(2)}) collective-permute-start(bf16[64,2048]{1,0:T(8,128)(2,1)S(1)} %add_convert_fusion.2), channel_id=1, source_target_pairs={{4,0},{5,1},{8,4},{9,5},{12,8},{13,9},{14,12},{15,13},{10,14},{11,... | collective-permute-start | bytes 786440 | tf_op jit(solution)/shard_map/ppermute | solution.py:260
  121.4 6.4 %collective-permute-start.36 = (bf16[64,2048]{1,0:T(8,128)(2,1)S(1)}, bf16[64,2048]{1,0:T(8,128)(2,1)S(1)}, u32[]{:S(2)}, u32[]{:S(2)}) collective-permute-start(bf16[64,2048]{1,0:T(8,128)(2,1)S(1)} %add_convert_fusion.9), channel_id=1, source_target_pairs={{0,4},{1,5},{4,8},{5,9},{8,12},{9,13},{12,14},{13,15},{14,10},{15,... | collective-permute-start | bytes 786440 | tf_op jit(solution)/shard_map/ppermute | solution.py:260
  122.4 6.4 %collective-permute-start.45 = (bf16[64,2048]{1,0:T(8,128)(2,1)S(1)}, bf16[64,2048]{1,0:T(8,128)(2,1)S(1)}, u32[]{:S(2)}, u32[]{:S(2)}) collective-permute-start(bf16[64,2048]{1,0:T(8,128)(2,1)S(1)} %add_convert_fusion.1), channel_id=1, source_target_pairs={{4,0},{5,1},{8,4},{9,5},{12,8},{13,9},{14,12},{15,13},{10,14},{11,... | collective-permute-start | bytes 786440 | tf_op jit(solution)/shard_map/ppermute | solution.py:260
  (4 other events, 51.1 us)

commit v5 on v4

--- a/solution.py
+++ b/solution.py
@@ -263,8 +263,6 @@
 
     tie = lax.optimization_barrier
     left, right = {0: message}, {0: message}
-    gate_from, unused = tie((gate_weight, message))
-    twin_gate = send(gate_from, swap)
     for hop in range(1, far + 1):
         if hop == 3:
             inputs, unused = tie(((queries, residual, norm_gain), (left[1], right[1])))
@@ -273,22 +271,25 @@
                 inputs[1].astype(jnp.float32),
                 jnp.broadcast_to(inputs[2][None, :], (8, inputs[2].shape[0])),
             )
-            left[2], staged, twin_gate = tie((left[2], staged, twin_gate))
-            up_from, unused = tie((up_weight, left[2]))
-            twin_up = send(up_from, swap)
+            left[2], staged = tie((left[2], staged))
         left[hop] = send(left[hop - 1], onward)
         if hop < far:
             right[hop] = send(right[hop - 1], back)
     plane = [message] + [left[h] for h in range(1, far + 1)] + [right[h] for h in range(1, far)]
     everything = plane + [send(m, swap) for m in plane]
-    everything, down_from, twin_up = tie((everything, down_weight, twin_up))
-    weights = (gate_weight, up_weight, down_weight, twin_gate, twin_up, send(down_from, swap))
+    everything, own_weights = tie((everything, (gate_weight, up_weight, down_weight)))
+    twin_gate, twin_up, twin_down = [send(w, swap) for w in own_weights]
     hidden_upper, upper = attend(0, staged, everything)
     everything, upper = tie((everything, upper))
     hidden_lower, lower = attend(1, staged, everything)
+    lower, twin_gate, twin_up = tie((lower, twin_gate, twin_up))
+    weights = (gate_weight, up_weight, down_weight, twin_gate, twin_up, twin_down)
 
     from_left, from_right = {(0, 0): upper, (0, 1): lower}, {(0, 0): upper, (0, 1): lower}
     outs = {}
+
+    def later(array, than):
+        return tie((array, than))[0]
 
     def experts_on(tokens, used, after):
         used, after = tie((used, after))
@@ -327,12 +328,15 @@
     sums_back[1] = send(far_lower, back)
     own_out, unused = experts_on([(upper, 0, 0), (lower, 0, 1)], [message], (far_upper, far_lower))
     for hop in range(far - 1, 0, -1):
+        onto, backto = sums_on[0], sums_back[1]
         if hop < far - 1:
+            sums_on[1] = later(sums_on[1], earlier[0])
+            sums_back[0] = later(sums_back[0], earlier[1])
             sums_on[1] = send(add_parts(sums_on[1], out_right[hop, 1]), onward)
             sums_back[0] = send(add_parts(sums_back[0], out_left[hop, 0]), back)
-        onto, backto = sums_on[0], sums_back[1]
-        if hop == far - 1:
-            onto, backto, own_out = tie((onto, backto, own_out))
+        if hop == 1:
+            onto, backto = later(onto, own_out), later(backto, own_out)
+        earlier = (onto, backto)
         sums_on[0] = send(add_parts(onto, out_right[hop, 0]), onward)
         sums_back[1] = send(add_parts(backto, out_left[hop, 1]), back)
     hidden_state = (hidden_upper, hidden_lower)

time: 130 us -> 124 us (0.954)
  waiting for transfers between devices: 63.5 us -> 57 us
    ppermute x46, waiting for transfers between devices: 63.5 us -> 57 us  [send(): return lax.ppermute(array, 'ctx', pairs)]
  transfers between devices with their start and end apart: 46 -> 46, of which waited for: 22 -> 26; matrix products, arithmetic and copies ran while one was open for 1% -> 2% of each run, Pallas kernels for 17% -> 18%
where the time goes in v5:
time: 124 us; the launch traced here: 123 us
  waiting for transfers between devices  57 us (46%)
  starting transfers between devices  38.9 us (31%)
  Pallas kernels  23.6 us (19%)
  other arithmetic  2.89 us (2%)
    ppermute x46, waiting for transfers between devices, send(): return lax.ppermute(array, 'ctx', pairs)  57 us
    ppermute x46, starting transfers between devices, send(): return lax.ppermute(array, 'ctx', pairs)  38.9 us
    pallas_call x8, Pallas kernels, run_experts(): pl.pallas_call(functools.partial(expert_kernel, [piece[1:] for piece in p...  14.7 us
    pallas_call x2, Pallas kernels, attend(): pl.pallas_call(functools.partial(attend_kernel, count, half), out_shape=(...  7.3 us
  transfers between devices with their start and end apart: 46, of which 26 were waited for; matrix products, arithmetic and copies ran while one was open for 2% of the time, Pallas kernels for 18%

profile of v5, /device:TPU:0, one launch (start us, length us, event | category | flops | bytes accessed | tf_op | source)
XLA Modules:
  0.0 123.5 jit_solution(16137020492236246110)
XLA Ops:
  0.8 1.6 %pack_message.1.refs_3_.refs_2_ = bf16[144,512]{1,0:T(8,128)(2,1)} custom-call(s32[1]{0:T(128)S(6)} %copy.12.pos_ref, bf16[128,256]{1,0:T(8,128)(2,1)} %key_ref.1, bf16[128,256]{1,0:T(8,128)(2,1)} %value_ref.1, s32[8,128]{1,0:T(8,128)} %bitcast.2, f32[8,128]{1,0:T(8,128)} %bitcast.3), custom_call_target="tpu_custom_call" | custom-call | tf_op jit(solution)/shard_map/pack_message/pallas_call | solution.py:54
  2.4 3.0 %collective-permute-start.2 = (bf16[144,512]{1,0:T(8,128)(2,1)}, bf16[144,512]{1,0:T(8,128)(2,1)S(1)}, u32[]{:S(2)}, u32[]{:S(2)}) collective-permute-start(bf16[144,512]{1,0:T(8,128)(2,1)} %pack_message.1.refs_3_.refs_2_), channel_id=1, source_target_pairs={{4,0},{5,1},{8,4},{9,5},{12,8},{13,9},{14,12},{15,13},{10,14},{11,... | collective-permute-start | bytes 442376 | tf_op jit(solution)/shard_map/ppermute | solution.py:260
  5.4 4.1 %collective-permute-done.2.refs_8_.refs_3_ = bf16[144,512]{1,0:T(8,128)(2,1)S(1)} collective-permute-done((bf16[144,512]{1,0:T(8,128)(2,1)}, bf16[144,512]{1,0:T(8,128)(2,1)S(1)}, u32[]{:S(2)}, u32[]{:S(2)}) %collective-permute-start.2) | collective-permute-done | bytes 147488 | tf_op jit(solution)/shard_map/ppermute | solution.py:260
  9.5 1.3 %collective-permute-done.refs_4_.refs_2_ = bf16[144,512]{1,0:T(8,128)(2,1)S(1)} collective-permute-done((bf16[144,512]{1,0:T(8,128)(2,1)}, bf16[144,512]{1,0:T(8,128)(2,1)S(1)}, u32[]{:S(2)}, u32[]{:S(2)}) %collective-permute-start) | collective-permute-done | bytes 147488 | tf_op jit(solution)/shard_map/ppermute | solution.py:260
  12.4 1.7 %collective-permute-start.5 = (bf16[144,512]{1,0:T(8,128)(2,1)S(1)}, bf16[144,512]{1,0:T(8,128)(2,1)S(1)}, u32[]{:S(2)}, u32[]{:S(2)}) collective-permute-start(bf16[144,512]{1,0:T(8,128)(2,1)S(1)} %collective-permute-done.2.refs_8_.refs_3_), channel_id=1, source_target_pairs={{4,0},{5,1},{8,4},{9,5},{12,8},{13,9},{14,12},{15,13},{10,14},{11,... | collective-permute-start | bytes 442376 | tf_op jit(solution)/shard_map/ppermute | solution.py:260
  14.1 1.9 %collective-permute-done.1.refs_5_.refs_2_ = bf16[144,512]{1,0:T(8,128)(2,1)S(1)} collective-permute-done((bf16[144,512]{1,0:T(8,128)(2,1)S(1)}, bf16[144,512]{1,0:T(8,128)(2,1)S(1)}, u32[]{:S(2)}, u32[]{:S(2)}) %collective-permute-start.1) | collective-permute-done | bytes 147488 | tf_op jit(solution)/shard_map/ppermute | solution.py:260
  17.6 1.7 %collective-permute-start.6 = (bf16[144,512]{1,0:T(8,128)(2,1)S(1)}, bf16[144,512]{1,0:T(8,128)(2,1)S(1)}, u32[]{:S(2)}, u32[]{:S(2)}) collective-permute-start(bf16[144,512]{1,0:T(8,128)(2,1)S(1)} %collective-permute-done.5.refs_9_.refs_3_), channel_id=1, source_target_pairs={{4,0},{5,1},{8,4},{9,5},{12,8},{13,9},{14,12},{15,13},{10,14},{11,... | collective-permute-start | bytes 442376 | tf_op jit(solution)/shard_map/ppermute | solution.py:260
  19.3 1.9 %collective-permute-done.3.refs_6_.refs_2_ = bf16[144,512]{1,0:T(8,128)(2,1)S(1)} collective-permute-done((bf16[144,512]{1,0:T(8,128)(2,1)S(1)}, bf16[144,512]{1,0:T(8,128)(2,1)S(1)}, u32[]{:S(2)}, u32[]{:S(2)}) %collective-permute-start.3) | collective-permute-done | bytes 147488 | tf_op jit(solution)/shard_map/ppermute | solution.py:260
  23.2 3.1 %collective-permute-done.4.refs_7_.refs_2_ = bf16[144,512]{1,0:T(8,128)(2,1)S(1)} collective-permute-done((bf16[144,512]{1,0:T(8,128)(2,1)S(1)}, bf16[144,512]{1,0:T(8,128)(2,1)S(1)}, u32[]{:S(2)}, u32[]{:S(2)}) %collective-permute-start.4) | collective-permute-done | bytes 147488 | tf_op jit(solution)/shard_map/ppermute | solution.py:260
  26.4 1.3 %collective-permute-done.11.refs_15_ = bf16[144,512]{1,0:T(8,128)(2,1)S(1)} collective-permute-done((bf16[144,512]{1,0:T(8,128)(2,1)S(1)}, bf16[144,512]{1,0:T(8,128)(2,1)S(1)}, u32[]{:S(2)}, u32[]{:S(2)}) %collective-permute-start.11) | collective-permute-done | bytes 147488 | tf_op jit(solution)/shard_map/ppermute | solution.py:260
  28.4 3.6 %attend.2 = (f32[64,2048]{1,0:T(8,128)S(1)}, bf16[64,2048]{1,0:T(8,128)(2,1)S(1)}) custom-call(bf16[128,2048]{1,0:T(8,128)(2,1)S(1)} %broadcast_multiply_fusion.refs_0_, f32[128,2048]{1,0:T(8,128)S(1)} %convert_element_type.117.refs_1_, f32[8,2048]{1,0:T(8,128)S(1)} %broadcast_in_dim.2.refs_2_, bf16[144,512]{1,0:T(8,128)(2,1)S(1)} %copy-done.3, ...), custom_call_target="tpu_custom_call" | custom-call | flops 2147483648 | bytes 4194304 | tf_op jit(solution)/shard_map/attend/pallas_call | solution.py:152
  32.1 1.6 %collective-permute-start.19 = (bf16[64,2048]{1,0:T(8,128)(2,1)S(1)}, bf16[64,2048]{1,0:T(8,128)(2,1)S(1)}, u32[]{:S(2)}, u32[]{:S(2)}) collective-permute-start(bf16[64,2048]{1,0:T(8,128)(2,1)S(1)} %get-tuple-element.138.refs_0_), channel_id=1, source_target_pairs={{4,0},{5,1},{8,4},{9,5},{12,8},{13,9},{14,12},{15,13},{10,14},{11,... | collective-permute-start | bytes 786440 | tf_op jit(solution)/shard_map/ppermute | solution.py:260
  34.1 3.6 %attend.3 = (f32[64,2048]{1,0:T(8,128)S(1)}, bf16[64,2048]{1,0:T(8,128)(2,1)S(1)}) custom-call(bf16[128,2048]{1,0:T(8,128)(2,1)S(1)} %broadcast_multiply_fusion.refs_0_, f32[128,2048]{1,0:T(8,128)S(1)} %convert_element_type.117.refs_1_, f32[8,2048]{1,0:T(8,128)S(1)} %broadcast_in_dim.2.refs_2_, bf16[144,512]{1,0:T(8,128)(2,1)S(1)} %copy-done.3, ...), custom_call_target="tpu_custom_call" | custom-call | flops 2147483648 | bytes 4194304 | tf_op jit(solution)/shard_map/attend/pallas_call | solution.py:152
  37.8 1.6 %collective-permute-start.22 = (bf16[64,2048]{1,0:T(8,128)(2,1)S(1)}, bf16[64,2048]{1,0:T(8,128)(2,1)S(1)}, u32[]{:S(2)}, u32[]{:S(2)}) collective-permute-start(bf16[64,2048]{1,0:T(8,128)(2,1)S(1)} %get-tuple-element.158.refs_1_), channel_id=1, source_target_pairs={{4,0},{5,1},{8,4},{9,5},{12,8},{13,9},{14,12},{15,13},{10,14},{11,... | collective-permute-start | bytes 786440 | tf_op jit(solution)/shard_map/ppermute | solution.py:260
  41.0 1.6 %collective-permute-start.20 = (bf16[64,2048]{1,0:T(8,128)(2,1)S(1)}, bf16[64,2048]{1,0:T(8,128)(2,1)S(1)}, u32[]{:S(2)}, u32[]{:S(2)}) collective-permute-start(bf16[64,2048]{1,0:T(8,128)(2,1)S(1)} %collective-permute-done.19.refs_1_), channel_id=1, source_target_pairs={{4,0},{5,1},{8,4},{9,5},{12,8},{13,9},{14,12},{15,13},{10,14},{11,... | collective-permute-start | bytes 786440 | tf_op jit(solution)/shard_map/ppermute | solution.py:260
  43.1 1.8 %experts.8 = (bf16[64,2048]{1,0:T(8,128)(2,1)S(1)}, bf16[64,2048]{1,0:T(8,128)(2,1)S(1)}) custom-call(bf16[64,2048]{1,0:T(8,128)(2,1)S(1)} %collective-permute-done.17.refs_0_, bf16[64,2048]{1,0:T(8,128)(2,1)S(1)} %collective-permute-done.19.refs_1_, bf16[144,512]{1,0:T(8,128)(2,1)S(1)} %collective-permute-done.refs_4_.refs_2_, ...), custom_call_target="tpu_custom_call" | custom-call | flops 1207959552 | bytes 9437184 | tf_op jit(solution)/shard_map/experts/pallas_call | solution.py:220
  44.9 2.2 %collective-permute-done.22.refs_1_ = bf16[64,2048]{1,0:T(8,128)(2,1)S(1)} collective-permute-done((bf16[64,2048]{1,0:T(8,128)(2,1)S(1)}, bf16[64,2048]{1,0:T(8,128)(2,1)S(1)}, u32[]{:S(2)}, u32[]{:S(2)}) %collective-permute-start.22) | collective-permute-done | bytes 262176 | tf_op jit(solution)/shard_map/ppermute | solution.py:260
  47.1 1.6 %collective-permute-done.21.refs_0_ = bf16[64,2048]{1,0:T(8,128)(2,1)S(1)} collective-permute-done((bf16[64,2048]{1,0:T(8,128)(2,1)S(1)}, bf16[64,2048]{1,0:T(8,128)(2,1)S(1)}, u32[]{:S(2)}, u32[]{:S(2)}) %collective-permute-start.21) | collective-permute-done | bytes 262176 | tf_op jit(solution)/shard_map/ppermute | solution.py:260
  49.1 1.6 %collective-permute-start.27 = (bf16[64,2048]{1,0:T(8,128)(2,1)S(1)}, bf16[64,2048]{1,0:T(8,128)(2,1)S(1)}, u32[]{:S(2)}, u32[]{:S(2)}) collective-permute-start(bf16[64,2048]{1,0:T(8,128)(2,1)S(1)} %collective-permute-done.22.refs_1_), channel_id=1, source_target_pairs={{4,0},{5,1},{8,4},{9,5},{12,8},{13,9},{14,12},{15,13},{10,14},{11,... | collective-permute-start | bytes 786440 | tf_op jit(solution)/shard_map/ppermute | solution.py:260
  50.7 1.8 %experts.9 = (bf16[64,2048]{1,0:T(8,128)(2,1)S(1)}, bf16[64,2048]{1,0:T(8,128)(2,1)S(1)}) custom-call(bf16[64,2048]{1,0:T(8,128)(2,1)S(1)} %collective-permute-done.21.refs_0_, bf16[64,2048]{1,0:T(8,128)(2,1)S(1)} %collective-permute-done.22.refs_1_, bf16[144,512]{1,0:T(8,128)(2,1)S(1)} %collective-permute-done.refs_4_.refs_2_, ...), custom_call_target="tpu_custom_call" | custom-call | flops 1207959552 | bytes 9437184 | tf_op jit(solution)/shard_map/experts/pallas_call | solution.py:220
  52.7 1.6 %collective-permute-done.18.refs_0_ = bf16[64,2048]{1,0:T(8,128)(2,1)S(1)} collective-permute-done((bf16[64,2048]{1,0:T(8,128)(2,1)S(1)}, bf16[64,2048]{1,0:T(8,128)(2,1)S(1)}, u32[]{:S(2)}, u32[]{:S(2)}) %collective-permute-start.18) | collective-permute-done | bytes 262176 | tf_op jit(solution)/shard_map/ppermute | solution.py:260
  54.8 1.6 %collective-permute-start.25 = (bf16[64,2048]{1,0:T(8,128)(2,1)S(1)}, bf16[64,2048]{1,0:T(8,128)(2,1)S(1)}, u32[]{:S(2)}, u32[]{:S(2)}) collective-permute-start(bf16[64,2048]{1,0:T(8,128)(2,1)S(1)} %collective-permute-done.20.refs_1_), channel_id=1, source_target_pairs={{4,0},{5,1},{8,4},{9,5},{12,8},{13,9},{14,12},{15,13},{10,14},{11,... | collective-permute-start | bytes 786440 | tf_op jit(solution)/shard_map/ppermute | solution.py:260
  56.3 1.8 %experts.10 = (bf16[64,2048]{1,0:T(8,128)(2,1)S(1)}, bf16[64,2048]{1,0:T(8,128)(2,1)S(1)}) custom-call(bf16[64,2048]{1,0:T(8,128)(2,1)S(1)} %collective-permute-done.18.refs_0_, bf16[64,2048]{1,0:T(8,128)(2,1)S(1)} %collective-permute-done.20.refs_1_, bf16[144,512]{1,0:T(8,128)(2,1)S(1)} %collective-permute-done.1.refs_5_.refs_2_, ...), custom_call_target="tpu_custom_call" | custom-call | flops 1207959552 | bytes 9437184 | tf_op jit(solution)/shard_map/experts/pallas_call | solution.py:220
  58.2 1.7 %collective-permute-done.26.refs_0_ = bf16[64,2048]{1,0:T(8,128)(2,1)S(1)} collective-permute-done((bf16[64,2048]{1,0:T(8,128)(2,1)S(1)}, bf16[64,2048]{1,0:T(8,128)(2,1)S(1)}, u32[]{:S(2)}, u32[]{:S(2)}) %collective-permute-start.26) | collective-permute-done | bytes 262176 | tf_op jit(solution)/shard_map/ppermute | solution.py:260
  60.4 1.6 %collective-permute-start.30 = (bf16[64,2048]{1,0:T(8,128)(2,1)S(1)}, bf16[64,2048]{1,0:T(8,128)(2,1)S(1)}, u32[]{:S(2)}, u32[]{:S(2)}) collective-permute-start(bf16[64,2048]{1,0:T(8,128)(2,1)S(1)} %collective-permute-done.27.refs_1_), channel_id=1, source_target_pairs={{4,0},{5,1},{8,4},{9,5},{12,8},{13,9},{14,12},{15,13},{10,14},{11,... | collective-permute-start | bytes 786440 | tf_op jit(solution)/shard_map/ppermute | solution.py:260
  62.0 1.8 %experts.11 = (bf16[64,2048]{1,0:T(8,128)(2,1)S(1)}, bf16[64,2048]{1,0:T(8,128)(2,1)S(1)}) custom-call(bf16[64,2048]{1,0:T(8,128)(2,1)S(1)} %collective-permute-done.26.refs_0_, bf16[64,2048]{1,0:T(8,128)(2,1)S(1)} %collective-permute-done.27.refs_1_, bf16[144,512]{1,0:T(8,128)(2,1)S(1)} %collective-permute-done.1.refs_5_.refs_2_, ...), custom_call_target="tpu_custom_call" | custom-call | flops 1207959552 | bytes 9437184 | tf_op jit(solution)/shard_map/experts/pallas_call | solution.py:220
  63.8 1.7 %collective-permute-done.24.refs_0_ = bf16[64,2048]{1,0:T(8,128)(2,1)S(1)} collective-permute-done((bf16[64,2048]{1,0:T(8,128)(2,1)S(1)}, bf16[64,2048]{1,0:T(8,128)(2,1)S(1)}, u32[]{:S(2)}, u32[]{:S(2)}) %collective-permute-start.24) | collective-permute-done | bytes 262176 | tf_op jit(solution)/shard_map/ppermute | solution.py:260
  66.0 1.8 %experts.12 = (bf16[64,2048]{1,0:T(8,128)(2,1)S(1)}, bf16[64,2048]{1,0:T(8,128)(2,1)S(1)}) custom-call(bf16[64,2048]{1,0:T(8,128)(2,1)S(1)} %collective-permute-done.24.refs_0_, bf16[64,2048]{1,0:T(8,128)(2,1)S(1)} %collective-permute-done.25.refs_1_, bf16[144,512]{1,0:T(8,128)(2,1)S(1)} %collective-permute-done.3.refs_6_.refs_2_, ...), custom_call_target="tpu_custom_call" | custom-call | flops 1207959552 | bytes 9437184 | tf_op jit(solution)/shard_map/experts/pallas_call | solution.py:220
  67.8 3.3 %collective-permute-done.29.refs_0_ = bf16[64,2048]{1,0:T(8,128)(2,1)S(1)} collective-permute-done((bf16[64,2048]{1,0:T(8,128)(2,1)S(1)}, bf16[64,2048]{1,0:T(8,128)(2,1)S(1)}, u32[]{:S(2)}, u32[]{:S(2)}) %collective-permute-start.29) | collective-permute-done | bytes 262176 | tf_op jit(solution)/shard_map/ppermute | solution.py:260
  71.2 1.6 %collective-permute-start.31 = (bf16[64,2048]{1,0:T(8,128)(2,1)S(1)}, bf16[64,2048]{1,0:T(8,128)(2,1)S(1)}, u32[]{:S(2)}, u32[]{:S(2)}) collective-permute-start(bf16[64,2048]{1,0:T(8,128)(2,1)S(1)} %collective-permute-done.30.refs_1_), channel_id=1, source_target_pairs={{4,0},{5,1},{8,4},{9,5},{12,8},{13,9},{14,12},{15,13},{10,14},{11,... | collective-permute-start | bytes 786440 | tf_op jit(solution)/shard_map/ppermute | solution.py:260
  72.7 1.8 %experts.13 = (bf16[64,2048]{1,0:T(8,128)(2,1)S(1)}, bf16[64,2048]{1,0:T(8,128)(2,1)S(1)}) custom-call(bf16[64,2048]{1,0:T(8,128)(2,1)S(1)} %collective-permute-done.29.refs_0_, bf16[64,2048]{1,0:T(8,128)(2,1)S(1)} %collective-permute-done.30.refs_1_, bf16[144,512]{1,0:T(8,128)(2,1)S(1)} %collective-permute-done.3.refs_6_.refs_2_, ...), custom_call_target="tpu_custom_call" | custom-call | flops 1207959552 | bytes 9437184 | tf_op jit(solution)/shard_map/experts/pallas_call | solution.py:220
  75.1 1.3 %collective-permute-done.28.refs_0_ = bf16[64,2048]{1,0:T(8,128)(2,1)S(1)} collective-permute-done((bf16[64,2048]{1,0:T(8,128)(2,1)S(1)}, bf16[64,2048]{1,0:T(8,128)(2,1)S(1)}, u32[]{:S(2)}, u32[]{:S(2)}) %collective-permute-start.28) | collective-permute-done | bytes 262176 | tf_op jit(solution)/shard_map/ppermute | solution.py:260
  77.5 1.8 %experts.14 = (bf16[64,2048]{1,0:T(8,128)(2,1)S(1)}, bf16[64,2048]{1,0:T(8,128)(2,1)S(1)}) custom-call(bf16[64,2048]{1,0:T(8,128)(2,1)S(1)} %collective-permute-done.28.refs_0_, bf16[64,2048]{1,0:T(8,128)(2,1)S(1)} %collective-permute-done.31.refs_1_, bf16[144,512]{1,0:T(8,128)(2,1)S(1)} %collective-permute-done.4.refs_7_.refs_2_, ...), custom_call_target="tpu_custom_call" | custom-call | flops 1207959552 | bytes 9437184 | tf_op jit(solution)/shard_map/experts/pallas_call | solution.py:220
  79.9 1.6 %collective-permute-start.36 = (bf16[64,2048]{1,0:T(8,128)(2,1)S(1)}, bf16[64,2048]{1,0:T(8,128)(2,1)S(1)}, u32[]{:S(2)}, u32[]{:S(2)}) collective-permute-start(bf16[64,2048]{1,0:T(8,128)(2,1)S(1)} %get-tuple-element.214), channel_id=1, source_target_pairs={{4,0},{5,1},{8,4},{9,5},{12,8},{13,9},{14,12},{15,13},{10,14},{11,... | collective-permute-start | bytes 786440 | tf_op jit(solution)/shard_map/ppermute | solution.py:260
  81.5 1.6 %collective-permute-start.37 = (bf16[64,2048]{1,0:T(8,128)(2,1)S(1)}, bf16[64,2048]{1,0:T(8,128)(2,1)S(1)}, u32[]{:S(2)}, u32[]{:S(2)}) collective-permute-start(bf16[64,2048]{1,0:T(8,128)(2,1)S(1)} %get-tuple-element.208), channel_id=1, source_target_pairs={{4,0},{5,1},{8,4},{9,5},{12,8},{13,9},{14,12},{15,13},{10,14},{11,... | collective-permute-start | bytes 786440 | tf_op jit(solution)/shard_map/ppermute | solution.py:260
  83.0 1.8 %experts.15 = (bf16[64,2048]{1,0:T(8,128)(2,1)S(1)}, bf16[64,2048]{1,0:T(8,128)(2,1)S(1)}) custom-call(bf16[64,2048]{1,0:T(8,128)(2,1)S(1)} %get-tuple-element.138.refs_0_, bf16[64,2048]{1,0:T(8,128)(2,1)S(1)} %get-tuple-element.158.refs_1_, bf16[144,512]{1,0:T(8,128)(2,1)S(1)} %copy-done.3, bf16[1,2048,384]{2,1,0:T(8,128)(2,1)S(1)} %copy-done, ...), custom_call_target="tpu_custom_call" | custom-call | flops 1207959552 | bytes 9437184 | tf_op jit(solution)/shard_map/experts/pallas_call | solution.py:220
  84.9 2.0 %collective-permute-done.32 = bf16[64,2048]{1,0:T(8,128)(2,1)S(1)} collective-permute-done((bf16[64,2048]{1,0:T(8,128)(2,1)S(1)}, bf16[64,2048]{1,0:T(8,128)(2,1)S(1)}, u32[]{:S(2)}, u32[]{:S(2)}) %collective-permute-start.32) | collective-permute-done | bytes 262176 | tf_op jit(solution)/shard_map/ppermute | solution.py:260
  88.0 3.8 %collective-permute-done.37 = bf16[64,2048]{1,0:T(8,128)(2,1)S(1)} collective-permute-done((bf16[64,2048]{1,0:T(8,128)(2,1)S(1)}, bf16[64,2048]{1,0:T(8,128)(2,1)S(1)}, u32[]{:S(2)}, u32[]{:S(2)}) %collective-permute-start.37) | collective-permute-done | bytes 262176 | tf_op jit(solution)/shard_map/ppermute | solution.py:260
  91.9 1.6 %collective-permute-start.38 = (bf16[64,2048]{1,0:T(8,128)(2,1)S(1)}, bf16[64,2048]{1,0:T(8,128)(2,1)S(1)}, u32[]{:S(2)}, u32[]{:S(2)}) collective-permute-start(bf16[64,2048]{1,0:T(8,128)(2,1)S(1)} %add_convert_fusion.8), channel_id=1, source_target_pairs={{4,0},{5,1},{8,4},{9,5},{12,8},{13,9},{14,12},{15,13},{10,14},{11,... | collective-permute-start | bytes 786440 | tf_op jit(solution)/shard_map/ppermute | solution.py:260
  93.6 1.6 %collective-permute-start.39 = (bf16[64,2048]{1,0:T(8,128)(2,1)S(1)}, bf16[64,2048]{1,0:T(8,128)(2,1)S(1)}, u32[]{:S(2)}, u32[]{:S(2)}) collective-permute-start(bf16[64,2048]{1,0:T(8,128)(2,1)S(1)} %add_convert_fusion.7), channel_id=1, source_target_pairs={{4,0},{5,1},{8,4},{9,5},{12,8},{13,9},{14,12},{15,13},{10,14},{11,... | collective-permute-start | bytes 786440 | tf_op jit(solution)/shard_map/ppermute | solution.py:260
  96.1 2.8 %collective-permute-done.33 = bf16[64,2048]{1,0:T(8,128)(2,1)S(1)} collective-permute-done((bf16[64,2048]{1,0:T(8,128)(2,1)S(1)}, bf16[64,2048]{1,0:T(8,128)(2,1)S(1)}, u32[]{:S(2)}, u32[]{:S(2)}) %collective-permute-start.33) | collective-permute-done | bytes 262176 | tf_op jit(solution)/shard_map/ppermute | solution.py:260
  100.1 3.8 %collective-permute-done.39 = bf16[64,2048]{1,0:T(8,128)(2,1)S(1)} collective-permute-done((bf16[64,2048]{1,0:T(8,128)(2,1)S(1)}, bf16[64,2048]{1,0:T(8,128)(2,1)S(1)}, u32[]{:S(2)}, u32[]{:S(2)}) %collective-permute-start.39) | collective-permute-done | bytes 262176 | tf_op jit(solution)/shard_map/ppermute | solution.py:260
  104.0 1.6 %collective-permute-start.40 = (bf16[64,2048]{1,0:T(8,128)(2,1)S(1)}, bf16[64,2048]{1,0:T(8,128)(2,1)S(1)}, u32[]{:S(2)}, u32[]{:S(2)}) collective-permute-start(bf16[64,2048]{1,0:T(8,128)(2,1)S(1)} %add_convert_fusion.6), channel_id=1, source_target_pairs={{4,0},{5,1},{8,4},{9,5},{12,8},{13,9},{14,12},{15,13},{10,14},{11,... | collective-permute-start | bytes 786440 | tf_op jit(solution)/shard_map/ppermute | solution.py:260
  105.7 1.6 %collective-permute-start.44 = (bf16[64,2048]{1,0:T(8,128)(2,1)S(1)}, bf16[64,2048]{1,0:T(8,128)(2,1)S(1)}, u32[]{:S(2)}, u32[]{:S(2)}) collective-permute-start(bf16[64,2048]{1,0:T(8,128)(2,1)S(1)} %add_convert_fusion.2), channel_id=1, source_target_pairs={{4,0},{5,1},{8,4},{9,5},{12,8},{13,9},{14,12},{15,13},{10,14},{11,... | collective-permute-start | bytes 786440 | tf_op jit(solution)/shard_map/ppermute | solution.py:260
  107.3 3.3 %collective-permute-done.34 = bf16[64,2048]{1,0:T(8,128)(2,1)S(1)} collective-permute-done((bf16[64,2048]{1,0:T(8,128)(2,1)S(1)}, bf16[64,2048]{1,0:T(8,128)(2,1)S(1)}, u32[]{:S(2)}, u32[]{:S(2)}) %collective-permute-start.34) | collective-permute-done | bytes 262176 | tf_op jit(solution)/shard_map/ppermute | solution.py:260
  111.7 4.4 %collective-permute-done.44 = bf16[64,2048]{1,0:T(8,128)(2,1)S(1)} collective-permute-done((bf16[64,2048]{1,0:T(8,128)(2,1)S(1)}, bf16[64,2048]{1,0:T(8,128)(2,1)S(1)}, u32[]{:S(2)}, u32[]{:S(2)}) %collective-permute-start.44) | collective-permute-done | bytes 262176 | tf_op jit(solution)/shard_map/ppermute | solution.py:260
  116.1 1.6 %collective-permute-start.45 = (bf16[64,2048]{1,0:T(8,128)(2,1)S(1)}, bf16[64,2048]{1,0:T(8,128)(2,1)S(1)}, u32[]{:S(2)}, u32[]{:S(2)}) collective-permute-start(bf16[64,2048]{1,0:T(8,128)(2,1)S(1)} %add_convert_fusion.1), channel_id=1, source_target_pairs={{4,0},{5,1},{8,4},{9,5},{12,8},{13,9},{14,12},{15,13},{10,14},{11,... | collective-permute-start | bytes 786440 | tf_op jit(solution)/shard_map/ppermute | solution.py:260
  117.9 4.6 %collective-permute-done.45 = bf16[64,2048]{1,0:T(8,128)(2,1)S(1)} collective-permute-done((bf16[64,2048]{1,0:T(8,128)(2,1)S(1)}, bf16[64,2048]{1,0:T(8,128)(2,1)S(1)}, u32[]{:S(2)}, u32[]{:S(2)}) %collective-permute-start.45) | collective-permute-done | bytes 262176 | tf_op jit(solution)/shard_map/ppermute | solution.py:260
  (83 shorter events, 18.0 us)
Async XLA Ops:
  0.0 16.0 %copy-start.5 = (f32[2048]{0:T(1024)S(1)}, f32[2048]{0:T(1024)}, u32[]{:S(2)}) copy-start(f32[2048]{0:T(1024)} %param.16) | copy-start | bytes 24580
  0.0 27.7 %copy-start = (bf16[1,2048,384]{2,1,0:T(8,128)(2,1)S(1)}, bf16[1,2048,384]{2,1,0:T(8,128)(2,1)}, u32[]{:S(2)}) copy-start(bf16[1,2048,384]{2,1,0:T(8,128)(2,1)} %refs_3_.3) | copy-start | bytes 4718596
  2.4 7.2 %collective-permute-start.2 = (bf16[144,512]{1,0:T(8,128)(2,1)}, bf16[144,512]{1,0:T(8,128)(2,1)S(1)}, u32[]{:S(2)}, u32[]{:S(2)}) collective-permute-start(bf16[144,512]{1,0:T(8,128)(2,1)} %pack_message.1.refs_3_.refs_2_), channel_id=1, source_target_pairs={{4,0},{5,1},{8,4},{9,5},{12,8},{13,9},{14,12},{15,13},{10,14},{11,... | collective-permute-start | bytes 442376 | tf_op jit(solution)/shard_map/ppermute | solution.py:260
  5.3 5.5 %collective-permute-start = (bf16[144,512]{1,0:T(8,128)(2,1)}, bf16[144,512]{1,0:T(8,128)(2,1)S(1)}, u32[]{:S(2)}, u32[]{:S(2)}) collective-permute-start(bf16[144,512]{1,0:T(8,128)(2,1)} %pack_message.1.refs_3_.refs_2_), channel_id=1, source_target_pairs={{0,4},{1,5},{4,8},{5,9},{8,12},{9,13},{12,14},{13,15},{14,10},{15,... | collective-permute-start | bytes 442376 | tf_op jit(solution)/shard_map/ppermute | solution.py:260
  10.8 5.1 %collective-permute-start.1 = (bf16[144,512]{1,0:T(8,128)(2,1)S(1)}, bf16[144,512]{1,0:T(8,128)(2,1)S(1)}, u32[]{:S(2)}, u32[]{:S(2)}) collective-permute-start(bf16[144,512]{1,0:T(8,128)(2,1)S(1)} %collective-permute-done.refs_4_.refs_2_), channel_id=1, source_target_pairs={{0,4},{1,5},{4,8},{5,9},{8,12},{9,13},{12,14},{13,15},{14,10},{15,... | collective-permute-start | bytes 442376 | tf_op jit(solution)/shard_map/ppermute | solution.py:260
  12.4 5.2 %collective-permute-start.5 = (bf16[144,512]{1,0:T(8,128)(2,1)S(1)}, bf16[144,512]{1,0:T(8,128)(2,1)S(1)}, u32[]{:S(2)}, u32[]{:S(2)}) collective-permute-start(bf16[144,512]{1,0:T(8,128)(2,1)S(1)} %collective-permute-done.2.refs_8_.refs_3_), channel_id=1, source_target_pairs={{4,0},{5,1},{8,4},{9,5},{12,8},{13,9},{14,12},{15,13},{10,14},{11,... | collective-permute-start | bytes 442376 | tf_op jit(solution)/shard_map/ppermute | solution.py:260
  16.0 5.2 %collective-permute-start.3 = (bf16[144,512]{1,0:T(8,128)(2,1)S(1)}, bf16[144,512]{1,0:T(8,128)(2,1)S(1)}, u32[]{:S(2)}, u32[]{:S(2)}) collective-permute-start(bf16[144,512]{1,0:T(8,128)(2,1)S(1)} %collective-permute-done.1.refs_5_.refs_2_), channel_id=1, source_target_pairs={{0,4},{1,5},{4,8},{5,9},{8,12},{9,13},{12,14},{13,15},{14,10},{15,... | collective-permute-start | bytes 442376 | tf_op jit(solution)/shard_map/ppermute | solution.py:260
  16.4 5.1 %collective-permute-start.7 = (bf16[144,512]{1,0:T(8,128)(2,1)S(1)}, bf16[144,512]{1,0:T(8,128)(2,1)S(1)}, u32[]{:S(2)}, u32[]{:S(2)}) collective-permute-start(bf16[144,512]{1,0:T(8,128)(2,1)S(1)} %copy-done.3), channel_id=1, source_target_pairs={{0,1},{1,0},{2,3},{3,2},{4,5},{5,4},{6,7},{7,6},{8,9},{9,8},{10,11... | collective-permute-start | bytes 442376 | tf_op jit(solution)/shard_map/ppermute | solution.py:260
  16.4 5.1 %collective-permute-start.12 = (bf16[144,512]{1,0:T(8,128)(2,1)S(1)}, bf16[144,512]{1,0:T(8,128)(2,1)S(1)}, u32[]{:S(2)}, u32[]{:S(2)}) collective-permute-start(bf16[144,512]{1,0:T(8,128)(2,1)S(1)} %collective-permute-done.2.refs_8_.refs_3_), channel_id=1, source_target_pairs={{0,1},{1,0},{2,3},{3,2},{4,5},{5,4},{6,7},{7,6},{8,9},{9,8},{10,11... | collective-permute-start | bytes 442376 | tf_op jit(solution)/shard_map/ppermute | solution.py:260
  16.9 5.2 %collective-permute-start.8 = (bf16[144,512]{1,0:T(8,128)(2,1)S(1)}, bf16[144,512]{1,0:T(8,128)(2,1)S(1)}, u32[]{:S(2)}, u32[]{:S(2)}) collective-permute-start(bf16[144,512]{1,0:T(8,128)(2,1)S(1)} %collective-permute-done.refs_4_.refs_2_), channel_id=1, source_target_pairs={{0,1},{1,0},{2,3},{3,2},{4,5},{5,4},{6,7},{7,6},{8,9},{9,8},{10,11... | collective-permute-start | bytes 442376 | tf_op jit(solution)/shard_map/ppermute | solution.py:260
  17.6 5.6 %collective-permute-start.6 = (bf16[144,512]{1,0:T(8,128)(2,1)S(1)}, bf16[144,512]{1,0:T(8,128)(2,1)S(1)}, u32[]{:S(2)}, u32[]{:S(2)}) collective-permute-start(bf16[144,512]{1,0:T(8,128)(2,1)S(1)} %collective-permute-done.5.refs_9_.refs_3_), channel_id=1, source_target_pairs={{4,0},{5,1},{8,4},{9,5},{12,8},{13,9},{14,12},{15,13},{10,14},{11,... | collective-permute-start | bytes 442376 | tf_op jit(solution)/shard_map/ppermute | solution.py:260
  21.2 5.1 %collective-permute-start.4 = (bf16[144,512]{1,0:T(8,128)(2,1)S(1)}, bf16[144,512]{1,0:T(8,128)(2,1)S(1)}, u32[]{:S(2)}, u32[]{:S(2)}) collective-permute-start(bf16[144,512]{1,0:T(8,128)(2,1)S(1)} %collective-permute-done.3.refs_6_.refs_2_), channel_id=1, source_target_pairs={{0,4},{1,5},{4,8},{5,9},{8,12},{9,13},{12,14},{13,15},{14,10},{15,... | collective-permute-start | bytes 442376 | tf_op jit(solution)/shard_map/ppermute | solution.py:260
  21.6 4.8 %collective-permute-start.9 = (bf16[144,512]{1,0:T(8,128)(2,1)S(1)}, bf16[144,512]{1,0:T(8,128)(2,1)S(1)}, u32[]{:S(2)}, u32[]{:S(2)}) collective-permute-start(bf16[144,512]{1,0:T(8,128)(2,1)S(1)} %collective-permute-done.1.refs_5_.refs_2_), channel_id=1, source_target_pairs={{0,1},{1,0},{2,3},{3,2},{4,5},{5,4},{6,7},{7,6},{8,9},{9,8},{10,11... | collective-permute-start | bytes 442376 | tf_op jit(solution)/shard_map/ppermute | solution.py:260
  21.6 4.8 %collective-permute-start.13 = (bf16[144,512]{1,0:T(8,128)(2,1)S(1)}, bf16[144,512]{1,0:T(8,128)(2,1)S(1)}, u32[]{:S(2)}, u32[]{:S(2)}) collective-permute-start(bf16[144,512]{1,0:T(8,128)(2,1)S(1)} %collective-permute-done.5.refs_9_.refs_3_), channel_id=1, source_target_pairs={{0,1},{1,0},{2,3},{3,2},{4,5},{5,4},{6,7},{7,6},{8,9},{9,8},{10,11... | collective-permute-start | bytes 442376 | tf_op jit(solution)/shard_map/ppermute | solution.py:260
  22.1 4.3 %collective-permute-start.10 = (bf16[144,512]{1,0:T(8,128)(2,1)S(1)}, bf16[144,512]{1,0:T(8,128)(2,1)S(1)}, u32[]{:S(2)}, u32[]{:S(2)}) collective-permute-start(bf16[144,512]{1,0:T(8,128)(2,1)S(1)} %collective-permute-done.3.refs_6_.refs_2_), channel_id=1, source_target_pairs={{0,1},{1,0},{2,3},{3,2},{4,5},{5,4},{6,7},{7,6},{8,9},{9,8},{10,11... | collective-permute-start | bytes 442376 | tf_op jit(solution)/shard_map/ppermute | solution.py:260
  23.2 3.2 %collective-permute-start.14 = (bf16[144,512]{1,0:T(8,128)(2,1)S(1)}, bf16[144,512]{1,0:T(8,128)(2,1)S(1)}, u32[]{:S(2)}, u32[]{:S(2)}) collective-permute-start(bf16[144,512]{1,0:T(8,128)(2,1)S(1)} %collective-permute-done.6.refs_10_.refs_3_), channel_id=1, source_target_pairs={{0,1},{1,0},{2,3},{3,2},{4,5},{5,4},{6,7},{7,6},{8,9},{9,8},{10,11... | collective-permute-start | bytes 442376 | tf_op jit(solution)/shard_map/ppermute | solution.py:260
  26.3 1.4 %collective-permute-start.11 = (bf16[144,512]{1,0:T(8,128)(2,1)S(1)}, bf16[144,512]{1,0:T(8,128)(2,1)S(1)}, u32[]{:S(2)}, u32[]{:S(2)}) collective-permute-start(bf16[144,512]{1,0:T(8,128)(2,1)S(1)} %collective-permute-done.4.refs_7_.refs_2_), channel_id=1, source_target_pairs={{0,1},{1,0},{2,3},{3,2},{4,5},{5,4},{6,7},{7,6},{8,9},{9,8},{10,11... | collective-permute-start | bytes 442376 | tf_op jit(solution)/shard_map/ppermute | solution.py:260
  27.7 10.1 %collective-permute-start.15 = (bf16[1,2048,384]{2,1,0:T(8,128)(2,1)S(1)}, bf16[1,2048,384]{2,1,0:T(8,128)(2,1)S(1)}, u32[]{:S(2)}, u32[]{:S(2)}) collective-permute-start(bf16[1,2048,384]{2,1,0:T(8,128)(2,1)S(1)} %copy-done), channel_id=1, source_target_pairs={{0,1},{1,0},{2,3},{3,2},{4,5},{5,4},{6,7},{7,6},{8,9},{9,8},{10,11... | collective-permute-start | bytes 4718600 | tf_op jit(solution)/shard_map/ppermute | solution.py:260
  27.9 10.0 %collective-permute-start.16 = (bf16[1,2048,384]{2,1,0:T(8,128)(2,1)}, bf16[1,2048,384]{2,1,0:T(8,128)(2,1)S(1)}, u32[]{:S(2)}, u32[]{:S(2)}) collective-permute-start(bf16[1,2048,384]{2,1,0:T(8,128)(2,1)} %refs_4_.15), channel_id=1, source_target_pairs={{0,1},{1,0},{2,3},{3,2},{4,5},{5,4},{6,7},{7,6},{8,9},{9,8},{10,11... | collective-permute-start | bytes 4718600 | tf_op jit(solution)/shard_map/ppermute | solution.py:260
  28.2 14.8 %collective-permute-start.23 = (bf16[1,384,2048]{2,1,0:T(8,128)(2,1)}, bf16[1,384,2048]{2,1,0:T(8,128)(2,1)S(1)}, u32[]{:S(2)}, u32[]{:S(2)}) collective-permute-start(bf16[1,384,2048]{2,1,0:T(8,128)(2,1)} %refs_5_.15), channel_id=1, source_target_pairs={{0,1},{1,0},{2,3},{3,2},{4,5},{5,4},{6,7},{7,6},{8,9},{9,8},{10,11... | collective-permute-start | bytes 4718600 | tf_op jit(solution)/shard_map/ppermute | solution.py:260
  32.1 9.0 %collective-permute-start.19 = (bf16[64,2048]{1,0:T(8,128)(2,1)S(1)}, bf16[64,2048]{1,0:T(8,128)(2,1)S(1)}, u32[]{:S(2)}, u32[]{:S(2)}) collective-permute-start(bf16[64,2048]{1,0:T(8,128)(2,1)S(1)} %get-tuple-element.138.refs_0_), channel_id=1, source_target_pairs={{4,0},{5,1},{8,4},{9,5},{12,8},{13,9},{14,12},{15,13},{10,14},{11,... | collective-permute-start | bytes 786440 | tf_op jit(solution)/shard_map/ppermute | solution.py:260
  33.7 8.9 %collective-permute-start.17 = (bf16[64,2048]{1,0:T(8,128)(2,1)S(1)}, bf16[64,2048]{1,0:T(8,128)(2,1)S(1)}, u32[]{:S(2)}, u32[]{:S(2)}) collective-permute-start(bf16[64,2048]{1,0:T(8,128)(2,1)S(1)} %get-tuple-element.138.refs_0_), channel_id=1, source_target_pairs={{0,4},{1,5},{4,8},{5,9},{8,12},{9,13},{12,14},{13,15},{14,10},{15,... | collective-permute-start | bytes 786440 | tf_op jit(solution)/shard_map/ppermute | solution.py:260
  37.8 9.3 %collective-permute-start.22 = (bf16[64,2048]{1,0:T(8,128)(2,1)S(1)}, bf16[64,2048]{1,0:T(8,128)(2,1)S(1)}, u32[]{:S(2)}, u32[]{:S(2)}) collective-permute-start(bf16[64,2048]{1,0:T(8,128)(2,1)S(1)} %get-tuple-element.158.refs_1_), channel_id=1, source_target_pairs={{4,0},{5,1},{8,4},{9,5},{12,8},{13,9},{14,12},{15,13},{10,14},{11,... | collective-permute-start | bytes 786440 | tf_op jit(solution)/shard_map/ppermute | solution.py:260
  39.5 9.2 %collective-permute-start.21 = (bf16[64,2048]{1,0:T(8,128)(2,1)S(1)}, bf16[64,2048]{1,0:T(8,128)(2,1)S(1)}, u32[]{:S(2)}, u32[]{:S(2)}) collective-permute-start(bf16[64,2048]{1,0:T(8,128)(2,1)S(1)} %get-tuple-element.158.refs_1_), channel_id=1, source_target_pairs={{0,4},{1,5},{4,8},{5,9},{8,12},{9,13},{12,14},{13,15},{14,10},{15,... | collective-permute-start | bytes 786440 | tf_op jit(solution)/shard_map/ppermute | solution.py:260
  41.0 11.7 %collective-permute-start.20 = (bf16[64,2048]{1,0:T(8,128)(2,1)S(1)}, bf16[64,2048]{1,0:T(8,128)(2,1)S(1)}, u32[]{:S(2)}, u32[]{:S(2)}) collective-permute-start(bf16[64,2048]{1,0:T(8,128)(2,1)S(1)} %collective-permute-done.19.refs_1_), channel_id=1, source_target_pairs={{4,0},{5,1},{8,4},{9,5},{12,8},{13,9},{14,12},{15,13},{10,14},{11,... | collective-permute-start | bytes 786440 | tf_op jit(solution)/shard_map/ppermute | solution.py:260
  42.6 11.7 %collective-permute-start.18 = (bf16[64,2048]{1,0:T(8,128)(2,1)S(1)}, bf16[64,2048]{1,0:T(8,128)(2,1)S(1)}, u32[]{:S(2)}, u32[]{:S(2)}) collective-permute-start(bf16[64,2048]{1,0:T(8,128)(2,1)S(1)} %collective-permute-done.17.refs_0_), channel_id=1, source_target_pairs={{0,4},{1,5},{4,8},{5,9},{8,12},{9,13},{12,14},{13,15},{14,10},{15,... | collective-permute-start | bytes 786440 | tf_op jit(solution)/shard_map/ppermute | solution.py:260
  48.7 11.2 %collective-permute-start.26 = (bf16[64,2048]{1,0:T(8,128)(2,1)S(1)}, bf16[64,2048]{1,0:T(8,128)(2,1)S(1)}, u32[]{:S(2)}, u32[]{:S(2)}) collective-permute-start(bf16[64,2048]{1,0:T(8,128)(2,1)S(1)} %collective-permute-done.21.refs_0_), channel_id=1, source_target_pairs={{0,4},{1,5},{4,8},{5,9},{8,12},{9,13},{12,14},{13,15},{14,10},{15,... | collective-permute-start | bytes 786440 | tf_op jit(solution)/shard_map/ppermute | solution.py:260
  49.1 10.8 %collective-permute-start.27 = (bf16[64,2048]{1,0:T(8,128)(2,1)S(1)}, bf16[64,2048]{1,0:T(8,128)(2,1)S(1)}, u32[]{:S(2)}, u32[]{:S(2)}) collective-permute-start(bf16[64,2048]{1,0:T(8,128)(2,1)S(1)} %collective-permute-done.22.refs_1_), channel_id=1, source_target_pairs={{4,0},{5,1},{8,4},{9,5},{12,8},{13,9},{14,12},{15,13},{10,14},{11,... | collective-permute-start | bytes 786440 | tf_op jit(solution)/shard_map/ppermute | solution.py:260
  54.3 11.2 %collective-permute-start.24 = (bf16[64,2048]{1,0:T(8,128)(2,1)S(1)}, bf16[64,2048]{1,0:T(8,128)(2,1)S(1)}, u32[]{:S(2)}, u32[]{:S(2)}) collective-permute-start(bf16[64,2048]{1,0:T(8,128)(2,1)S(1)} %collective-permute-done.18.refs_0_), channel_id=1, source_target_pairs={{0,4},{1,5},{4,8},{5,9},{8,12},{9,13},{12,14},{13,15},{14,10},{15,... | collective-permute-start | bytes 786440 | tf_op jit(solution)/shard_map/ppermute | solution.py:260
  54.8 10.8 %collective-permute-start.25 = (bf16[64,2048]{1,0:T(8,128)(2,1)S(1)}, bf16[64,2048]{1,0:T(8,128)(2,1)S(1)}, u32[]{:S(2)}, u32[]{:S(2)}) collective-permute-start(bf16[64,2048]{1,0:T(8,128)(2,1)S(1)} %collective-permute-done.20.refs_1_), channel_id=1, source_target_pairs={{4,0},{5,1},{8,4},{9,5},{12,8},{13,9},{14,12},{15,13},{10,14},{11,... | collective-permute-start | bytes 786440 | tf_op jit(solution)/shard_map/ppermute | solution.py:260
  59.9 11.2 %collective-permute-start.29 = (bf16[64,2048]{1,0:T(8,128)(2,1)S(1)}, bf16[64,2048]{1,0:T(8,128)(2,1)S(1)}, u32[]{:S(2)}, u32[]{:S(2)}) collective-permute-start(bf16[64,2048]{1,0:T(8,128)(2,1)S(1)} %collective-permute-done.26.refs_0_), channel_id=1, source_target_pairs={{0,4},{1,5},{4,8},{5,9},{8,12},{9,13},{12,14},{13,15},{14,10},{15,... | collective-permute-start | bytes 786440 | tf_op jit(solution)/shard_map/ppermute | solution.py:260
  60.4 10.8 %collective-permute-start.30 = (bf16[64,2048]{1,0:T(8,128)(2,1)S(1)}, bf16[64,2048]{1,0:T(8,128)(2,1)S(1)}, u32[]{:S(2)}, u32[]{:S(2)}) collective-permute-start(bf16[64,2048]{1,0:T(8,128)(2,1)S(1)} %collective-permute-done.27.refs_1_), channel_id=1, source_target_pairs={{4,0},{5,1},{8,4},{9,5},{12,8},{13,9},{14,12},{15,13},{10,14},{11,... | collective-permute-start | bytes 786440 | tf_op jit(solution)/shard_map/ppermute | solution.py:260
  65.5 10.9 %collective-permute-start.28 = (bf16[64,2048]{1,0:T(8,128)(2,1)S(1)}, bf16[64,2048]{1,0:T(8,128)(2,1)S(1)}, u32[]{:S(2)}, u32[]{:S(2)}) collective-permute-start(bf16[64,2048]{1,0:T(8,128)(2,1)S(1)} %collective-permute-done.24.refs_0_), channel_id=1, source_target_pairs={{0,4},{1,5},{4,8},{5,9},{8,12},{9,13},{12,14},{13,15},{14,10},{15,... | collective-permute-start | bytes 786440 | tf_op jit(solution)/shard_map/ppermute | solution.py:260
  71.2 6.4 %collective-permute-start.31 = (bf16[64,2048]{1,0:T(8,128)(2,1)S(1)}, bf16[64,2048]{1,0:T(8,128)(2,1)S(1)}, u32[]{:S(2)}, u32[]{:S(2)}) collective-permute-start(bf16[64,2048]{1,0:T(8,128)(2,1)S(1)} %collective-permute-done.30.refs_1_), channel_id=1, source_target_pairs={{4,0},{5,1},{8,4},{9,5},{12,8},{13,9},{14,12},{15,13},{10,14},{11,... | collective-permute-start | bytes 786440 | tf_op jit(solution)/shard_map/ppermute | solution.py:260
  74.6 10.3 %collective-permute-start.41 = (bf16[64,2048]{1,0:T(8,128)(2,1)S(1)}, bf16[64,2048]{1,0:T(8,128)(2,1)S(1)}, u32[]{:S(2)}, u32[]{:S(2)}) collective-permute-start(bf16[64,2048]{1,0:T(8,128)(2,1)S(1)} %get-tuple-element.205), channel_id=1, source_target_pairs={{0,4},{1,5},{4,8},{5,9},{8,12},{9,13},{12,14},{13,15},{14,10},{15,... | collective-permute-start | bytes 786440 | tf_op jit(solution)/shard_map/ppermute | solution.py:260
  79.4 7.5 %collective-permute-start.32 = (bf16[64,2048]{1,0:T(8,128)(2,1)S(1)}, bf16[64,2048]{1,0:T(8,128)(2,1)S(1)}, u32[]{:S(2)}, u32[]{:S(2)}) collective-permute-start(bf16[64,2048]{1,0:T(8,128)(2,1)S(1)} %get-tuple-element.207), channel_id=1, source_target_pairs={{0,4},{1,5},{4,8},{5,9},{8,12},{9,13},{12,14},{13,15},{14,10},{15,... | collective-permute-start | bytes 786440 | tf_op jit(solution)/shard_map/ppermute | solution.py:260
  79.9 8.1 %collective-permute-start.36 = (bf16[64,2048]{1,0:T(8,128)(2,1)S(1)}, bf16[64,2048]{1,0:T(8,128)(2,1)S(1)}, u32[]{:S(2)}, u32[]{:S(2)}) collective-permute-start(bf16[64,2048]{1,0:T(8,128)(2,1)S(1)} %get-tuple-element.214), channel_id=1, source_target_pairs={{4,0},{5,1},{8,4},{9,5},{12,8},{13,9},{14,12},{15,13},{10,14},{11,... | collective-permute-start | bytes 786440 | tf_op jit(solution)/shard_map/ppermute | solution.py:260
  81.5 10.4 %collective-permute-start.37 = (bf16[64,2048]{1,0:T(8,128)(2,1)S(1)}, bf16[64,2048]{1,0:T(8,128)(2,1)S(1)}, u32[]{:S(2)}, u32[]{:S(2)}) collective-permute-start(bf16[64,2048]{1,0:T(8,128)(2,1)S(1)} %get-tuple-element.208), channel_id=1, source_target_pairs={{4,0},{5,1},{8,4},{9,5},{12,8},{13,9},{14,12},{15,13},{10,14},{11,... | collective-permute-start | bytes 786440 | tf_op jit(solution)/shard_map/ppermute | solution.py:260
  87.0 9.1 %collective-permute-start.42 = (bf16[64,2048]{1,0:T(8,128)(2,1)S(1)}, bf16[64,2048]{1,0:T(8,128)(2,1)S(1)}, u32[]{:S(2)}, u32[]{:S(2)}) collective-permute-start(bf16[64,2048]{1,0:T(8,128)(2,1)S(1)} %add_convert_fusion.4), channel_id=1, source_target_pairs={{0,4},{1,5},{4,8},{5,9},{8,12},{9,13},{12,14},{13,15},{14,10},{15,... | collective-permute-start | bytes 786440 | tf_op jit(solution)/shard_map/ppermute | solution.py:260
  87.6 11.3 %collective-permute-start.33 = (bf16[64,2048]{1,0:T(8,128)(2,1)S(1)}, bf16[64,2048]{1,0:T(8,128)(2,1)S(1)}, u32[]{:S(2)}, u32[]{:S(2)}) collective-permute-start(bf16[64,2048]{1,0:T(8,128)(2,1)S(1)} %add_convert_fusion.11), channel_id=1, source_target_pairs={{0,4},{1,5},{4,8},{5,9},{8,12},{9,13},{12,14},{13,15},{14,10},{15,... | collective-permute-start | bytes 786440 | tf_op jit(solution)/shard_map/ppermute | solution.py:260
  91.9 8.2 %collective-permute-start.38 = (bf16[64,2048]{1,0:T(8,128)(2,1)S(1)}, bf16[64,2048]{1,0:T(8,128)(2,1)S(1)}, u32[]{:S(2)}, u32[]{:S(2)}) collective-permute-start(bf16[64,2048]{1,0:T(8,128)(2,1)S(1)} %add_convert_fusion.8), channel_id=1, source_target_pairs={{4,0},{5,1},{8,4},{9,5},{12,8},{13,9},{14,12},{15,13},{10,14},{11,... | collective-permute-start | bytes 786440 | tf_op jit(solution)/shard_map/ppermute | solution.py:260
  93.6 10.3 %collective-permute-start.39 = (bf16[64,2048]{1,0:T(8,128)(2,1)S(1)}, bf16[64,2048]{1,0:T(8,128)(2,1)S(1)}, u32[]{:S(2)}, u32[]{:S(2)}) collective-permute-start(bf16[64,2048]{1,0:T(8,128)(2,1)S(1)} %add_convert_fusion.7), channel_id=1, source_target_pairs={{4,0},{5,1},{8,4},{9,5},{12,8},{13,9},{14,12},{15,13},{10,14},{11,... | collective-permute-start | bytes 786440 | tf_op jit(solution)/shard_map/ppermute | solution.py:260
  98.9 18.9 %collective-permute-start.43 = (bf16[64,2048]{1,0:T(8,128)(2,1)S(1)}, bf16[64,2048]{1,0:T(8,128)(2,1)S(1)}, u32[]{:S(2)}, u32[]{:S(2)}) collective-permute-start(bf16[64,2048]{1,0:T(8,128)(2,1)S(1)} %add_convert_fusion.3), channel_id=1, source_target_pairs={{0,4},{1,5},{4,8},{5,9},{8,12},{9,13},{12,14},{13,15},{14,10},{15,... | collective-permute-start | bytes 786440 | tf_op jit(solution)/shard_map/ppermute | solution.py:260
  99.6 11.0 %collective-permute-start.34 = (bf16[64,2048]{1,0:T(8,128)(2,1)S(1)}, bf16[64,2048]{1,0:T(8,128)(2,1)S(1)}, u32[]{:S(2)}, u32[]{:S(2)}) collective-permute-start(bf16[64,2048]{1,0:T(8,128)(2,1)S(1)} %add_convert_fusion.10), channel_id=1, source_target_pairs={{0,4},{1,5},{4,8},{5,9},{8,12},{9,13},{12,14},{13,15},{14,10},{15,... | collective-permute-start | bytes 786440 | tf_op jit(solution)/shard_map/ppermute | solution.py:260
  104.0 13.7 %collective-permute-start.40 = (bf16[64,2048]{1,0:T(8,128)(2,1)S(1)}, bf16[64,2048]{1,0:T(8,128)(2,1)S(1)}, u32[]{:S(2)}, u32[]{:S(2)}) collective-permute-start(bf16[64,2048]{1,0:T(8,128)(2,1)S(1)} %add_convert_fusion.6), channel_id=1, source_target_pairs={{4,0},{5,1},{8,4},{9,5},{12,8},{13,9},{14,12},{15,13},{10,14},{11,... | collective-permute-start | bytes 786440 | tf_op jit(solution)/shard_map/ppermute | solution.py:260
  105.7 10.3 %collective-permute-start.44 = (bf16[64,2048]{1,0:T(8,128)(2,1)S(1)}, bf16[64,2048]{1,0:T(8,128)(2,1)S(1)}, u32[]{:S(2)}, u32[]{:S(2)}) collective-permute-start(bf16[64,2048]{1,0:T(8,128)(2,1)S(1)} %add_convert_fusion.2), channel_id=1, source_target_pairs={{4,0},{5,1},{8,4},{9,5},{12,8},{13,9},{14,12},{15,13},{10,14},{11,... | collective-permute-start | bytes 786440 | tf_op jit(solution)/shard_map/ppermute | solution.py:260
  110.7 7.0 %collective-permute-start.35 = (bf16[64,2048]{1,0:T(8,128)(2,1)S(1)}, bf16[64,2048]{1,0:T(8,128)(2,1)S(1)}, u32[]{:S(2)}, u32[]{:S(2)}) collective-permute-start(bf16[64,2048]{1,0:T(8,128)(2,1)S(1)} %add_convert_fusion.9), channel_id=1, source_target_pairs={{0,4},{1,5},{4,8},{5,9},{8,12},{9,13},{12,14},{13,15},{14,10},{15,... | collective-permute-start | bytes 786440 | tf_op jit(solution)/shard_map/ppermute | solution.py:260
  116.1 6.4 %collective-permute-start.45 = (bf16[64,2048]{1,0:T(8,128)(2,1)S(1)}, bf16[64,2048]{1,0:T(8,128)(2,1)S(1)}, u32[]{:S(2)}, u32[]{:S(2)}) collective-permute-start(bf16[64,2048]{1,0:T(8,128)(2,1)S(1)} %add_convert_fusion.1), channel_id=1, source_target_pairs={{4,0},{5,1},{8,4},{9,5},{12,8},{13,9},{14,12},{15,13},{10,14},{11,... | collective-permute-start | bytes 786440 | tf_op jit(solution)/shard_map/ppermute | solution.py:260
  (4 other events, 48.4 us)

commit v6 on v5

--- a/solution.py
+++ b/solution.py
@@ -326,7 +326,9 @@
     )
     sums_on[0] = send(far_upper, onward)
     sums_back[1] = send(far_lower, back)
-    own_out, unused = experts_on([(upper, 0, 0), (lower, 0, 1)], [message], (far_upper, far_lower))
+    own_out, unused = experts_on(
+        [(upper, 0, 0), (lower, 0, 1)], [message], (far_upper, far_lower, sums_on[1], sums_back[0])
+    )
     for hop in range(far - 1, 0, -1):
         onto, backto = sums_on[0], sums_back[1]
         if hop < far - 1:
@@ -336,9 +338,8 @@
             sums_back[0] = send(add_parts(sums_back[0], out_left[hop, 0]), back)
         if hop == 1:
             onto, backto = later(onto, own_out), later(backto, own_out)
-        earlier = (onto, backto)
-        sums_on[0] = send(add_parts(onto, out_right[hop, 0]), onward)
-        sums_back[1] = send(add_parts(backto, out_left[hop, 1]), back)
+        earlier = (add_parts(onto, out_right[hop, 0]), add_parts(backto, out_left[hop, 1]))
+        sums_on[0], sums_back[1] = send(earlier[0], onward), send(earlier[1], back)
     hidden_state = (hidden_upper, hidden_lower)
     return jnp.concatenate(
         [

time: 124 us -> 120 us (0.968)
  waiting for transfers between devices: 57 us -> 53.4 us
    ppermute x46, waiting for transfers between devices: 57 us -> 53.4 us  [send(): return lax.ppermute(array, 'ctx', pairs)]
where the time goes in v6:
time: 120 us
  waiting for transfers between devices  53.4 us (44%)
  starting transfers between devices  38.6 us (32%)
  Pallas kernels  23.6 us (20%)
  other arithmetic  2.9 us (2%)
    ppermute x46, waiting for transfers between devices, send(): return lax.ppermute(array, 'ctx', pairs)  53.4 us
    ppermute x46, starting transfers between devices, send(): return lax.ppermute(array, 'ctx', pairs)  38.6 us
    pallas_call x8, Pallas kernels, run_experts(): pl.pallas_call(functools.partial(expert_kernel, [piece[1:] for piece in p...  14.7 us
    pallas_call x2, Pallas kernels, attend(): pl.pallas_call(functools.partial(attend_kernel, count, half), out_shape=(...  7.3 us
  transfers between devices with their start and end apart: 46, of which 26 were waited for; matrix products, arithmetic and copies ran while one was open for 2% of the time, Pallas kernels for 18%

profile of v6, /device:TPU:0, one launch (start us, length us, event | category | flops | bytes accessed | tf_op | source)
XLA Modules:
  0.0 119.6 jit_solution(9980265762835765106)
XLA Ops:
  0.8 1.6 %pack_message.1.refs_3_.refs_2_ = bf16[144,512]{1,0:T(8,128)(2,1)} custom-call(s32[1]{0:T(128)S(6)} %copy.12.pos_ref, bf16[128,256]{1,0:T(8,128)(2,1)} %key_ref.1, bf16[128,256]{1,0:T(8,128)(2,1)} %value_ref.1, s32[8,128]{1,0:T(8,128)} %bitcast.2, f32[8,128]{1,0:T(8,128)} %bitcast.3), custom_call_target="tpu_custom_call" | custom-call | tf_op jit(solution)/shard_map/pack_message/pallas_call | solution.py:54
  2.4 3.0 %collective-permute-start.2 = (bf16[144,512]{1,0:T(8,128)(2,1)}, bf16[144,512]{1,0:T(8,128)(2,1)S(1)}, u32[]{:S(2)}, u32[]{:S(2)}) collective-permute-start(bf16[144,512]{1,0:T(8,128)(2,1)} %pack_message.1.refs_3_.refs_2_), channel_id=1, source_target_pairs={{4,0},{5,1},{8,4},{9,5},{12,8},{13,9},{14,12},{15,13},{10,14},{11,... | collective-permute-start | bytes 442376 | tf_op jit(solution)/shard_map/ppermute | solution.py:260
  5.4 4.1 %collective-permute-done.2.refs_8_.refs_3_ = bf16[144,512]{1,0:T(8,128)(2,1)S(1)} collective-permute-done((bf16[144,512]{1,0:T(8,128)(2,1)}, bf16[144,512]{1,0:T(8,128)(2,1)S(1)}, u32[]{:S(2)}, u32[]{:S(2)}) %collective-permute-start.2) | collective-permute-done | bytes 147488 | tf_op jit(solution)/shard_map/ppermute | solution.py:260
  9.5 1.3 %collective-permute-done.refs_4_.refs_2_ = bf16[144,512]{1,0:T(8,128)(2,1)S(1)} collective-permute-done((bf16[144,512]{1,0:T(8,128)(2,1)}, bf16[144,512]{1,0:T(8,128)(2,1)S(1)}, u32[]{:S(2)}, u32[]{:S(2)}) %collective-permute-start) | collective-permute-done | bytes 147488 | tf_op jit(solution)/shard_map/ppermute | solution.py:260
  12.4 1.7 %collective-permute-start.5 = (bf16[144,512]{1,0:T(8,128)(2,1)S(1)}, bf16[144,512]{1,0:T(8,128)(2,1)S(1)}, u32[]{:S(2)}, u32[]{:S(2)}) collective-permute-start(bf16[144,512]{1,0:T(8,128)(2,1)S(1)} %collective-permute-done.2.refs_8_.refs_3_), channel_id=1, source_target_pairs={{4,0},{5,1},{8,4},{9,5},{12,8},{13,9},{14,12},{15,13},{10,14},{11,... | collective-permute-start | bytes 442376 | tf_op jit(solution)/shard_map/ppermute | solution.py:260
  14.1 1.9 %collective-permute-done.1.refs_5_.refs_2_ = bf16[144,512]{1,0:T(8,128)(2,1)S(1)} collective-permute-done((bf16[144,512]{1,0:T(8,128)(2,1)S(1)}, bf16[144,512]{1,0:T(8,128)(2,1)S(1)}, u32[]{:S(2)}, u32[]{:S(2)}) %collective-permute-start.1) | collective-permute-done | bytes 147488 | tf_op jit(solution)/shard_map/ppermute | solution.py:260
  17.6 1.7 %collective-permute-start.6 = (bf16[144,512]{1,0:T(8,128)(2,1)S(1)}, bf16[144,512]{1,0:T(8,128)(2,1)S(1)}, u32[]{:S(2)}, u32[]{:S(2)}) collective-permute-start(bf16[144,512]{1,0:T(8,128)(2,1)S(1)} %collective-permute-done.5.refs_9_.refs_3_), channel_id=1, source_target_pairs={{4,0},{5,1},{8,4},{9,5},{12,8},{13,9},{14,12},{15,13},{10,14},{11,... | collective-permute-start | bytes 442376 | tf_op jit(solution)/shard_map/ppermute | solution.py:260
  19.3 1.9 %collective-permute-done.3.refs_6_.refs_2_ = bf16[144,512]{1,0:T(8,128)(2,1)S(1)} collective-permute-done((bf16[144,512]{1,0:T(8,128)(2,1)S(1)}, bf16[144,512]{1,0:T(8,128)(2,1)S(1)}, u32[]{:S(2)}, u32[]{:S(2)}) %collective-permute-start.3) | collective-permute-done | bytes 147488 | tf_op jit(solution)/shard_map/ppermute | solution.py:260
  23.2 3.1 %collective-permute-done.4.refs_7_.refs_2_ = bf16[144,512]{1,0:T(8,128)(2,1)S(1)} collective-permute-done((bf16[144,512]{1,0:T(8,128)(2,1)S(1)}, bf16[144,512]{1,0:T(8,128)(2,1)S(1)}, u32[]{:S(2)}, u32[]{:S(2)}) %collective-permute-start.4) | collective-permute-done | bytes 147488 | tf_op jit(solution)/shard_map/ppermute | solution.py:260
  26.4 1.3 %collective-permute-done.11.refs_15_ = bf16[144,512]{1,0:T(8,128)(2,1)S(1)} collective-permute-done((bf16[144,512]{1,0:T(8,128)(2,1)S(1)}, bf16[144,512]{1,0:T(8,128)(2,1)S(1)}, u32[]{:S(2)}, u32[]{:S(2)}) %collective-permute-start.11) | collective-permute-done | bytes 147488 | tf_op jit(solution)/shard_map/ppermute | solution.py:260
  28.4 3.6 %attend.2 = (f32[64,2048]{1,0:T(8,128)S(1)}, bf16[64,2048]{1,0:T(8,128)(2,1)S(1)}) custom-call(bf16[128,2048]{1,0:T(8,128)(2,1)S(1)} %broadcast_multiply_fusion.refs_0_, f32[128,2048]{1,0:T(8,128)S(1)} %convert_element_type.117.refs_1_, f32[8,2048]{1,0:T(8,128)S(1)} %broadcast_in_dim.2.refs_2_, bf16[144,512]{1,0:T(8,128)(2,1)S(1)} %copy-done.3, ...), custom_call_target="tpu_custom_call" | custom-call | flops 2147483648 | bytes 4194304 | tf_op jit(solution)/shard_map/attend/pallas_call | solution.py:152
  32.1 1.6 %collective-permute-start.19 = (bf16[64,2048]{1,0:T(8,128)(2,1)S(1)}, bf16[64,2048]{1,0:T(8,128)(2,1)S(1)}, u32[]{:S(2)}, u32[]{:S(2)}) collective-permute-start(bf16[64,2048]{1,0:T(8,128)(2,1)S(1)} %get-tuple-element.138.refs_0_), channel_id=1, source_target_pairs={{4,0},{5,1},{8,4},{9,5},{12,8},{13,9},{14,12},{15,13},{10,14},{11,... | collective-permute-start | bytes 786440 | tf_op jit(solution)/shard_map/ppermute | solution.py:260
  34.1 3.6 %attend.3 = (f32[64,2048]{1,0:T(8,128)S(1)}, bf16[64,2048]{1,0:T(8,128)(2,1)S(1)}) custom-call(bf16[128,2048]{1,0:T(8,128)(2,1)S(1)} %broadcast_multiply_fusion.refs_0_, f32[128,2048]{1,0:T(8,128)S(1)} %convert_element_type.117.refs_1_, f32[8,2048]{1,0:T(8,128)S(1)} %broadcast_in_dim.2.refs_2_, bf16[144,512]{1,0:T(8,128)(2,1)S(1)} %copy-done.3, ...), custom_call_target="tpu_custom_call" | custom-call | flops 2147483648 | bytes 4194304 | tf_op jit(solution)/shard_map/attend/pallas_call | solution.py:152
  37.8 1.6 %collective-permute-start.22 = (bf16[64,2048]{1,0:T(8,128)(2,1)S(1)}, bf16[64,2048]{1,0:T(8,128)(2,1)S(1)}, u32[]{:S(2)}, u32[]{:S(2)}) collective-permute-start(bf16[64,2048]{1,0:T(8,128)(2,1)S(1)} %get-tuple-element.158.refs_1_), channel_id=1, source_target_pairs={{4,0},{5,1},{8,4},{9,5},{12,8},{13,9},{14,12},{15,13},{10,14},{11,... | collective-permute-start | bytes 786440 | tf_op jit(solution)/shard_map/ppermute | solution.py:260
  41.0 1.6 %collective-permute-start.20 = (bf16[64,2048]{1,0:T(8,128)(2,1)S(1)}, bf16[64,2048]{1,0:T(8,128)(2,1)S(1)}, u32[]{:S(2)}, u32[]{:S(2)}) collective-permute-start(bf16[64,2048]{1,0:T(8,128)(2,1)S(1)} %collective-permute-done.19.refs_1_), channel_id=1, source_target_pairs={{4,0},{5,1},{8,4},{9,5},{12,8},{13,9},{14,12},{15,13},{10,14},{11,... | collective-permute-start | bytes 786440 | tf_op jit(solution)/shard_map/ppermute | solution.py:260
  43.1 1.8 %experts.8 = (bf16[64,2048]{1,0:T(8,128)(2,1)S(1)}, bf16[64,2048]{1,0:T(8,128)(2,1)S(1)}) custom-call(bf16[64,2048]{1,0:T(8,128)(2,1)S(1)} %collective-permute-done.17.refs_0_, bf16[64,2048]{1,0:T(8,128)(2,1)S(1)} %collective-permute-done.19.refs_1_, bf16[144,512]{1,0:T(8,128)(2,1)S(1)} %collective-permute-done.refs_4_.refs_2_, ...), custom_call_target="tpu_custom_call" | custom-call | flops 1207959552 | bytes 9437184 | tf_op jit(solution)/shard_map/experts/pallas_call | solution.py:220
  44.9 2.2 %collective-permute-done.22.refs_1_ = bf16[64,2048]{1,0:T(8,128)(2,1)S(1)} collective-permute-done((bf16[64,2048]{1,0:T(8,128)(2,1)S(1)}, bf16[64,2048]{1,0:T(8,128)(2,1)S(1)}, u32[]{:S(2)}, u32[]{:S(2)}) %collective-permute-start.22) | collective-permute-done | bytes 262176 | tf_op jit(solution)/shard_map/ppermute | solution.py:260
  47.1 1.6 %collective-permute-done.21.refs_0_ = bf16[64,2048]{1,0:T(8,128)(2,1)S(1)} collective-permute-done((bf16[64,2048]{1,0:T(8,128)(2,1)S(1)}, bf16[64,2048]{1,0:T(8,128)(2,1)S(1)}, u32[]{:S(2)}, u32[]{:S(2)}) %collective-permute-start.21) | collective-permute-done | bytes 262176 | tf_op jit(solution)/shard_map/ppermute | solution.py:260
  49.1 1.6 %collective-permute-start.27 = (bf16[64,2048]{1,0:T(8,128)(2,1)S(1)}, bf16[64,2048]{1,0:T(8,128)(2,1)S(1)}, u32[]{:S(2)}, u32[]{:S(2)}) collective-permute-start(bf16[64,2048]{1,0:T(8,128)(2,1)S(1)} %collective-permute-done.22.refs_1_), channel_id=1, source_target_pairs={{4,0},{5,1},{8,4},{9,5},{12,8},{13,9},{14,12},{15,13},{10,14},{11,... | collective-permute-start | bytes 786440 | tf_op jit(solution)/shard_map/ppermute | solution.py:260
  50.7 1.8 %experts.9 = (bf16[64,2048]{1,0:T(8,128)(2,1)S(1)}, bf16[64,2048]{1,0:T(8,128)(2,1)S(1)}) custom-call(bf16[64,2048]{1,0:T(8,128)(2,1)S(1)} %collective-permute-done.21.refs_0_, bf16[64,2048]{1,0:T(8,128)(2,1)S(1)} %collective-permute-done.22.refs_1_, bf16[144,512]{1,0:T(8,128)(2,1)S(1)} %collective-permute-done.refs_4_.refs_2_, ...), custom_call_target="tpu_custom_call" | custom-call | flops 1207959552 | bytes 9437184 | tf_op jit(solution)/shard_map/experts/pallas_call | solution.py:220
  52.7 1.6 %collective-permute-done.18.refs_0_ = bf16[64,2048]{1,0:T(8,128)(2,1)S(1)} collective-permute-done((bf16[64,2048]{1,0:T(8,128)(2,1)S(1)}, bf16[64,2048]{1,0:T(8,128)(2,1)S(1)}, u32[]{:S(2)}, u32[]{:S(2)}) %collective-permute-start.18) | collective-permute-done | bytes 262176 | tf_op jit(solution)/shard_map/ppermute | solution.py:260
  54.8 1.6 %collective-permute-start.25 = (bf16[64,2048]{1,0:T(8,128)(2,1)S(1)}, bf16[64,2048]{1,0:T(8,128)(2,1)S(1)}, u32[]{:S(2)}, u32[]{:S(2)}) collective-permute-start(bf16[64,2048]{1,0:T(8,128)(2,1)S(1)} %collective-permute-done.20.refs_1_), channel_id=1, source_target_pairs={{4,0},{5,1},{8,4},{9,5},{12,8},{13,9},{14,12},{15,13},{10,14},{11,... | collective-permute-start | bytes 786440 | tf_op jit(solution)/shard_map/ppermute | solution.py:260
  56.3 1.8 %experts.10 = (bf16[64,2048]{1,0:T(8,128)(2,1)S(1)}, bf16[64,2048]{1,0:T(8,128)(2,1)S(1)}) custom-call(bf16[64,2048]{1,0:T(8,128)(2,1)S(1)} %collective-permute-done.18.refs_0_, bf16[64,2048]{1,0:T(8,128)(2,1)S(1)} %collective-permute-done.20.refs_1_, bf16[144,512]{1,0:T(8,128)(2,1)S(1)} %collective-permute-done.1.refs_5_.refs_2_, ...), custom_call_target="tpu_custom_call" | custom-call | flops 1207959552 | bytes 9437184 | tf_op jit(solution)/shard_map/experts/pallas_call | solution.py:220
  58.2 1.7 %collective-permute-done.26.refs_0_ = bf16[64,2048]{1,0:T(8,128)(2,1)S(1)} collective-permute-done((bf16[64,2048]{1,0:T(8,128)(2,1)S(1)}, bf16[64,2048]{1,0:T(8,128)(2,1)S(1)}, u32[]{:S(2)}, u32[]{:S(2)}) %collective-permute-start.26) | collective-permute-done | bytes 262176 | tf_op jit(solution)/shard_map/ppermute | solution.py:260
  60.4 1.6 %collective-permute-start.30 = (bf16[64,2048]{1,0:T(8,128)(2,1)S(1)}, bf16[64,2048]{1,0:T(8,128)(2,1)S(1)}, u32[]{:S(2)}, u32[]{:S(2)}) collective-permute-start(bf16[64,2048]{1,0:T(8,128)(2,1)S(1)} %collective-permute-done.27.refs_1_), channel_id=1, source_target_pairs={{4,0},{5,1},{8,4},{9,5},{12,8},{13,9},{14,12},{15,13},{10,14},{11,... | collective-permute-start | bytes 786440 | tf_op jit(solution)/shard_map/ppermute | solution.py:260
  62.0 1.8 %experts.11 = (bf16[64,2048]{1,0:T(8,128)(2,1)S(1)}, bf16[64,2048]{1,0:T(8,128)(2,1)S(1)}) custom-call(bf16[64,2048]{1,0:T(8,128)(2,1)S(1)} %collective-permute-done.26.refs_0_, bf16[64,2048]{1,0:T(8,128)(2,1)S(1)} %collective-permute-done.27.refs_1_, bf16[144,512]{1,0:T(8,128)(2,1)S(1)} %collective-permute-done.1.refs_5_.refs_2_, ...), custom_call_target="tpu_custom_call" | custom-call | flops 1207959552 | bytes 9437184 | tf_op jit(solution)/shard_map/experts/pallas_call | solution.py:220
  63.8 1.7 %collective-permute-done.24.refs_0_ = bf16[64,2048]{1,0:T(8,128)(2,1)S(1)} collective-permute-done((bf16[64,2048]{1,0:T(8,128)(2,1)S(1)}, bf16[64,2048]{1,0:T(8,128)(2,1)S(1)}, u32[]{:S(2)}, u32[]{:S(2)}) %collective-permute-start.24) | collective-permute-done | bytes 262176 | tf_op jit(solution)/shard_map/ppermute | solution.py:260
  66.0 1.8 %experts.12 = (bf16[64,2048]{1,0:T(8,128)(2,1)S(1)}, bf16[64,2048]{1,0:T(8,128)(2,1)S(1)}) custom-call(bf16[64,2048]{1,0:T(8,128)(2,1)S(1)} %collective-permute-done.24.refs_0_, bf16[64,2048]{1,0:T(8,128)(2,1)S(1)} %collective-permute-done.25.refs_1_, bf16[144,512]{1,0:T(8,128)(2,1)S(1)} %collective-permute-done.3.refs_6_.refs_2_, ...), custom_call_target="tpu_custom_call" | custom-call | flops 1207959552 | bytes 9437184 | tf_op jit(solution)/shard_map/experts/pallas_call | solution.py:220
  67.8 3.3 %collective-permute-done.29.refs_0_ = bf16[64,2048]{1,0:T(8,128)(2,1)S(1)} collective-permute-done((bf16[64,2048]{1,0:T(8,128)(2,1)S(1)}, bf16[64,2048]{1,0:T(8,128)(2,1)S(1)}, u32[]{:S(2)}, u32[]{:S(2)}) %collective-permute-start.29) | collective-permute-done | bytes 262176 | tf_op jit(solution)/shard_map/ppermute | solution.py:260
  71.2 1.6 %collective-permute-start.31 = (bf16[64,2048]{1,0:T(8,128)(2,1)S(1)}, bf16[64,2048]{1,0:T(8,128)(2,1)S(1)}, u32[]{:S(2)}, u32[]{:S(2)}) collective-permute-start(bf16[64,2048]{1,0:T(8,128)(2,1)S(1)} %collective-permute-done.30.refs_1_), channel_id=1, source_target_pairs={{4,0},{5,1},{8,4},{9,5},{12,8},{13,9},{14,12},{15,13},{10,14},{11,... | collective-permute-start | bytes 786440 | tf_op jit(solution)/shard_map/ppermute | solution.py:260
  72.7 1.8 %experts.13 = (bf16[64,2048]{1,0:T(8,128)(2,1)S(1)}, bf16[64,2048]{1,0:T(8,128)(2,1)S(1)}) custom-call(bf16[64,2048]{1,0:T(8,128)(2,1)S(1)} %collective-permute-done.29.refs_0_, bf16[64,2048]{1,0:T(8,128)(2,1)S(1)} %collective-permute-done.30.refs_1_, bf16[144,512]{1,0:T(8,128)(2,1)S(1)} %collective-permute-done.3.refs_6_.refs_2_, ...), custom_call_target="tpu_custom_call" | custom-call | flops 1207959552 | bytes 9437184 | tf_op jit(solution)/shard_map/experts/pallas_call | solution.py:220
  75.1 1.6 %collective-permute-start.33 = (bf16[64,2048]{1,0:T(8,128)(2,1)S(1)}, bf16[64,2048]{1,0:T(8,128)(2,1)S(1)}, u32[]{:S(2)}, u32[]{:S(2)}) collective-permute-start(bf16[64,2048]{1,0:T(8,128)(2,1)S(1)} %get-tuple-element.209), channel_id=1, source_target_pairs={{4,0},{5,1},{8,4},{9,5},{12,8},{13,9},{14,12},{15,13},{10,14},{11,... | collective-permute-start | bytes 786440 | tf_op jit(solution)/shard_map/ppermute | solution.py:260
  76.7 3.4 %collective-permute-done.31.refs_1_ = bf16[64,2048]{1,0:T(8,128)(2,1)S(1)} collective-permute-done((bf16[64,2048]{1,0:T(8,128)(2,1)S(1)}, bf16[64,2048]{1,0:T(8,128)(2,1)S(1)}, u32[]{:S(2)}, u32[]{:S(2)}) %collective-permute-start.31) | collective-permute-done | bytes 262176 | tf_op jit(solution)/shard_map/ppermute | solution.py:260
  80.0 1.8 %experts.14 = (bf16[64,2048]{1,0:T(8,128)(2,1)S(1)}, bf16[64,2048]{1,0:T(8,128)(2,1)S(1)}) custom-call(bf16[64,2048]{1,0:T(8,128)(2,1)S(1)} %collective-permute-done.28.refs_0_, bf16[64,2048]{1,0:T(8,128)(2,1)S(1)} %collective-permute-done.31.refs_1_, bf16[144,512]{1,0:T(8,128)(2,1)S(1)} %collective-permute-done.4.refs_7_.refs_2_, ...), custom_call_target="tpu_custom_call" | custom-call | flops 1207959552 | bytes 9437184 | tf_op jit(solution)/shard_map/experts/pallas_call | solution.py:220
  82.6 1.6 %collective-permute-start.38 = (bf16[64,2048]{1,0:T(8,128)(2,1)S(1)}, bf16[64,2048]{1,0:T(8,128)(2,1)S(1)}, u32[]{:S(2)}, u32[]{:S(2)}) collective-permute-start(bf16[64,2048]{1,0:T(8,128)(2,1)S(1)} %get-tuple-element.208), channel_id=1, source_target_pairs={{4,0},{5,1},{8,4},{9,5},{12,8},{13,9},{14,12},{15,13},{10,14},{11,... | collective-permute-start | bytes 786440 | tf_op jit(solution)/shard_map/ppermute | solution.py:260
  84.2 1.5 %collective-permute-done.33 = bf16[64,2048]{1,0:T(8,128)(2,1)S(1)} collective-permute-done((bf16[64,2048]{1,0:T(8,128)(2,1)S(1)}, bf16[64,2048]{1,0:T(8,128)(2,1)S(1)}, u32[]{:S(2)}, u32[]{:S(2)}) %collective-permute-start.33) | collective-permute-done | bytes 262176 | tf_op jit(solution)/shard_map/ppermute | solution.py:260
  85.7 1.8 %experts.15 = (bf16[64,2048]{1,0:T(8,128)(2,1)S(1)}, bf16[64,2048]{1,0:T(8,128)(2,1)S(1)}) custom-call(bf16[64,2048]{1,0:T(8,128)(2,1)S(1)} %get-tuple-element.138.refs_0_, bf16[64,2048]{1,0:T(8,128)(2,1)S(1)} %get-tuple-element.158.refs_1_, bf16[144,512]{1,0:T(8,128)(2,1)S(1)} %copy-done.3, bf16[1,2048,384]{2,1,0:T(8,128)(2,1)S(1)} %copy-done, ...), custom_call_target="tpu_custom_call" | custom-call | flops 1207959552 | bytes 9437184 | tf_op jit(solution)/shard_map/experts/pallas_call | solution.py:220
  87.5 2.6 %collective-permute-done.34 = bf16[64,2048]{1,0:T(8,128)(2,1)S(1)} collective-permute-done((bf16[64,2048]{1,0:T(8,128)(2,1)S(1)}, bf16[64,2048]{1,0:T(8,128)(2,1)S(1)}, u32[]{:S(2)}, u32[]{:S(2)}) %collective-permute-start.34) | collective-permute-done | bytes 262176 | tf_op jit(solution)/shard_map/ppermute | solution.py:260
  90.9 2.1 %collective-permute-start.40 = (bf16[64,2048]{1,0:T(8,128)(2,1)S(1)}, bf16[64,2048]{1,0:T(8,128)(2,1)S(1)}, u32[]{:S(2)}, u32[]{:S(2)}) collective-permute-start(bf16[64,2048]{1,0:T(8,128)(2,1)S(1)} %add_convert_fusion.8), channel_id=1, source_target_pairs={{4,0},{5,1},{8,4},{9,5},{12,8},{13,9},{14,12},{15,13},{10,14},{11,... | collective-permute-start | bytes 786440 | tf_op jit(solution)/shard_map/ppermute | solution.py:260
  93.0 1.6 %collective-permute-start.39 = (bf16[64,2048]{1,0:T(8,128)(2,1)S(1)}, bf16[64,2048]{1,0:T(8,128)(2,1)S(1)}, u32[]{:S(2)}, u32[]{:S(2)}) collective-permute-start(bf16[64,2048]{1,0:T(8,128)(2,1)S(1)} %add_convert_fusion.7), channel_id=1, source_target_pairs={{4,0},{5,1},{8,4},{9,5},{12,8},{13,9},{14,12},{15,13},{10,14},{11,... | collective-permute-start | bytes 786440 | tf_op jit(solution)/shard_map/ppermute | solution.py:260
  94.6 4.8 %collective-permute-done.35 = bf16[64,2048]{1,0:T(8,128)(2,1)S(1)} collective-permute-done((bf16[64,2048]{1,0:T(8,128)(2,1)S(1)}, bf16[64,2048]{1,0:T(8,128)(2,1)S(1)}, u32[]{:S(2)}, u32[]{:S(2)}) %collective-permute-start.35) | collective-permute-done | bytes 262176 | tf_op jit(solution)/shard_map/ppermute | solution.py:260
  100.0 5.0 %collective-permute-done.42 = bf16[64,2048]{1,0:T(8,128)(2,1)S(1)} collective-permute-done((bf16[64,2048]{1,0:T(8,128)(2,1)S(1)}, bf16[64,2048]{1,0:T(8,128)(2,1)S(1)}, u32[]{:S(2)}, u32[]{:S(2)}) %collective-permute-start.42) | collective-permute-done | bytes 262176 | tf_op jit(solution)/shard_map/ppermute | solution.py:260
  105.7 1.6 %collective-permute-start.44 = (bf16[64,2048]{1,0:T(8,128)(2,1)S(1)}, bf16[64,2048]{1,0:T(8,128)(2,1)S(1)}, u32[]{:S(2)}, u32[]{:S(2)}) collective-permute-start(bf16[64,2048]{1,0:T(8,128)(2,1)S(1)} %add_convert_fusion.6), channel_id=1, source_target_pairs={{4,0},{5,1},{8,4},{9,5},{12,8},{13,9},{14,12},{15,13},{10,14},{11,... | collective-permute-start | bytes 786440 | tf_op jit(solution)/shard_map/ppermute | solution.py:260
  107.4 1.6 %collective-permute-start.41 = (bf16[64,2048]{1,0:T(8,128)(2,1)S(1)}, bf16[64,2048]{1,0:T(8,128)(2,1)S(1)}, u32[]{:S(2)}, u32[]{:S(2)}) collective-permute-start(bf16[64,2048]{1,0:T(8,128)(2,1)S(1)} %add_convert_fusion.5), channel_id=1, source_target_pairs={{4,0},{5,1},{8,4},{9,5},{12,8},{13,9},{14,12},{15,13},{10,14},{11,... | collective-permute-start | bytes 786440 | tf_op jit(solution)/shard_map/ppermute | solution.py:260
  109.0 1.6 %collective-permute-done.36 = bf16[64,2048]{1,0:T(8,128)(2,1)S(1)} collective-permute-done((bf16[64,2048]{1,0:T(8,128)(2,1)S(1)}, bf16[64,2048]{1,0:T(8,128)(2,1)S(1)}, u32[]{:S(2)}, u32[]{:S(2)}) %collective-permute-start.36) | collective-permute-done | bytes 262176 | tf_op jit(solution)/shard_map/ppermute | solution.py:260
  112.2 1.6 %collective-permute-start.45 = (bf16[64,2048]{1,0:T(8,128)(2,1)S(1)}, bf16[64,2048]{1,0:T(8,128)(2,1)S(1)}, u32[]{:S(2)}, u32[]{:S(2)}) collective-permute-start(bf16[64,2048]{1,0:T(8,128)(2,1)S(1)} %add_convert_fusion.1), channel_id=1, source_target_pairs={{4,0},{5,1},{8,4},{9,5},{12,8},{13,9},{14,12},{15,13},{10,14},{11,... | collective-permute-start | bytes 786440 | tf_op jit(solution)/shard_map/ppermute | solution.py:260
  114.9 2.2 %collective-permute-done.37 = bf16[64,2048]{1,0:T(8,128)(2,1)S(1)} collective-permute-done((bf16[64,2048]{1,0:T(8,128)(2,1)S(1)}, bf16[64,2048]{1,0:T(8,128)(2,1)S(1)}, u32[]{:S(2)}, u32[]{:S(2)}) %collective-permute-start.37) | collective-permute-done | bytes 262176 | tf_op jit(solution)/shard_map/ppermute | solution.py:260
  117.3 1.3 %collective-permute-done.45 = bf16[64,2048]{1,0:T(8,128)(2,1)S(1)} collective-permute-done((bf16[64,2048]{1,0:T(8,128)(2,1)S(1)}, bf16[64,2048]{1,0:T(8,128)(2,1)S(1)}, u32[]{:S(2)}, u32[]{:S(2)}) %collective-permute-start.45) | collective-permute-done | bytes 262176 | tf_op jit(solution)/shard_map/ppermute | solution.py:260
  (83 shorter events, 17.3 us)
Async XLA Ops:
  0.0 16.0 %copy-start.5 = (f32[2048]{0:T(1024)S(1)}, f32[2048]{0:T(1024)}, u32[]{:S(2)}) copy-start(f32[2048]{0:T(1024)} %param.16) | copy-start | bytes 24580
  0.0 27.7 %copy-start = (bf16[1,2048,384]{2,1,0:T(8,128)(2,1)S(1)}, bf16[1,2048,384]{2,1,0:T(8,128)(2,1)}, u32[]{:S(2)}) copy-start(bf16[1,2048,384]{2,1,0:T(8,128)(2,1)} %refs_3_.3) | copy-start | bytes 4718596
  2.4 7.2 %collective-permute-start.2 = (bf16[144,512]{1,0:T(8,128)(2,1)}, bf16[144,512]{1,0:T(8,128)(2,1)S(1)}, u32[]{:S(2)}, u32[]{:S(2)}) collective-permute-start(bf16[144,512]{1,0:T(8,128)(2,1)} %pack_message.1.refs_3_.refs_2_), channel_id=1, source_target_pairs={{4,0},{5,1},{8,4},{9,5},{12,8},{13,9},{14,12},{15,13},{10,14},{11,... | collective-permute-start | bytes 442376 | tf_op jit(solution)/shard_map/ppermute | solution.py:260
  5.3 5.5 %collective-permute-start = (bf16[144,512]{1,0:T(8,128)(2,1)}, bf16[144,512]{1,0:T(8,128)(2,1)S(1)}, u32[]{:S(2)}, u32[]{:S(2)}) collective-permute-start(bf16[144,512]{1,0:T(8,128)(2,1)} %pack_message.1.refs_3_.refs_2_), channel_id=1, source_target_pairs={{0,4},{1,5},{4,8},{5,9},{8,12},{9,13},{12,14},{13,15},{14,10},{15,... | collective-permute-start | bytes 442376 | tf_op jit(solution)/shard_map/ppermute | solution.py:260
  10.8 5.1 %collective-permute-start.1 = (bf16[144,512]{1,0:T(8,128)(2,1)S(1)}, bf16[144,512]{1,0:T(8,128)(2,1)S(1)}, u32[]{:S(2)}, u32[]{:S(2)}) collective-permute-start(bf16[144,512]{1,0:T(8,128)(2,1)S(1)} %collective-permute-done.refs_4_.refs_2_), channel_id=1, source_target_pairs={{0,4},{1,5},{4,8},{5,9},{8,12},{9,13},{12,14},{13,15},{14,10},{15,... | collective-permute-start | bytes 442376 | tf_op jit(solution)/shard_map/ppermute | solution.py:260
  12.4 5.2 %collective-permute-start.5 = (bf16[144,512]{1,0:T(8,128)(2,1)S(1)}, bf16[144,512]{1,0:T(8,128)(2,1)S(1)}, u32[]{:S(2)}, u32[]{:S(2)}) collective-permute-start(bf16[144,512]{1,0:T(8,128)(2,1)S(1)} %collective-permute-done.2.refs_8_.refs_3_), channel_id=1, source_target_pairs={{4,0},{5,1},{8,4},{9,5},{12,8},{13,9},{14,12},{15,13},{10,14},{11,... | collective-permute-start | bytes 442376 | tf_op jit(solution)/shard_map/ppermute | solution.py:260
  16.0 5.2 %collective-permute-start.3 = (bf16[144,512]{1,0:T(8,128)(2,1)S(1)}, bf16[144,512]{1,0:T(8,128)(2,1)S(1)}, u32[]{:S(2)}, u32[]{:S(2)}) collective-permute-start(bf16[144,512]{1,0:T(8,128)(2,1)S(1)} %collective-permute-done.1.refs_5_.refs_2_), channel_id=1, source_target_pairs={{0,4},{1,5},{4,8},{5,9},{8,12},{9,13},{12,14},{13,15},{14,10},{15,... | collective-permute-start | bytes 442376 | tf_op jit(solution)/shard_map/ppermute | solution.py:260
  16.4 5.1 %collective-permute-start.7 = (bf16[144,512]{1,0:T(8,128)(2,1)S(1)}, bf16[144,512]{1,0:T(8,128)(2,1)S(1)}, u32[]{:S(2)}, u32[]{:S(2)}) collective-permute-start(bf16[144,512]{1,0:T(8,128)(2,1)S(1)} %copy-done.3), channel_id=1, source_target_pairs={{0,1},{1,0},{2,3},{3,2},{4,5},{5,4},{6,7},{7,6},{8,9},{9,8},{10,11... | collective-permute-start | bytes 442376 | tf_op jit(solution)/shard_map/ppermute | solution.py:260
  16.4 5.1 %collective-permute-start.12 = (bf16[144,512]{1,0:T(8,128)(2,1)S(1)}, bf16[144,512]{1,0:T(8,128)(2,1)S(1)}, u32[]{:S(2)}, u32[]{:S(2)}) collective-permute-start(bf16[144,512]{1,0:T(8,128)(2,1)S(1)} %collective-permute-done.2.refs_8_.refs_3_), channel_id=1, source_target_pairs={{0,1},{1,0},{2,3},{3,2},{4,5},{5,4},{6,7},{7,6},{8,9},{9,8},{10,11... | collective-permute-start | bytes 442376 | tf_op jit(solution)/shard_map/ppermute | solution.py:260
  16.9 5.2 %collective-permute-start.8 = (bf16[144,512]{1,0:T(8,128)(2,1)S(1)}, bf16[144,512]{1,0:T(8,128)(2,1)S(1)}, u32[]{:S(2)}, u32[]{:S(2)}) collective-permute-start(bf16[144,512]{1,0:T(8,128)(2,1)S(1)} %collective-permute-done.refs_4_.refs_2_), channel_id=1, source_target_pairs={{0,1},{1,0},{2,3},{3,2},{4,5},{5,4},{6,7},{7,6},{8,9},{9,8},{10,11... | collective-permute-start | bytes 442376 | tf_op jit(solution)/shard_map/ppermute | solution.py:260
  17.6 5.6 %collective-permute-start.6 = (bf16[144,512]{1,0:T(8,128)(2,1)S(1)}, bf16[144,512]{1,0:T(8,128)(2,1)S(1)}, u32[]{:S(2)}, u32[]{:S(2)}) collective-permute-start(bf16[144,512]{1,0:T(8,128)(2,1)S(1)} %collective-permute-done.5.refs_9_.refs_3_), channel_id=1, source_target_pairs={{4,0},{5,1},{8,4},{9,5},{12,8},{13,9},{14,12},{15,13},{10,14},{11,... | collective-permute-start | bytes 442376 | tf_op jit(solution)/shard_map/ppermute | solution.py:260
  21.2 5.1 %collective-permute-start.4 = (bf16[144,512]{1,0:T(8,128)(2,1)S(1)}, bf16[144,512]{1,0:T(8,128)(2,1)S(1)}, u32[]{:S(2)}, u32[]{:S(2)}) collective-permute-start(bf16[144,512]{1,0:T(8,128)(2,1)S(1)} %collective-permute-done.3.refs_6_.refs_2_), channel_id=1, source_target_pairs={{0,4},{1,5},{4,8},{5,9},{8,12},{9,13},{12,14},{13,15},{14,10},{15,... | collective-permute-start | bytes 442376 | tf_op jit(solution)/shard_map/ppermute | solution.py:260
  21.6 4.8 %collective-permute-start.9 = (bf16[144,512]{1,0:T(8,128)(2,1)S(1)}, bf16[144,512]{1,0:T(8,128)(2,1)S(1)}, u32[]{:S(2)}, u32[]{:S(2)}) collective-permute-start(bf16[144,512]{1,0:T(8,128)(2,1)S(1)} %collective-permute-done.1.refs_5_.refs_2_), channel_id=1, source_target_pairs={{0,1},{1,0},{2,3},{3,2},{4,5},{5,4},{6,7},{7,6},{8,9},{9,8},{10,11... | collective-permute-start | bytes 442376 | tf_op jit(solution)/shard_map/ppermute | solution.py:260
  21.6 4.8 %collective-permute-start.13 = (bf16[144,512]{1,0:T(8,128)(2,1)S(1)}, bf16[144,512]{1,0:T(8,128)(2,1)S(1)}, u32[]{:S(2)}, u32[]{:S(2)}) collective-permute-start(bf16[144,512]{1,0:T(8,128)(2,1)S(1)} %collective-permute-done.5.refs_9_.refs_3_), channel_id=1, source_target_pairs={{0,1},{1,0},{2,3},{3,2},{4,5},{5,4},{6,7},{7,6},{8,9},{9,8},{10,11... | collective-permute-start | bytes 442376 | tf_op jit(solution)/shard_map/ppermute | solution.py:260
  22.1 4.3 %collective-permute-start.10 = (bf16[144,512]{1,0:T(8,128)(2,1)S(1)}, bf16[144,512]{1,0:T(8,128)(2,1)S(1)}, u32[]{:S(2)}, u32[]{:S(2)}) collective-permute-start(bf16[144,512]{1,0:T(8,128)(2,1)S(1)} %collective-permute-done.3.refs_6_.refs_2_), channel_id=1, source_target_pairs={{0,1},{1,0},{2,3},{3,2},{4,5},{5,4},{6,7},{7,6},{8,9},{9,8},{10,11... | collective-permute-start | bytes 442376 | tf_op jit(solution)/shard_map/ppermute | solution.py:260
  23.2 3.2 %collective-permute-start.14 = (bf16[144,512]{1,0:T(8,128)(2,1)S(1)}, bf16[144,512]{1,0:T(8,128)(2,1)S(1)}, u32[]{:S(2)}, u32[]{:S(2)}) collective-permute-start(bf16[144,512]{1,0:T(8,128)(2,1)S(1)} %collective-permute-done.6.refs_10_.refs_3_), channel_id=1, source_target_pairs={{0,1},{1,0},{2,3},{3,2},{4,5},{5,4},{6,7},{7,6},{8,9},{9,8},{10,11... | collective-permute-start | bytes 442376 | tf_op jit(solution)/shard_map/ppermute | solution.py:260
  26.3 1.4 %collective-permute-start.11 = (bf16[144,512]{1,0:T(8,128)(2,1)S(1)}, bf16[144,512]{1,0:T(8,128)(2,1)S(1)}, u32[]{:S(2)}, u32[]{:S(2)}) collective-permute-start(bf16[144,512]{1,0:T(8,128)(2,1)S(1)} %collective-permute-done.4.refs_7_.refs_2_), channel_id=1, source_target_pairs={{0,1},{1,0},{2,3},{3,2},{4,5},{5,4},{6,7},{7,6},{8,9},{9,8},{10,11... | collective-permute-start | bytes 442376 | tf_op jit(solution)/shard_map/ppermute | solution.py:260
  27.7 10.1 %collective-permute-start.15 = (bf16[1,2048,384]{2,1,0:T(8,128)(2,1)S(1)}, bf16[1,2048,384]{2,1,0:T(8,128)(2,1)S(1)}, u32[]{:S(2)}, u32[]{:S(2)}) collective-permute-start(bf16[1,2048,384]{2,1,0:T(8,128)(2,1)S(1)} %copy-done), channel_id=1, source_target_pairs={{0,1},{1,0},{2,3},{3,2},{4,5},{5,4},{6,7},{7,6},{8,9},{9,8},{10,11... | collective-permute-start | bytes 4718600 | tf_op jit(solution)/shard_map/ppermute | solution.py:260
  27.9 10.0 %collective-permute-start.16 = (bf16[1,2048,384]{2,1,0:T(8,128)(2,1)}, bf16[1,2048,384]{2,1,0:T(8,128)(2,1)S(1)}, u32[]{:S(2)}, u32[]{:S(2)}) collective-permute-start(bf16[1,2048,384]{2,1,0:T(8,128)(2,1)} %refs_4_.15), channel_id=1, source_target_pairs={{0,1},{1,0},{2,3},{3,2},{4,5},{5,4},{6,7},{7,6},{8,9},{9,8},{10,11... | collective-permute-start | bytes 4718600 | tf_op jit(solution)/shard_map/ppermute | solution.py:260
  28.2 14.8 %collective-permute-start.23 = (bf16[1,384,2048]{2,1,0:T(8,128)(2,1)}, bf16[1,384,2048]{2,1,0:T(8,128)(2,1)S(1)}, u32[]{:S(2)}, u32[]{:S(2)}) collective-permute-start(bf16[1,384,2048]{2,1,0:T(8,128)(2,1)} %refs_5_.15), channel_id=1, source_target_pairs={{0,1},{1,0},{2,3},{3,2},{4,5},{5,4},{6,7},{7,6},{8,9},{9,8},{10,11... | collective-permute-start | bytes 4718600 | tf_op jit(solution)/shard_map/ppermute | solution.py:260
  32.1 9.0 %collective-permute-start.19 = (bf16[64,2048]{1,0:T(8,128)(2,1)S(1)}, bf16[64,2048]{1,0:T(8,128)(2,1)S(1)}, u32[]{:S(2)}, u32[]{:S(2)}) collective-permute-start(bf16[64,2048]{1,0:T(8,128)(2,1)S(1)} %get-tuple-element.138.refs_0_), channel_id=1, source_target_pairs={{4,0},{5,1},{8,4},{9,5},{12,8},{13,9},{14,12},{15,13},{10,14},{11,... | collective-permute-start | bytes 786440 | tf_op jit(solution)/shard_map/ppermute | solution.py:260
  33.7 8.9 %collective-permute-start.17 = (bf16[64,2048]{1,0:T(8,128)(2,1)S(1)}, bf16[64,2048]{1,0:T(8,128)(2,1)S(1)}, u32[]{:S(2)}, u32[]{:S(2)}) collective-permute-start(bf16[64,2048]{1,0:T(8,128)(2,1)S(1)} %get-tuple-element.138.refs_0_), channel_id=1, source_target_pairs={{0,4},{1,5},{4,8},{5,9},{8,12},{9,13},{12,14},{13,15},{14,10},{15,... | collective-permute-start | bytes 786440 | tf_op jit(solution)/shard_map/ppermute | solution.py:260
  37.8 9.3 %collective-permute-start.22 = (bf16[64,2048]{1,0:T(8,128)(2,1)S(1)}, bf16[64,2048]{1,0:T(8,128)(2,1)S(1)}, u32[]{:S(2)}, u32[]{:S(2)}) collective-permute-start(bf16[64,2048]{1,0:T(8,128)(2,1)S(1)} %get-tuple-element.158.refs_1_), channel_id=1, source_target_pairs={{4,0},{5,1},{8,4},{9,5},{12,8},{13,9},{14,12},{15,13},{10,14},{11,... | collective-permute-start | bytes 786440 | tf_op jit(solution)/shard_map/ppermute | solution.py:260
  39.5 9.2 %collective-permute-start.21 = (bf16[64,2048]{1,0:T(8,128)(2,1)S(1)}, bf16[64,2048]{1,0:T(8,128)(2,1)S(1)}, u32[]{:S(2)}, u32[]{:S(2)}) collective-permute-start(bf16[64,2048]{1,0:T(8,128)(2,1)S(1)} %get-tuple-element.158.refs_1_), channel_id=1, source_target_pairs={{0,4},{1,5},{4,8},{5,9},{8,12},{9,13},{12,14},{13,15},{14,10},{15,... | collective-permute-start | bytes 786440 | tf_op jit(solution)/shard_map/ppermute | solution.py:260
  41.0 11.7 %collective-permute-start.20 = (bf16[64,2048]{1,0:T(8,128)(2,1)S(1)}, bf16[64,2048]{1,0:T(8,128)(2,1)S(1)}, u32[]{:S(2)}, u32[]{:S(2)}) collective-permute-start(bf16[64,2048]{1,0:T(8,128)(2,1)S(1)} %collective-permute-done.19.refs_1_), channel_id=1, source_target_pairs={{4,0},{5,1},{8,4},{9,5},{12,8},{13,9},{14,12},{15,13},{10,14},{11,... | collective-permute-start | bytes 786440 | tf_op jit(solution)/shard_map/ppermute | solution.py:260
  42.6 11.7 %collective-permute-start.18 = (bf16[64,2048]{1,0:T(8,128)(2,1)S(1)}, bf16[64,2048]{1,0:T(8,128)(2,1)S(1)}, u32[]{:S(2)}, u32[]{:S(2)}) collective-permute-start(bf16[64,2048]{1,0:T(8,128)(2,1)S(1)} %collective-permute-done.17.refs_0_), channel_id=1, source_target_pairs={{0,4},{1,5},{4,8},{5,9},{8,12},{9,13},{12,14},{13,15},{14,10},{15,... | collective-permute-start | bytes 786440 | tf_op jit(solution)/shard_map/ppermute | solution.py:260
  48.7 11.2 %collective-permute-start.26 = (bf16[64,2048]{1,0:T(8,128)(2,1)S(1)}, bf16[64,2048]{1,0:T(8,128)(2,1)S(1)}, u32[]{:S(2)}, u32[]{:S(2)}) collective-permute-start(bf16[64,2048]{1,0:T(8,128)(2,1)S(1)} %collective-permute-done.21.refs_0_), channel_id=1, source_target_pairs={{0,4},{1,5},{4,8},{5,9},{8,12},{9,13},{12,14},{13,15},{14,10},{15,... | collective-permute-start | bytes 786440 | tf_op jit(solution)/shard_map/ppermute | solution.py:260
  49.1 10.8 %collective-permute-start.27 = (bf16[64,2048]{1,0:T(8,128)(2,1)S(1)}, bf16[64,2048]{1,0:T(8,128)(2,1)S(1)}, u32[]{:S(2)}, u32[]{:S(2)}) collective-permute-start(bf16[64,2048]{1,0:T(8,128)(2,1)S(1)} %collective-permute-done.22.refs_1_), channel_id=1, source_target_pairs={{4,0},{5,1},{8,4},{9,5},{12,8},{13,9},{14,12},{15,13},{10,14},{11,... | collective-permute-start | bytes 786440 | tf_op jit(solution)/shard_map/ppermute | solution.py:260
  54.3 11.2 %collective-permute-start.24 = (bf16[64,2048]{1,0:T(8,128)(2,1)S(1)}, bf16[64,2048]{1,0:T(8,128)(2,1)S(1)}, u32[]{:S(2)}, u32[]{:S(2)}) collective-permute-start(bf16[64,2048]{1,0:T(8,128)(2,1)S(1)} %collective-permute-done.18.refs_0_), channel_id=1, source_target_pairs={{0,4},{1,5},{4,8},{5,9},{8,12},{9,13},{12,14},{13,15},{14,10},{15,... | collective-permute-start | bytes 786440 | tf_op jit(solution)/shard_map/ppermute | solution.py:260
  54.8 10.8 %collective-permute-start.25 = (bf16[64,2048]{1,0:T(8,128)(2,1)S(1)}, bf16[64,2048]{1,0:T(8,128)(2,1)S(1)}, u32[]{:S(2)}, u32[]{:S(2)}) collective-permute-start(bf16[64,2048]{1,0:T(8,128)(2,1)S(1)} %collective-permute-done.20.refs_1_), channel_id=1, source_target_pairs={{4,0},{5,1},{8,4},{9,5},{12,8},{13,9},{14,12},{15,13},{10,14},{11,... | collective-permute-start | bytes 786440 | tf_op jit(solution)/shard_map/ppermute | solution.py:260
  59.9 11.2 %collective-permute-start.29 = (bf16[64,2048]{1,0:T(8,128)(2,1)S(1)}, bf16[64,2048]{1,0:T(8,128)(2,1)S(1)}, u32[]{:S(2)}, u32[]{:S(2)}) collective-permute-start(bf16[64,2048]{1,0:T(8,128)(2,1)S(1)} %collective-permute-done.26.refs_0_), channel_id=1, source_target_pairs={{0,4},{1,5},{4,8},{5,9},{8,12},{9,13},{12,14},{13,15},{14,10},{15,... | collective-permute-start | bytes 786440 | tf_op jit(solution)/shard_map/ppermute | solution.py:260
  60.4 10.8 %collective-permute-start.30 = (bf16[64,2048]{1,0:T(8,128)(2,1)S(1)}, bf16[64,2048]{1,0:T(8,128)(2,1)S(1)}, u32[]{:S(2)}, u32[]{:S(2)}) collective-permute-start(bf16[64,2048]{1,0:T(8,128)(2,1)S(1)} %collective-permute-done.27.refs_1_), channel_id=1, source_target_pairs={{4,0},{5,1},{8,4},{9,5},{12,8},{13,9},{14,12},{15,13},{10,14},{11,... | collective-permute-start | bytes 786440 | tf_op jit(solution)/shard_map/ppermute | solution.py:260
  65.5 11.1 %collective-permute-start.28 = (bf16[64,2048]{1,0:T(8,128)(2,1)S(1)}, bf16[64,2048]{1,0:T(8,128)(2,1)S(1)}, u32[]{:S(2)}, u32[]{:S(2)}) collective-permute-start(bf16[64,2048]{1,0:T(8,128)(2,1)S(1)} %collective-permute-done.24.refs_0_), channel_id=1, source_target_pairs={{0,4},{1,5},{4,8},{5,9},{8,12},{9,13},{12,14},{13,15},{14,10},{15,... | collective-permute-start | bytes 786440 | tf_op jit(solution)/shard_map/ppermute | solution.py:260
  71.2 8.9 %collective-permute-start.31 = (bf16[64,2048]{1,0:T(8,128)(2,1)S(1)}, bf16[64,2048]{1,0:T(8,128)(2,1)S(1)}, u32[]{:S(2)}, u32[]{:S(2)}) collective-permute-start(bf16[64,2048]{1,0:T(8,128)(2,1)S(1)} %collective-permute-done.30.refs_1_), channel_id=1, source_target_pairs={{4,0},{5,1},{8,4},{9,5},{12,8},{13,9},{14,12},{15,13},{10,14},{11,... | collective-permute-start | bytes 786440 | tf_op jit(solution)/shard_map/ppermute | solution.py:260
  74.6 11.1 %collective-permute-start.32 = (bf16[64,2048]{1,0:T(8,128)(2,1)S(1)}, bf16[64,2048]{1,0:T(8,128)(2,1)S(1)}, u32[]{:S(2)}, u32[]{:S(2)}) collective-permute-start(bf16[64,2048]{1,0:T(8,128)(2,1)S(1)} %get-tuple-element.205), channel_id=1, source_target_pairs={{0,4},{1,5},{4,8},{5,9},{8,12},{9,13},{12,14},{13,15},{14,10},{15,... | collective-permute-start | bytes 786440 | tf_op jit(solution)/shard_map/ppermute | solution.py:260
  75.1 10.6 %collective-permute-start.33 = (bf16[64,2048]{1,0:T(8,128)(2,1)S(1)}, bf16[64,2048]{1,0:T(8,128)(2,1)S(1)}, u32[]{:S(2)}, u32[]{:S(2)}) collective-permute-start(bf16[64,2048]{1,0:T(8,128)(2,1)S(1)} %get-tuple-element.209), channel_id=1, source_target_pairs={{4,0},{5,1},{8,4},{9,5},{12,8},{13,9},{14,12},{15,13},{10,14},{11,... | collective-permute-start | bytes 786440 | tf_op jit(solution)/shard_map/ppermute | solution.py:260
  81.9 8.2 %collective-permute-start.34 = (bf16[64,2048]{1,0:T(8,128)(2,1)S(1)}, bf16[64,2048]{1,0:T(8,128)(2,1)S(1)}, u32[]{:S(2)}, u32[]{:S(2)}) collective-permute-start(bf16[64,2048]{1,0:T(8,128)(2,1)S(1)} %get-tuple-element.207), channel_id=1, source_target_pairs={{0,4},{1,5},{4,8},{5,9},{8,12},{9,13},{12,14},{13,15},{14,10},{15,... | collective-permute-start | bytes 786440 | tf_op jit(solution)/shard_map/ppermute | solution.py:260
  82.6 8.2 %collective-permute-start.38 = (bf16[64,2048]{1,0:T(8,128)(2,1)S(1)}, bf16[64,2048]{1,0:T(8,128)(2,1)S(1)}, u32[]{:S(2)}, u32[]{:S(2)}) collective-permute-start(bf16[64,2048]{1,0:T(8,128)(2,1)S(1)} %get-tuple-element.208), channel_id=1, source_target_pairs={{4,0},{5,1},{8,4},{9,5},{12,8},{13,9},{14,12},{15,13},{10,14},{11,... | collective-permute-start | bytes 786440 | tf_op jit(solution)/shard_map/ppermute | solution.py:260
  90.2 9.3 %collective-permute-start.35 = (bf16[64,2048]{1,0:T(8,128)(2,1)S(1)}, bf16[64,2048]{1,0:T(8,128)(2,1)S(1)}, u32[]{:S(2)}, u32[]{:S(2)}) collective-permute-start(bf16[64,2048]{1,0:T(8,128)(2,1)S(1)} %add_convert_fusion.11), channel_id=1, source_target_pairs={{0,4},{1,5},{4,8},{5,9},{8,12},{9,13},{12,14},{13,15},{14,10},{15,... | collective-permute-start | bytes 786440 | tf_op jit(solution)/shard_map/ppermute | solution.py:260
  90.7 14.3 %collective-permute-start.42 = (bf16[64,2048]{1,0:T(8,128)(2,1)S(1)}, bf16[64,2048]{1,0:T(8,128)(2,1)S(1)}, u32[]{:S(2)}, u32[]{:S(2)}) collective-permute-start(bf16[64,2048]{1,0:T(8,128)(2,1)S(1)} %add_convert_fusion.3), channel_id=1, source_target_pairs={{0,4},{1,5},{4,8},{5,9},{8,12},{9,13},{12,14},{13,15},{14,10},{15,... | collective-permute-start | bytes 786440 | tf_op jit(solution)/shard_map/ppermute | solution.py:260
  90.9 14.8 %collective-permute-start.40 = (bf16[64,2048]{1,0:T(8,128)(2,1)S(1)}, bf16[64,2048]{1,0:T(8,128)(2,1)S(1)}, u32[]{:S(2)}, u32[]{:S(2)}) collective-permute-start(bf16[64,2048]{1,0:T(8,128)(2,1)S(1)} %add_convert_fusion.8), channel_id=1, source_target_pairs={{4,0},{5,1},{8,4},{9,5},{12,8},{13,9},{14,12},{15,13},{10,14},{11,... | collective-permute-start | bytes 786440 | tf_op jit(solution)/shard_map/ppermute | solution.py:260
  93.0 14.4 %collective-permute-start.39 = (bf16[64,2048]{1,0:T(8,128)(2,1)S(1)}, bf16[64,2048]{1,0:T(8,128)(2,1)S(1)}, u32[]{:S(2)}, u32[]{:S(2)}) collective-permute-start(bf16[64,2048]{1,0:T(8,128)(2,1)S(1)} %add_convert_fusion.7), channel_id=1, source_target_pairs={{4,0},{5,1},{8,4},{9,5},{12,8},{13,9},{14,12},{15,13},{10,14},{11,... | collective-permute-start | bytes 786440 | tf_op jit(solution)/shard_map/ppermute | solution.py:260
  99.5 11.2 %collective-permute-start.36 = (bf16[64,2048]{1,0:T(8,128)(2,1)S(1)}, bf16[64,2048]{1,0:T(8,128)(2,1)S(1)}, u32[]{:S(2)}, u32[]{:S(2)}) collective-permute-start(bf16[64,2048]{1,0:T(8,128)(2,1)S(1)} %add_convert_fusion.10), channel_id=1, source_target_pairs={{0,4},{1,5},{4,8},{5,9},{8,12},{9,13},{12,14},{13,15},{14,10},{15,... | collective-permute-start | bytes 786440 | tf_op jit(solution)/shard_map/ppermute | solution.py:260
  105.1 12.2 %collective-permute-start.43 = (bf16[64,2048]{1,0:T(8,128)(2,1)S(1)}, bf16[64,2048]{1,0:T(8,128)(2,1)S(1)}, u32[]{:S(2)}, u32[]{:S(2)}) collective-permute-start(bf16[64,2048]{1,0:T(8,128)(2,1)S(1)} %add_convert_fusion.2), channel_id=1, source_target_pairs={{0,4},{1,5},{4,8},{5,9},{8,12},{9,13},{12,14},{13,15},{14,10},{15,... | collective-permute-start | bytes 786440 | tf_op jit(solution)/shard_map/ppermute | solution.py:260
  105.7 6.4 %collective-permute-start.44 = (bf16[64,2048]{1,0:T(8,128)(2,1)S(1)}, bf16[64,2048]{1,0:T(8,128)(2,1)S(1)}, u32[]{:S(2)}, u32[]{:S(2)}) collective-permute-start(bf16[64,2048]{1,0:T(8,128)(2,1)S(1)} %add_convert_fusion.6), channel_id=1, source_target_pairs={{4,0},{5,1},{8,4},{9,5},{12,8},{13,9},{14,12},{15,13},{10,14},{11,... | collective-permute-start | bytes 786440 | tf_op jit(solution)/shard_map/ppermute | solution.py:260
  107.4 7.5 %collective-permute-start.41 = (bf16[64,2048]{1,0:T(8,128)(2,1)S(1)}, bf16[64,2048]{1,0:T(8,128)(2,1)S(1)}, u32[]{:S(2)}, u32[]{:S(2)}) collective-permute-start(bf16[64,2048]{1,0:T(8,128)(2,1)S(1)} %add_convert_fusion.5), channel_id=1, source_target_pairs={{4,0},{5,1},{8,4},{9,5},{12,8},{13,9},{14,12},{15,13},{10,14},{11,... | collective-permute-start | bytes 786440 | tf_op jit(solution)/shard_map/ppermute | solution.py:260
  110.8 6.4 %collective-permute-start.37 = (bf16[64,2048]{1,0:T(8,128)(2,1)S(1)}, bf16[64,2048]{1,0:T(8,128)(2,1)S(1)}, u32[]{:S(2)}, u32[]{:S(2)}) collective-permute-start(bf16[64,2048]{1,0:T(8,128)(2,1)S(1)} %add_convert_fusion.9), channel_id=1, source_target_pairs={{0,4},{1,5},{4,8},{5,9},{8,12},{9,13},{12,14},{13,15},{14,10},{15,... | collective-permute-start | bytes 786440 | tf_op jit(solution)/shard_map/ppermute | solution.py:260
  112.2 6.4 %collective-permute-start.45 = (bf16[64,2048]{1,0:T(8,128)(2,1)S(1)}, bf16[64,2048]{1,0:T(8,128)(2,1)S(1)}, u32[]{:S(2)}, u32[]{:S(2)}) collective-permute-start(bf16[64,2048]{1,0:T(8,128)(2,1)S(1)} %add_convert_fusion.1), channel_id=1, source_target_pairs={{4,0},{5,1},{8,4},{9,5},{12,8},{13,9},{14,12},{15,13},{10,14},{11,... | collective-permute-start | bytes 786440 | tf_op jit(solution)/shard_map/ppermute | solution.py:260
  (4 other events, 48.4 us)

commit v7 on v6

--- a/solution.py
+++ b/solution.py
@@ -26,8 +26,13 @@
         for core in range(CORES)
     ]
     back = [(b, a) for a, b in onward]
+    across = [
+        (order[i] * CORES + core, order[(i + chips // 2) % chips] * CORES + core)
+        for i in range(chips)
+        for core in range(CORES)
+    ]
     swap = [(i, i ^ 1) for i in range(chips * CORES)]
-    return onward, back, swap
+    return onward, back, across, swap
 
 
 def pack_kernel(pos_ref, key_ref, value_ref, routes_ref, combine_ref, out_ref):
@@ -96,8 +101,8 @@
     step = min(512, span)
     pair = 4
     squares = jnp.zeros((some, HEAD_SIZE), jnp.float32)
-    for first in range(0, heads, pair):
-        a = first // group
+
+    def scores_of(first):
         stacked = jnp.concatenate(
             [
                 jnp.concatenate([query_ref[mine, h * HEAD_SIZE : (h + 1) * HEAD_SIZE], eye], axis=1)
@@ -105,15 +110,22 @@
             ],
             axis=0,
         )
-        scores = [
+        return [
             lax.dot_general(
                 stacked,
-                key_ext[a, at : at + step, :],
+                key_ext[first // group, at : at + step, :],
                 (((1,), (1,)), ((), ())),
                 preferred_element_type=jnp.float32,
             )
             for at in range(0, span, step)
         ]
+
+    ready = scores_of(0)
+    for first in range(0, heads, pair):
+        a = first // group
+        scores = ready
+        if first + pair < heads:
+            ready = scores_of(first + pair)
         best = functools.reduce(jnp.maximum, scores)
         best = jnp.max(best, axis=1, keepdims=True)
         total = None
@@ -254,7 +266,7 @@
 ):
     chips = lax.axis_size("ctx") // CORES
     far = chips // 2
-    onward, back, swap = ring_pairs(chips)
+    onward, back, across, swap = ring_pairs(chips)
 
     def send(array, pairs):
         return lax.ppermute(array, "ctx", pairs)
@@ -272,10 +284,14 @@
                 jnp.broadcast_to(inputs[2][None, :], (8, inputs[2].shape[0])),
             )
             left[2], staged = tie((left[2], staged))
-        left[hop] = send(left[hop - 1], onward)
         if hop < far:
+            left[hop] = send(left[hop - 1], onward)
             right[hop] = send(right[hop - 1], back)
+        if hop == 1:
+            left[far] = send(message, across)
     plane = [message] + [left[h] for h in range(1, far + 1)] + [right[h] for h in range(1, far)]
+    left[far], unused = tie((left[far], right[far - 1]))
+    plane[far] = left[far]
     everything = plane + [send(m, swap) for m in plane]
     everything, own_weights = tie((everything, (gate_weight, up_weight, down_weight)))
     twin_gate, twin_up, twin_down = [send(w, swap) for w in own_weights]

time: 120 us -> 120 us (level)
  starting transfers between devices: 38.6 us -> 42.6 us
  waiting for transfers between devices: 53.4 us -> 50.7 us
    ppermute x46, starting transfers between devices: 38.6 us -> 42.6 us  [send(): return lax.ppermute(array, 'ctx', pairs)]
    ppermute x46, waiting for transfers between devices: 53.4 us -> 50.7 us  [send(): return lax.ppermute(array, 'ctx', pairs)]
  transfers between devices with their start and end apart: 46 -> 46, of which waited for: 26 -> 25; matrix products, arithmetic and copies ran while one was open for 2% -> 2% of each run, Pallas kernels for 18% -> 18%
where the time goes in v7:
time: 120 us
  waiting for transfers between devices  50.7 us (42%)
  starting transfers between devices  42.6 us (36%)
  Pallas kernels  22.8 us (19%)
  other arithmetic  2.9 us (2%)
    ppermute x46, waiting for transfers between devices, send(): return lax.ppermute(array, 'ctx', pairs)  50.7 us
    ppermute x46, starting transfers between devices, send(): return lax.ppermute(array, 'ctx', pairs)  42.6 us
    pallas_call x8, Pallas kernels, run_experts(): pl.pallas_call(functools.partial(expert_kernel, [piece[1:] for piece in p...  14.7 us
    pallas_call x2, Pallas kernels, attend(): pl.pallas_call(functools.partial(attend_kernel, count, half), out_shape=(...  6.59 us
  transfers between devices with their start and end apart: 46, of which 25 were waited for; matrix products, arithmetic and copies ran while one was open for 2% of the time, Pallas kernels for 18%

profile of v7, /device:TPU:0, one launch (start us, length us, event | category | flops | bytes accessed | tf_op | source)
XLA Modules:
  0.0 120.2 jit_solution(15799956888298747571)
XLA Ops:
  0.8 1.6 %pack_message.1.refs_3_.refs_2_ = bf16[144,512]{1,0:T(8,128)(2,1)} custom-call(s32[1]{0:T(128)S(6)} %copy.12.pos_ref, bf16[128,256]{1,0:T(8,128)(2,1)} %key_ref.1, bf16[128,256]{1,0:T(8,128)(2,1)} %value_ref.1, s32[8,128]{1,0:T(8,128)} %bitcast.2, f32[8,128]{1,0:T(8,128)} %bitcast.3), custom_call_target="tpu_custom_call" | custom-call | tf_op jit(solution)/shard_map/pack_message/pallas_call | solution.py:59
  2.4 3.0 %collective-permute-start.2 = (bf16[144,512]{1,0:T(8,128)(2,1)}, bf16[144,512]{1,0:T(8,128)(2,1)S(1)}, u32[]{:S(2)}, u32[]{:S(2)}) collective-permute-start(bf16[144,512]{1,0:T(8,128)(2,1)} %pack_message.1.refs_3_.refs_2_), channel_id=1, source_target_pairs={{4,0},{5,1},{8,4},{9,5},{12,8},{13,9},{14,12},{15,13},{10,14},{11,... | collective-permute-start | bytes 442376 | tf_op jit(solution)/shard_map/ppermute | solution.py:272
  5.4 5.0 %collective-permute-start.4 = (bf16[144,512]{1,0:T(8,128)(2,1)}, bf16[144,512]{1,0:T(8,128)(2,1)S(1)}, u32[]{:S(2)}, u32[]{:S(2)}) collective-permute-start(bf16[144,512]{1,0:T(8,128)(2,1)} %pack_message.1.refs_3_.refs_2_), channel_id=1, source_target_pairs={{0,14},{1,15},{4,10},{5,11},{8,6},{9,7},{12,2},{13,3},{14,0},{15,1... | collective-permute-start | bytes 442376 | tf_op jit(solution)/shard_map/ppermute | solution.py:272
  10.8 1.6 %collective-permute-start.5 = (bf16[144,512]{1,0:T(8,128)(2,1)S(1)}, bf16[144,512]{1,0:T(8,128)(2,1)S(1)}, u32[]{:S(2)}, u32[]{:S(2)}) collective-permute-start(bf16[144,512]{1,0:T(8,128)(2,1)S(1)} %collective-permute-done.2.refs_8_.refs_3_), channel_id=1, source_target_pairs={{4,0},{5,1},{8,4},{9,5},{12,8},{13,9},{14,12},{15,13},{10,14},{11,... | collective-permute-start | bytes 442376 | tf_op jit(solution)/shard_map/ppermute | solution.py:272
  12.9 1.1 broadcast_multiply_fusion.refs_0_
  14.0 4.4 %collective-permute-done.5.refs_9_.refs_3_ = bf16[144,512]{1,0:T(8,128)(2,1)S(1)} collective-permute-done((bf16[144,512]{1,0:T(8,128)(2,1)S(1)}, bf16[144,512]{1,0:T(8,128)(2,1)S(1)}, u32[]{:S(2)}, u32[]{:S(2)}) %collective-permute-start.5) | collective-permute-done | bytes 147488 | tf_op jit(solution)/shard_map/ppermute | solution.py:272
  18.3 2.0 %collective-permute-start.6 = (bf16[144,512]{1,0:T(8,128)(2,1)S(1)}, bf16[144,512]{1,0:T(8,128)(2,1)S(1)}, u32[]{:S(2)}, u32[]{:S(2)}) collective-permute-start(bf16[144,512]{1,0:T(8,128)(2,1)S(1)} %collective-permute-done.5.refs_9_.refs_3_), channel_id=1, source_target_pairs={{4,0},{5,1},{8,4},{9,5},{12,8},{13,9},{14,12},{15,13},{10,14},{11,... | collective-permute-start | bytes 442376 | tf_op jit(solution)/shard_map/ppermute | solution.py:272
  21.9 3.0 %collective-permute-done.6.refs_10_.refs_3_ = bf16[144,512]{1,0:T(8,128)(2,1)S(1)} collective-permute-done((bf16[144,512]{1,0:T(8,128)(2,1)S(1)}, bf16[144,512]{1,0:T(8,128)(2,1)S(1)}, u32[]{:S(2)}, u32[]{:S(2)}) %collective-permute-start.6) | collective-permute-done | bytes 147488 | tf_op jit(solution)/shard_map/ppermute | solution.py:272
  25.9 1.7 %collective-permute-done.3.refs_6_.refs_2_ = bf16[144,512]{1,0:T(8,128)(2,1)S(1)} collective-permute-done((bf16[144,512]{1,0:T(8,128)(2,1)S(1)}, bf16[144,512]{1,0:T(8,128)(2,1)S(1)}, u32[]{:S(2)}, u32[]{:S(2)}) %collective-permute-start.3) | collective-permute-done | bytes 147488 | tf_op jit(solution)/shard_map/ppermute | solution.py:272
  27.6 1.3 %collective-permute-done.10.refs_14_ = bf16[144,512]{1,0:T(8,128)(2,1)S(1)} collective-permute-done((bf16[144,512]{1,0:T(8,128)(2,1)S(1)}, bf16[144,512]{1,0:T(8,128)(2,1)S(1)}, u32[]{:S(2)}, u32[]{:S(2)}) %collective-permute-start.10) | collective-permute-done | bytes 147488 | tf_op jit(solution)/shard_map/ppermute | solution.py:272
  29.6 3.3 %attend.2 = (f32[64,2048]{1,0:T(8,128)S(1)}, bf16[64,2048]{1,0:T(8,128)(2,1)S(1)}) custom-call(bf16[128,2048]{1,0:T(8,128)(2,1)S(1)} %broadcast_multiply_fusion.refs_0_, f32[128,2048]{1,0:T(8,128)S(1)} %convert_element_type.117.refs_1_, f32[8,2048]{1,0:T(8,128)S(1)} %broadcast_in_dim.2.refs_2_, bf16[144,512]{1,0:T(8,128)(2,1)S(1)} %copy-done.3, ...), custom_call_target="tpu_custom_call" | custom-call | flops 2147483648 | bytes 4194304 | tf_op jit(solution)/shard_map/attend/pallas_call | solution.py:164
  33.0 1.8 %collective-permute-start.19 = (bf16[64,2048]{1,0:T(8,128)(2,1)S(1)}, bf16[64,2048]{1,0:T(8,128)(2,1)S(1)}, u32[]{:S(2)}, u32[]{:S(2)}) collective-permute-start(bf16[64,2048]{1,0:T(8,128)(2,1)S(1)} %get-tuple-element.140.refs_0_), channel_id=1, source_target_pairs={{4,0},{5,1},{8,4},{9,5},{12,8},{13,9},{14,12},{15,13},{10,14},{11,... | collective-permute-start | bytes 786440 | tf_op jit(solution)/shard_map/ppermute | solution.py:272
  35.1 3.3 %attend.3 = (f32[64,2048]{1,0:T(8,128)S(1)}, bf16[64,2048]{1,0:T(8,128)(2,1)S(1)}) custom-call(bf16[128,2048]{1,0:T(8,128)(2,1)S(1)} %broadcast_multiply_fusion.refs_0_, f32[128,2048]{1,0:T(8,128)S(1)} %convert_element_type.117.refs_1_, f32[8,2048]{1,0:T(8,128)S(1)} %broadcast_in_dim.2.refs_2_, bf16[144,512]{1,0:T(8,128)(2,1)S(1)} %copy-done.3, ...), custom_call_target="tpu_custom_call" | custom-call | flops 2147483648 | bytes 4194304 | tf_op jit(solution)/shard_map/attend/pallas_call | solution.py:164
  38.4 1.8 %collective-permute-start.22 = (bf16[64,2048]{1,0:T(8,128)(2,1)S(1)}, bf16[64,2048]{1,0:T(8,128)(2,1)S(1)}, u32[]{:S(2)}, u32[]{:S(2)}) collective-permute-start(bf16[64,2048]{1,0:T(8,128)(2,1)S(1)} %get-tuple-element.160.refs_1_), channel_id=1, source_target_pairs={{4,0},{5,1},{8,4},{9,5},{12,8},{13,9},{14,12},{15,13},{10,14},{11,... | collective-permute-start | bytes 786440 | tf_op jit(solution)/shard_map/ppermute | solution.py:272
  40.5 1.7 %collective-permute-done.19.refs_1_ = bf16[64,2048]{1,0:T(8,128)(2,1)S(1)} collective-permute-done((bf16[64,2048]{1,0:T(8,128)(2,1)S(1)}, bf16[64,2048]{1,0:T(8,128)(2,1)S(1)}, u32[]{:S(2)}, u32[]{:S(2)}) %collective-permute-start.19) | collective-permute-done | bytes 262176 | tf_op jit(solution)/shard_map/ppermute | solution.py:272
  42.2 1.7 %collective-permute-start.20 = (bf16[64,2048]{1,0:T(8,128)(2,1)S(1)}, bf16[64,2048]{1,0:T(8,128)(2,1)S(1)}, u32[]{:S(2)}, u32[]{:S(2)}) collective-permute-start(bf16[64,2048]{1,0:T(8,128)(2,1)S(1)} %collective-permute-done.19.refs_1_), channel_id=1, source_target_pairs={{4,0},{5,1},{8,4},{9,5},{12,8},{13,9},{14,12},{15,13},{10,14},{11,... | collective-permute-start | bytes 786440 | tf_op jit(solution)/shard_map/ppermute | solution.py:272
  44.2 1.8 %experts.8 = (bf16[64,2048]{1,0:T(8,128)(2,1)S(1)}, bf16[64,2048]{1,0:T(8,128)(2,1)S(1)}) custom-call(bf16[64,2048]{1,0:T(8,128)(2,1)S(1)} %collective-permute-done.17.refs_0_, bf16[64,2048]{1,0:T(8,128)(2,1)S(1)} %collective-permute-done.19.refs_1_, bf16[144,512]{1,0:T(8,128)(2,1)S(1)} %collective-permute-done.refs_4_.refs_2_, ...), custom_call_target="tpu_custom_call" | custom-call | flops 1207959552 | bytes 9437184 | tf_op jit(solution)/shard_map/experts/pallas_call | solution.py:232
  46.0 1.7 %collective-permute-done.22.refs_1_ = bf16[64,2048]{1,0:T(8,128)(2,1)S(1)} collective-permute-done((bf16[64,2048]{1,0:T(8,128)(2,1)S(1)}, bf16[64,2048]{1,0:T(8,128)(2,1)S(1)}, u32[]{:S(2)}, u32[]{:S(2)}) %collective-permute-start.22) | collective-permute-done | bytes 262176 | tf_op jit(solution)/shard_map/ppermute | solution.py:272
  47.8 1.6 %collective-permute-done.21.refs_0_ = bf16[64,2048]{1,0:T(8,128)(2,1)S(1)} collective-permute-done((bf16[64,2048]{1,0:T(8,128)(2,1)S(1)}, bf16[64,2048]{1,0:T(8,128)(2,1)S(1)}, u32[]{:S(2)}, u32[]{:S(2)}) %collective-permute-start.21) | collective-permute-done | bytes 262176 | tf_op jit(solution)/shard_map/ppermute | solution.py:272
  49.7 1.7 %collective-permute-start.27 = (bf16[64,2048]{1,0:T(8,128)(2,1)S(1)}, bf16[64,2048]{1,0:T(8,128)(2,1)S(1)}, u32[]{:S(2)}, u32[]{:S(2)}) collective-permute-start(bf16[64,2048]{1,0:T(8,128)(2,1)S(1)} %collective-permute-done.22.refs_1_), channel_id=1, source_target_pairs={{4,0},{5,1},{8,4},{9,5},{12,8},{13,9},{14,12},{15,13},{10,14},{11,... | collective-permute-start | bytes 786440 | tf_op jit(solution)/shard_map/ppermute | solution.py:272
  51.4 1.8 %experts.9 = (bf16[64,2048]{1,0:T(8,128)(2,1)S(1)}, bf16[64,2048]{1,0:T(8,128)(2,1)S(1)}) custom-call(bf16[64,2048]{1,0:T(8,128)(2,1)S(1)} %collective-permute-done.21.refs_0_, bf16[64,2048]{1,0:T(8,128)(2,1)S(1)} %collective-permute-done.22.refs_1_, bf16[144,512]{1,0:T(8,128)(2,1)S(1)} %collective-permute-done.refs_4_.refs_2_, ...), custom_call_target="tpu_custom_call" | custom-call | flops 1207959552 | bytes 9437184 | tf_op jit(solution)/shard_map/experts/pallas_call | solution.py:232
  53.4 1.6 %collective-permute-done.18.refs_0_ = bf16[64,2048]{1,0:T(8,128)(2,1)S(1)} collective-permute-done((bf16[64,2048]{1,0:T(8,128)(2,1)S(1)}, bf16[64,2048]{1,0:T(8,128)(2,1)S(1)}, u32[]{:S(2)}, u32[]{:S(2)}) %collective-permute-start.18) | collective-permute-done | bytes 262176 | tf_op jit(solution)/shard_map/ppermute | solution.py:272
  55.3 1.7 %collective-permute-start.25 = (bf16[64,2048]{1,0:T(8,128)(2,1)S(1)}, bf16[64,2048]{1,0:T(8,128)(2,1)S(1)}, u32[]{:S(2)}, u32[]{:S(2)}) collective-permute-start(bf16[64,2048]{1,0:T(8,128)(2,1)S(1)} %collective-permute-done.20.refs_1_), channel_id=1, source_target_pairs={{4,0},{5,1},{8,4},{9,5},{12,8},{13,9},{14,12},{15,13},{10,14},{11,... | collective-permute-start | bytes 786440 | tf_op jit(solution)/shard_map/ppermute | solution.py:272
  57.0 1.8 %experts.10 = (bf16[64,2048]{1,0:T(8,128)(2,1)S(1)}, bf16[64,2048]{1,0:T(8,128)(2,1)S(1)}) custom-call(bf16[64,2048]{1,0:T(8,128)(2,1)S(1)} %collective-permute-done.18.refs_0_, bf16[64,2048]{1,0:T(8,128)(2,1)S(1)} %collective-permute-done.20.refs_1_, bf16[144,512]{1,0:T(8,128)(2,1)S(1)} %collective-permute-done.1.refs_5_.refs_2_, ...), custom_call_target="tpu_custom_call" | custom-call | flops 1207959552 | bytes 9437184 | tf_op jit(solution)/shard_map/experts/pallas_call | solution.py:232
  58.9 1.7 %collective-permute-done.26.refs_0_ = bf16[64,2048]{1,0:T(8,128)(2,1)S(1)} collective-permute-done((bf16[64,2048]{1,0:T(8,128)(2,1)S(1)}, bf16[64,2048]{1,0:T(8,128)(2,1)S(1)}, u32[]{:S(2)}, u32[]{:S(2)}) %collective-permute-start.26) | collective-permute-done | bytes 262176 | tf_op jit(solution)/shard_map/ppermute | solution.py:272
  60.9 1.7 %collective-permute-start.30 = (bf16[64,2048]{1,0:T(8,128)(2,1)S(1)}, bf16[64,2048]{1,0:T(8,128)(2,1)S(1)}, u32[]{:S(2)}, u32[]{:S(2)}) collective-permute-start(bf16[64,2048]{1,0:T(8,128)(2,1)S(1)} %collective-permute-done.27.refs_1_), channel_id=1, source_target_pairs={{4,0},{5,1},{8,4},{9,5},{12,8},{13,9},{14,12},{15,13},{10,14},{11,... | collective-permute-start | bytes 786440 | tf_op jit(solution)/shard_map/ppermute | solution.py:272
  62.6 1.8 %experts.11 = (bf16[64,2048]{1,0:T(8,128)(2,1)S(1)}, bf16[64,2048]{1,0:T(8,128)(2,1)S(1)}) custom-call(bf16[64,2048]{1,0:T(8,128)(2,1)S(1)} %collective-permute-done.26.refs_0_, bf16[64,2048]{1,0:T(8,128)(2,1)S(1)} %collective-permute-done.27.refs_1_, bf16[144,512]{1,0:T(8,128)(2,1)S(1)} %collective-permute-done.1.refs_5_.refs_2_, ...), custom_call_target="tpu_custom_call" | custom-call | flops 1207959552 | bytes 9437184 | tf_op jit(solution)/shard_map/experts/pallas_call | solution.py:232
  64.5 1.7 %collective-permute-done.24.refs_0_ = bf16[64,2048]{1,0:T(8,128)(2,1)S(1)} collective-permute-done((bf16[64,2048]{1,0:T(8,128)(2,1)S(1)}, bf16[64,2048]{1,0:T(8,128)(2,1)S(1)}, u32[]{:S(2)}, u32[]{:S(2)}) %collective-permute-start.24) | collective-permute-done | bytes 262176 | tf_op jit(solution)/shard_map/ppermute | solution.py:272
  66.5 1.8 %experts.12 = (bf16[64,2048]{1,0:T(8,128)(2,1)S(1)}, bf16[64,2048]{1,0:T(8,128)(2,1)S(1)}) custom-call(bf16[64,2048]{1,0:T(8,128)(2,1)S(1)} %collective-permute-done.24.refs_0_, bf16[64,2048]{1,0:T(8,128)(2,1)S(1)} %collective-permute-done.25.refs_1_, bf16[144,512]{1,0:T(8,128)(2,1)S(1)} %collective-permute-done.3.refs_6_.refs_2_, ...), custom_call_target="tpu_custom_call" | custom-call | flops 1207959552 | bytes 9437184 | tf_op jit(solution)/shard_map/experts/pallas_call | solution.py:232
  68.4 3.5 %collective-permute-done.29.refs_0_ = bf16[64,2048]{1,0:T(8,128)(2,1)S(1)} collective-permute-done((bf16[64,2048]{1,0:T(8,128)(2,1)S(1)}, bf16[64,2048]{1,0:T(8,128)(2,1)S(1)}, u32[]{:S(2)}, u32[]{:S(2)}) %collective-permute-start.29) | collective-permute-done | bytes 262176 | tf_op jit(solution)/shard_map/ppermute | solution.py:272
  72.9 1.8 %experts.13 = (bf16[64,2048]{1,0:T(8,128)(2,1)S(1)}, bf16[64,2048]{1,0:T(8,128)(2,1)S(1)}) custom-call(bf16[64,2048]{1,0:T(8,128)(2,1)S(1)} %collective-permute-done.29.refs_0_, bf16[64,2048]{1,0:T(8,128)(2,1)S(1)} %collective-permute-done.30.refs_1_, bf16[144,512]{1,0:T(8,128)(2,1)S(1)} %collective-permute-done.3.refs_6_.refs_2_, ...), custom_call_target="tpu_custom_call" | custom-call | flops 1207959552 | bytes 9437184 | tf_op jit(solution)/shard_map/experts/pallas_call | solution.py:232
  74.7 1.1 collective-permute-start.32
  77.5 3.5 %collective-permute-done.31.refs_1_ = bf16[64,2048]{1,0:T(8,128)(2,1)S(1)} collective-permute-done((bf16[64,2048]{1,0:T(8,128)(2,1)S(1)}, bf16[64,2048]{1,0:T(8,128)(2,1)S(1)}, u32[]{:S(2)}, u32[]{:S(2)}) %collective-permute-start.31) | collective-permute-done | bytes 262176 | tf_op jit(solution)/shard_map/ppermute | solution.py:272
  81.0 1.8 %experts.14 = (bf16[64,2048]{1,0:T(8,128)(2,1)S(1)}, bf16[64,2048]{1,0:T(8,128)(2,1)S(1)}) custom-call(bf16[64,2048]{1,0:T(8,128)(2,1)S(1)} %collective-permute-done.28.refs_0_, bf16[64,2048]{1,0:T(8,128)(2,1)S(1)} %collective-permute-done.31.refs_1_, bf16[144,512]{1,0:T(8,128)(2,1)S(1)} %collective-permute-done.4.refs_7_.refs_2_, ...), custom_call_target="tpu_custom_call" | custom-call | flops 1207959552 | bytes 9437184 | tf_op jit(solution)/shard_map/experts/pallas_call | solution.py:232
  83.3 1.8 %collective-permute-start.38 = (bf16[64,2048]{1,0:T(8,128)(2,1)S(1)}, bf16[64,2048]{1,0:T(8,128)(2,1)S(1)}, u32[]{:S(2)}, u32[]{:S(2)}) collective-permute-start(bf16[64,2048]{1,0:T(8,128)(2,1)S(1)} %get-tuple-element.210), channel_id=1, source_target_pairs={{4,0},{5,1},{8,4},{9,5},{12,8},{13,9},{14,12},{15,13},{10,14},{11,... | collective-permute-start | bytes 786440 | tf_op jit(solution)/shard_map/ppermute | solution.py:272
  85.1 1.5 %collective-permute-done.33 = bf16[64,2048]{1,0:T(8,128)(2,1)S(1)} collective-permute-done((bf16[64,2048]{1,0:T(8,128)(2,1)S(1)}, bf16[64,2048]{1,0:T(8,128)(2,1)S(1)}, u32[]{:S(2)}, u32[]{:S(2)}) %collective-permute-start.33) | collective-permute-done | bytes 262176 | tf_op jit(solution)/shard_map/ppermute | solution.py:272
  86.6 1.8 %experts.15 = (bf16[64,2048]{1,0:T(8,128)(2,1)S(1)}, bf16[64,2048]{1,0:T(8,128)(2,1)S(1)}) custom-call(bf16[64,2048]{1,0:T(8,128)(2,1)S(1)} %get-tuple-element.140.refs_0_, bf16[64,2048]{1,0:T(8,128)(2,1)S(1)} %get-tuple-element.160.refs_1_, bf16[144,512]{1,0:T(8,128)(2,1)S(1)} %copy-done.3, bf16[1,2048,384]{2,1,0:T(8,128)(2,1)S(1)} %copy-done, ...), custom_call_target="tpu_custom_call" | custom-call | flops 1207959552 | bytes 9437184 | tf_op jit(solution)/shard_map/experts/pallas_call | solution.py:232
  88.5 2.5 %collective-permute-done.34 = bf16[64,2048]{1,0:T(8,128)(2,1)S(1)} collective-permute-done((bf16[64,2048]{1,0:T(8,128)(2,1)S(1)}, bf16[64,2048]{1,0:T(8,128)(2,1)S(1)}, u32[]{:S(2)}, u32[]{:S(2)}) %collective-permute-start.34) | collective-permute-done | bytes 262176 | tf_op jit(solution)/shard_map/ppermute | solution.py:272
  91.9 1.6 %collective-permute-start.40 = (bf16[64,2048]{1,0:T(8,128)(2,1)S(1)}, bf16[64,2048]{1,0:T(8,128)(2,1)S(1)}, u32[]{:S(2)}, u32[]{:S(2)}) collective-permute-start(bf16[64,2048]{1,0:T(8,128)(2,1)S(1)} %add_convert_fusion.8), channel_id=1, source_target_pairs={{4,0},{5,1},{8,4},{9,5},{12,8},{13,9},{14,12},{15,13},{10,14},{11,... | collective-permute-start | bytes 786440 | tf_op jit(solution)/shard_map/ppermute | solution.py:272
  93.5 1.9 %collective-permute-start.39 = (bf16[64,2048]{1,0:T(8,128)(2,1)S(1)}, bf16[64,2048]{1,0:T(8,128)(2,1)S(1)}, u32[]{:S(2)}, u32[]{:S(2)}) collective-permute-start(bf16[64,2048]{1,0:T(8,128)(2,1)S(1)} %add_convert_fusion.7), channel_id=1, source_target_pairs={{4,0},{5,1},{8,4},{9,5},{12,8},{13,9},{14,12},{15,13},{10,14},{11,... | collective-permute-start | bytes 786440 | tf_op jit(solution)/shard_map/ppermute | solution.py:272
  95.5 4.8 %collective-permute-done.35 = bf16[64,2048]{1,0:T(8,128)(2,1)S(1)} collective-permute-done((bf16[64,2048]{1,0:T(8,128)(2,1)S(1)}, bf16[64,2048]{1,0:T(8,128)(2,1)S(1)}, u32[]{:S(2)}, u32[]{:S(2)}) %collective-permute-start.35) | collective-permute-done | bytes 262176 | tf_op jit(solution)/shard_map/ppermute | solution.py:272
  100.6 5.3 %collective-permute-done.42 = bf16[64,2048]{1,0:T(8,128)(2,1)S(1)} collective-permute-done((bf16[64,2048]{1,0:T(8,128)(2,1)S(1)}, bf16[64,2048]{1,0:T(8,128)(2,1)S(1)}, u32[]{:S(2)}, u32[]{:S(2)}) %collective-permute-start.42) | collective-permute-done | bytes 262176 | tf_op jit(solution)/shard_map/ppermute | solution.py:272
  106.2 1.9 %collective-permute-start.44 = (bf16[64,2048]{1,0:T(8,128)(2,1)S(1)}, bf16[64,2048]{1,0:T(8,128)(2,1)S(1)}, u32[]{:S(2)}, u32[]{:S(2)}) collective-permute-start(bf16[64,2048]{1,0:T(8,128)(2,1)S(1)} %add_convert_fusion.6), channel_id=1, source_target_pairs={{4,0},{5,1},{8,4},{9,5},{12,8},{13,9},{14,12},{15,13},{10,14},{11,... | collective-permute-start | bytes 786440 | tf_op jit(solution)/shard_map/ppermute | solution.py:272
  108.2 1.1 collective-permute-start.41
  109.3 2.2 %collective-permute-done.36 = bf16[64,2048]{1,0:T(8,128)(2,1)S(1)} collective-permute-done((bf16[64,2048]{1,0:T(8,128)(2,1)S(1)}, bf16[64,2048]{1,0:T(8,128)(2,1)S(1)}, u32[]{:S(2)}, u32[]{:S(2)}) %collective-permute-start.36) | collective-permute-done | bytes 262176 | tf_op jit(solution)/shard_map/ppermute | solution.py:272
  112.8 1.9 %collective-permute-start.45 = (bf16[64,2048]{1,0:T(8,128)(2,1)S(1)}, bf16[64,2048]{1,0:T(8,128)(2,1)S(1)}, u32[]{:S(2)}, u32[]{:S(2)}) collective-permute-start(bf16[64,2048]{1,0:T(8,128)(2,1)S(1)} %add_convert_fusion.1), channel_id=1, source_target_pairs={{4,0},{5,1},{8,4},{9,5},{12,8},{13,9},{14,12},{15,13},{10,14},{11,... | collective-permute-start | bytes 786440 | tf_op jit(solution)/shard_map/ppermute | solution.py:272
  115.5 2.5 %collective-permute-done.37 = bf16[64,2048]{1,0:T(8,128)(2,1)S(1)} collective-permute-done((bf16[64,2048]{1,0:T(8,128)(2,1)S(1)}, bf16[64,2048]{1,0:T(8,128)(2,1)S(1)}, u32[]{:S(2)}, u32[]{:S(2)}) %collective-permute-start.37) | collective-permute-done | bytes 262176 | tf_op jit(solution)/shard_map/ppermute | solution.py:272
  118.1 1.0 collective-permute-done.45
  (83 shorter events, 14.6 us)
Async XLA Ops:
  0.0 29.0 %copy-start = (bf16[1,2048,384]{2,1,0:T(8,128)(2,1)S(1)}, bf16[1,2048,384]{2,1,0:T(8,128)(2,1)}, u32[]{:S(2)}) copy-start(bf16[1,2048,384]{2,1,0:T(8,128)(2,1)} %refs_3_.3) | copy-start | bytes 4718596
  2.4 27.3 %copy-start.3 = (bf16[144,512]{1,0:T(8,128)(2,1)S(1)}, bf16[144,512]{1,0:T(8,128)(2,1)}, u32[]{:S(2)}) copy-start(bf16[144,512]{1,0:T(8,128)(2,1)} %pack_message.1.refs_3_.refs_2_) | copy-start | bytes 442372
  2.4 8.0 %collective-permute-start.2 = (bf16[144,512]{1,0:T(8,128)(2,1)}, bf16[144,512]{1,0:T(8,128)(2,1)S(1)}, u32[]{:S(2)}, u32[]{:S(2)}) collective-permute-start(bf16[144,512]{1,0:T(8,128)(2,1)} %pack_message.1.refs_3_.refs_2_), channel_id=1, source_target_pairs={{4,0},{5,1},{8,4},{9,5},{12,8},{13,9},{14,12},{15,13},{10,14},{11,... | collective-permute-start | bytes 442376 | tf_op jit(solution)/shard_map/ppermute | solution.py:272
  5.3 5.5 %collective-permute-start = (bf16[144,512]{1,0:T(8,128)(2,1)}, bf16[144,512]{1,0:T(8,128)(2,1)S(1)}, u32[]{:S(2)}, u32[]{:S(2)}) collective-permute-start(bf16[144,512]{1,0:T(8,128)(2,1)} %pack_message.1.refs_3_.refs_2_), channel_id=1, source_target_pairs={{0,4},{1,5},{4,8},{5,9},{8,12},{9,13},{12,14},{13,15},{14,10},{15,... | collective-permute-start | bytes 442376 | tf_op jit(solution)/shard_map/ppermute | solution.py:272
  5.4 19.5 %collective-permute-start.7 = (bf16[144,512]{1,0:T(8,128)(2,1)}, bf16[144,512]{1,0:T(8,128)(2,1)S(1)}, u32[]{:S(2)}, u32[]{:S(2)}) collective-permute-start(bf16[144,512]{1,0:T(8,128)(2,1)} %pack_message.1.refs_3_.refs_2_), channel_id=1, source_target_pairs={{0,1},{1,0},{2,3},{3,2},{4,5},{5,4},{6,7},{7,6},{8,9},{9,8},{10,11... | collective-permute-start | bytes 442376 | tf_op jit(solution)/shard_map/ppermute | solution.py:272
  5.4 15.6 %collective-permute-start.4 = (bf16[144,512]{1,0:T(8,128)(2,1)}, bf16[144,512]{1,0:T(8,128)(2,1)S(1)}, u32[]{:S(2)}, u32[]{:S(2)}) collective-permute-start(bf16[144,512]{1,0:T(8,128)(2,1)} %pack_message.1.refs_3_.refs_2_), channel_id=1, source_target_pairs={{0,14},{1,15},{4,10},{5,11},{8,6},{9,7},{12,2},{13,3},{14,0},{15,1... | collective-permute-start | bytes 442376 | tf_op jit(solution)/shard_map/ppermute | solution.py:272
  10.8 7.5 %collective-permute-start.5 = (bf16[144,512]{1,0:T(8,128)(2,1)S(1)}, bf16[144,512]{1,0:T(8,128)(2,1)S(1)}, u32[]{:S(2)}, u32[]{:S(2)}) collective-permute-start(bf16[144,512]{1,0:T(8,128)(2,1)S(1)} %collective-permute-done.2.refs_8_.refs_3_), channel_id=1, source_target_pairs={{4,0},{5,1},{8,4},{9,5},{12,8},{13,9},{14,12},{15,13},{10,14},{11,... | collective-permute-start | bytes 442376 | tf_op jit(solution)/shard_map/ppermute | solution.py:272
  12.4 8.3 %collective-permute-start.1 = (bf16[144,512]{1,0:T(8,128)(2,1)S(1)}, bf16[144,512]{1,0:T(8,128)(2,1)S(1)}, u32[]{:S(2)}, u32[]{:S(2)}) collective-permute-start(bf16[144,512]{1,0:T(8,128)(2,1)S(1)} %collective-permute-done.refs_4_.refs_2_), channel_id=1, source_target_pairs={{0,4},{1,5},{4,8},{5,9},{8,12},{9,13},{12,14},{13,15},{14,10},{15,... | collective-permute-start | bytes 442376 | tf_op jit(solution)/shard_map/ppermute | solution.py:272
  18.3 6.6 %collective-permute-start.6 = (bf16[144,512]{1,0:T(8,128)(2,1)S(1)}, bf16[144,512]{1,0:T(8,128)(2,1)S(1)}, u32[]{:S(2)}, u32[]{:S(2)}) collective-permute-start(bf16[144,512]{1,0:T(8,128)(2,1)S(1)} %collective-permute-done.5.refs_9_.refs_3_), channel_id=1, source_target_pairs={{4,0},{5,1},{8,4},{9,5},{12,8},{13,9},{14,12},{15,13},{10,14},{11,... | collective-permute-start | bytes 442376 | tf_op jit(solution)/shard_map/ppermute | solution.py:272
  20.4 5.0 %collective-permute-start.12 = (bf16[144,512]{1,0:T(8,128)(2,1)S(1)}, bf16[144,512]{1,0:T(8,128)(2,1)S(1)}, u32[]{:S(2)}, u32[]{:S(2)}) collective-permute-start(bf16[144,512]{1,0:T(8,128)(2,1)S(1)} %collective-permute-done.2.refs_8_.refs_3_), channel_id=1, source_target_pairs={{0,1},{1,0},{2,3},{3,2},{4,5},{5,4},{6,7},{7,6},{8,9},{9,8},{10,11... | collective-permute-start | bytes 442376 | tf_op jit(solution)/shard_map/ppermute | solution.py:272
  20.7 4.8 %collective-permute-start.8 = (bf16[144,512]{1,0:T(8,128)(2,1)S(1)}, bf16[144,512]{1,0:T(8,128)(2,1)S(1)}, u32[]{:S(2)}, u32[]{:S(2)}) collective-permute-start(bf16[144,512]{1,0:T(8,128)(2,1)S(1)} %collective-permute-done.refs_4_.refs_2_), channel_id=1, source_target_pairs={{0,1},{1,0},{2,3},{3,2},{4,5},{5,4},{6,7},{7,6},{8,9},{9,8},{10,11... | collective-permute-start | bytes 442376 | tf_op jit(solution)/shard_map/ppermute | solution.py:272
  21.0 6.6 %collective-permute-start.3 = (bf16[144,512]{1,0:T(8,128)(2,1)S(1)}, bf16[144,512]{1,0:T(8,128)(2,1)S(1)}, u32[]{:S(2)}, u32[]{:S(2)}) collective-permute-start(bf16[144,512]{1,0:T(8,128)(2,1)S(1)} %collective-permute-done.1.refs_5_.refs_2_), channel_id=1, source_target_pairs={{0,4},{1,5},{4,8},{5,9},{8,12},{9,13},{12,14},{13,15},{14,10},{15,... | collective-permute-start | bytes 442376 | tf_op jit(solution)/shard_map/ppermute | solution.py:272
  24.9 2.7 %collective-permute-start.9 = (bf16[144,512]{1,0:T(8,128)(2,1)S(1)}, bf16[144,512]{1,0:T(8,128)(2,1)S(1)}, u32[]{:S(2)}, u32[]{:S(2)}) collective-permute-start(bf16[144,512]{1,0:T(8,128)(2,1)S(1)} %collective-permute-done.1.refs_5_.refs_2_), channel_id=1, source_target_pairs={{0,1},{1,0},{2,3},{3,2},{4,5},{5,4},{6,7},{7,6},{8,9},{9,8},{10,11... | collective-permute-start | bytes 442376 | tf_op jit(solution)/shard_map/ppermute | solution.py:272
  24.9 2.7 %collective-permute-start.13 = (bf16[144,512]{1,0:T(8,128)(2,1)S(1)}, bf16[144,512]{1,0:T(8,128)(2,1)S(1)}, u32[]{:S(2)}, u32[]{:S(2)}) collective-permute-start(bf16[144,512]{1,0:T(8,128)(2,1)S(1)} %collective-permute-done.5.refs_9_.refs_3_), channel_id=1, source_target_pairs={{0,1},{1,0},{2,3},{3,2},{4,5},{5,4},{6,7},{7,6},{8,9},{9,8},{10,11... | collective-permute-start | bytes 442376 | tf_op jit(solution)/shard_map/ppermute | solution.py:272
  25.4 2.2 %collective-permute-start.11 = (bf16[144,512]{1,0:T(8,128)(2,1)S(1)}, bf16[144,512]{1,0:T(8,128)(2,1)S(1)}, u32[]{:S(2)}, u32[]{:S(2)}) collective-permute-start(bf16[144,512]{1,0:T(8,128)(2,1)S(1)} %collective-permute-done.4.refs_7_.refs_2_), channel_id=1, source_target_pairs={{0,1},{1,0},{2,3},{3,2},{4,5},{5,4},{6,7},{7,6},{8,9},{9,8},{10,11... | collective-permute-start | bytes 442376 | tf_op jit(solution)/shard_map/ppermute | solution.py:272
  25.5 2.1 %collective-permute-start.14 = (bf16[144,512]{1,0:T(8,128)(2,1)S(1)}, bf16[144,512]{1,0:T(8,128)(2,1)S(1)}, u32[]{:S(2)}, u32[]{:S(2)}) collective-permute-start(bf16[144,512]{1,0:T(8,128)(2,1)S(1)} %collective-permute-done.6.refs_10_.refs_3_), channel_id=1, source_target_pairs={{0,1},{1,0},{2,3},{3,2},{4,5},{5,4},{6,7},{7,6},{8,9},{9,8},{10,11... | collective-permute-start | bytes 442376 | tf_op jit(solution)/shard_map/ppermute | solution.py:272
  27.6 1.4 %collective-permute-start.10 = (bf16[144,512]{1,0:T(8,128)(2,1)S(1)}, bf16[144,512]{1,0:T(8,128)(2,1)S(1)}, u32[]{:S(2)}, u32[]{:S(2)}) collective-permute-start(bf16[144,512]{1,0:T(8,128)(2,1)S(1)} %collective-permute-done.3.refs_6_.refs_2_), channel_id=1, source_target_pairs={{0,1},{1,0},{2,3},{3,2},{4,5},{5,4},{6,7},{7,6},{8,9},{9,8},{10,11... | collective-permute-start | bytes 442376 | tf_op jit(solution)/shard_map/ppermute | solution.py:272
  29.0 9.4 %collective-permute-start.15 = (bf16[1,2048,384]{2,1,0:T(8,128)(2,1)S(1)}, bf16[1,2048,384]{2,1,0:T(8,128)(2,1)S(1)}, u32[]{:S(2)}, u32[]{:S(2)}) collective-permute-start(bf16[1,2048,384]{2,1,0:T(8,128)(2,1)S(1)} %copy-done), channel_id=1, source_target_pairs={{0,1},{1,0},{2,3},{3,2},{4,5},{5,4},{6,7},{7,6},{8,9},{9,8},{10,11... | collective-permute-start | bytes 4718600 | tf_op jit(solution)/shard_map/ppermute | solution.py:272
  29.1 9.2 %collective-permute-start.16 = (bf16[1,2048,384]{2,1,0:T(8,128)(2,1)}, bf16[1,2048,384]{2,1,0:T(8,128)(2,1)S(1)}, u32[]{:S(2)}, u32[]{:S(2)}) collective-permute-start(bf16[1,2048,384]{2,1,0:T(8,128)(2,1)} %refs_4_.15), channel_id=1, source_target_pairs={{0,1},{1,0},{2,3},{3,2},{4,5},{5,4},{6,7},{7,6},{8,9},{9,8},{10,11... | collective-permute-start | bytes 4718600 | tf_op jit(solution)/shard_map/ppermute | solution.py:272
  29.5 14.7 %collective-permute-start.23 = (bf16[1,384,2048]{2,1,0:T(8,128)(2,1)}, bf16[1,384,2048]{2,1,0:T(8,128)(2,1)S(1)}, u32[]{:S(2)}, u32[]{:S(2)}) collective-permute-start(bf16[1,384,2048]{2,1,0:T(8,128)(2,1)} %refs_5_.15), channel_id=1, source_target_pairs={{0,1},{1,0},{2,3},{3,2},{4,5},{5,4},{6,7},{7,6},{8,9},{9,8},{10,11... | collective-permute-start | bytes 4718600 | tf_op jit(solution)/shard_map/ppermute | solution.py:272
  33.0 9.2 %collective-permute-start.19 = (bf16[64,2048]{1,0:T(8,128)(2,1)S(1)}, bf16[64,2048]{1,0:T(8,128)(2,1)S(1)}, u32[]{:S(2)}, u32[]{:S(2)}) collective-permute-start(bf16[64,2048]{1,0:T(8,128)(2,1)S(1)} %get-tuple-element.140.refs_0_), channel_id=1, source_target_pairs={{4,0},{5,1},{8,4},{9,5},{12,8},{13,9},{14,12},{15,13},{10,14},{11,... | collective-permute-start | bytes 786440 | tf_op jit(solution)/shard_map/ppermute | solution.py:272
  34.8 9.1 %collective-permute-start.17 = (bf16[64,2048]{1,0:T(8,128)(2,1)S(1)}, bf16[64,2048]{1,0:T(8,128)(2,1)S(1)}, u32[]{:S(2)}, u32[]{:S(2)}) collective-permute-start(bf16[64,2048]{1,0:T(8,128)(2,1)S(1)} %get-tuple-element.140.refs_0_), channel_id=1, source_target_pairs={{0,4},{1,5},{4,8},{5,9},{8,12},{9,13},{12,14},{13,15},{14,10},{15,... | collective-permute-start | bytes 786440 | tf_op jit(solution)/shard_map/ppermute | solution.py:272
  38.4 9.4 %collective-permute-start.22 = (bf16[64,2048]{1,0:T(8,128)(2,1)S(1)}, bf16[64,2048]{1,0:T(8,128)(2,1)S(1)}, u32[]{:S(2)}, u32[]{:S(2)}) collective-permute-start(bf16[64,2048]{1,0:T(8,128)(2,1)S(1)} %get-tuple-element.160.refs_1_), channel_id=1, source_target_pairs={{4,0},{5,1},{8,4},{9,5},{12,8},{13,9},{14,12},{15,13},{10,14},{11,... | collective-permute-start | bytes 786440 | tf_op jit(solution)/shard_map/ppermute | solution.py:272
  40.2 9.2 %collective-permute-start.21 = (bf16[64,2048]{1,0:T(8,128)(2,1)S(1)}, bf16[64,2048]{1,0:T(8,128)(2,1)S(1)}, u32[]{:S(2)}, u32[]{:S(2)}) collective-permute-start(bf16[64,2048]{1,0:T(8,128)(2,1)S(1)} %get-tuple-element.160.refs_1_), channel_id=1, source_target_pairs={{0,4},{1,5},{4,8},{5,9},{8,12},{9,13},{12,14},{13,15},{14,10},{15,... | collective-permute-start | bytes 786440 | tf_op jit(solution)/shard_map/ppermute | solution.py:272
  42.2 11.2 %collective-permute-start.20 = (bf16[64,2048]{1,0:T(8,128)(2,1)S(1)}, bf16[64,2048]{1,0:T(8,128)(2,1)S(1)}, u32[]{:S(2)}, u32[]{:S(2)}) collective-permute-start(bf16[64,2048]{1,0:T(8,128)(2,1)S(1)} %collective-permute-done.19.refs_1_), channel_id=1, source_target_pairs={{4,0},{5,1},{8,4},{9,5},{12,8},{13,9},{14,12},{15,13},{10,14},{11,... | collective-permute-start | bytes 786440 | tf_op jit(solution)/shard_map/ppermute | solution.py:272
  43.9 11.1 %collective-permute-start.18 = (bf16[64,2048]{1,0:T(8,128)(2,1)S(1)}, bf16[64,2048]{1,0:T(8,128)(2,1)S(1)}, u32[]{:S(2)}, u32[]{:S(2)}) collective-permute-start(bf16[64,2048]{1,0:T(8,128)(2,1)S(1)} %collective-permute-done.17.refs_0_), channel_id=1, source_target_pairs={{0,4},{1,5},{4,8},{5,9},{8,12},{9,13},{12,14},{13,15},{14,10},{15,... | collective-permute-start | bytes 786440 | tf_op jit(solution)/shard_map/ppermute | solution.py:272
  49.4 11.2 %collective-permute-start.26 = (bf16[64,2048]{1,0:T(8,128)(2,1)S(1)}, bf16[64,2048]{1,0:T(8,128)(2,1)S(1)}, u32[]{:S(2)}, u32[]{:S(2)}) collective-permute-start(bf16[64,2048]{1,0:T(8,128)(2,1)S(1)} %collective-permute-done.21.refs_0_), channel_id=1, source_target_pairs={{0,4},{1,5},{4,8},{5,9},{8,12},{9,13},{12,14},{13,15},{14,10},{15,... | collective-permute-start | bytes 786440 | tf_op jit(solution)/shard_map/ppermute | solution.py:272
  49.7 10.9 %collective-permute-start.27 = (bf16[64,2048]{1,0:T(8,128)(2,1)S(1)}, bf16[64,2048]{1,0:T(8,128)(2,1)S(1)}, u32[]{:S(2)}, u32[]{:S(2)}) collective-permute-start(bf16[64,2048]{1,0:T(8,128)(2,1)S(1)} %collective-permute-done.22.refs_1_), channel_id=1, source_target_pairs={{4,0},{5,1},{8,4},{9,5},{12,8},{13,9},{14,12},{15,13},{10,14},{11,... | collective-permute-start | bytes 786440 | tf_op jit(solution)/shard_map/ppermute | solution.py:272
  55.0 11.2 %collective-permute-start.24 = (bf16[64,2048]{1,0:T(8,128)(2,1)S(1)}, bf16[64,2048]{1,0:T(8,128)(2,1)S(1)}, u32[]{:S(2)}, u32[]{:S(2)}) collective-permute-start(bf16[64,2048]{1,0:T(8,128)(2,1)S(1)} %collective-permute-done.18.refs_0_), channel_id=1, source_target_pairs={{0,4},{1,5},{4,8},{5,9},{8,12},{9,13},{12,14},{13,15},{14,10},{15,... | collective-permute-start | bytes 786440 | tf_op jit(solution)/shard_map/ppermute | solution.py:272
  55.3 10.9 %collective-permute-start.25 = (bf16[64,2048]{1,0:T(8,128)(2,1)S(1)}, bf16[64,2048]{1,0:T(8,128)(2,1)S(1)}, u32[]{:S(2)}, u32[]{:S(2)}) collective-permute-start(bf16[64,2048]{1,0:T(8,128)(2,1)S(1)} %collective-permute-done.20.refs_1_), channel_id=1, source_target_pairs={{4,0},{5,1},{8,4},{9,5},{12,8},{13,9},{14,12},{15,13},{10,14},{11,... | collective-permute-start | bytes 786440 | tf_op jit(solution)/shard_map/ppermute | solution.py:272
  60.6 11.2 %collective-permute-start.29 = (bf16[64,2048]{1,0:T(8,128)(2,1)S(1)}, bf16[64,2048]{1,0:T(8,128)(2,1)S(1)}, u32[]{:S(2)}, u32[]{:S(2)}) collective-permute-start(bf16[64,2048]{1,0:T(8,128)(2,1)S(1)} %collective-permute-done.26.refs_0_), channel_id=1, source_target_pairs={{0,4},{1,5},{4,8},{5,9},{8,12},{9,13},{12,14},{13,15},{14,10},{15,... | collective-permute-start | bytes 786440 | tf_op jit(solution)/shard_map/ppermute | solution.py:272
  60.9 10.9 %collective-permute-start.30 = (bf16[64,2048]{1,0:T(8,128)(2,1)S(1)}, bf16[64,2048]{1,0:T(8,128)(2,1)S(1)}, u32[]{:S(2)}, u32[]{:S(2)}) collective-permute-start(bf16[64,2048]{1,0:T(8,128)(2,1)S(1)} %collective-permute-done.27.refs_1_), channel_id=1, source_target_pairs={{4,0},{5,1},{8,4},{9,5},{12,8},{13,9},{14,12},{15,13},{10,14},{11,... | collective-permute-start | bytes 786440 | tf_op jit(solution)/shard_map/ppermute | solution.py:272
  66.2 11.2 %collective-permute-start.28 = (bf16[64,2048]{1,0:T(8,128)(2,1)S(1)}, bf16[64,2048]{1,0:T(8,128)(2,1)S(1)}, u32[]{:S(2)}, u32[]{:S(2)}) collective-permute-start(bf16[64,2048]{1,0:T(8,128)(2,1)S(1)} %collective-permute-done.24.refs_0_), channel_id=1, source_target_pairs={{0,4},{1,5},{4,8},{5,9},{8,12},{9,13},{12,14},{13,15},{14,10},{15,... | collective-permute-start | bytes 786440 | tf_op jit(solution)/shard_map/ppermute | solution.py:272
  71.8 9.2 %collective-permute-start.31 = (bf16[64,2048]{1,0:T(8,128)(2,1)S(1)}, bf16[64,2048]{1,0:T(8,128)(2,1)S(1)}, u32[]{:S(2)}, u32[]{:S(2)}) collective-permute-start(bf16[64,2048]{1,0:T(8,128)(2,1)S(1)} %collective-permute-done.30.refs_1_), channel_id=1, source_target_pairs={{4,0},{5,1},{8,4},{9,5},{12,8},{13,9},{14,12},{15,13},{10,14},{11,... | collective-permute-start | bytes 786440 | tf_op jit(solution)/shard_map/ppermute | solution.py:272
  74.7 11.9 %collective-permute-start.32 = (bf16[64,2048]{1,0:T(8,128)(2,1)S(1)}, bf16[64,2048]{1,0:T(8,128)(2,1)S(1)}, u32[]{:S(2)}, u32[]{:S(2)}) collective-permute-start(bf16[64,2048]{1,0:T(8,128)(2,1)S(1)} %get-tuple-element.207), channel_id=1, source_target_pairs={{0,4},{1,5},{4,8},{5,9},{8,12},{9,13},{12,14},{13,15},{14,10},{15,... | collective-permute-start | bytes 786440 | tf_op jit(solution)/shard_map/ppermute | solution.py:272
  75.8 10.8 %collective-permute-start.33 = (bf16[64,2048]{1,0:T(8,128)(2,1)S(1)}, bf16[64,2048]{1,0:T(8,128)(2,1)S(1)}, u32[]{:S(2)}, u32[]{:S(2)}) collective-permute-start(bf16[64,2048]{1,0:T(8,128)(2,1)S(1)} %get-tuple-element.211), channel_id=1, source_target_pairs={{4,0},{5,1},{8,4},{9,5},{12,8},{13,9},{14,12},{15,13},{10,14},{11,... | collective-permute-start | bytes 786440 | tf_op jit(solution)/shard_map/ppermute | solution.py:272
  82.8 8.1 %collective-permute-start.34 = (bf16[64,2048]{1,0:T(8,128)(2,1)S(1)}, bf16[64,2048]{1,0:T(8,128)(2,1)S(1)}, u32[]{:S(2)}, u32[]{:S(2)}) collective-permute-start(bf16[64,2048]{1,0:T(8,128)(2,1)S(1)} %get-tuple-element.209), channel_id=1, source_target_pairs={{0,4},{1,5},{4,8},{5,9},{8,12},{9,13},{12,14},{13,15},{14,10},{15,... | collective-permute-start | bytes 786440 | tf_op jit(solution)/shard_map/ppermute | solution.py:272
  83.3 8.5 %collective-permute-start.38 = (bf16[64,2048]{1,0:T(8,128)(2,1)S(1)}, bf16[64,2048]{1,0:T(8,128)(2,1)S(1)}, u32[]{:S(2)}, u32[]{:S(2)}) collective-permute-start(bf16[64,2048]{1,0:T(8,128)(2,1)S(1)} %get-tuple-element.210), channel_id=1, source_target_pairs={{4,0},{5,1},{8,4},{9,5},{12,8},{13,9},{14,12},{15,13},{10,14},{11,... | collective-permute-start | bytes 786440 | tf_op jit(solution)/shard_map/ppermute | solution.py:272
  91.0 9.3 %collective-permute-start.35 = (bf16[64,2048]{1,0:T(8,128)(2,1)S(1)}, bf16[64,2048]{1,0:T(8,128)(2,1)S(1)}, u32[]{:S(2)}, u32[]{:S(2)}) collective-permute-start(bf16[64,2048]{1,0:T(8,128)(2,1)S(1)} %add_convert_fusion.11), channel_id=1, source_target_pairs={{0,4},{1,5},{4,8},{5,9},{8,12},{9,13},{12,14},{13,15},{14,10},{15,... | collective-permute-start | bytes 786440 | tf_op jit(solution)/shard_map/ppermute | solution.py:272
  91.3 14.6 %collective-permute-start.42 = (bf16[64,2048]{1,0:T(8,128)(2,1)S(1)}, bf16[64,2048]{1,0:T(8,128)(2,1)S(1)}, u32[]{:S(2)}, u32[]{:S(2)}) collective-permute-start(bf16[64,2048]{1,0:T(8,128)(2,1)S(1)} %add_convert_fusion.3), channel_id=1, source_target_pairs={{0,4},{1,5},{4,8},{5,9},{8,12},{9,13},{12,14},{13,15},{14,10},{15,... | collective-permute-start | bytes 786440 | tf_op jit(solution)/shard_map/ppermute | solution.py:272
  91.9 14.3 %collective-permute-start.40 = (bf16[64,2048]{1,0:T(8,128)(2,1)S(1)}, bf16[64,2048]{1,0:T(8,128)(2,1)S(1)}, u32[]{:S(2)}, u32[]{:S(2)}) collective-permute-start(bf16[64,2048]{1,0:T(8,128)(2,1)S(1)} %add_convert_fusion.8), channel_id=1, source_target_pairs={{4,0},{5,1},{8,4},{9,5},{12,8},{13,9},{14,12},{15,13},{10,14},{11,... | collective-permute-start | bytes 786440 | tf_op jit(solution)/shard_map/ppermute | solution.py:272
  93.5 14.7 %collective-permute-start.39 = (bf16[64,2048]{1,0:T(8,128)(2,1)S(1)}, bf16[64,2048]{1,0:T(8,128)(2,1)S(1)}, u32[]{:S(2)}, u32[]{:S(2)}) collective-permute-start(bf16[64,2048]{1,0:T(8,128)(2,1)S(1)} %add_convert_fusion.7), channel_id=1, source_target_pairs={{4,0},{5,1},{8,4},{9,5},{12,8},{13,9},{14,12},{15,13},{10,14},{11,... | collective-permute-start | bytes 786440 | tf_op jit(solution)/shard_map/ppermute | solution.py:272
  100.4 11.2 %collective-permute-start.36 = (bf16[64,2048]{1,0:T(8,128)(2,1)S(1)}, bf16[64,2048]{1,0:T(8,128)(2,1)S(1)}, u32[]{:S(2)}, u32[]{:S(2)}) collective-permute-start(bf16[64,2048]{1,0:T(8,128)(2,1)S(1)} %add_convert_fusion.10), channel_id=1, source_target_pairs={{0,4},{1,5},{4,8},{5,9},{8,12},{9,13},{12,14},{13,15},{14,10},{15,... | collective-permute-start | bytes 786440 | tf_op jit(solution)/shard_map/ppermute | solution.py:272
  106.0 12.2 %collective-permute-start.43 = (bf16[64,2048]{1,0:T(8,128)(2,1)S(1)}, bf16[64,2048]{1,0:T(8,128)(2,1)S(1)}, u32[]{:S(2)}, u32[]{:S(2)}) collective-permute-start(bf16[64,2048]{1,0:T(8,128)(2,1)S(1)} %add_convert_fusion.2), channel_id=1, source_target_pairs={{0,4},{1,5},{4,8},{5,9},{8,12},{9,13},{12,14},{13,15},{14,10},{15,... | collective-permute-start | bytes 786440 | tf_op jit(solution)/shard_map/ppermute | solution.py:272
  106.2 6.5 %collective-permute-start.44 = (bf16[64,2048]{1,0:T(8,128)(2,1)S(1)}, bf16[64,2048]{1,0:T(8,128)(2,1)S(1)}, u32[]{:S(2)}, u32[]{:S(2)}) collective-permute-start(bf16[64,2048]{1,0:T(8,128)(2,1)S(1)} %add_convert_fusion.6), channel_id=1, source_target_pairs={{4,0},{5,1},{8,4},{9,5},{12,8},{13,9},{14,12},{15,13},{10,14},{11,... | collective-permute-start | bytes 786440 | tf_op jit(solution)/shard_map/ppermute | solution.py:272
  108.2 7.3 %collective-permute-start.41 = (bf16[64,2048]{1,0:T(8,128)(2,1)S(1)}, bf16[64,2048]{1,0:T(8,128)(2,1)S(1)}, u32[]{:S(2)}, u32[]{:S(2)}) collective-permute-start(bf16[64,2048]{1,0:T(8,128)(2,1)S(1)} %add_convert_fusion.5), channel_id=1, source_target_pairs={{4,0},{5,1},{8,4},{9,5},{12,8},{13,9},{14,12},{15,13},{10,14},{11,... | collective-permute-start | bytes 786440 | tf_op jit(solution)/shard_map/ppermute | solution.py:272
  111.6 6.4 %collective-permute-start.37 = (bf16[64,2048]{1,0:T(8,128)(2,1)S(1)}, bf16[64,2048]{1,0:T(8,128)(2,1)S(1)}, u32[]{:S(2)}, u32[]{:S(2)}) collective-permute-start(bf16[64,2048]{1,0:T(8,128)(2,1)S(1)} %add_convert_fusion.9), channel_id=1, source_target_pairs={{0,4},{1,5},{4,8},{5,9},{8,12},{9,13},{12,14},{13,15},{14,10},{15,... | collective-permute-start | bytes 786440 | tf_op jit(solution)/shard_map/ppermute | solution.py:272
  112.8 6.4 %collective-permute-start.45 = (bf16[64,2048]{1,0:T(8,128)(2,1)S(1)}, bf16[64,2048]{1,0:T(8,128)(2,1)S(1)}, u32[]{:S(2)}, u32[]{:S(2)}) collective-permute-start(bf16[64,2048]{1,0:T(8,128)(2,1)S(1)} %add_convert_fusion.1), channel_id=1, source_target_pairs={{4,0},{5,1},{8,4},{9,5},{12,8},{13,9},{14,12},{15,13},{10,14},{11,... | collective-permute-start | bytes 786440 | tf_op jit(solution)/shard_map/ppermute | solution.py:272
  (4 other events, 63.7 us)

commit v8 on v6

--- a/solution.py
+++ b/solution.py
@@ -60,10 +60,22 @@
     )(stretch_pos, keys, values, routes.T, combine.T)
 
 
-def attend_kernel(count, half, *refs):
-    query_ref, residual_ref, gain_ref = refs[:3]
-    messages = refs[3 : 3 + count]
-    hidden_ref, normed_ref, key_ext, value_ext = refs[3 + count :]
+def attend_kernel(count, half, begun, ended, *refs):
+    refs = list(refs)
+
+    def take(number):
+        taken, refs[:number] = refs[:number], []
+        return taken
+
+    query_ref, own_ref = take(2)
+    messages = take(count)
+    if begun:
+        begun_sums, begun_best = take(2)
+    if ended:
+        residual_ref, gain_ref, hidden_ref, normed_ref = take(4)
+    else:
+        sums_ref, best_ref = take(2)
+    key_ext, value_ext = refs
     features = query_ref.shape[1]
     some = query_ref.shape[0] // 2
     mine = slice(half * some, (half + 1) * some)
@@ -76,7 +88,7 @@
     sub = lax.broadcasted_iota(jnp.int32, (rows, rows), 0)
     lane = lax.broadcasted_iota(jnp.int32, (rows, rows), 1)
     ahead = (sub - lane).astype(jnp.float32)
-    own_pos = messages[0][rows : rows + EXTRA, 256 : 256 + rows][0:1].astype(jnp.float32)
+    own_pos = own_ref[rows : rows + EXTRA, 256 : 256 + rows][0:1].astype(jnp.float32)
     ones = jnp.ones((rows, HEAD_SIZE), jnp.bfloat16)
     for block in range(count):
         ref = messages[block]
@@ -93,11 +105,11 @@
             value_ext[a, at, HEAD_SIZE : 2 * HEAD_SIZE] = ones
     eye = jnp.where(sub == lane, 1.0, 0.0).astype(jnp.bfloat16)[mine]
     rate = math.log2(math.e) / math.sqrt(HEAD_SIZE) / QUERY_SCALE
-    step = min(512, span)
+    step = min(512 if span % 512 == 0 else 256, span)
     pair = 4
     squares = jnp.zeros((some, HEAD_SIZE), jnp.float32)
-    for first in range(0, heads, pair):
-        a = first // group
+
+    def scores_of(first):
         stacked = jnp.concatenate(
             [
                 jnp.concatenate([query_ref[mine, h * HEAD_SIZE : (h + 1) * HEAD_SIZE], eye], axis=1)
@@ -105,18 +117,31 @@
             ],
             axis=0,
         )
-        scores = [
+        return [
             lax.dot_general(
                 stacked,
-                key_ext[a, at : at + step, :],
+                key_ext[first // group, at : at + step, :],
                 (((1,), (1,)), ((), ())),
                 preferred_element_type=jnp.float32,
             )
             for at in range(0, span, step)
         ]
+
+    ready = scores_of(0)
+    for first in range(0, heads, pair):
+        a = first // group
+        scores = ready
+        if first + pair < heads:
+            ready = scores_of(first + pair)
         best = functools.reduce(jnp.maximum, scores)
         best = jnp.max(best, axis=1, keepdims=True)
         total = None
+        at = slice(first * some, (first + pair) * some)
+        if begun:
+            before = begun_best[at]
+            best = jnp.maximum(best, before[:, 0:1])
+            shrink = jnp.exp2((before - best) * rate)
+            total = begun_sums[at] * jnp.concatenate([shrink, shrink], axis=1)
         for i, part in enumerate(scores):
             probs = jnp.exp2((part - best) * rate).astype(jnp.bfloat16)
             term = jnp.dot(
@@ -125,6 +150,10 @@
                 preferred_element_type=jnp.float32,
             )
             total = term if total is None else total + term
+        if not ended:
+            sums_ref[at] = total
+            best_ref[at] = jnp.broadcast_to(best, (pair * some, HEAD_SIZE))
+            continue
         attended = (total[:, 0:HEAD_SIZE] / total[:, HEAD_SIZE:]).astype(jnp.bfloat16)
         for j in range(pair):
             cols = slice((first + j) * HEAD_SIZE, (first + j + 1) * HEAD_SIZE)
@@ -133,6 +162,8 @@
             ].astype(jnp.float32)
             hidden_ref[:, cols] = state
             squares = squares + state * state
+    if not ended:
+        return
     meansq = jnp.sum(squares, axis=1, keepdims=True) / float(heads * HEAD_SIZE)
     inverse = lax.rsqrt(meansq + 1e-06)
     for h in range(heads):
@@ -142,21 +173,17 @@
         )
 
 
-def attend(half, staged, messages):
-    rows, features = staged[0].shape
-    some = rows // 2
-    count = len(messages)
+def attend_call(half, begun, ended, queries, messages, inputs, out_shape):
+    rows, features = queries.shape
+    count = len(messages) - 1
     kv_heads = messages[0].shape[1] // (2 * HEAD_SIZE)
     vmem = pl.BlockSpec(memory_space=pltpu.VMEM)
     span = count * rows
     return pl.pallas_call(
-        functools.partial(attend_kernel, count, half),
-        out_shape=(
-            jax.ShapeDtypeStruct((some, features), jnp.float32),
-            jax.ShapeDtypeStruct((some, features), jnp.bfloat16),
-        ),
-        in_specs=[vmem] * (3 + count),
-        out_specs=(vmem, vmem),
+        functools.partial(attend_kernel, count, half, begun, ended),
+        out_shape=out_shape,
+        in_specs=[vmem] * (1 + len(messages) + len(inputs)),
+        out_specs=(vmem,) * len(out_shape),
         scratch_shapes=[
             pltpu.VMEM((kv_heads, span, 2 * HEAD_SIZE), jnp.bfloat16),
             pltpu.VMEM((kv_heads, span, 2 * HEAD_SIZE), jnp.bfloat16),
@@ -166,7 +193,41 @@
             flops=4 * rows * span * features, bytes_accessed=4 * 1024 * 1024, transcendentals=0
         ),
         name="attend",
-    )(*staged, *messages)
+    )(queries, *messages, *inputs)
+
+
+def attend_start(half, queries, own, messages):
+    rows, features = queries.shape
+    lines = rows // 2 * (features // HEAD_SIZE)
+    return attend_call(
+        half,
+        False,
+        False,
+        queries,
+        [own] + messages,
+        (),
+        (
+            jax.ShapeDtypeStruct((lines, 2 * HEAD_SIZE), jnp.float32),
+            jax.ShapeDtypeStruct((lines, HEAD_SIZE), jnp.float32),
+        ),
+    )
+
+
+def attend(half, staged, own, messages, begun=()):
+    queries, residual, gain = staged
+    rows, features = queries.shape
+    return attend_call(
+        half,
+        len(begun) > 0,
+        True,
+        queries,
+        [own] + messages,
+        (*begun, residual, gain),
+        (
+            jax.ShapeDtypeStruct((rows // 2, features), jnp.float32),
+            jax.ShapeDtypeStruct((rows // 2, features), jnp.bfloat16),
+        ),
+    )
 
 
 def expert_kernel(places, count, *refs):
@@ -276,12 +337,17 @@
         if hop < far:
             right[hop] = send(right[hop - 1], back)
     plane = [message] + [left[h] for h in range(1, far + 1)] + [right[h] for h in range(1, far)]
-    everything = plane + [send(m, swap) for m in plane]
+    near = [message] + [left[h] for h in range(1, far)] + [right[h] for h in range(1, far)]
+    near = near + [send(m, swap) for m in near]
+    begun = attend_start(0, staged[0], message, near)
+    left[far], begun = tie((left[far], begun))
+    distant = [left[far], send(left[far], swap)]
+    everything = near + distant
     everything, own_weights = tie((everything, (gate_weight, up_weight, down_weight)))
     twin_gate, twin_up, twin_down = [send(w, swap) for w in own_weights]
-    hidden_upper, upper = attend(0, staged, everything)
+    hidden_upper, upper = attend(0, staged, message, everything[len(near) :], begun)
     everything, upper = tie((everything, upper))
-    hidden_lower, lower = attend(1, staged, everything)
+    hidden_lower, lower = attend(1, staged, message, everything)
     lower, twin_gate, twin_up = tie((lower, twin_gate, twin_up))
     weights = (gate_weight, up_weight, down_weight, twin_gate, twin_up, twin_down)
 

time: 120 us -> 121 us (level)
  waiting for transfers between devices: 53.4 us -> 57.4 us
  starting transfers between devices: 38.6 us -> 36.1 us
    ppermute x46, waiting for transfers between devices: 53.4 us -> 57.4 us  [send(): return lax.ppermute(array, 'ctx', pairs)]
    ppermute x46, starting transfers between devices: 38.6 us -> 36.1 us  [send(): return lax.ppermute(array, 'ctx', pairs)]
    pallas_call x2 -> x3, Pallas kernels: 7.3 us -> 7.16 us  [attend_call(): pl.pallas_call(functools.partial(attend_kernel, count, half, begun, ended...]
  transfers between devices with their start and end apart: 46 -> 46, of which waited for: 26 -> 27; matrix products, arithmetic and copies ran while one was open for 2% -> 2% of each run, Pallas kernels for 18% -> 18%
where the time goes in v8:
time: 121 us
  waiting for transfers between devices  57.4 us (47%)
  starting transfers between devices  36.1 us (30%)
  Pallas kernels  23.4 us (19%)
  other arithmetic  2.89 us (2%)
    ppermute x46, waiting for transfers between devices, send(): return lax.ppermute(array, 'ctx', pairs)  57.4 us
    ppermute x46, starting transfers between devices, send(): return lax.ppermute(array, 'ctx', pairs)  36.1 us
    pallas_call x8, Pallas kernels, run_experts(): pl.pallas_call(functools.partial(expert_kernel, [piece[1:] for piece in p...  14.7 us
    pallas_call x3, Pallas kernels, attend_call(): pl.pallas_call(functools.partial(attend_kernel, count, half, begun, ended...  7.16 us
  transfers between devices with their start and end apart: 46, of which 27 were waited for; matrix products, arithmetic and copies ran while one was open for 2% of the time, Pallas kernels for 18%

profile of v8, /device:TPU:0, one launch (start us, length us, event | category | flops | bytes accessed | tf_op | source)
XLA Modules:
  0.0 120.9 jit_solution(17058093524643956989)
XLA Ops:
  0.7 1.6 %pack_message.1.refs_1_.refs_2_ = bf16[144,512]{1,0:T(8,128)(2,1)} custom-call(s32[1]{0:T(128)S(6)} %copy.12.pos_ref, bf16[128,256]{1,0:T(8,128)(2,1)} %key_ref.1, bf16[128,256]{1,0:T(8,128)(2,1)} %value_ref.1, s32[8,128]{1,0:T(8,128)} %bitcast.2, f32[8,128]{1,0:T(8,128)} %bitcast.3), custom_call_target="tpu_custom_call" | custom-call | tf_op jit(solution)/shard_map/pack_message/pallas_call | solution.py:54
  2.3 3.0 %collective-permute-start.2 = (bf16[144,512]{1,0:T(8,128)(2,1)}, bf16[144,512]{1,0:T(8,128)(2,1)S(1)}, u32[]{:S(2)}, u32[]{:S(2)}) collective-permute-start(bf16[144,512]{1,0:T(8,128)(2,1)} %pack_message.1.refs_1_.refs_2_), channel_id=1, source_target_pairs={{4,0},{5,1},{8,4},{9,5},{12,8},{13,9},{14,12},{15,13},{10,14},{11,... | collective-permute-start | bytes 442376 | tf_op jit(solution)/shard_map/ppermute | solution.py:321
  5.3 4.1 %collective-permute-done.2.refs_6_.refs_3_ = bf16[144,512]{1,0:T(8,128)(2,1)S(1)} collective-permute-done((bf16[144,512]{1,0:T(8,128)(2,1)}, bf16[144,512]{1,0:T(8,128)(2,1)S(1)}, u32[]{:S(2)}, u32[]{:S(2)}) %collective-permute-start.2) | collective-permute-done | bytes 147488 | tf_op jit(solution)/shard_map/ppermute | solution.py:321
  9.4 1.3 %collective-permute-done.refs_3_.refs_2_ = bf16[144,512]{1,0:T(8,128)(2,1)S(1)} collective-permute-done((bf16[144,512]{1,0:T(8,128)(2,1)}, bf16[144,512]{1,0:T(8,128)(2,1)S(1)}, u32[]{:S(2)}, u32[]{:S(2)}) %collective-permute-start) | collective-permute-done | bytes 147488 | tf_op jit(solution)/shard_map/ppermute | solution.py:321
  10.8 1.6 %collective-permute-start.4 = (bf16[144,512]{1,0:T(8,128)(2,1)S(1)}, bf16[144,512]{1,0:T(8,128)(2,1)S(1)}, u32[]{:S(2)}, u32[]{:S(2)}) collective-permute-start(bf16[144,512]{1,0:T(8,128)(2,1)S(1)} %collective-permute-done.2.refs_6_.refs_3_), channel_id=1, source_target_pairs={{4,0},{5,1},{8,4},{9,5},{12,8},{13,9},{14,12},{15,13},{10,14},{11,... | collective-permute-start | bytes 442376 | tf_op jit(solution)/shard_map/ppermute | solution.py:321
  14.1 3.4 %collective-permute-done.1.refs_4_.refs_2_ = bf16[144,512]{1,0:T(8,128)(2,1)S(1)} collective-permute-done((bf16[144,512]{1,0:T(8,128)(2,1)S(1)}, bf16[144,512]{1,0:T(8,128)(2,1)S(1)}, u32[]{:S(2)}, u32[]{:S(2)}) %collective-permute-start.1) | collective-permute-done | bytes 147488 | tf_op jit(solution)/shard_map/ppermute | solution.py:321
  17.5 1.6 %collective-permute-start.5 = (bf16[144,512]{1,0:T(8,128)(2,1)S(1)}, bf16[144,512]{1,0:T(8,128)(2,1)S(1)}, u32[]{:S(2)}, u32[]{:S(2)}) collective-permute-start(bf16[144,512]{1,0:T(8,128)(2,1)S(1)} %collective-permute-done.4.refs_7_.refs_3_), channel_id=1, source_target_pairs={{4,0},{5,1},{8,4},{9,5},{12,8},{13,9},{14,12},{15,13},{10,14},{11,... | collective-permute-start | bytes 442376 | tf_op jit(solution)/shard_map/ppermute | solution.py:321
  20.2 2.5 %collective-permute-done.5.refs_8_.refs_3_ = bf16[144,512]{1,0:T(8,128)(2,1)S(1)} collective-permute-done((bf16[144,512]{1,0:T(8,128)(2,1)S(1)}, bf16[144,512]{1,0:T(8,128)(2,1)S(1)}, u32[]{:S(2)}, u32[]{:S(2)}) %collective-permute-start.5) | collective-permute-done | bytes 147488 | tf_op jit(solution)/shard_map/ppermute | solution.py:321
  22.7 1.6 %collective-permute-done.3.refs_5_.refs_2_ = bf16[144,512]{1,0:T(8,128)(2,1)S(1)} collective-permute-done((bf16[144,512]{1,0:T(8,128)(2,1)S(1)}, bf16[144,512]{1,0:T(8,128)(2,1)S(1)}, u32[]{:S(2)}, u32[]{:S(2)}) %collective-permute-start.3) | collective-permute-done | bytes 147488 | tf_op jit(solution)/shard_map/ppermute | solution.py:321
  25.7 2.8 %attend.3 = (f32[1024,256]{1,0:T(8,128)S(1)}, f32[1024,128]{1,0:T(8,128)S(1)}) custom-call(bf16[128,2048]{1,0:T(8,128)(2,1)S(1)} %broadcast_multiply_fusion.refs_0_, bf16[144,512]{1,0:T(8,128)(2,1)S(1)} %copy-done.3, bf16[144,512]{1,0:T(8,128)(2,1)S(1)} %copy-done.3, bf16[144,512]{1,0:T(8,128)(2,1)S(1)} %collective-permute-done.refs_3_.refs_2_, ...), custom_call_target="tpu_custom_call" | custom-call | flops 1879048192 | bytes 4194304 | tf_op jit(solution)/shard_map/attend/pallas_call | solution.py:182
  28.5 2.1 %collective-permute-done.13.refs_2_.refs_16_ = bf16[144,512]{1,0:T(8,128)(2,1)S(1)} collective-permute-done((bf16[144,512]{1,0:T(8,128)(2,1)S(1)}, bf16[144,512]{1,0:T(8,128)(2,1)S(1)}, u32[]{:S(2)}, u32[]{:S(2)}) %collective-permute-start.13) | collective-permute-done | bytes 147488 | tf_op jit(solution)/shard_map/ppermute | solution.py:321
  30.6 1.4 %collective-permute-done.14.refs_3_.refs_17_ = bf16[144,512]{1,0:T(8,128)(2,1)S(1)} collective-permute-done((bf16[144,512]{1,0:T(8,128)(2,1)S(1)}, bf16[144,512]{1,0:T(8,128)(2,1)S(1)}, u32[]{:S(2)}, u32[]{:S(2)}) %collective-permute-start.14) | collective-permute-done | bytes 147488 | tf_op jit(solution)/shard_map/ppermute | solution.py:321
  33.7 1.6 %collective-permute-start.19 = (bf16[64,2048]{1,0:T(8,128)(2,1)S(1)}, bf16[64,2048]{1,0:T(8,128)(2,1)S(1)}, u32[]{:S(2)}, u32[]{:S(2)}) collective-permute-start(bf16[64,2048]{1,0:T(8,128)(2,1)S(1)} %get-tuple-element.148.refs_0_), channel_id=1, source_target_pairs={{4,0},{5,1},{8,4},{9,5},{12,8},{13,9},{14,12},{15,13},{10,14},{11,... | collective-permute-start | bytes 786440 | tf_op jit(solution)/shard_map/ppermute | solution.py:321
  35.8 3.3 %attend.5 = (f32[64,2048]{1,0:T(8,128)S(1)}, bf16[64,2048]{1,0:T(8,128)(2,1)S(1)}) custom-call(bf16[128,2048]{1,0:T(8,128)(2,1)S(1)} %broadcast_multiply_fusion.refs_0_, bf16[144,512]{1,0:T(8,128)(2,1)S(1)} %copy-done.3, bf16[144,512]{1,0:T(8,128)(2,1)S(1)} %copy-done.3, bf16[144,512]{1,0:T(8,128)(2,1)S(1)} %collective-permute-done.refs_3_.refs_2_, ...), custom_call_target="tpu_custom_call" | custom-call | flops 2147483648 | bytes 4194304 | tf_op jit(solution)/shard_map/attend/pallas_call | solution.py:182
  39.1 1.7 %collective-permute-start.22 = (bf16[64,2048]{1,0:T(8,128)(2,1)S(1)}, bf16[64,2048]{1,0:T(8,128)(2,1)S(1)}, u32[]{:S(2)}, u32[]{:S(2)}) collective-permute-start(bf16[64,2048]{1,0:T(8,128)(2,1)S(1)} %get-tuple-element.168.refs_1_), channel_id=1, source_target_pairs={{4,0},{5,1},{8,4},{9,5},{12,8},{13,9},{14,12},{15,13},{10,14},{11,... | collective-permute-start | bytes 786440 | tf_op jit(solution)/shard_map/ppermute | solution.py:321
  41.2 1.7 %collective-permute-done.19.refs_1_ = bf16[64,2048]{1,0:T(8,128)(2,1)S(1)} collective-permute-done((bf16[64,2048]{1,0:T(8,128)(2,1)S(1)}, bf16[64,2048]{1,0:T(8,128)(2,1)S(1)}, u32[]{:S(2)}, u32[]{:S(2)}) %collective-permute-start.19) | collective-permute-done | bytes 262176 | tf_op jit(solution)/shard_map/ppermute | solution.py:321
  42.9 1.6 %collective-permute-start.20 = (bf16[64,2048]{1,0:T(8,128)(2,1)S(1)}, bf16[64,2048]{1,0:T(8,128)(2,1)S(1)}, u32[]{:S(2)}, u32[]{:S(2)}) collective-permute-start(bf16[64,2048]{1,0:T(8,128)(2,1)S(1)} %collective-permute-done.19.refs_1_), channel_id=1, source_target_pairs={{4,0},{5,1},{8,4},{9,5},{12,8},{13,9},{14,12},{15,13},{10,14},{11,... | collective-permute-start | bytes 786440 | tf_op jit(solution)/shard_map/ppermute | solution.py:321
  44.9 1.8 %experts.8 = (bf16[64,2048]{1,0:T(8,128)(2,1)S(1)}, bf16[64,2048]{1,0:T(8,128)(2,1)S(1)}) custom-call(bf16[64,2048]{1,0:T(8,128)(2,1)S(1)} %collective-permute-done.17.refs_0_, bf16[64,2048]{1,0:T(8,128)(2,1)S(1)} %collective-permute-done.19.refs_1_, bf16[144,512]{1,0:T(8,128)(2,1)S(1)} %collective-permute-done.refs_3_.refs_2_, ...), custom_call_target="tpu_custom_call" | custom-call | flops 1207959552 | bytes 9437184 | tf_op jit(solution)/shard_map/experts/pallas_call | solution.py:281
  46.7 1.7 %collective-permute-done.22.refs_1_ = bf16[64,2048]{1,0:T(8,128)(2,1)S(1)} collective-permute-done((bf16[64,2048]{1,0:T(8,128)(2,1)S(1)}, bf16[64,2048]{1,0:T(8,128)(2,1)S(1)}, u32[]{:S(2)}, u32[]{:S(2)}) %collective-permute-start.22) | collective-permute-done | bytes 262176 | tf_op jit(solution)/shard_map/ppermute | solution.py:321
  48.5 1.5 %collective-permute-done.21.refs_0_ = bf16[64,2048]{1,0:T(8,128)(2,1)S(1)} collective-permute-done((bf16[64,2048]{1,0:T(8,128)(2,1)S(1)}, bf16[64,2048]{1,0:T(8,128)(2,1)S(1)}, u32[]{:S(2)}, u32[]{:S(2)}) %collective-permute-start.21) | collective-permute-done | bytes 262176 | tf_op jit(solution)/shard_map/ppermute | solution.py:321
  50.4 1.6 %collective-permute-start.27 = (bf16[64,2048]{1,0:T(8,128)(2,1)S(1)}, bf16[64,2048]{1,0:T(8,128)(2,1)S(1)}, u32[]{:S(2)}, u32[]{:S(2)}) collective-permute-start(bf16[64,2048]{1,0:T(8,128)(2,1)S(1)} %collective-permute-done.22.refs_1_), channel_id=1, source_target_pairs={{4,0},{5,1},{8,4},{9,5},{12,8},{13,9},{14,12},{15,13},{10,14},{11,... | collective-permute-start | bytes 786440 | tf_op jit(solution)/shard_map/ppermute | solution.py:321
  52.0 1.8 %experts.9 = (bf16[64,2048]{1,0:T(8,128)(2,1)S(1)}, bf16[64,2048]{1,0:T(8,128)(2,1)S(1)}) custom-call(bf16[64,2048]{1,0:T(8,128)(2,1)S(1)} %collective-permute-done.21.refs_0_, bf16[64,2048]{1,0:T(8,128)(2,1)S(1)} %collective-permute-done.22.refs_1_, bf16[144,512]{1,0:T(8,128)(2,1)S(1)} %collective-permute-done.refs_3_.refs_2_, ...), custom_call_target="tpu_custom_call" | custom-call | flops 1207959552 | bytes 9437184 | tf_op jit(solution)/shard_map/experts/pallas_call | solution.py:281
  54.1 1.5 %collective-permute-done.18.refs_0_ = bf16[64,2048]{1,0:T(8,128)(2,1)S(1)} collective-permute-done((bf16[64,2048]{1,0:T(8,128)(2,1)S(1)}, bf16[64,2048]{1,0:T(8,128)(2,1)S(1)}, u32[]{:S(2)}, u32[]{:S(2)}) %collective-permute-start.18) | collective-permute-done | bytes 262176 | tf_op jit(solution)/shard_map/ppermute | solution.py:321
  56.0 1.6 %collective-permute-start.25 = (bf16[64,2048]{1,0:T(8,128)(2,1)S(1)}, bf16[64,2048]{1,0:T(8,128)(2,1)S(1)}, u32[]{:S(2)}, u32[]{:S(2)}) collective-permute-start(bf16[64,2048]{1,0:T(8,128)(2,1)S(1)} %collective-permute-done.20.refs_1_), channel_id=1, source_target_pairs={{4,0},{5,1},{8,4},{9,5},{12,8},{13,9},{14,12},{15,13},{10,14},{11,... | collective-permute-start | bytes 786440 | tf_op jit(solution)/shard_map/ppermute | solution.py:321
  57.6 1.8 %experts.10 = (bf16[64,2048]{1,0:T(8,128)(2,1)S(1)}, bf16[64,2048]{1,0:T(8,128)(2,1)S(1)}) custom-call(bf16[64,2048]{1,0:T(8,128)(2,1)S(1)} %collective-permute-done.18.refs_0_, bf16[64,2048]{1,0:T(8,128)(2,1)S(1)} %collective-permute-done.20.refs_1_, bf16[144,512]{1,0:T(8,128)(2,1)S(1)} %collective-permute-done.1.refs_4_.refs_2_, ...), custom_call_target="tpu_custom_call" | custom-call | flops 1207959552 | bytes 9437184 | tf_op jit(solution)/shard_map/experts/pallas_call | solution.py:281
  59.5 1.7 %collective-permute-done.26.refs_0_ = bf16[64,2048]{1,0:T(8,128)(2,1)S(1)} collective-permute-done((bf16[64,2048]{1,0:T(8,128)(2,1)S(1)}, bf16[64,2048]{1,0:T(8,128)(2,1)S(1)}, u32[]{:S(2)}, u32[]{:S(2)}) %collective-permute-start.26) | collective-permute-done | bytes 262176 | tf_op jit(solution)/shard_map/ppermute | solution.py:321
  61.7 1.6 %collective-permute-start.30 = (bf16[64,2048]{1,0:T(8,128)(2,1)S(1)}, bf16[64,2048]{1,0:T(8,128)(2,1)S(1)}, u32[]{:S(2)}, u32[]{:S(2)}) collective-permute-start(bf16[64,2048]{1,0:T(8,128)(2,1)S(1)} %collective-permute-done.27.refs_1_), channel_id=1, source_target_pairs={{4,0},{5,1},{8,4},{9,5},{12,8},{13,9},{14,12},{15,13},{10,14},{11,... | collective-permute-start | bytes 786440 | tf_op jit(solution)/shard_map/ppermute | solution.py:321
  63.3 1.8 %experts.11 = (bf16[64,2048]{1,0:T(8,128)(2,1)S(1)}, bf16[64,2048]{1,0:T(8,128)(2,1)S(1)}) custom-call(bf16[64,2048]{1,0:T(8,128)(2,1)S(1)} %collective-permute-done.26.refs_0_, bf16[64,2048]{1,0:T(8,128)(2,1)S(1)} %collective-permute-done.27.refs_1_, bf16[144,512]{1,0:T(8,128)(2,1)S(1)} %collective-permute-done.1.refs_4_.refs_2_, ...), custom_call_target="tpu_custom_call" | custom-call | flops 1207959552 | bytes 9437184 | tf_op jit(solution)/shard_map/experts/pallas_call | solution.py:281
  65.1 1.7 %collective-permute-done.24.refs_0_ = bf16[64,2048]{1,0:T(8,128)(2,1)S(1)} collective-permute-done((bf16[64,2048]{1,0:T(8,128)(2,1)S(1)}, bf16[64,2048]{1,0:T(8,128)(2,1)S(1)}, u32[]{:S(2)}, u32[]{:S(2)}) %collective-permute-start.24) | collective-permute-done | bytes 262176 | tf_op jit(solution)/shard_map/ppermute | solution.py:321
  67.3 1.8 %experts.12 = (bf16[64,2048]{1,0:T(8,128)(2,1)S(1)}, bf16[64,2048]{1,0:T(8,128)(2,1)S(1)}) custom-call(bf16[64,2048]{1,0:T(8,128)(2,1)S(1)} %collective-permute-done.24.refs_0_, bf16[64,2048]{1,0:T(8,128)(2,1)S(1)} %collective-permute-done.25.refs_1_, bf16[144,512]{1,0:T(8,128)(2,1)S(1)} %collective-permute-done.3.refs_5_.refs_2_, ...), custom_call_target="tpu_custom_call" | custom-call | flops 1207959552 | bytes 9437184 | tf_op jit(solution)/shard_map/experts/pallas_call | solution.py:281
  69.1 3.3 %collective-permute-done.29.refs_0_ = bf16[64,2048]{1,0:T(8,128)(2,1)S(1)} collective-permute-done((bf16[64,2048]{1,0:T(8,128)(2,1)S(1)}, bf16[64,2048]{1,0:T(8,128)(2,1)S(1)}, u32[]{:S(2)}, u32[]{:S(2)}) %collective-permute-start.29) | collective-permute-done | bytes 262176 | tf_op jit(solution)/shard_map/ppermute | solution.py:321
  72.9 1.8 %experts.13 = (bf16[64,2048]{1,0:T(8,128)(2,1)S(1)}, bf16[64,2048]{1,0:T(8,128)(2,1)S(1)}) custom-call(bf16[64,2048]{1,0:T(8,128)(2,1)S(1)} %collective-permute-done.29.refs_0_, bf16[64,2048]{1,0:T(8,128)(2,1)S(1)} %collective-permute-done.30.refs_1_, bf16[144,512]{1,0:T(8,128)(2,1)S(1)} %collective-permute-done.3.refs_5_.refs_2_, ...), custom_call_target="tpu_custom_call" | custom-call | flops 1207959552 | bytes 9437184 | tf_op jit(solution)/shard_map/experts/pallas_call | solution.py:281
  74.8 1.6 %collective-permute-start.32 = (bf16[64,2048]{1,0:T(8,128)(2,1)S(1)}, bf16[64,2048]{1,0:T(8,128)(2,1)S(1)}, u32[]{:S(2)}, u32[]{:S(2)}) collective-permute-start(bf16[64,2048]{1,0:T(8,128)(2,1)S(1)} %get-tuple-element.215), channel_id=1, source_target_pairs={{0,4},{1,5},{4,8},{5,9},{8,12},{9,13},{12,14},{13,15},{14,10},{15,... | collective-permute-start | bytes 786440 | tf_op jit(solution)/shard_map/ppermute | solution.py:321
  78.1 3.4 %collective-permute-done.31.refs_1_ = bf16[64,2048]{1,0:T(8,128)(2,1)S(1)} collective-permute-done((bf16[64,2048]{1,0:T(8,128)(2,1)S(1)}, bf16[64,2048]{1,0:T(8,128)(2,1)S(1)}, u32[]{:S(2)}, u32[]{:S(2)}) %collective-permute-start.31) | collective-permute-done | bytes 262176 | tf_op jit(solution)/shard_map/ppermute | solution.py:321
  81.5 1.8 %experts.14 = (bf16[64,2048]{1,0:T(8,128)(2,1)S(1)}, bf16[64,2048]{1,0:T(8,128)(2,1)S(1)}) custom-call(bf16[64,2048]{1,0:T(8,128)(2,1)S(1)} %collective-permute-done.28.refs_0_, bf16[64,2048]{1,0:T(8,128)(2,1)S(1)} %collective-permute-done.31.refs_1_, bf16[144,512]{1,0:T(8,128)(2,1)S(1)} %collective-permute-done.13.refs_2_.refs_16_, ...), custom_call_target="tpu_custom_call" | custom-call | flops 1207959552 | bytes 9437184 | tf_op jit(solution)/shard_map/experts/pallas_call | solution.py:281
  84.1 1.6 %collective-permute-start.38 = (bf16[64,2048]{1,0:T(8,128)(2,1)S(1)}, bf16[64,2048]{1,0:T(8,128)(2,1)S(1)}, u32[]{:S(2)}, u32[]{:S(2)}) collective-permute-start(bf16[64,2048]{1,0:T(8,128)(2,1)S(1)} %get-tuple-element.218), channel_id=1, source_target_pairs={{4,0},{5,1},{8,4},{9,5},{12,8},{13,9},{14,12},{15,13},{10,14},{11,... | collective-permute-start | bytes 786440 | tf_op jit(solution)/shard_map/ppermute | solution.py:321
  85.6 1.5 %collective-permute-done.33 = bf16[64,2048]{1,0:T(8,128)(2,1)S(1)} collective-permute-done((bf16[64,2048]{1,0:T(8,128)(2,1)S(1)}, bf16[64,2048]{1,0:T(8,128)(2,1)S(1)}, u32[]{:S(2)}, u32[]{:S(2)}) %collective-permute-start.33) | collective-permute-done | bytes 262176 | tf_op jit(solution)/shard_map/ppermute | solution.py:321
  87.1 1.8 %experts.15 = (bf16[64,2048]{1,0:T(8,128)(2,1)S(1)}, bf16[64,2048]{1,0:T(8,128)(2,1)S(1)}) custom-call(bf16[64,2048]{1,0:T(8,128)(2,1)S(1)} %get-tuple-element.148.refs_0_, bf16[64,2048]{1,0:T(8,128)(2,1)S(1)} %get-tuple-element.168.refs_1_, bf16[144,512]{1,0:T(8,128)(2,1)S(1)} %copy-done.3, bf16[1,2048,384]{2,1,0:T(8,128)(2,1)S(1)} %copy-done, ...), custom_call_target="tpu_custom_call" | custom-call | flops 1207959552 | bytes 9437184 | tf_op jit(solution)/shard_map/experts/pallas_call | solution.py:281
  89.0 2.4 %collective-permute-done.34 = bf16[64,2048]{1,0:T(8,128)(2,1)S(1)} collective-permute-done((bf16[64,2048]{1,0:T(8,128)(2,1)S(1)}, bf16[64,2048]{1,0:T(8,128)(2,1)S(1)}, u32[]{:S(2)}, u32[]{:S(2)}) %collective-permute-start.34) | collective-permute-done | bytes 262176 | tf_op jit(solution)/shard_map/ppermute | solution.py:321
  92.7 1.5 %collective-permute-start.40 = (bf16[64,2048]{1,0:T(8,128)(2,1)S(1)}, bf16[64,2048]{1,0:T(8,128)(2,1)S(1)}, u32[]{:S(2)}, u32[]{:S(2)}) collective-permute-start(bf16[64,2048]{1,0:T(8,128)(2,1)S(1)} %add_convert_fusion.8), channel_id=1, source_target_pairs={{4,0},{5,1},{8,4},{9,5},{12,8},{13,9},{14,12},{15,13},{10,14},{11,... | collective-permute-start | bytes 786440 | tf_op jit(solution)/shard_map/ppermute | solution.py:321
  94.3 1.6 %collective-permute-start.39 = (bf16[64,2048]{1,0:T(8,128)(2,1)S(1)}, bf16[64,2048]{1,0:T(8,128)(2,1)S(1)}, u32[]{:S(2)}, u32[]{:S(2)}) collective-permute-start(bf16[64,2048]{1,0:T(8,128)(2,1)S(1)} %add_convert_fusion.7), channel_id=1, source_target_pairs={{4,0},{5,1},{8,4},{9,5},{12,8},{13,9},{14,12},{15,13},{10,14},{11,... | collective-permute-start | bytes 786440 | tf_op jit(solution)/shard_map/ppermute | solution.py:321
  95.9 4.8 %collective-permute-done.35 = bf16[64,2048]{1,0:T(8,128)(2,1)S(1)} collective-permute-done((bf16[64,2048]{1,0:T(8,128)(2,1)S(1)}, bf16[64,2048]{1,0:T(8,128)(2,1)S(1)}, u32[]{:S(2)}, u32[]{:S(2)}) %collective-permute-start.35) | collective-permute-done | bytes 262176 | tf_op jit(solution)/shard_map/ppermute | solution.py:321
  101.3 5.0 %collective-permute-done.42 = bf16[64,2048]{1,0:T(8,128)(2,1)S(1)} collective-permute-done((bf16[64,2048]{1,0:T(8,128)(2,1)S(1)}, bf16[64,2048]{1,0:T(8,128)(2,1)S(1)}, u32[]{:S(2)}, u32[]{:S(2)}) %collective-permute-start.42) | collective-permute-done | bytes 262176 | tf_op jit(solution)/shard_map/ppermute | solution.py:321
  107.0 1.6 %collective-permute-start.44 = (bf16[64,2048]{1,0:T(8,128)(2,1)S(1)}, bf16[64,2048]{1,0:T(8,128)(2,1)S(1)}, u32[]{:S(2)}, u32[]{:S(2)}) collective-permute-start(bf16[64,2048]{1,0:T(8,128)(2,1)S(1)} %add_convert_fusion.6), channel_id=1, source_target_pairs={{4,0},{5,1},{8,4},{9,5},{12,8},{13,9},{14,12},{15,13},{10,14},{11,... | collective-permute-start | bytes 786440 | tf_op jit(solution)/shard_map/ppermute | solution.py:321
  109.3 2.7 %collective-permute-done.36 = bf16[64,2048]{1,0:T(8,128)(2,1)S(1)} collective-permute-done((bf16[64,2048]{1,0:T(8,128)(2,1)S(1)}, bf16[64,2048]{1,0:T(8,128)(2,1)S(1)}, u32[]{:S(2)}, u32[]{:S(2)}) %collective-permute-start.36) | collective-permute-done | bytes 262176 | tf_op jit(solution)/shard_map/ppermute | solution.py:321
  113.5 1.6 %collective-permute-start.45 = (bf16[64,2048]{1,0:T(8,128)(2,1)S(1)}, bf16[64,2048]{1,0:T(8,128)(2,1)S(1)}, u32[]{:S(2)}, u32[]{:S(2)}) collective-permute-start(bf16[64,2048]{1,0:T(8,128)(2,1)S(1)} %add_convert_fusion.1), channel_id=1, source_target_pairs={{4,0},{5,1},{8,4},{9,5},{12,8},{13,9},{14,12},{15,13},{10,14},{11,... | collective-permute-start | bytes 786440 | tf_op jit(solution)/shard_map/ppermute | solution.py:321
  116.2 2.2 %collective-permute-done.37 = bf16[64,2048]{1,0:T(8,128)(2,1)S(1)} collective-permute-done((bf16[64,2048]{1,0:T(8,128)(2,1)S(1)}, bf16[64,2048]{1,0:T(8,128)(2,1)S(1)}, u32[]{:S(2)}, u32[]{:S(2)}) %collective-permute-start.37) | collective-permute-done | bytes 262176 | tf_op jit(solution)/shard_map/ppermute | solution.py:321
  118.6 1.3 %collective-permute-done.45 = bf16[64,2048]{1,0:T(8,128)(2,1)S(1)} collective-permute-done((bf16[64,2048]{1,0:T(8,128)(2,1)S(1)}, bf16[64,2048]{1,0:T(8,128)(2,1)S(1)}, u32[]{:S(2)}, u32[]{:S(2)}) %collective-permute-start.45) | collective-permute-done | bytes 262176 | tf_op jit(solution)/shard_map/ppermute | solution.py:321
  (84 shorter events, 19.1 us)
Async XLA Ops:
  0.0 17.5 %copy-start.5 = (f32[2048]{0:T(1024)S(1)}, f32[2048]{0:T(1024)}, u32[]{:S(2)}) copy-start(f32[2048]{0:T(1024)} %param.16) | copy-start | bytes 24580
  2.3 23.4 %copy-start.3 = (bf16[144,512]{1,0:T(8,128)(2,1)S(1)}, bf16[144,512]{1,0:T(8,128)(2,1)}, u32[]{:S(2)}) copy-start(bf16[144,512]{1,0:T(8,128)(2,1)} %pack_message.1.refs_1_.refs_2_) | copy-start | bytes 442372
  2.3 7.2 %collective-permute-start.2 = (bf16[144,512]{1,0:T(8,128)(2,1)}, bf16[144,512]{1,0:T(8,128)(2,1)S(1)}, u32[]{:S(2)}, u32[]{:S(2)}) collective-permute-start(bf16[144,512]{1,0:T(8,128)(2,1)} %pack_message.1.refs_1_.refs_2_), channel_id=1, source_target_pairs={{4,0},{5,1},{8,4},{9,5},{12,8},{13,9},{14,12},{15,13},{10,14},{11,... | collective-permute-start | bytes 442376 | tf_op jit(solution)/shard_map/ppermute | solution.py:321
  5.2 5.5 %collective-permute-start = (bf16[144,512]{1,0:T(8,128)(2,1)}, bf16[144,512]{1,0:T(8,128)(2,1)S(1)}, u32[]{:S(2)}, u32[]{:S(2)}) collective-permute-start(bf16[144,512]{1,0:T(8,128)(2,1)} %pack_message.1.refs_1_.refs_2_), channel_id=1, source_target_pairs={{0,4},{1,5},{4,8},{5,9},{8,12},{9,13},{12,14},{13,15},{14,10},{15,... | collective-permute-start | bytes 442376 | tf_op jit(solution)/shard_map/ppermute | solution.py:321
  5.3 14.3 %collective-permute-start.6 = (bf16[144,512]{1,0:T(8,128)(2,1)}, bf16[144,512]{1,0:T(8,128)(2,1)S(1)}, u32[]{:S(2)}, u32[]{:S(2)}) collective-permute-start(bf16[144,512]{1,0:T(8,128)(2,1)} %pack_message.1.refs_1_.refs_2_), channel_id=1, source_target_pairs={{0,1},{1,0},{2,3},{3,2},{4,5},{5,4},{6,7},{7,6},{8,9},{9,8},{10,11... | collective-permute-start | bytes 442376 | tf_op jit(solution)/shard_map/ppermute | solution.py:321
  10.8 6.8 %collective-permute-start.4 = (bf16[144,512]{1,0:T(8,128)(2,1)S(1)}, bf16[144,512]{1,0:T(8,128)(2,1)S(1)}, u32[]{:S(2)}, u32[]{:S(2)}) collective-permute-start(bf16[144,512]{1,0:T(8,128)(2,1)S(1)} %collective-permute-done.2.refs_6_.refs_3_), channel_id=1, source_target_pairs={{4,0},{5,1},{8,4},{9,5},{12,8},{13,9},{14,12},{15,13},{10,14},{11,... | collective-permute-start | bytes 442376 | tf_op jit(solution)/shard_map/ppermute | solution.py:321
  12.3 5.1 %collective-permute-start.1 = (bf16[144,512]{1,0:T(8,128)(2,1)S(1)}, bf16[144,512]{1,0:T(8,128)(2,1)S(1)}, u32[]{:S(2)}, u32[]{:S(2)}) collective-permute-start(bf16[144,512]{1,0:T(8,128)(2,1)S(1)} %collective-permute-done.refs_3_.refs_2_), channel_id=1, source_target_pairs={{0,4},{1,5},{4,8},{5,9},{8,12},{9,13},{12,14},{13,15},{14,10},{15,... | collective-permute-start | bytes 442376 | tf_op jit(solution)/shard_map/ppermute | solution.py:321
  14.0 6.1 %collective-permute-start.10 = (bf16[144,512]{1,0:T(8,128)(2,1)S(1)}, bf16[144,512]{1,0:T(8,128)(2,1)S(1)}, u32[]{:S(2)}, u32[]{:S(2)}) collective-permute-start(bf16[144,512]{1,0:T(8,128)(2,1)S(1)} %collective-permute-done.2.refs_6_.refs_3_), channel_id=1, source_target_pairs={{0,1},{1,0},{2,3},{3,2},{4,5},{5,4},{6,7},{7,6},{8,9},{9,8},{10,11... | collective-permute-start | bytes 442376 | tf_op jit(solution)/shard_map/ppermute | solution.py:321
  17.5 5.2 %collective-permute-start.5 = (bf16[144,512]{1,0:T(8,128)(2,1)S(1)}, bf16[144,512]{1,0:T(8,128)(2,1)S(1)}, u32[]{:S(2)}, u32[]{:S(2)}) collective-permute-start(bf16[144,512]{1,0:T(8,128)(2,1)S(1)} %collective-permute-done.4.refs_7_.refs_3_), channel_id=1, source_target_pairs={{4,0},{5,1},{8,4},{9,5},{12,8},{13,9},{14,12},{15,13},{10,14},{11,... | collective-permute-start | bytes 442376 | tf_op jit(solution)/shard_map/ppermute | solution.py:321
  19.2 5.1 %collective-permute-start.3 = (bf16[144,512]{1,0:T(8,128)(2,1)S(1)}, bf16[144,512]{1,0:T(8,128)(2,1)S(1)}, u32[]{:S(2)}, u32[]{:S(2)}) collective-permute-start(bf16[144,512]{1,0:T(8,128)(2,1)S(1)} %collective-permute-done.1.refs_4_.refs_2_), channel_id=1, source_target_pairs={{0,4},{1,5},{4,8},{5,9},{8,12},{9,13},{12,14},{13,15},{14,10},{15,... | collective-permute-start | bytes 442376 | tf_op jit(solution)/shard_map/ppermute | solution.py:321
  19.6 4.7 %collective-permute-start.7 = (bf16[144,512]{1,0:T(8,128)(2,1)S(1)}, bf16[144,512]{1,0:T(8,128)(2,1)S(1)}, u32[]{:S(2)}, u32[]{:S(2)}) collective-permute-start(bf16[144,512]{1,0:T(8,128)(2,1)S(1)} %collective-permute-done.refs_3_.refs_2_), channel_id=1, source_target_pairs={{0,1},{1,0},{2,3},{3,2},{4,5},{5,4},{6,7},{7,6},{8,9},{9,8},{10,11... | collective-permute-start | bytes 442376 | tf_op jit(solution)/shard_map/ppermute | solution.py:321
  19.6 5.2 %collective-permute-start.8 = (bf16[144,512]{1,0:T(8,128)(2,1)S(1)}, bf16[144,512]{1,0:T(8,128)(2,1)S(1)}, u32[]{:S(2)}, u32[]{:S(2)}) collective-permute-start(bf16[144,512]{1,0:T(8,128)(2,1)S(1)} %collective-permute-done.1.refs_4_.refs_2_), channel_id=1, source_target_pairs={{0,1},{1,0},{2,3},{3,2},{4,5},{5,4},{6,7},{7,6},{8,9},{9,8},{10,11... | collective-permute-start | bytes 442376 | tf_op jit(solution)/shard_map/ppermute | solution.py:321
  20.1 4.6 %collective-permute-start.11 = (bf16[144,512]{1,0:T(8,128)(2,1)S(1)}, bf16[144,512]{1,0:T(8,128)(2,1)S(1)}, u32[]{:S(2)}, u32[]{:S(2)}) collective-permute-start(bf16[144,512]{1,0:T(8,128)(2,1)S(1)} %collective-permute-done.4.refs_7_.refs_3_), channel_id=1, source_target_pairs={{0,1},{1,0},{2,3},{3,2},{4,5},{5,4},{6,7},{7,6},{8,9},{9,8},{10,11... | collective-permute-start | bytes 442376 | tf_op jit(solution)/shard_map/ppermute | solution.py:321
  22.7 2.0 %collective-permute-start.12 = (bf16[144,512]{1,0:T(8,128)(2,1)S(1)}, bf16[144,512]{1,0:T(8,128)(2,1)S(1)}, u32[]{:S(2)}, u32[]{:S(2)}) collective-permute-start(bf16[144,512]{1,0:T(8,128)(2,1)S(1)} %collective-permute-done.5.refs_8_.refs_3_), channel_id=1, source_target_pairs={{0,1},{1,0},{2,3},{3,2},{4,5},{5,4},{6,7},{7,6},{8,9},{9,8},{10,11... | collective-permute-start | bytes 442376 | tf_op jit(solution)/shard_map/ppermute | solution.py:321
  24.3 1.4 %collective-permute-start.9 = (bf16[144,512]{1,0:T(8,128)(2,1)S(1)}, bf16[144,512]{1,0:T(8,128)(2,1)S(1)}, u32[]{:S(2)}, u32[]{:S(2)}) collective-permute-start(bf16[144,512]{1,0:T(8,128)(2,1)S(1)} %collective-permute-done.3.refs_5_.refs_2_), channel_id=1, source_target_pairs={{0,1},{1,0},{2,3},{3,2},{4,5},{5,4},{6,7},{7,6},{8,9},{9,8},{10,11... | collective-permute-start | bytes 442376 | tf_op jit(solution)/shard_map/ppermute | solution.py:321
  24.3 6.3 %collective-permute-start.13 = (bf16[144,512]{1,0:T(8,128)(2,1)S(1)}, bf16[144,512]{1,0:T(8,128)(2,1)S(1)}, u32[]{:S(2)}, u32[]{:S(2)}) collective-permute-start(bf16[144,512]{1,0:T(8,128)(2,1)S(1)} %collective-permute-done.3.refs_5_.refs_2_), channel_id=1, source_target_pairs={{0,4},{1,5},{4,8},{5,9},{8,12},{9,13},{12,14},{13,15},{14,10},{15,... | collective-permute-start | bytes 442376 | tf_op jit(solution)/shard_map/ppermute | solution.py:321
  30.6 1.4 %collective-permute-start.14 = (bf16[144,512]{1,0:T(8,128)(2,1)S(1)}, bf16[144,512]{1,0:T(8,128)(2,1)S(1)}, u32[]{:S(2)}, u32[]{:S(2)}) collective-permute-start(bf16[144,512]{1,0:T(8,128)(2,1)S(1)} %collective-permute-done.13.refs_2_.refs_16_), channel_id=1, source_target_pairs={{0,1},{1,0},{2,3},{3,2},{4,5},{5,4},{6,7},{7,6},{8,9},{9,8},{10,11... | collective-permute-start | bytes 442376 | tf_op jit(solution)/shard_map/ppermute | solution.py:321
  31.9 7.1 %collective-permute-start.15 = (bf16[1,2048,384]{2,1,0:T(8,128)(2,1)S(1)}, bf16[1,2048,384]{2,1,0:T(8,128)(2,1)S(1)}, u32[]{:S(2)}, u32[]{:S(2)}) collective-permute-start(bf16[1,2048,384]{2,1,0:T(8,128)(2,1)S(1)} %copy-done), channel_id=1, source_target_pairs={{0,1},{1,0},{2,3},{3,2},{4,5},{5,4},{6,7},{7,6},{8,9},{9,8},{10,11... | collective-permute-start | bytes 4718600 | tf_op jit(solution)/shard_map/ppermute | solution.py:321
  32.1 7.0 %collective-permute-start.16 = (bf16[1,2048,384]{2,1,0:T(8,128)(2,1)S(1)}, bf16[1,2048,384]{2,1,0:T(8,128)(2,1)S(1)}, u32[]{:S(2)}, u32[]{:S(2)}) collective-permute-start(bf16[1,2048,384]{2,1,0:T(8,128)(2,1)S(1)} %copy-done.1), channel_id=1, source_target_pairs={{0,1},{1,0},{2,3},{3,2},{4,5},{5,4},{6,7},{7,6},{8,9},{9,8},{10,11... | collective-permute-start | bytes 4718600 | tf_op jit(solution)/shard_map/ppermute | solution.py:321
  32.5 12.4 %collective-permute-start.23 = (bf16[1,384,2048]{2,1,0:T(8,128)(2,1)S(1)}, bf16[1,384,2048]{2,1,0:T(8,128)(2,1)S(1)}, u32[]{:S(2)}, u32[]{:S(2)}) collective-permute-start(bf16[1,384,2048]{2,1,0:T(8,128)(2,1)S(1)} %copy-done.2), channel_id=1, source_target_pairs={{0,1},{1,0},{2,3},{3,2},{4,5},{5,4},{6,7},{7,6},{8,9},{9,8},{10,11... | collective-permute-start | bytes 4718600 | tf_op jit(solution)/shard_map/ppermute | solution.py:321
  33.7 9.2 %collective-permute-start.19 = (bf16[64,2048]{1,0:T(8,128)(2,1)S(1)}, bf16[64,2048]{1,0:T(8,128)(2,1)S(1)}, u32[]{:S(2)}, u32[]{:S(2)}) collective-permute-start(bf16[64,2048]{1,0:T(8,128)(2,1)S(1)} %get-tuple-element.148.refs_0_), channel_id=1, source_target_pairs={{4,0},{5,1},{8,4},{9,5},{12,8},{13,9},{14,12},{15,13},{10,14},{11,... | collective-permute-start | bytes 786440 | tf_op jit(solution)/shard_map/ppermute | solution.py:321
  35.3 9.1 %collective-permute-start.17 = (bf16[64,2048]{1,0:T(8,128)(2,1)S(1)}, bf16[64,2048]{1,0:T(8,128)(2,1)S(1)}, u32[]{:S(2)}, u32[]{:S(2)}) collective-permute-start(bf16[64,2048]{1,0:T(8,128)(2,1)S(1)} %get-tuple-element.148.refs_0_), channel_id=1, source_target_pairs={{0,4},{1,5},{4,8},{5,9},{8,12},{9,13},{12,14},{13,15},{14,10},{15,... | collective-permute-start | bytes 786440 | tf_op jit(solution)/shard_map/ppermute | solution.py:321
  39.1 9.4 %collective-permute-start.22 = (bf16[64,2048]{1,0:T(8,128)(2,1)S(1)}, bf16[64,2048]{1,0:T(8,128)(2,1)S(1)}, u32[]{:S(2)}, u32[]{:S(2)}) collective-permute-start(bf16[64,2048]{1,0:T(8,128)(2,1)S(1)} %get-tuple-element.168.refs_1_), channel_id=1, source_target_pairs={{4,0},{5,1},{8,4},{9,5},{12,8},{13,9},{14,12},{15,13},{10,14},{11,... | collective-permute-start | bytes 786440 | tf_op jit(solution)/shard_map/ppermute | solution.py:321
  40.7 9.2 %collective-permute-start.21 = (bf16[64,2048]{1,0:T(8,128)(2,1)S(1)}, bf16[64,2048]{1,0:T(8,128)(2,1)S(1)}, u32[]{:S(2)}, u32[]{:S(2)}) collective-permute-start(bf16[64,2048]{1,0:T(8,128)(2,1)S(1)} %get-tuple-element.168.refs_1_), channel_id=1, source_target_pairs={{0,4},{1,5},{4,8},{5,9},{8,12},{9,13},{12,14},{13,15},{14,10},{15,... | collective-permute-start | bytes 786440 | tf_op jit(solution)/shard_map/ppermute | solution.py:321
  42.9 11.2 %collective-permute-start.20 = (bf16[64,2048]{1,0:T(8,128)(2,1)S(1)}, bf16[64,2048]{1,0:T(8,128)(2,1)S(1)}, u32[]{:S(2)}, u32[]{:S(2)}) collective-permute-start(bf16[64,2048]{1,0:T(8,128)(2,1)S(1)} %collective-permute-done.19.refs_1_), channel_id=1, source_target_pairs={{4,0},{5,1},{8,4},{9,5},{12,8},{13,9},{14,12},{15,13},{10,14},{11,... | collective-permute-start | bytes 786440 | tf_op jit(solution)/shard_map/ppermute | solution.py:321
  44.4 11.2 %collective-permute-start.18 = (bf16[64,2048]{1,0:T(8,128)(2,1)S(1)}, bf16[64,2048]{1,0:T(8,128)(2,1)S(1)}, u32[]{:S(2)}, u32[]{:S(2)}) collective-permute-start(bf16[64,2048]{1,0:T(8,128)(2,1)S(1)} %collective-permute-done.17.refs_0_), channel_id=1, source_target_pairs={{0,4},{1,5},{4,8},{5,9},{8,12},{9,13},{12,14},{13,15},{14,10},{15,... | collective-permute-start | bytes 786440 | tf_op jit(solution)/shard_map/ppermute | solution.py:321
  50.0 11.2 %collective-permute-start.26 = (bf16[64,2048]{1,0:T(8,128)(2,1)S(1)}, bf16[64,2048]{1,0:T(8,128)(2,1)S(1)}, u32[]{:S(2)}, u32[]{:S(2)}) collective-permute-start(bf16[64,2048]{1,0:T(8,128)(2,1)S(1)} %collective-permute-done.21.refs_0_), channel_id=1, source_target_pairs={{0,4},{1,5},{4,8},{5,9},{8,12},{9,13},{12,14},{13,15},{14,10},{15,... | collective-permute-start | bytes 786440 | tf_op jit(solution)/shard_map/ppermute | solution.py:321
  50.4 10.8 %collective-permute-start.27 = (bf16[64,2048]{1,0:T(8,128)(2,1)S(1)}, bf16[64,2048]{1,0:T(8,128)(2,1)S(1)}, u32[]{:S(2)}, u32[]{:S(2)}) collective-permute-start(bf16[64,2048]{1,0:T(8,128)(2,1)S(1)} %collective-permute-done.22.refs_1_), channel_id=1, source_target_pairs={{4,0},{5,1},{8,4},{9,5},{12,8},{13,9},{14,12},{15,13},{10,14},{11,... | collective-permute-start | bytes 786440 | tf_op jit(solution)/shard_map/ppermute | solution.py:321
  55.6 11.2 %collective-permute-start.24 = (bf16[64,2048]{1,0:T(8,128)(2,1)S(1)}, bf16[64,2048]{1,0:T(8,128)(2,1)S(1)}, u32[]{:S(2)}, u32[]{:S(2)}) collective-permute-start(bf16[64,2048]{1,0:T(8,128)(2,1)S(1)} %collective-permute-done.18.refs_0_), channel_id=1, source_target_pairs={{0,4},{1,5},{4,8},{5,9},{8,12},{9,13},{12,14},{13,15},{14,10},{15,... | collective-permute-start | bytes 786440 | tf_op jit(solution)/shard_map/ppermute | solution.py:321
  56.0 10.8 %collective-permute-start.25 = (bf16[64,2048]{1,0:T(8,128)(2,1)S(1)}, bf16[64,2048]{1,0:T(8,128)(2,1)S(1)}, u32[]{:S(2)}, u32[]{:S(2)}) collective-permute-start(bf16[64,2048]{1,0:T(8,128)(2,1)S(1)} %collective-permute-done.20.refs_1_), channel_id=1, source_target_pairs={{4,0},{5,1},{8,4},{9,5},{12,8},{13,9},{14,12},{15,13},{10,14},{11,... | collective-permute-start | bytes 786440 | tf_op jit(solution)/shard_map/ppermute | solution.py:321
  61.2 11.2 %collective-permute-start.29 = (bf16[64,2048]{1,0:T(8,128)(2,1)S(1)}, bf16[64,2048]{1,0:T(8,128)(2,1)S(1)}, u32[]{:S(2)}, u32[]{:S(2)}) collective-permute-start(bf16[64,2048]{1,0:T(8,128)(2,1)S(1)} %collective-permute-done.26.refs_0_), channel_id=1, source_target_pairs={{0,4},{1,5},{4,8},{5,9},{8,12},{9,13},{12,14},{13,15},{14,10},{15,... | collective-permute-start | bytes 786440 | tf_op jit(solution)/shard_map/ppermute | solution.py:321
  61.7 10.8 %collective-permute-start.30 = (bf16[64,2048]{1,0:T(8,128)(2,1)S(1)}, bf16[64,2048]{1,0:T(8,128)(2,1)S(1)}, u32[]{:S(2)}, u32[]{:S(2)}) collective-permute-start(bf16[64,2048]{1,0:T(8,128)(2,1)S(1)} %collective-permute-done.27.refs_1_), channel_id=1, source_target_pairs={{4,0},{5,1},{8,4},{9,5},{12,8},{13,9},{14,12},{15,13},{10,14},{11,... | collective-permute-start | bytes 786440 | tf_op jit(solution)/shard_map/ppermute | solution.py:321
  66.8 11.2 %collective-permute-start.28 = (bf16[64,2048]{1,0:T(8,128)(2,1)S(1)}, bf16[64,2048]{1,0:T(8,128)(2,1)S(1)}, u32[]{:S(2)}, u32[]{:S(2)}) collective-permute-start(bf16[64,2048]{1,0:T(8,128)(2,1)S(1)} %collective-permute-done.24.refs_0_), channel_id=1, source_target_pairs={{0,4},{1,5},{4,8},{5,9},{8,12},{9,13},{12,14},{13,15},{14,10},{15,... | collective-permute-start | bytes 786440 | tf_op jit(solution)/shard_map/ppermute | solution.py:321
  72.5 9.0 %collective-permute-start.31 = (bf16[64,2048]{1,0:T(8,128)(2,1)S(1)}, bf16[64,2048]{1,0:T(8,128)(2,1)S(1)}, u32[]{:S(2)}, u32[]{:S(2)}) collective-permute-start(bf16[64,2048]{1,0:T(8,128)(2,1)S(1)} %collective-permute-done.30.refs_1_), channel_id=1, source_target_pairs={{4,0},{5,1},{8,4},{9,5},{12,8},{13,9},{14,12},{15,13},{10,14},{11,... | collective-permute-start | bytes 786440 | tf_op jit(solution)/shard_map/ppermute | solution.py:321
  74.8 12.3 %collective-permute-start.32 = (bf16[64,2048]{1,0:T(8,128)(2,1)S(1)}, bf16[64,2048]{1,0:T(8,128)(2,1)S(1)}, u32[]{:S(2)}, u32[]{:S(2)}) collective-permute-start(bf16[64,2048]{1,0:T(8,128)(2,1)S(1)} %get-tuple-element.215), channel_id=1, source_target_pairs={{0,4},{1,5},{4,8},{5,9},{8,12},{9,13},{12,14},{13,15},{14,10},{15,... | collective-permute-start | bytes 786440 | tf_op jit(solution)/shard_map/ppermute | solution.py:321
  76.4 10.7 %collective-permute-start.33 = (bf16[64,2048]{1,0:T(8,128)(2,1)S(1)}, bf16[64,2048]{1,0:T(8,128)(2,1)S(1)}, u32[]{:S(2)}, u32[]{:S(2)}) collective-permute-start(bf16[64,2048]{1,0:T(8,128)(2,1)S(1)} %get-tuple-element.219), channel_id=1, source_target_pairs={{4,0},{5,1},{8,4},{9,5},{12,8},{13,9},{14,12},{15,13},{10,14},{11,... | collective-permute-start | bytes 786440 | tf_op jit(solution)/shard_map/ppermute | solution.py:321
  83.3 8.0 %collective-permute-start.34 = (bf16[64,2048]{1,0:T(8,128)(2,1)S(1)}, bf16[64,2048]{1,0:T(8,128)(2,1)S(1)}, u32[]{:S(2)}, u32[]{:S(2)}) collective-permute-start(bf16[64,2048]{1,0:T(8,128)(2,1)S(1)} %get-tuple-element.217), channel_id=1, source_target_pairs={{0,4},{1,5},{4,8},{5,9},{8,12},{9,13},{12,14},{13,15},{14,10},{15,... | collective-permute-start | bytes 786440 | tf_op jit(solution)/shard_map/ppermute | solution.py:321
  84.1 8.5 %collective-permute-start.38 = (bf16[64,2048]{1,0:T(8,128)(2,1)S(1)}, bf16[64,2048]{1,0:T(8,128)(2,1)S(1)}, u32[]{:S(2)}, u32[]{:S(2)}) collective-permute-start(bf16[64,2048]{1,0:T(8,128)(2,1)S(1)} %get-tuple-element.218), channel_id=1, source_target_pairs={{4,0},{5,1},{8,4},{9,5},{12,8},{13,9},{14,12},{15,13},{10,14},{11,... | collective-permute-start | bytes 786440 | tf_op jit(solution)/shard_map/ppermute | solution.py:321
  91.4 9.3 %collective-permute-start.35 = (bf16[64,2048]{1,0:T(8,128)(2,1)S(1)}, bf16[64,2048]{1,0:T(8,128)(2,1)S(1)}, u32[]{:S(2)}, u32[]{:S(2)}) collective-permute-start(bf16[64,2048]{1,0:T(8,128)(2,1)S(1)} %add_convert_fusion.11), channel_id=1, source_target_pairs={{0,4},{1,5},{4,8},{5,9},{8,12},{9,13},{12,14},{13,15},{14,10},{15,... | collective-permute-start | bytes 786440 | tf_op jit(solution)/shard_map/ppermute | solution.py:321
  92.0 14.3 %collective-permute-start.42 = (bf16[64,2048]{1,0:T(8,128)(2,1)S(1)}, bf16[64,2048]{1,0:T(8,128)(2,1)S(1)}, u32[]{:S(2)}, u32[]{:S(2)}) collective-permute-start(bf16[64,2048]{1,0:T(8,128)(2,1)S(1)} %add_convert_fusion.3), channel_id=1, source_target_pairs={{0,4},{1,5},{4,8},{5,9},{8,12},{9,13},{12,14},{13,15},{14,10},{15,... | collective-permute-start | bytes 786440 | tf_op jit(solution)/shard_map/ppermute | solution.py:321
  92.7 14.2 %collective-permute-start.40 = (bf16[64,2048]{1,0:T(8,128)(2,1)S(1)}, bf16[64,2048]{1,0:T(8,128)(2,1)S(1)}, u32[]{:S(2)}, u32[]{:S(2)}) collective-permute-start(bf16[64,2048]{1,0:T(8,128)(2,1)S(1)} %add_convert_fusion.8), channel_id=1, source_target_pairs={{4,0},{5,1},{8,4},{9,5},{12,8},{13,9},{14,12},{15,13},{10,14},{11,... | collective-permute-start | bytes 786440 | tf_op jit(solution)/shard_map/ppermute | solution.py:321
  94.3 14.3 %collective-permute-start.39 = (bf16[64,2048]{1,0:T(8,128)(2,1)S(1)}, bf16[64,2048]{1,0:T(8,128)(2,1)S(1)}, u32[]{:S(2)}, u32[]{:S(2)}) collective-permute-start(bf16[64,2048]{1,0:T(8,128)(2,1)S(1)} %add_convert_fusion.7), channel_id=1, source_target_pairs={{4,0},{5,1},{8,4},{9,5},{12,8},{13,9},{14,12},{15,13},{10,14},{11,... | collective-permute-start | bytes 786440 | tf_op jit(solution)/shard_map/ppermute | solution.py:321
  100.8 11.2 %collective-permute-start.36 = (bf16[64,2048]{1,0:T(8,128)(2,1)S(1)}, bf16[64,2048]{1,0:T(8,128)(2,1)S(1)}, u32[]{:S(2)}, u32[]{:S(2)}) collective-permute-start(bf16[64,2048]{1,0:T(8,128)(2,1)S(1)} %add_convert_fusion.10), channel_id=1, source_target_pairs={{0,4},{1,5},{4,8},{5,9},{8,12},{9,13},{12,14},{13,15},{14,10},{15,... | collective-permute-start | bytes 786440 | tf_op jit(solution)/shard_map/ppermute | solution.py:321
  106.4 12.2 %collective-permute-start.43 = (bf16[64,2048]{1,0:T(8,128)(2,1)S(1)}, bf16[64,2048]{1,0:T(8,128)(2,1)S(1)}, u32[]{:S(2)}, u32[]{:S(2)}) collective-permute-start(bf16[64,2048]{1,0:T(8,128)(2,1)S(1)} %add_convert_fusion.2), channel_id=1, source_target_pairs={{0,4},{1,5},{4,8},{5,9},{8,12},{9,13},{12,14},{13,15},{14,10},{15,... | collective-permute-start | bytes 786440 | tf_op jit(solution)/shard_map/ppermute | solution.py:321
  107.0 6.4 %collective-permute-start.44 = (bf16[64,2048]{1,0:T(8,128)(2,1)S(1)}, bf16[64,2048]{1,0:T(8,128)(2,1)S(1)}, u32[]{:S(2)}, u32[]{:S(2)}) collective-permute-start(bf16[64,2048]{1,0:T(8,128)(2,1)S(1)} %add_convert_fusion.6), channel_id=1, source_target_pairs={{4,0},{5,1},{8,4},{9,5},{12,8},{13,9},{14,12},{15,13},{10,14},{11,... | collective-permute-start | bytes 786440 | tf_op jit(solution)/shard_map/ppermute | solution.py:321
  108.7 7.6 %collective-permute-start.41 = (bf16[64,2048]{1,0:T(8,128)(2,1)S(1)}, bf16[64,2048]{1,0:T(8,128)(2,1)S(1)}, u32[]{:S(2)}, u32[]{:S(2)}) collective-permute-start(bf16[64,2048]{1,0:T(8,128)(2,1)S(1)} %add_convert_fusion.5), channel_id=1, source_target_pairs={{4,0},{5,1},{8,4},{9,5},{12,8},{13,9},{14,12},{15,13},{10,14},{11,... | collective-permute-start | bytes 786440 | tf_op jit(solution)/shard_map/ppermute | solution.py:321
  112.0 6.4 %collective-permute-start.37 = (bf16[64,2048]{1,0:T(8,128)(2,1)S(1)}, bf16[64,2048]{1,0:T(8,128)(2,1)S(1)}, u32[]{:S(2)}, u32[]{:S(2)}) collective-permute-start(bf16[64,2048]{1,0:T(8,128)(2,1)S(1)} %add_convert_fusion.9), channel_id=1, source_target_pairs={{0,4},{1,5},{4,8},{5,9},{8,12},{9,13},{12,14},{13,15},{14,10},{15,... | collective-permute-start | bytes 786440 | tf_op jit(solution)/shard_map/ppermute | solution.py:321
  113.5 6.4 %collective-permute-start.45 = (bf16[64,2048]{1,0:T(8,128)(2,1)S(1)}, bf16[64,2048]{1,0:T(8,128)(2,1)S(1)}, u32[]{:S(2)}, u32[]{:S(2)}) collective-permute-start(bf16[64,2048]{1,0:T(8,128)(2,1)S(1)} %add_convert_fusion.1), channel_id=1, source_target_pairs={{4,0},{5,1},{8,4},{9,5},{12,8},{13,9},{14,12},{15,13},{10,14},{11,... | collective-permute-start | bytes 786440 | tf_op jit(solution)/shard_map/ppermute | solution.py:321
  (4 other events, 57.9 us)

commit v9 on v8

--- a/solution.py
+++ b/solution.py
@@ -190,7 +190,9 @@
         ],
         compiler_params=pltpu.CompilerParams(vmem_limit_bytes=28 * 1024 * 1024),
         cost_estimate=pl.CostEstimate(
-            flops=4 * rows * span * features, bytes_accessed=4 * 1024 * 1024, transcendentals=0
+            flops=4 * rows * span * features if ended else 0,
+            bytes_accessed=4 * 1024 * 1024 if ended else 1024,
+            transcendentals=0,
         ),
         name="attend",
     )(queries, *messages, *inputs)
@@ -338,10 +340,11 @@
             right[hop] = send(right[hop - 1], back)
     plane = [message] + [left[h] for h in range(1, far + 1)] + [right[h] for h in range(1, far)]
     near = [message] + [left[h] for h in range(1, far)] + [right[h] for h in range(1, far)]
-    near = near + [send(m, swap) for m in near]
+    last = [left[far - 1], right[far - 1]]
+    near = near + [send(m, swap) for m in near if all(m is not other for other in last)]
     begun = attend_start(0, staged[0], message, near)
     left[far], begun = tie((left[far], begun))
-    distant = [left[far], send(left[far], swap)]
+    distant = [left[far]] + [send(m, swap) for m in [*last, left[far]]]
     everything = near + distant
     everything, own_weights = tie((everything, (gate_weight, up_weight, down_weight)))
     twin_gate, twin_up, twin_down = [send(w, swap) for w in own_weights]

time: 121 us -> 119 us (0.983)
  waiting for transfers between devices: 57.4 us -> 52.7 us
  starting transfers between devices: 36.1 us -> 38.2 us
    ppermute x46, waiting for transfers between devices: 57.4 us -> 52.7 us  [send(): return lax.ppermute(array, 'ctx', pairs)]
    ppermute x46, starting transfers between devices: 36.1 us -> 38.2 us  [send(): return lax.ppermute(array, 'ctx', pairs)]
  transfers between devices with their start and end apart: 46 -> 46, of which waited for: 27 -> 25; matrix products, arithmetic and copies ran while one was open for 2% -> 2% of each run, Pallas kernels for 18% -> 19%
where the time goes in v9:
time: 119 us; the launch traced here: 118 us
  waiting for transfers between devices  52.7 us (44%)
  starting transfers between devices  38.2 us (32%)
  Pallas kernels  23.5 us (20%)
  other arithmetic  3.01 us (3%)
    ppermute x46, waiting for transfers between devices, send(): return lax.ppermute(array, 'ctx', pairs)  52.7 us
    ppermute x46, starting transfers between devices, send(): return lax.ppermute(array, 'ctx', pairs)  38.2 us
    pallas_call x8, Pallas kernels, run_experts(): pl.pallas_call(functools.partial(expert_kernel, [piece[1:] for piece in p...  14.7 us
    pallas_call x3, Pallas kernels, attend_call(): pl.pallas_call(functools.partial(attend_kernel, count, half, begun, ended...  7.23 us
  transfers between devices with their start and end apart: 46, of which 25 were waited for; matrix products, arithmetic and copies ran while one was open for 2% of the time, Pallas kernels for 19%

profile of v9, /device:TPU:0, one launch (start us, length us, event | category | flops | bytes accessed | tf_op | source)
XLA Modules:
  0.0 118.4 jit_solution(5040924341988002159)
XLA Ops:
  0.7 1.6 %pack_message.1.refs_1_.refs_2_ = bf16[144,512]{1,0:T(8,128)(2,1)} custom-call(s32[1]{0:T(128)S(6)} %copy.12.pos_ref, bf16[128,256]{1,0:T(8,128)(2,1)} %key_ref.1, bf16[128,256]{1,0:T(8,128)(2,1)} %value_ref.1, s32[8,128]{1,0:T(8,128)} %bitcast.2, f32[8,128]{1,0:T(8,128)} %bitcast.3), custom_call_target="tpu_custom_call" | custom-call | tf_op jit(solution)/shard_map/pack_message/pallas_call | solution.py:54
  2.3 3.0 %collective-permute-start.2 = (bf16[144,512]{1,0:T(8,128)(2,1)}, bf16[144,512]{1,0:T(8,128)(2,1)S(1)}, u32[]{:S(2)}, u32[]{:S(2)}) collective-permute-start(bf16[144,512]{1,0:T(8,128)(2,1)} %pack_message.1.refs_1_.refs_2_), channel_id=1, source_target_pairs={{4,0},{5,1},{8,4},{9,5},{12,8},{13,9},{14,12},{15,13},{10,14},{11,... | collective-permute-start | bytes 442376 | tf_op jit(solution)/shard_map/ppermute | solution.py:323
  5.3 4.1 %collective-permute-done.2.refs_6_.refs_3_ = bf16[144,512]{1,0:T(8,128)(2,1)S(1)} collective-permute-done((bf16[144,512]{1,0:T(8,128)(2,1)}, bf16[144,512]{1,0:T(8,128)(2,1)S(1)}, u32[]{:S(2)}, u32[]{:S(2)}) %collective-permute-start.2) | collective-permute-done | bytes 147488 | tf_op jit(solution)/shard_map/ppermute | solution.py:323
  9.4 1.3 %collective-permute-done.refs_3_.refs_2_ = bf16[144,512]{1,0:T(8,128)(2,1)S(1)} collective-permute-done((bf16[144,512]{1,0:T(8,128)(2,1)}, bf16[144,512]{1,0:T(8,128)(2,1)S(1)}, u32[]{:S(2)}, u32[]{:S(2)}) %collective-permute-start) | collective-permute-done | bytes 147488 | tf_op jit(solution)/shard_map/ppermute | solution.py:323
  12.5 1.7 %collective-permute-start.4 = (bf16[144,512]{1,0:T(8,128)(2,1)S(1)}, bf16[144,512]{1,0:T(8,128)(2,1)S(1)}, u32[]{:S(2)}, u32[]{:S(2)}) collective-permute-start(bf16[144,512]{1,0:T(8,128)(2,1)S(1)} %collective-permute-done.2.refs_6_.refs_3_), channel_id=1, source_target_pairs={{4,0},{5,1},{8,4},{9,5},{12,8},{13,9},{14,12},{15,13},{10,14},{11,... | collective-permute-start | bytes 442376 | tf_op jit(solution)/shard_map/ppermute | solution.py:323
  14.3 1.6 %collective-permute-done.1.refs_4_.refs_2_ = bf16[144,512]{1,0:T(8,128)(2,1)S(1)} collective-permute-done((bf16[144,512]{1,0:T(8,128)(2,1)S(1)}, bf16[144,512]{1,0:T(8,128)(2,1)S(1)}, u32[]{:S(2)}, u32[]{:S(2)}) %collective-permute-start.1) | collective-permute-done | bytes 147488 | tf_op jit(solution)/shard_map/ppermute | solution.py:323
  16.3 2.5 %collective-permute-done.4.refs_7_.refs_3_ = bf16[144,512]{1,0:T(8,128)(2,1)S(1)} collective-permute-done((bf16[144,512]{1,0:T(8,128)(2,1)S(1)}, bf16[144,512]{1,0:T(8,128)(2,1)S(1)}, u32[]{:S(2)}, u32[]{:S(2)}) %collective-permute-start.4) | collective-permute-done | bytes 147488 | tf_op jit(solution)/shard_map/ppermute | solution.py:323
  18.8 1.7 %collective-permute-start.5 = (bf16[144,512]{1,0:T(8,128)(2,1)S(1)}, bf16[144,512]{1,0:T(8,128)(2,1)S(1)}, u32[]{:S(2)}, u32[]{:S(2)}) collective-permute-start(bf16[144,512]{1,0:T(8,128)(2,1)S(1)} %collective-permute-done.4.refs_7_.refs_3_), channel_id=1, source_target_pairs={{4,0},{5,1},{8,4},{9,5},{12,8},{13,9},{14,12},{15,13},{10,14},{11,... | collective-permute-start | bytes 442376 | tf_op jit(solution)/shard_map/ppermute | solution.py:323
  21.5 2.7 %collective-permute-done.5.refs_8_.refs_3_ = bf16[144,512]{1,0:T(8,128)(2,1)S(1)} collective-permute-done((bf16[144,512]{1,0:T(8,128)(2,1)S(1)}, bf16[144,512]{1,0:T(8,128)(2,1)S(1)}, u32[]{:S(2)}, u32[]{:S(2)}) %collective-permute-start.5) | collective-permute-done | bytes 147488 | tf_op jit(solution)/shard_map/ppermute | solution.py:323
  24.2 2.5 %attend.3 = (f32[1024,256]{1,0:T(8,128)S(1)}, f32[1024,128]{1,0:T(8,128)S(1)}) custom-call(bf16[128,2048]{1,0:T(8,128)(2,1)S(1)} %broadcast_multiply_fusion.refs_0_, bf16[144,512]{1,0:T(8,128)(2,1)S(1)} %copy-done.3, bf16[144,512]{1,0:T(8,128)(2,1)S(1)} %copy-done.3, bf16[144,512]{1,0:T(8,128)(2,1)S(1)} %collective-permute-done.refs_3_.refs_2_, ...), custom_call_target="tpu_custom_call" | custom-call | bytes 1024 | tf_op jit(solution)/shard_map/attend/pallas_call | solution.py:182
  29.2 1.4 %attend.4 = (f32[64,2048]{1,0:T(8,128)S(1)}, bf16[64,2048]{1,0:T(8,128)(2,1)S(1)}) custom-call(bf16[128,2048]{1,0:T(8,128)(2,1)S(1)} %broadcast_multiply_fusion.refs_0_, bf16[144,512]{1,0:T(8,128)(2,1)S(1)} %copy-done.3, bf16[144,512]{1,0:T(8,128)(2,1)S(1)} %collective-permute-done.11.refs_2_.refs_14_, ...), custom_call_target="tpu_custom_call" | custom-call | flops 536870912 | bytes 4194304 | tf_op jit(solution)/shard_map/attend/pallas_call | solution.py:182
  30.6 1.7 %collective-permute-start.19 = (bf16[64,2048]{1,0:T(8,128)(2,1)S(1)}, bf16[64,2048]{1,0:T(8,128)(2,1)S(1)}, u32[]{:S(2)}, u32[]{:S(2)}) collective-permute-start(bf16[64,2048]{1,0:T(8,128)(2,1)S(1)} %get-tuple-element.148.refs_0_), channel_id=1, source_target_pairs={{4,0},{5,1},{8,4},{9,5},{12,8},{13,9},{14,12},{15,13},{10,14},{11,... | collective-permute-start | bytes 786440 | tf_op jit(solution)/shard_map/ppermute | solution.py:323
  32.7 3.3 %attend.5 = (f32[64,2048]{1,0:T(8,128)S(1)}, bf16[64,2048]{1,0:T(8,128)(2,1)S(1)}) custom-call(bf16[128,2048]{1,0:T(8,128)(2,1)S(1)} %broadcast_multiply_fusion.refs_0_, bf16[144,512]{1,0:T(8,128)(2,1)S(1)} %copy-done.3, bf16[144,512]{1,0:T(8,128)(2,1)S(1)} %copy-done.3, bf16[144,512]{1,0:T(8,128)(2,1)S(1)} %collective-permute-done.refs_3_.refs_2_, ...), custom_call_target="tpu_custom_call" | custom-call | flops 2147483648 | bytes 4194304 | tf_op jit(solution)/shard_map/attend/pallas_call | solution.py:182
  36.0 1.7 %collective-permute-start.22 = (bf16[64,2048]{1,0:T(8,128)(2,1)S(1)}, bf16[64,2048]{1,0:T(8,128)(2,1)S(1)}, u32[]{:S(2)}, u32[]{:S(2)}) collective-permute-start(bf16[64,2048]{1,0:T(8,128)(2,1)S(1)} %get-tuple-element.168.refs_1_), channel_id=1, source_target_pairs={{4,0},{5,1},{8,4},{9,5},{12,8},{13,9},{14,12},{15,13},{10,14},{11,... | collective-permute-start | bytes 786440 | tf_op jit(solution)/shard_map/ppermute | solution.py:323
  38.1 1.5 %collective-permute-done.19.refs_1_ = bf16[64,2048]{1,0:T(8,128)(2,1)S(1)} collective-permute-done((bf16[64,2048]{1,0:T(8,128)(2,1)S(1)}, bf16[64,2048]{1,0:T(8,128)(2,1)S(1)}, u32[]{:S(2)}, u32[]{:S(2)}) %collective-permute-start.19) | collective-permute-done | bytes 262176 | tf_op jit(solution)/shard_map/ppermute | solution.py:323
  39.7 1.7 %collective-permute-start.20 = (bf16[64,2048]{1,0:T(8,128)(2,1)S(1)}, bf16[64,2048]{1,0:T(8,128)(2,1)S(1)}, u32[]{:S(2)}, u32[]{:S(2)}) collective-permute-start(bf16[64,2048]{1,0:T(8,128)(2,1)S(1)} %collective-permute-done.19.refs_1_), channel_id=1, source_target_pairs={{4,0},{5,1},{8,4},{9,5},{12,8},{13,9},{14,12},{15,13},{10,14},{11,... | collective-permute-start | bytes 786440 | tf_op jit(solution)/shard_map/ppermute | solution.py:323
  41.7 1.8 %experts.8 = (bf16[64,2048]{1,0:T(8,128)(2,1)S(1)}, bf16[64,2048]{1,0:T(8,128)(2,1)S(1)}) custom-call(bf16[64,2048]{1,0:T(8,128)(2,1)S(1)} %collective-permute-done.17.refs_0_, bf16[64,2048]{1,0:T(8,128)(2,1)S(1)} %collective-permute-done.19.refs_1_, bf16[144,512]{1,0:T(8,128)(2,1)S(1)} %collective-permute-done.refs_3_.refs_2_, ...), custom_call_target="tpu_custom_call" | custom-call | flops 1207959552 | bytes 9437184 | tf_op jit(solution)/shard_map/experts/pallas_call | solution.py:283
  43.5 1.7 %collective-permute-done.22.refs_1_ = bf16[64,2048]{1,0:T(8,128)(2,1)S(1)} collective-permute-done((bf16[64,2048]{1,0:T(8,128)(2,1)S(1)}, bf16[64,2048]{1,0:T(8,128)(2,1)S(1)}, u32[]{:S(2)}, u32[]{:S(2)}) %collective-permute-start.22) | collective-permute-done | bytes 262176 | tf_op jit(solution)/shard_map/ppermute | solution.py:323
  45.3 1.7 %collective-permute-done.21.refs_0_ = bf16[64,2048]{1,0:T(8,128)(2,1)S(1)} collective-permute-done((bf16[64,2048]{1,0:T(8,128)(2,1)S(1)}, bf16[64,2048]{1,0:T(8,128)(2,1)S(1)}, u32[]{:S(2)}, u32[]{:S(2)}) %collective-permute-start.21) | collective-permute-done | bytes 262176 | tf_op jit(solution)/shard_map/ppermute | solution.py:323
  47.4 1.7 %collective-permute-start.27 = (bf16[64,2048]{1,0:T(8,128)(2,1)S(1)}, bf16[64,2048]{1,0:T(8,128)(2,1)S(1)}, u32[]{:S(2)}, u32[]{:S(2)}) collective-permute-start(bf16[64,2048]{1,0:T(8,128)(2,1)S(1)} %collective-permute-done.22.refs_1_), channel_id=1, source_target_pairs={{4,0},{5,1},{8,4},{9,5},{12,8},{13,9},{14,12},{15,13},{10,14},{11,... | collective-permute-start | bytes 786440 | tf_op jit(solution)/shard_map/ppermute | solution.py:323
  49.0 1.8 %experts.9 = (bf16[64,2048]{1,0:T(8,128)(2,1)S(1)}, bf16[64,2048]{1,0:T(8,128)(2,1)S(1)}) custom-call(bf16[64,2048]{1,0:T(8,128)(2,1)S(1)} %collective-permute-done.21.refs_0_, bf16[64,2048]{1,0:T(8,128)(2,1)S(1)} %collective-permute-done.22.refs_1_, bf16[144,512]{1,0:T(8,128)(2,1)S(1)} %collective-permute-done.refs_3_.refs_2_, ...), custom_call_target="tpu_custom_call" | custom-call | flops 1207959552 | bytes 9437184 | tf_op jit(solution)/shard_map/experts/pallas_call | solution.py:283
  50.9 1.7 %collective-permute-done.18.refs_0_ = bf16[64,2048]{1,0:T(8,128)(2,1)S(1)} collective-permute-done((bf16[64,2048]{1,0:T(8,128)(2,1)S(1)}, bf16[64,2048]{1,0:T(8,128)(2,1)S(1)}, u32[]{:S(2)}, u32[]{:S(2)}) %collective-permute-start.18) | collective-permute-done | bytes 262176 | tf_op jit(solution)/shard_map/ppermute | solution.py:323
  53.0 1.7 %collective-permute-start.25 = (bf16[64,2048]{1,0:T(8,128)(2,1)S(1)}, bf16[64,2048]{1,0:T(8,128)(2,1)S(1)}, u32[]{:S(2)}, u32[]{:S(2)}) collective-permute-start(bf16[64,2048]{1,0:T(8,128)(2,1)S(1)} %collective-permute-done.20.refs_1_), channel_id=1, source_target_pairs={{4,0},{5,1},{8,4},{9,5},{12,8},{13,9},{14,12},{15,13},{10,14},{11,... | collective-permute-start | bytes 786440 | tf_op jit(solution)/shard_map/ppermute | solution.py:323
  54.7 1.8 %experts.10 = (bf16[64,2048]{1,0:T(8,128)(2,1)S(1)}, bf16[64,2048]{1,0:T(8,128)(2,1)S(1)}) custom-call(bf16[64,2048]{1,0:T(8,128)(2,1)S(1)} %collective-permute-done.18.refs_0_, bf16[64,2048]{1,0:T(8,128)(2,1)S(1)} %collective-permute-done.20.refs_1_, bf16[144,512]{1,0:T(8,128)(2,1)S(1)} %collective-permute-done.1.refs_4_.refs_2_, ...), custom_call_target="tpu_custom_call" | custom-call | flops 1207959552 | bytes 9437184 | tf_op jit(solution)/shard_map/experts/pallas_call | solution.py:283
  56.5 1.7 %collective-permute-done.26.refs_0_ = bf16[64,2048]{1,0:T(8,128)(2,1)S(1)} collective-permute-done((bf16[64,2048]{1,0:T(8,128)(2,1)S(1)}, bf16[64,2048]{1,0:T(8,128)(2,1)S(1)}, u32[]{:S(2)}, u32[]{:S(2)}) %collective-permute-start.26) | collective-permute-done | bytes 262176 | tf_op jit(solution)/shard_map/ppermute | solution.py:323
  58.6 1.7 %collective-permute-start.30 = (bf16[64,2048]{1,0:T(8,128)(2,1)S(1)}, bf16[64,2048]{1,0:T(8,128)(2,1)S(1)}, u32[]{:S(2)}, u32[]{:S(2)}) collective-permute-start(bf16[64,2048]{1,0:T(8,128)(2,1)S(1)} %collective-permute-done.27.refs_1_), channel_id=1, source_target_pairs={{4,0},{5,1},{8,4},{9,5},{12,8},{13,9},{14,12},{15,13},{10,14},{11,... | collective-permute-start | bytes 786440 | tf_op jit(solution)/shard_map/ppermute | solution.py:323
  60.3 1.8 %experts.11 = (bf16[64,2048]{1,0:T(8,128)(2,1)S(1)}, bf16[64,2048]{1,0:T(8,128)(2,1)S(1)}) custom-call(bf16[64,2048]{1,0:T(8,128)(2,1)S(1)} %collective-permute-done.26.refs_0_, bf16[64,2048]{1,0:T(8,128)(2,1)S(1)} %collective-permute-done.27.refs_1_, bf16[144,512]{1,0:T(8,128)(2,1)S(1)} %collective-permute-done.1.refs_4_.refs_2_, ...), custom_call_target="tpu_custom_call" | custom-call | flops 1207959552 | bytes 9437184 | tf_op jit(solution)/shard_map/experts/pallas_call | solution.py:283
  62.1 1.7 %collective-permute-done.24.refs_0_ = bf16[64,2048]{1,0:T(8,128)(2,1)S(1)} collective-permute-done((bf16[64,2048]{1,0:T(8,128)(2,1)S(1)}, bf16[64,2048]{1,0:T(8,128)(2,1)S(1)}, u32[]{:S(2)}, u32[]{:S(2)}) %collective-permute-start.24) | collective-permute-done | bytes 262176 | tf_op jit(solution)/shard_map/ppermute | solution.py:323
  64.2 1.8 %experts.12 = (bf16[64,2048]{1,0:T(8,128)(2,1)S(1)}, bf16[64,2048]{1,0:T(8,128)(2,1)S(1)}) custom-call(bf16[64,2048]{1,0:T(8,128)(2,1)S(1)} %collective-permute-done.24.refs_0_, bf16[64,2048]{1,0:T(8,128)(2,1)S(1)} %collective-permute-done.25.refs_1_, bf16[144,512]{1,0:T(8,128)(2,1)S(1)} %collective-permute-done.3.refs_5_.refs_2_, ...), custom_call_target="tpu_custom_call" | custom-call | flops 1207959552 | bytes 9437184 | tf_op jit(solution)/shard_map/experts/pallas_call | solution.py:283
  66.1 3.4 %collective-permute-done.29.refs_0_ = bf16[64,2048]{1,0:T(8,128)(2,1)S(1)} collective-permute-done((bf16[64,2048]{1,0:T(8,128)(2,1)S(1)}, bf16[64,2048]{1,0:T(8,128)(2,1)S(1)}, u32[]{:S(2)}, u32[]{:S(2)}) %collective-permute-start.29) | collective-permute-done | bytes 262176 | tf_op jit(solution)/shard_map/ppermute | solution.py:323
  69.5 1.6 %collective-permute-start.31 = (bf16[64,2048]{1,0:T(8,128)(2,1)S(1)}, bf16[64,2048]{1,0:T(8,128)(2,1)S(1)}, u32[]{:S(2)}, u32[]{:S(2)}) collective-permute-start(bf16[64,2048]{1,0:T(8,128)(2,1)S(1)} %collective-permute-done.30.refs_1_), channel_id=1, source_target_pairs={{4,0},{5,1},{8,4},{9,5},{12,8},{13,9},{14,12},{15,13},{10,14},{11,... | collective-permute-start | bytes 786440 | tf_op jit(solution)/shard_map/ppermute | solution.py:323
  71.0 1.8 %experts.13 = (bf16[64,2048]{1,0:T(8,128)(2,1)S(1)}, bf16[64,2048]{1,0:T(8,128)(2,1)S(1)}) custom-call(bf16[64,2048]{1,0:T(8,128)(2,1)S(1)} %collective-permute-done.29.refs_0_, bf16[64,2048]{1,0:T(8,128)(2,1)S(1)} %collective-permute-done.30.refs_1_, bf16[144,512]{1,0:T(8,128)(2,1)S(1)} %collective-permute-done.3.refs_5_.refs_2_, ...), custom_call_target="tpu_custom_call" | custom-call | flops 1207959552 | bytes 9437184 | tf_op jit(solution)/shard_map/experts/pallas_call | solution.py:283
  73.4 1.6 %collective-permute-start.33 = (bf16[64,2048]{1,0:T(8,128)(2,1)S(1)}, bf16[64,2048]{1,0:T(8,128)(2,1)S(1)}, u32[]{:S(2)}, u32[]{:S(2)}) collective-permute-start(bf16[64,2048]{1,0:T(8,128)(2,1)S(1)} %get-tuple-element.219), channel_id=1, source_target_pairs={{4,0},{5,1},{8,4},{9,5},{12,8},{13,9},{14,12},{15,13},{10,14},{11,... | collective-permute-start | bytes 786440 | tf_op jit(solution)/shard_map/ppermute | solution.py:323
  75.0 3.2 %collective-permute-done.31.refs_1_ = bf16[64,2048]{1,0:T(8,128)(2,1)S(1)} collective-permute-done((bf16[64,2048]{1,0:T(8,128)(2,1)S(1)}, bf16[64,2048]{1,0:T(8,128)(2,1)S(1)}, u32[]{:S(2)}, u32[]{:S(2)}) %collective-permute-start.31) | collective-permute-done | bytes 262176 | tf_op jit(solution)/shard_map/ppermute | solution.py:323
  78.2 1.8 %experts.14 = (bf16[64,2048]{1,0:T(8,128)(2,1)S(1)}, bf16[64,2048]{1,0:T(8,128)(2,1)S(1)}) custom-call(bf16[64,2048]{1,0:T(8,128)(2,1)S(1)} %collective-permute-done.28.refs_0_, bf16[64,2048]{1,0:T(8,128)(2,1)S(1)} %collective-permute-done.31.refs_1_, bf16[144,512]{1,0:T(8,128)(2,1)S(1)} %collective-permute-done.11.refs_2_.refs_14_, ...), custom_call_target="tpu_custom_call" | custom-call | flops 1207959552 | bytes 9437184 | tf_op jit(solution)/shard_map/experts/pallas_call | solution.py:283
  80.9 1.5 %collective-permute-start.38 = (bf16[64,2048]{1,0:T(8,128)(2,1)S(1)}, bf16[64,2048]{1,0:T(8,128)(2,1)S(1)}, u32[]{:S(2)}, u32[]{:S(2)}) collective-permute-start(bf16[64,2048]{1,0:T(8,128)(2,1)S(1)} %get-tuple-element.218), channel_id=1, source_target_pairs={{4,0},{5,1},{8,4},{9,5},{12,8},{13,9},{14,12},{15,13},{10,14},{11,... | collective-permute-start | bytes 786440 | tf_op jit(solution)/shard_map/ppermute | solution.py:323
  82.3 1.5 %collective-permute-done.33 = bf16[64,2048]{1,0:T(8,128)(2,1)S(1)} collective-permute-done((bf16[64,2048]{1,0:T(8,128)(2,1)S(1)}, bf16[64,2048]{1,0:T(8,128)(2,1)S(1)}, u32[]{:S(2)}, u32[]{:S(2)}) %collective-permute-start.33) | collective-permute-done | bytes 262176 | tf_op jit(solution)/shard_map/ppermute | solution.py:323
  83.8 1.8 %experts.15 = (bf16[64,2048]{1,0:T(8,128)(2,1)S(1)}, bf16[64,2048]{1,0:T(8,128)(2,1)S(1)}) custom-call(bf16[64,2048]{1,0:T(8,128)(2,1)S(1)} %get-tuple-element.148.refs_0_, bf16[64,2048]{1,0:T(8,128)(2,1)S(1)} %get-tuple-element.168.refs_1_, bf16[144,512]{1,0:T(8,128)(2,1)S(1)} %copy-done.3, bf16[1,2048,384]{2,1,0:T(8,128)(2,1)S(1)} %copy-done, ...), custom_call_target="tpu_custom_call" | custom-call | flops 1207959552 | bytes 9437184 | tf_op jit(solution)/shard_map/experts/pallas_call | solution.py:283
  85.7 2.3 %collective-permute-done.34 = bf16[64,2048]{1,0:T(8,128)(2,1)S(1)} collective-permute-done((bf16[64,2048]{1,0:T(8,128)(2,1)S(1)}, bf16[64,2048]{1,0:T(8,128)(2,1)S(1)}, u32[]{:S(2)}, u32[]{:S(2)}) %collective-permute-start.34) | collective-permute-done | bytes 262176 | tf_op jit(solution)/shard_map/ppermute | solution.py:323
  88.9 1.6 %collective-permute-start.42 = (bf16[64,2048]{1,0:T(8,128)(2,1)S(1)}, bf16[64,2048]{1,0:T(8,128)(2,1)S(1)}, u32[]{:S(2)}, u32[]{:S(2)}) collective-permute-start(bf16[64,2048]{1,0:T(8,128)(2,1)S(1)} %add_convert_fusion.3), channel_id=1, source_target_pairs={{0,4},{1,5},{4,8},{5,9},{8,12},{9,13},{12,14},{13,15},{14,10},{15,... | collective-permute-start | bytes 786440 | tf_op jit(solution)/shard_map/ppermute | solution.py:323
  92.5 4.8 %collective-permute-done.35 = bf16[64,2048]{1,0:T(8,128)(2,1)S(1)} collective-permute-done((bf16[64,2048]{1,0:T(8,128)(2,1)S(1)}, bf16[64,2048]{1,0:T(8,128)(2,1)S(1)}, u32[]{:S(2)}, u32[]{:S(2)}) %collective-permute-start.35) | collective-permute-done | bytes 262176 | tf_op jit(solution)/shard_map/ppermute | solution.py:323
  98.2 4.8 %collective-permute-done.42 = bf16[64,2048]{1,0:T(8,128)(2,1)S(1)} collective-permute-done((bf16[64,2048]{1,0:T(8,128)(2,1)S(1)}, bf16[64,2048]{1,0:T(8,128)(2,1)S(1)}, u32[]{:S(2)}, u32[]{:S(2)}) %collective-permute-start.42) | collective-permute-done | bytes 262176 | tf_op jit(solution)/shard_map/ppermute | solution.py:323
  103.8 1.3 %collective-permute-start.44 = (bf16[64,2048]{1,0:T(8,128)(2,1)S(1)}, bf16[64,2048]{1,0:T(8,128)(2,1)S(1)}, u32[]{:S(2)}, u32[]{:S(2)}) collective-permute-start(bf16[64,2048]{1,0:T(8,128)(2,1)S(1)} %add_convert_fusion.6), channel_id=1, source_target_pairs={{4,0},{5,1},{8,4},{9,5},{12,8},{13,9},{14,12},{15,13},{10,14},{11,... | collective-permute-start | bytes 786440 | tf_op jit(solution)/shard_map/ppermute | solution.py:323
  105.2 1.6 %collective-permute-start.41 = (bf16[64,2048]{1,0:T(8,128)(2,1)S(1)}, bf16[64,2048]{1,0:T(8,128)(2,1)S(1)}, u32[]{:S(2)}, u32[]{:S(2)}) collective-permute-start(bf16[64,2048]{1,0:T(8,128)(2,1)S(1)} %add_convert_fusion.5), channel_id=1, source_target_pairs={{4,0},{5,1},{8,4},{9,5},{12,8},{13,9},{14,12},{15,13},{10,14},{11,... | collective-permute-start | bytes 786440 | tf_op jit(solution)/shard_map/ppermute | solution.py:323
  106.8 1.7 %collective-permute-done.36 = bf16[64,2048]{1,0:T(8,128)(2,1)S(1)} collective-permute-done((bf16[64,2048]{1,0:T(8,128)(2,1)S(1)}, bf16[64,2048]{1,0:T(8,128)(2,1)S(1)}, u32[]{:S(2)}, u32[]{:S(2)}) %collective-permute-start.36) | collective-permute-done | bytes 262176 | tf_op jit(solution)/shard_map/ppermute | solution.py:323
  109.4 1.6 %collective-permute-done.44 = bf16[64,2048]{1,0:T(8,128)(2,1)S(1)} collective-permute-done((bf16[64,2048]{1,0:T(8,128)(2,1)S(1)}, bf16[64,2048]{1,0:T(8,128)(2,1)S(1)}, u32[]{:S(2)}, u32[]{:S(2)}) %collective-permute-start.44) | collective-permute-done | bytes 262176 | tf_op jit(solution)/shard_map/ppermute | solution.py:323
  111.7 2.1 %collective-permute-done.41 = bf16[64,2048]{1,0:T(8,128)(2,1)S(1)} collective-permute-done((bf16[64,2048]{1,0:T(8,128)(2,1)S(1)}, bf16[64,2048]{1,0:T(8,128)(2,1)S(1)}, u32[]{:S(2)}, u32[]{:S(2)}) %collective-permute-start.41) | collective-permute-done | bytes 262176 | tf_op jit(solution)/shard_map/ppermute | solution.py:323
  115.1 2.3 %collective-permute-done.45 = bf16[64,2048]{1,0:T(8,128)(2,1)S(1)} collective-permute-done((bf16[64,2048]{1,0:T(8,128)(2,1)S(1)}, bf16[64,2048]{1,0:T(8,128)(2,1)S(1)}, u32[]{:S(2)}, u32[]{:S(2)}) %collective-permute-start.45) | collective-permute-done | bytes 262176 | tf_op jit(solution)/shard_map/ppermute | solution.py:323
  (84 shorter events, 18.2 us)
Async XLA Ops:
  2.3 21.9 %copy-start.3 = (bf16[144,512]{1,0:T(8,128)(2,1)S(1)}, bf16[144,512]{1,0:T(8,128)(2,1)}, u32[]{:S(2)}) copy-start(bf16[144,512]{1,0:T(8,128)(2,1)} %pack_message.1.refs_1_.refs_2_) | copy-start | bytes 442372
  2.3 7.2 %collective-permute-start.2 = (bf16[144,512]{1,0:T(8,128)(2,1)}, bf16[144,512]{1,0:T(8,128)(2,1)S(1)}, u32[]{:S(2)}, u32[]{:S(2)}) collective-permute-start(bf16[144,512]{1,0:T(8,128)(2,1)} %pack_message.1.refs_1_.refs_2_), channel_id=1, source_target_pairs={{4,0},{5,1},{8,4},{9,5},{12,8},{13,9},{14,12},{15,13},{10,14},{11,... | collective-permute-start | bytes 442376 | tf_op jit(solution)/shard_map/ppermute | solution.py:323
  5.2 5.5 %collective-permute-start = (bf16[144,512]{1,0:T(8,128)(2,1)}, bf16[144,512]{1,0:T(8,128)(2,1)S(1)}, u32[]{:S(2)}, u32[]{:S(2)}) collective-permute-start(bf16[144,512]{1,0:T(8,128)(2,1)} %pack_message.1.refs_1_.refs_2_), channel_id=1, source_target_pairs={{0,4},{1,5},{4,8},{5,9},{8,12},{9,13},{12,14},{13,15},{14,10},{15,... | collective-permute-start | bytes 442376 | tf_op jit(solution)/shard_map/ppermute | solution.py:323
  5.3 15.2 %collective-permute-start.6 = (bf16[144,512]{1,0:T(8,128)(2,1)}, bf16[144,512]{1,0:T(8,128)(2,1)S(1)}, u32[]{:S(2)}, u32[]{:S(2)}) collective-permute-start(bf16[144,512]{1,0:T(8,128)(2,1)} %pack_message.1.refs_1_.refs_2_), channel_id=1, source_target_pairs={{0,1},{1,0},{2,3},{3,2},{4,5},{5,4},{6,7},{7,6},{8,9},{9,8},{10,11... | collective-permute-start | bytes 442376 | tf_op jit(solution)/shard_map/ppermute | solution.py:323
  10.8 5.1 %collective-permute-start.1 = (bf16[144,512]{1,0:T(8,128)(2,1)S(1)}, bf16[144,512]{1,0:T(8,128)(2,1)S(1)}, u32[]{:S(2)}, u32[]{:S(2)}) collective-permute-start(bf16[144,512]{1,0:T(8,128)(2,1)S(1)} %collective-permute-done.refs_3_.refs_2_), channel_id=1, source_target_pairs={{0,4},{1,5},{4,8},{5,9},{8,12},{9,13},{12,14},{13,15},{14,10},{15,... | collective-permute-start | bytes 442376 | tf_op jit(solution)/shard_map/ppermute | solution.py:323
  11.1 17.7 %copy-start.2 = (bf16[1,384,2048]{2,1,0:T(8,128)(2,1)S(1)}, bf16[1,384,2048]{2,1,0:T(8,128)(2,1)}, u32[]{:S(2)}) copy-start(bf16[1,384,2048]{2,1,0:T(8,128)(2,1)} %refs_5_.15) | copy-start | bytes 4718596
  12.5 8.0 %collective-permute-start.9 = (bf16[144,512]{1,0:T(8,128)(2,1)S(1)}, bf16[144,512]{1,0:T(8,128)(2,1)S(1)}, u32[]{:S(2)}, u32[]{:S(2)}) collective-permute-start(bf16[144,512]{1,0:T(8,128)(2,1)S(1)} %collective-permute-done.2.refs_6_.refs_3_), channel_id=1, source_target_pairs={{0,1},{1,0},{2,3},{3,2},{4,5},{5,4},{6,7},{7,6},{8,9},{9,8},{10,11... | collective-permute-start | bytes 442376 | tf_op jit(solution)/shard_map/ppermute | solution.py:323
  12.5 6.2 %collective-permute-start.4 = (bf16[144,512]{1,0:T(8,128)(2,1)S(1)}, bf16[144,512]{1,0:T(8,128)(2,1)S(1)}, u32[]{:S(2)}, u32[]{:S(2)}) collective-permute-start(bf16[144,512]{1,0:T(8,128)(2,1)S(1)} %collective-permute-done.2.refs_6_.refs_3_), channel_id=1, source_target_pairs={{4,0},{5,1},{8,4},{9,5},{12,8},{13,9},{14,12},{15,13},{10,14},{11,... | collective-permute-start | bytes 442376 | tf_op jit(solution)/shard_map/ppermute | solution.py:323
  15.9 5.2 %collective-permute-start.3 = (bf16[144,512]{1,0:T(8,128)(2,1)S(1)}, bf16[144,512]{1,0:T(8,128)(2,1)S(1)}, u32[]{:S(2)}, u32[]{:S(2)}) collective-permute-start(bf16[144,512]{1,0:T(8,128)(2,1)S(1)} %collective-permute-done.1.refs_4_.refs_2_), channel_id=1, source_target_pairs={{0,4},{1,5},{4,8},{5,9},{8,12},{9,13},{12,14},{13,15},{14,10},{15,... | collective-permute-start | bytes 442376 | tf_op jit(solution)/shard_map/ppermute | solution.py:323
  16.3 5.1 %collective-permute-start.7 = (bf16[144,512]{1,0:T(8,128)(2,1)S(1)}, bf16[144,512]{1,0:T(8,128)(2,1)S(1)}, u32[]{:S(2)}, u32[]{:S(2)}) collective-permute-start(bf16[144,512]{1,0:T(8,128)(2,1)S(1)} %collective-permute-done.refs_3_.refs_2_), channel_id=1, source_target_pairs={{0,1},{1,0},{2,3},{3,2},{4,5},{5,4},{6,7},{7,6},{8,9},{9,8},{10,11... | collective-permute-start | bytes 442376 | tf_op jit(solution)/shard_map/ppermute | solution.py:323
  18.8 5.4 %collective-permute-start.5 = (bf16[144,512]{1,0:T(8,128)(2,1)S(1)}, bf16[144,512]{1,0:T(8,128)(2,1)S(1)}, u32[]{:S(2)}, u32[]{:S(2)}) collective-permute-start(bf16[144,512]{1,0:T(8,128)(2,1)S(1)} %collective-permute-done.4.refs_7_.refs_3_), channel_id=1, source_target_pairs={{4,0},{5,1},{8,4},{9,5},{12,8},{13,9},{14,12},{15,13},{10,14},{11,... | collective-permute-start | bytes 442376 | tf_op jit(solution)/shard_map/ppermute | solution.py:323
  20.5 3.7 %collective-permute-start.10 = (bf16[144,512]{1,0:T(8,128)(2,1)S(1)}, bf16[144,512]{1,0:T(8,128)(2,1)S(1)}, u32[]{:S(2)}, u32[]{:S(2)}) collective-permute-start(bf16[144,512]{1,0:T(8,128)(2,1)S(1)} %collective-permute-done.4.refs_7_.refs_3_), channel_id=1, source_target_pairs={{0,1},{1,0},{2,3},{3,2},{4,5},{5,4},{6,7},{7,6},{8,9},{9,8},{10,11... | collective-permute-start | bytes 442376 | tf_op jit(solution)/shard_map/ppermute | solution.py:323
  20.5 3.7 %collective-permute-start.8 = (bf16[144,512]{1,0:T(8,128)(2,1)S(1)}, bf16[144,512]{1,0:T(8,128)(2,1)S(1)}, u32[]{:S(2)}, u32[]{:S(2)}) collective-permute-start(bf16[144,512]{1,0:T(8,128)(2,1)S(1)} %collective-permute-done.1.refs_4_.refs_2_), channel_id=1, source_target_pairs={{0,1},{1,0},{2,3},{3,2},{4,5},{5,4},{6,7},{7,6},{8,9},{9,8},{10,11... | collective-permute-start | bytes 442376 | tf_op jit(solution)/shard_map/ppermute | solution.py:323
  21.1 5.7 %collective-permute-start.11 = (bf16[144,512]{1,0:T(8,128)(2,1)S(1)}, bf16[144,512]{1,0:T(8,128)(2,1)S(1)}, u32[]{:S(2)}, u32[]{:S(2)}) collective-permute-start(bf16[144,512]{1,0:T(8,128)(2,1)S(1)} %collective-permute-done.3.refs_5_.refs_2_), channel_id=1, source_target_pairs={{0,4},{1,5},{4,8},{5,9},{8,12},{9,13},{12,14},{13,15},{14,10},{15,... | collective-permute-start | bytes 442376 | tf_op jit(solution)/shard_map/ppermute | solution.py:323
  21.5 5.8 %collective-permute-start.12 = (bf16[144,512]{1,0:T(8,128)(2,1)S(1)}, bf16[144,512]{1,0:T(8,128)(2,1)S(1)}, u32[]{:S(2)}, u32[]{:S(2)}) collective-permute-start(bf16[144,512]{1,0:T(8,128)(2,1)S(1)} %collective-permute-done.3.refs_5_.refs_2_), channel_id=1, source_target_pairs={{0,1},{1,0},{2,3},{3,2},{4,5},{5,4},{6,7},{7,6},{8,9},{9,8},{10,11... | collective-permute-start | bytes 442376 | tf_op jit(solution)/shard_map/ppermute | solution.py:323
  24.2 3.1 %collective-permute-start.13 = (bf16[144,512]{1,0:T(8,128)(2,1)S(1)}, bf16[144,512]{1,0:T(8,128)(2,1)S(1)}, u32[]{:S(2)}, u32[]{:S(2)}) collective-permute-start(bf16[144,512]{1,0:T(8,128)(2,1)S(1)} %collective-permute-done.5.refs_8_.refs_3_), channel_id=1, source_target_pairs={{0,1},{1,0},{2,3},{3,2},{4,5},{5,4},{6,7},{7,6},{8,9},{9,8},{10,11... | collective-permute-start | bytes 442376 | tf_op jit(solution)/shard_map/ppermute | solution.py:323
  26.8 1.5 %collective-permute-start.14 = (bf16[144,512]{1,0:T(8,128)(2,1)S(1)}, bf16[144,512]{1,0:T(8,128)(2,1)S(1)}, u32[]{:S(2)}, u32[]{:S(2)}) collective-permute-start(bf16[144,512]{1,0:T(8,128)(2,1)S(1)} %collective-permute-done.11.refs_2_.refs_14_), channel_id=1, source_target_pairs={{0,1},{1,0},{2,3},{3,2},{4,5},{5,4},{6,7},{7,6},{8,9},{9,8},{10,11... | collective-permute-start | bytes 442376 | tf_op jit(solution)/shard_map/ppermute | solution.py:323
  28.3 7.7 %collective-permute-start.15 = (bf16[1,2048,384]{2,1,0:T(8,128)(2,1)S(1)}, bf16[1,2048,384]{2,1,0:T(8,128)(2,1)S(1)}, u32[]{:S(2)}, u32[]{:S(2)}) collective-permute-start(bf16[1,2048,384]{2,1,0:T(8,128)(2,1)S(1)} %copy-done), channel_id=1, source_target_pairs={{0,1},{1,0},{2,3},{3,2},{4,5},{5,4},{6,7},{7,6},{8,9},{9,8},{10,11... | collective-permute-start | bytes 4718600 | tf_op jit(solution)/shard_map/ppermute | solution.py:323
  28.7 7.4 %collective-permute-start.16 = (bf16[1,2048,384]{2,1,0:T(8,128)(2,1)S(1)}, bf16[1,2048,384]{2,1,0:T(8,128)(2,1)S(1)}, u32[]{:S(2)}, u32[]{:S(2)}) collective-permute-start(bf16[1,2048,384]{2,1,0:T(8,128)(2,1)S(1)} %copy-done.1), channel_id=1, source_target_pairs={{0,1},{1,0},{2,3},{3,2},{4,5},{5,4},{6,7},{7,6},{8,9},{9,8},{10,11... | collective-permute-start | bytes 4718600 | tf_op jit(solution)/shard_map/ppermute | solution.py:323
  28.8 12.9 %collective-permute-start.23 = (bf16[1,384,2048]{2,1,0:T(8,128)(2,1)S(1)}, bf16[1,384,2048]{2,1,0:T(8,128)(2,1)S(1)}, u32[]{:S(2)}, u32[]{:S(2)}) collective-permute-start(bf16[1,384,2048]{2,1,0:T(8,128)(2,1)S(1)} %copy-done.2), channel_id=1, source_target_pairs={{0,1},{1,0},{2,3},{3,2},{4,5},{5,4},{6,7},{7,6},{8,9},{9,8},{10,11... | collective-permute-start | bytes 4718600 | tf_op jit(solution)/shard_map/ppermute | solution.py:323
  30.6 9.1 %collective-permute-start.19 = (bf16[64,2048]{1,0:T(8,128)(2,1)S(1)}, bf16[64,2048]{1,0:T(8,128)(2,1)S(1)}, u32[]{:S(2)}, u32[]{:S(2)}) collective-permute-start(bf16[64,2048]{1,0:T(8,128)(2,1)S(1)} %get-tuple-element.148.refs_0_), channel_id=1, source_target_pairs={{4,0},{5,1},{8,4},{9,5},{12,8},{13,9},{14,12},{15,13},{10,14},{11,... | collective-permute-start | bytes 786440 | tf_op jit(solution)/shard_map/ppermute | solution.py:323
  32.3 9.0 %collective-permute-start.17 = (bf16[64,2048]{1,0:T(8,128)(2,1)S(1)}, bf16[64,2048]{1,0:T(8,128)(2,1)S(1)}, u32[]{:S(2)}, u32[]{:S(2)}) collective-permute-start(bf16[64,2048]{1,0:T(8,128)(2,1)S(1)} %get-tuple-element.148.refs_0_), channel_id=1, source_target_pairs={{0,4},{1,5},{4,8},{5,9},{8,12},{9,13},{12,14},{13,15},{14,10},{15,... | collective-permute-start | bytes 786440 | tf_op jit(solution)/shard_map/ppermute | solution.py:323
  36.0 9.2 %collective-permute-start.22 = (bf16[64,2048]{1,0:T(8,128)(2,1)S(1)}, bf16[64,2048]{1,0:T(8,128)(2,1)S(1)}, u32[]{:S(2)}, u32[]{:S(2)}) collective-permute-start(bf16[64,2048]{1,0:T(8,128)(2,1)S(1)} %get-tuple-element.168.refs_1_), channel_id=1, source_target_pairs={{4,0},{5,1},{8,4},{9,5},{12,8},{13,9},{14,12},{15,13},{10,14},{11,... | collective-permute-start | bytes 786440 | tf_op jit(solution)/shard_map/ppermute | solution.py:323
  37.8 9.2 %collective-permute-start.21 = (bf16[64,2048]{1,0:T(8,128)(2,1)S(1)}, bf16[64,2048]{1,0:T(8,128)(2,1)S(1)}, u32[]{:S(2)}, u32[]{:S(2)}) collective-permute-start(bf16[64,2048]{1,0:T(8,128)(2,1)S(1)} %get-tuple-element.168.refs_1_), channel_id=1, source_target_pairs={{0,4},{1,5},{4,8},{5,9},{8,12},{9,13},{12,14},{13,15},{14,10},{15,... | collective-permute-start | bytes 786440 | tf_op jit(solution)/shard_map/ppermute | solution.py:323
  39.7 11.2 %collective-permute-start.20 = (bf16[64,2048]{1,0:T(8,128)(2,1)S(1)}, bf16[64,2048]{1,0:T(8,128)(2,1)S(1)}, u32[]{:S(2)}, u32[]{:S(2)}) collective-permute-start(bf16[64,2048]{1,0:T(8,128)(2,1)S(1)} %collective-permute-done.19.refs_1_), channel_id=1, source_target_pairs={{4,0},{5,1},{8,4},{9,5},{12,8},{13,9},{14,12},{15,13},{10,14},{11,... | collective-permute-start | bytes 786440 | tf_op jit(solution)/shard_map/ppermute | solution.py:323
  41.4 11.3 %collective-permute-start.18 = (bf16[64,2048]{1,0:T(8,128)(2,1)S(1)}, bf16[64,2048]{1,0:T(8,128)(2,1)S(1)}, u32[]{:S(2)}, u32[]{:S(2)}) collective-permute-start(bf16[64,2048]{1,0:T(8,128)(2,1)S(1)} %collective-permute-done.17.refs_0_), channel_id=1, source_target_pairs={{0,4},{1,5},{4,8},{5,9},{8,12},{9,13},{12,14},{13,15},{14,10},{15,... | collective-permute-start | bytes 786440 | tf_op jit(solution)/shard_map/ppermute | solution.py:323
  47.0 11.2 %collective-permute-start.26 = (bf16[64,2048]{1,0:T(8,128)(2,1)S(1)}, bf16[64,2048]{1,0:T(8,128)(2,1)S(1)}, u32[]{:S(2)}, u32[]{:S(2)}) collective-permute-start(bf16[64,2048]{1,0:T(8,128)(2,1)S(1)} %collective-permute-done.21.refs_0_), channel_id=1, source_target_pairs={{0,4},{1,5},{4,8},{5,9},{8,12},{9,13},{12,14},{13,15},{14,10},{15,... | collective-permute-start | bytes 786440 | tf_op jit(solution)/shard_map/ppermute | solution.py:323
  47.4 10.9 %collective-permute-start.27 = (bf16[64,2048]{1,0:T(8,128)(2,1)S(1)}, bf16[64,2048]{1,0:T(8,128)(2,1)S(1)}, u32[]{:S(2)}, u32[]{:S(2)}) collective-permute-start(bf16[64,2048]{1,0:T(8,128)(2,1)S(1)} %collective-permute-done.22.refs_1_), channel_id=1, source_target_pairs={{4,0},{5,1},{8,4},{9,5},{12,8},{13,9},{14,12},{15,13},{10,14},{11,... | collective-permute-start | bytes 786440 | tf_op jit(solution)/shard_map/ppermute | solution.py:323
  52.6 11.2 %collective-permute-start.24 = (bf16[64,2048]{1,0:T(8,128)(2,1)S(1)}, bf16[64,2048]{1,0:T(8,128)(2,1)S(1)}, u32[]{:S(2)}, u32[]{:S(2)}) collective-permute-start(bf16[64,2048]{1,0:T(8,128)(2,1)S(1)} %collective-permute-done.18.refs_0_), channel_id=1, source_target_pairs={{0,4},{1,5},{4,8},{5,9},{8,12},{9,13},{12,14},{13,15},{14,10},{15,... | collective-permute-start | bytes 786440 | tf_op jit(solution)/shard_map/ppermute | solution.py:323
  53.0 10.9 %collective-permute-start.25 = (bf16[64,2048]{1,0:T(8,128)(2,1)S(1)}, bf16[64,2048]{1,0:T(8,128)(2,1)S(1)}, u32[]{:S(2)}, u32[]{:S(2)}) collective-permute-start(bf16[64,2048]{1,0:T(8,128)(2,1)S(1)} %collective-permute-done.20.refs_1_), channel_id=1, source_target_pairs={{4,0},{5,1},{8,4},{9,5},{12,8},{13,9},{14,12},{15,13},{10,14},{11,... | collective-permute-start | bytes 786440 | tf_op jit(solution)/shard_map/ppermute | solution.py:323
  58.2 11.2 %collective-permute-start.29 = (bf16[64,2048]{1,0:T(8,128)(2,1)S(1)}, bf16[64,2048]{1,0:T(8,128)(2,1)S(1)}, u32[]{:S(2)}, u32[]{:S(2)}) collective-permute-start(bf16[64,2048]{1,0:T(8,128)(2,1)S(1)} %collective-permute-done.26.refs_0_), channel_id=1, source_target_pairs={{0,4},{1,5},{4,8},{5,9},{8,12},{9,13},{12,14},{13,15},{14,10},{15,... | collective-permute-start | bytes 786440 | tf_op jit(solution)/shard_map/ppermute | solution.py:323
  58.6 10.9 %collective-permute-start.30 = (bf16[64,2048]{1,0:T(8,128)(2,1)S(1)}, bf16[64,2048]{1,0:T(8,128)(2,1)S(1)}, u32[]{:S(2)}, u32[]{:S(2)}) collective-permute-start(bf16[64,2048]{1,0:T(8,128)(2,1)S(1)} %collective-permute-done.27.refs_1_), channel_id=1, source_target_pairs={{4,0},{5,1},{8,4},{9,5},{12,8},{13,9},{14,12},{15,13},{10,14},{11,... | collective-permute-start | bytes 786440 | tf_op jit(solution)/shard_map/ppermute | solution.py:323
  63.9 11.1 %collective-permute-start.28 = (bf16[64,2048]{1,0:T(8,128)(2,1)S(1)}, bf16[64,2048]{1,0:T(8,128)(2,1)S(1)}, u32[]{:S(2)}, u32[]{:S(2)}) collective-permute-start(bf16[64,2048]{1,0:T(8,128)(2,1)S(1)} %collective-permute-done.24.refs_0_), channel_id=1, source_target_pairs={{0,4},{1,5},{4,8},{5,9},{8,12},{9,13},{12,14},{13,15},{14,10},{15,... | collective-permute-start | bytes 786440 | tf_op jit(solution)/shard_map/ppermute | solution.py:323
  69.5 8.7 %collective-permute-start.31 = (bf16[64,2048]{1,0:T(8,128)(2,1)S(1)}, bf16[64,2048]{1,0:T(8,128)(2,1)S(1)}, u32[]{:S(2)}, u32[]{:S(2)}) collective-permute-start(bf16[64,2048]{1,0:T(8,128)(2,1)S(1)} %collective-permute-done.30.refs_1_), channel_id=1, source_target_pairs={{4,0},{5,1},{8,4},{9,5},{12,8},{13,9},{14,12},{15,13},{10,14},{11,... | collective-permute-start | bytes 786440 | tf_op jit(solution)/shard_map/ppermute | solution.py:323
  72.9 10.9 %collective-permute-start.32 = (bf16[64,2048]{1,0:T(8,128)(2,1)S(1)}, bf16[64,2048]{1,0:T(8,128)(2,1)S(1)}, u32[]{:S(2)}, u32[]{:S(2)}) collective-permute-start(bf16[64,2048]{1,0:T(8,128)(2,1)S(1)} %get-tuple-element.215), channel_id=1, source_target_pairs={{0,4},{1,5},{4,8},{5,9},{8,12},{9,13},{12,14},{13,15},{14,10},{15,... | collective-permute-start | bytes 786440 | tf_op jit(solution)/shard_map/ppermute | solution.py:323
  73.4 10.4 %collective-permute-start.33 = (bf16[64,2048]{1,0:T(8,128)(2,1)S(1)}, bf16[64,2048]{1,0:T(8,128)(2,1)S(1)}, u32[]{:S(2)}, u32[]{:S(2)}) collective-permute-start(bf16[64,2048]{1,0:T(8,128)(2,1)S(1)} %get-tuple-element.219), channel_id=1, source_target_pairs={{4,0},{5,1},{8,4},{9,5},{12,8},{13,9},{14,12},{15,13},{10,14},{11,... | collective-permute-start | bytes 786440 | tf_op jit(solution)/shard_map/ppermute | solution.py:323
  80.0 7.9 %collective-permute-start.34 = (bf16[64,2048]{1,0:T(8,128)(2,1)S(1)}, bf16[64,2048]{1,0:T(8,128)(2,1)S(1)}, u32[]{:S(2)}, u32[]{:S(2)}) collective-permute-start(bf16[64,2048]{1,0:T(8,128)(2,1)S(1)} %get-tuple-element.217), channel_id=1, source_target_pairs={{0,4},{1,5},{4,8},{5,9},{8,12},{9,13},{12,14},{13,15},{14,10},{15,... | collective-permute-start | bytes 786440 | tf_op jit(solution)/shard_map/ppermute | solution.py:323
  80.9 9.6 %collective-permute-start.38 = (bf16[64,2048]{1,0:T(8,128)(2,1)S(1)}, bf16[64,2048]{1,0:T(8,128)(2,1)S(1)}, u32[]{:S(2)}, u32[]{:S(2)}) collective-permute-start(bf16[64,2048]{1,0:T(8,128)(2,1)S(1)} %get-tuple-element.218), channel_id=1, source_target_pairs={{4,0},{5,1},{8,4},{9,5},{12,8},{13,9},{14,12},{15,13},{10,14},{11,... | collective-permute-start | bytes 786440 | tf_op jit(solution)/shard_map/ppermute | solution.py:323
  88.0 9.3 %collective-permute-start.35 = (bf16[64,2048]{1,0:T(8,128)(2,1)S(1)}, bf16[64,2048]{1,0:T(8,128)(2,1)S(1)}, u32[]{:S(2)}, u32[]{:S(2)}) collective-permute-start(bf16[64,2048]{1,0:T(8,128)(2,1)S(1)} %add_convert_fusion.11), channel_id=1, source_target_pairs={{0,4},{1,5},{4,8},{5,9},{8,12},{9,13},{12,14},{13,15},{14,10},{15,... | collective-permute-start | bytes 786440 | tf_op jit(solution)/shard_map/ppermute | solution.py:323
  88.9 14.0 %collective-permute-start.42 = (bf16[64,2048]{1,0:T(8,128)(2,1)S(1)}, bf16[64,2048]{1,0:T(8,128)(2,1)S(1)}, u32[]{:S(2)}, u32[]{:S(2)}) collective-permute-start(bf16[64,2048]{1,0:T(8,128)(2,1)S(1)} %add_convert_fusion.3), channel_id=1, source_target_pairs={{0,4},{1,5},{4,8},{5,9},{8,12},{9,13},{12,14},{13,15},{14,10},{15,... | collective-permute-start | bytes 786440 | tf_op jit(solution)/shard_map/ppermute | solution.py:323
  90.5 13.3 %collective-permute-start.40 = (bf16[64,2048]{1,0:T(8,128)(2,1)S(1)}, bf16[64,2048]{1,0:T(8,128)(2,1)S(1)}, u32[]{:S(2)}, u32[]{:S(2)}) collective-permute-start(bf16[64,2048]{1,0:T(8,128)(2,1)S(1)} %add_convert_fusion.8), channel_id=1, source_target_pairs={{4,0},{5,1},{8,4},{9,5},{12,8},{13,9},{14,12},{15,13},{10,14},{11,... | collective-permute-start | bytes 786440 | tf_op jit(solution)/shard_map/ppermute | solution.py:323
  91.1 14.1 %collective-permute-start.39 = (bf16[64,2048]{1,0:T(8,128)(2,1)S(1)}, bf16[64,2048]{1,0:T(8,128)(2,1)S(1)}, u32[]{:S(2)}, u32[]{:S(2)}) collective-permute-start(bf16[64,2048]{1,0:T(8,128)(2,1)S(1)} %add_convert_fusion.7), channel_id=1, source_target_pairs={{4,0},{5,1},{8,4},{9,5},{12,8},{13,9},{14,12},{15,13},{10,14},{11,... | collective-permute-start | bytes 786440 | tf_op jit(solution)/shard_map/ppermute | solution.py:323
  97.4 11.2 %collective-permute-start.36 = (bf16[64,2048]{1,0:T(8,128)(2,1)S(1)}, bf16[64,2048]{1,0:T(8,128)(2,1)S(1)}, u32[]{:S(2)}, u32[]{:S(2)}) collective-permute-start(bf16[64,2048]{1,0:T(8,128)(2,1)S(1)} %add_convert_fusion.10), channel_id=1, source_target_pairs={{0,4},{1,5},{4,8},{5,9},{8,12},{9,13},{12,14},{13,15},{14,10},{15,... | collective-permute-start | bytes 786440 | tf_op jit(solution)/shard_map/ppermute | solution.py:323
  103.0 12.2 %collective-permute-start.43 = (bf16[64,2048]{1,0:T(8,128)(2,1)S(1)}, bf16[64,2048]{1,0:T(8,128)(2,1)S(1)}, u32[]{:S(2)}, u32[]{:S(2)}) collective-permute-start(bf16[64,2048]{1,0:T(8,128)(2,1)S(1)} %add_convert_fusion.2), channel_id=1, source_target_pairs={{0,4},{1,5},{4,8},{5,9},{8,12},{9,13},{12,14},{13,15},{14,10},{15,... | collective-permute-start | bytes 786440 | tf_op jit(solution)/shard_map/ppermute | solution.py:323
  103.8 7.1 %collective-permute-start.44 = (bf16[64,2048]{1,0:T(8,128)(2,1)S(1)}, bf16[64,2048]{1,0:T(8,128)(2,1)S(1)}, u32[]{:S(2)}, u32[]{:S(2)}) collective-permute-start(bf16[64,2048]{1,0:T(8,128)(2,1)S(1)} %add_convert_fusion.6), channel_id=1, source_target_pairs={{4,0},{5,1},{8,4},{9,5},{12,8},{13,9},{14,12},{15,13},{10,14},{11,... | collective-permute-start | bytes 786440 | tf_op jit(solution)/shard_map/ppermute | solution.py:323
  105.2 8.5 %collective-permute-start.41 = (bf16[64,2048]{1,0:T(8,128)(2,1)S(1)}, bf16[64,2048]{1,0:T(8,128)(2,1)S(1)}, u32[]{:S(2)}, u32[]{:S(2)}) collective-permute-start(bf16[64,2048]{1,0:T(8,128)(2,1)S(1)} %add_convert_fusion.5), channel_id=1, source_target_pairs={{4,0},{5,1},{8,4},{9,5},{12,8},{13,9},{14,12},{15,13},{10,14},{11,... | collective-permute-start | bytes 786440 | tf_op jit(solution)/shard_map/ppermute | solution.py:323
  108.6 6.4 %collective-permute-start.37 = (bf16[64,2048]{1,0:T(8,128)(2,1)S(1)}, bf16[64,2048]{1,0:T(8,128)(2,1)S(1)}, u32[]{:S(2)}, u32[]{:S(2)}) collective-permute-start(bf16[64,2048]{1,0:T(8,128)(2,1)S(1)} %add_convert_fusion.9), channel_id=1, source_target_pairs={{0,4},{1,5},{4,8},{5,9},{8,12},{9,13},{12,14},{13,15},{14,10},{15,... | collective-permute-start | bytes 786440 | tf_op jit(solution)/shard_map/ppermute | solution.py:323
  111.1 6.4 %collective-permute-start.45 = (bf16[64,2048]{1,0:T(8,128)(2,1)S(1)}, bf16[64,2048]{1,0:T(8,128)(2,1)S(1)}, u32[]{:S(2)}, u32[]{:S(2)}) collective-permute-start(bf16[64,2048]{1,0:T(8,128)(2,1)S(1)} %add_convert_fusion.1), channel_id=1, source_target_pairs={{4,0},{5,1},{8,4},{9,5},{12,8},{13,9},{14,12},{15,13},{10,14},{11,... | collective-permute-start | bytes 786440 | tf_op jit(solution)/shard_map/ppermute | solution.py:323
  (4 other events, 60.4 us)

commit v10 on v9

--- a/solution.py
+++ b/solution.py
@@ -401,8 +401,8 @@
     for hop in range(far - 1, 0, -1):
         onto, backto = sums_on[0], sums_back[1]
         if hop < far - 1:
-            sums_on[1] = later(sums_on[1], earlier[0])
-            sums_back[0] = later(sums_back[0], earlier[1])
+            sums_on[1] = later(sums_on[1], earlier)
+            sums_back[0] = later(sums_back[0], earlier)
             sums_on[1] = send(add_parts(sums_on[1], out_right[hop, 1]), onward)
             sums_back[0] = send(add_parts(sums_back[0], out_left[hop, 0]), back)
         if hop == 1:

time: 119 us -> 117 us (0.983)
  waiting for transfers between devices: 52.7 us -> 50.6 us
    ppermute x46, waiting for transfers between devices: 52.7 us -> 50.6 us  [send(): return lax.ppermute(array, 'ctx', pairs)]
where the time goes in v10:
time: 117 us
  waiting for transfers between devices  50.6 us (43%)
  starting transfers between devices  38.7 us (33%)
  Pallas kernels  23.5 us (20%)
  other arithmetic  3.01 us (3%)
    ppermute x46, waiting for transfers between devices, send(): return lax.ppermute(array, 'ctx', pairs)  50.6 us
    ppermute x46, starting transfers between devices, send(): return lax.ppermute(array, 'ctx', pairs)  38.7 us
    pallas_call x8, Pallas kernels, run_experts(): pl.pallas_call(functools.partial(expert_kernel, [piece[1:] for piece in p...  14.7 us
    pallas_call x3, Pallas kernels, attend_call(): pl.pallas_call(functools.partial(attend_kernel, count, half, begun, ended...  7.23 us
  transfers between devices with their start and end apart: 46, of which 25 were waited for; matrix products, arithmetic and copies ran while one was open for 2% of the time, Pallas kernels for 19%

profile of v10, /device:TPU:0, one launch (start us, length us, event | category | flops | bytes accessed | tf_op | source)
XLA Modules:
  0.0 116.8 jit_solution(7900302367172272353)
XLA Ops:
  0.7 1.6 %pack_message.1.refs_1_.refs_2_ = bf16[144,512]{1,0:T(8,128)(2,1)} custom-call(s32[1]{0:T(128)S(6)} %copy.12.pos_ref, bf16[128,256]{1,0:T(8,128)(2,1)} %key_ref.1, bf16[128,256]{1,0:T(8,128)(2,1)} %value_ref.1, s32[8,128]{1,0:T(8,128)} %bitcast.2, f32[8,128]{1,0:T(8,128)} %bitcast.3), custom_call_target="tpu_custom_call" | custom-call | tf_op jit(solution)/shard_map/pack_message/pallas_call | solution.py:54
  2.3 3.0 %collective-permute-start.2 = (bf16[144,512]{1,0:T(8,128)(2,1)}, bf16[144,512]{1,0:T(8,128)(2,1)S(1)}, u32[]{:S(2)}, u32[]{:S(2)}) collective-permute-start(bf16[144,512]{1,0:T(8,128)(2,1)} %pack_message.1.refs_1_.refs_2_), channel_id=1, source_target_pairs={{4,0},{5,1},{8,4},{9,5},{12,8},{13,9},{14,12},{15,13},{10,14},{11,... | collective-permute-start | bytes 442376 | tf_op jit(solution)/shard_map/ppermute | solution.py:323
  5.3 4.1 %collective-permute-done.2.refs_6_.refs_3_ = bf16[144,512]{1,0:T(8,128)(2,1)S(1)} collective-permute-done((bf16[144,512]{1,0:T(8,128)(2,1)}, bf16[144,512]{1,0:T(8,128)(2,1)S(1)}, u32[]{:S(2)}, u32[]{:S(2)}) %collective-permute-start.2) | collective-permute-done | bytes 147488 | tf_op jit(solution)/shard_map/ppermute | solution.py:323
  9.4 1.3 %collective-permute-done.refs_3_.refs_2_ = bf16[144,512]{1,0:T(8,128)(2,1)S(1)} collective-permute-done((bf16[144,512]{1,0:T(8,128)(2,1)}, bf16[144,512]{1,0:T(8,128)(2,1)S(1)}, u32[]{:S(2)}, u32[]{:S(2)}) %collective-permute-start) | collective-permute-done | bytes 147488 | tf_op jit(solution)/shard_map/ppermute | solution.py:323
  12.5 1.7 %collective-permute-start.4 = (bf16[144,512]{1,0:T(8,128)(2,1)S(1)}, bf16[144,512]{1,0:T(8,128)(2,1)S(1)}, u32[]{:S(2)}, u32[]{:S(2)}) collective-permute-start(bf16[144,512]{1,0:T(8,128)(2,1)S(1)} %collective-permute-done.2.refs_6_.refs_3_), channel_id=1, source_target_pairs={{4,0},{5,1},{8,4},{9,5},{12,8},{13,9},{14,12},{15,13},{10,14},{11,... | collective-permute-start | bytes 442376 | tf_op jit(solution)/shard_map/ppermute | solution.py:323
  14.3 1.6 %collective-permute-done.1.refs_4_.refs_2_ = bf16[144,512]{1,0:T(8,128)(2,1)S(1)} collective-permute-done((bf16[144,512]{1,0:T(8,128)(2,1)S(1)}, bf16[144,512]{1,0:T(8,128)(2,1)S(1)}, u32[]{:S(2)}, u32[]{:S(2)}) %collective-permute-start.1) | collective-permute-done | bytes 147488 | tf_op jit(solution)/shard_map/ppermute | solution.py:323
  16.3 2.5 %collective-permute-done.4.refs_7_.refs_3_ = bf16[144,512]{1,0:T(8,128)(2,1)S(1)} collective-permute-done((bf16[144,512]{1,0:T(8,128)(2,1)S(1)}, bf16[144,512]{1,0:T(8,128)(2,1)S(1)}, u32[]{:S(2)}, u32[]{:S(2)}) %collective-permute-start.4) | collective-permute-done | bytes 147488 | tf_op jit(solution)/shard_map/ppermute | solution.py:323
  18.8 1.7 %collective-permute-start.5 = (bf16[144,512]{1,0:T(8,128)(2,1)S(1)}, bf16[144,512]{1,0:T(8,128)(2,1)S(1)}, u32[]{:S(2)}, u32[]{:S(2)}) collective-permute-start(bf16[144,512]{1,0:T(8,128)(2,1)S(1)} %collective-permute-done.4.refs_7_.refs_3_), channel_id=1, source_target_pairs={{4,0},{5,1},{8,4},{9,5},{12,8},{13,9},{14,12},{15,13},{10,14},{11,... | collective-permute-start | bytes 442376 | tf_op jit(solution)/shard_map/ppermute | solution.py:323
  21.5 2.7 %collective-permute-done.5.refs_8_.refs_3_ = bf16[144,512]{1,0:T(8,128)(2,1)S(1)} collective-permute-done((bf16[144,512]{1,0:T(8,128)(2,1)S(1)}, bf16[144,512]{1,0:T(8,128)(2,1)S(1)}, u32[]{:S(2)}, u32[]{:S(2)}) %collective-permute-start.5) | collective-permute-done | bytes 147488 | tf_op jit(solution)/shard_map/ppermute | solution.py:323
  24.2 2.5 %attend.3 = (f32[1024,256]{1,0:T(8,128)S(1)}, f32[1024,128]{1,0:T(8,128)S(1)}) custom-call(bf16[128,2048]{1,0:T(8,128)(2,1)S(1)} %broadcast_multiply_fusion.refs_0_, bf16[144,512]{1,0:T(8,128)(2,1)S(1)} %copy-done.3, bf16[144,512]{1,0:T(8,128)(2,1)S(1)} %copy-done.3, bf16[144,512]{1,0:T(8,128)(2,1)S(1)} %collective-permute-done.refs_3_.refs_2_, ...), custom_call_target="tpu_custom_call" | custom-call | bytes 1024 | tf_op jit(solution)/shard_map/attend/pallas_call | solution.py:182
  29.2 1.4 %attend.4 = (f32[64,2048]{1,0:T(8,128)S(1)}, bf16[64,2048]{1,0:T(8,128)(2,1)S(1)}) custom-call(bf16[128,2048]{1,0:T(8,128)(2,1)S(1)} %broadcast_multiply_fusion.refs_0_, bf16[144,512]{1,0:T(8,128)(2,1)S(1)} %copy-done.3, bf16[144,512]{1,0:T(8,128)(2,1)S(1)} %collective-permute-done.11.refs_2_.refs_14_, ...), custom_call_target="tpu_custom_call" | custom-call | flops 536870912 | bytes 4194304 | tf_op jit(solution)/shard_map/attend/pallas_call | solution.py:182
  30.6 1.7 %collective-permute-start.19 = (bf16[64,2048]{1,0:T(8,128)(2,1)S(1)}, bf16[64,2048]{1,0:T(8,128)(2,1)S(1)}, u32[]{:S(2)}, u32[]{:S(2)}) collective-permute-start(bf16[64,2048]{1,0:T(8,128)(2,1)S(1)} %get-tuple-element.148.refs_0_), channel_id=1, source_target_pairs={{4,0},{5,1},{8,4},{9,5},{12,8},{13,9},{14,12},{15,13},{10,14},{11,... | collective-permute-start | bytes 786440 | tf_op jit(solution)/shard_map/ppermute | solution.py:323
  32.7 3.3 %attend.5 = (f32[64,2048]{1,0:T(8,128)S(1)}, bf16[64,2048]{1,0:T(8,128)(2,1)S(1)}) custom-call(bf16[128,2048]{1,0:T(8,128)(2,1)S(1)} %broadcast_multiply_fusion.refs_0_, bf16[144,512]{1,0:T(8,128)(2,1)S(1)} %copy-done.3, bf16[144,512]{1,0:T(8,128)(2,1)S(1)} %copy-done.3, bf16[144,512]{1,0:T(8,128)(2,1)S(1)} %collective-permute-done.refs_3_.refs_2_, ...), custom_call_target="tpu_custom_call" | custom-call | flops 2147483648 | bytes 4194304 | tf_op jit(solution)/shard_map/attend/pallas_call | solution.py:182
  36.0 1.7 %collective-permute-start.22 = (bf16[64,2048]{1,0:T(8,128)(2,1)S(1)}, bf16[64,2048]{1,0:T(8,128)(2,1)S(1)}, u32[]{:S(2)}, u32[]{:S(2)}) collective-permute-start(bf16[64,2048]{1,0:T(8,128)(2,1)S(1)} %get-tuple-element.168.refs_1_), channel_id=1, source_target_pairs={{4,0},{5,1},{8,4},{9,5},{12,8},{13,9},{14,12},{15,13},{10,14},{11,... | collective-permute-start | bytes 786440 | tf_op jit(solution)/shard_map/ppermute | solution.py:323
  38.1 1.5 %collective-permute-done.19.refs_1_ = bf16[64,2048]{1,0:T(8,128)(2,1)S(1)} collective-permute-done((bf16[64,2048]{1,0:T(8,128)(2,1)S(1)}, bf16[64,2048]{1,0:T(8,128)(2,1)S(1)}, u32[]{:S(2)}, u32[]{:S(2)}) %collective-permute-start.19) | collective-permute-done | bytes 262176 | tf_op jit(solution)/shard_map/ppermute | solution.py:323
  39.7 1.7 %collective-permute-start.20 = (bf16[64,2048]{1,0:T(8,128)(2,1)S(1)}, bf16[64,2048]{1,0:T(8,128)(2,1)S(1)}, u32[]{:S(2)}, u32[]{:S(2)}) collective-permute-start(bf16[64,2048]{1,0:T(8,128)(2,1)S(1)} %collective-permute-done.19.refs_1_), channel_id=1, source_target_pairs={{4,0},{5,1},{8,4},{9,5},{12,8},{13,9},{14,12},{15,13},{10,14},{11,... | collective-permute-start | bytes 786440 | tf_op jit(solution)/shard_map/ppermute | solution.py:323
  41.7 1.8 %experts.8 = (bf16[64,2048]{1,0:T(8,128)(2,1)S(1)}, bf16[64,2048]{1,0:T(8,128)(2,1)S(1)}) custom-call(bf16[64,2048]{1,0:T(8,128)(2,1)S(1)} %collective-permute-done.17.refs_0_, bf16[64,2048]{1,0:T(8,128)(2,1)S(1)} %collective-permute-done.19.refs_1_, bf16[144,512]{1,0:T(8,128)(2,1)S(1)} %collective-permute-done.refs_3_.refs_2_, ...), custom_call_target="tpu_custom_call" | custom-call | flops 1207959552 | bytes 9437184 | tf_op jit(solution)/shard_map/experts/pallas_call | solution.py:283
  43.5 1.7 %collective-permute-done.22.refs_1_ = bf16[64,2048]{1,0:T(8,128)(2,1)S(1)} collective-permute-done((bf16[64,2048]{1,0:T(8,128)(2,1)S(1)}, bf16[64,2048]{1,0:T(8,128)(2,1)S(1)}, u32[]{:S(2)}, u32[]{:S(2)}) %collective-permute-start.22) | collective-permute-done | bytes 262176 | tf_op jit(solution)/shard_map/ppermute | solution.py:323
  45.3 1.7 %collective-permute-done.21.refs_0_ = bf16[64,2048]{1,0:T(8,128)(2,1)S(1)} collective-permute-done((bf16[64,2048]{1,0:T(8,128)(2,1)S(1)}, bf16[64,2048]{1,0:T(8,128)(2,1)S(1)}, u32[]{:S(2)}, u32[]{:S(2)}) %collective-permute-start.21) | collective-permute-done | bytes 262176 | tf_op jit(solution)/shard_map/ppermute | solution.py:323
  47.4 1.7 %collective-permute-start.27 = (bf16[64,2048]{1,0:T(8,128)(2,1)S(1)}, bf16[64,2048]{1,0:T(8,128)(2,1)S(1)}, u32[]{:S(2)}, u32[]{:S(2)}) collective-permute-start(bf16[64,2048]{1,0:T(8,128)(2,1)S(1)} %collective-permute-done.22.refs_1_), channel_id=1, source_target_pairs={{4,0},{5,1},{8,4},{9,5},{12,8},{13,9},{14,12},{15,13},{10,14},{11,... | collective-permute-start | bytes 786440 | tf_op jit(solution)/shard_map/ppermute | solution.py:323
  49.0 1.8 %experts.9 = (bf16[64,2048]{1,0:T(8,128)(2,1)S(1)}, bf16[64,2048]{1,0:T(8,128)(2,1)S(1)}) custom-call(bf16[64,2048]{1,0:T(8,128)(2,1)S(1)} %collective-permute-done.21.refs_0_, bf16[64,2048]{1,0:T(8,128)(2,1)S(1)} %collective-permute-done.22.refs_1_, bf16[144,512]{1,0:T(8,128)(2,1)S(1)} %collective-permute-done.refs_3_.refs_2_, ...), custom_call_target="tpu_custom_call" | custom-call | flops 1207959552 | bytes 9437184 | tf_op jit(solution)/shard_map/experts/pallas_call | solution.py:283
  50.9 1.7 %collective-permute-done.18.refs_0_ = bf16[64,2048]{1,0:T(8,128)(2,1)S(1)} collective-permute-done((bf16[64,2048]{1,0:T(8,128)(2,1)S(1)}, bf16[64,2048]{1,0:T(8,128)(2,1)S(1)}, u32[]{:S(2)}, u32[]{:S(2)}) %collective-permute-start.18) | collective-permute-done | bytes 262176 | tf_op jit(solution)/shard_map/ppermute | solution.py:323
  53.0 1.7 %collective-permute-start.25 = (bf16[64,2048]{1,0:T(8,128)(2,1)S(1)}, bf16[64,2048]{1,0:T(8,128)(2,1)S(1)}, u32[]{:S(2)}, u32[]{:S(2)}) collective-permute-start(bf16[64,2048]{1,0:T(8,128)(2,1)S(1)} %collective-permute-done.20.refs_1_), channel_id=1, source_target_pairs={{4,0},{5,1},{8,4},{9,5},{12,8},{13,9},{14,12},{15,13},{10,14},{11,... | collective-permute-start | bytes 786440 | tf_op jit(solution)/shard_map/ppermute | solution.py:323
  54.7 1.8 %experts.10 = (bf16[64,2048]{1,0:T(8,128)(2,1)S(1)}, bf16[64,2048]{1,0:T(8,128)(2,1)S(1)}) custom-call(bf16[64,2048]{1,0:T(8,128)(2,1)S(1)} %collective-permute-done.18.refs_0_, bf16[64,2048]{1,0:T(8,128)(2,1)S(1)} %collective-permute-done.20.refs_1_, bf16[144,512]{1,0:T(8,128)(2,1)S(1)} %collective-permute-done.1.refs_4_.refs_2_, ...), custom_call_target="tpu_custom_call" | custom-call | flops 1207959552 | bytes 9437184 | tf_op jit(solution)/shard_map/experts/pallas_call | solution.py:283
  56.5 1.7 %collective-permute-done.26.refs_0_ = bf16[64,2048]{1,0:T(8,128)(2,1)S(1)} collective-permute-done((bf16[64,2048]{1,0:T(8,128)(2,1)S(1)}, bf16[64,2048]{1,0:T(8,128)(2,1)S(1)}, u32[]{:S(2)}, u32[]{:S(2)}) %collective-permute-start.26) | collective-permute-done | bytes 262176 | tf_op jit(solution)/shard_map/ppermute | solution.py:323
  58.6 1.7 %collective-permute-start.30 = (bf16[64,2048]{1,0:T(8,128)(2,1)S(1)}, bf16[64,2048]{1,0:T(8,128)(2,1)S(1)}, u32[]{:S(2)}, u32[]{:S(2)}) collective-permute-start(bf16[64,2048]{1,0:T(8,128)(2,1)S(1)} %collective-permute-done.27.refs_1_), channel_id=1, source_target_pairs={{4,0},{5,1},{8,4},{9,5},{12,8},{13,9},{14,12},{15,13},{10,14},{11,... | collective-permute-start | bytes 786440 | tf_op jit(solution)/shard_map/ppermute | solution.py:323
  60.3 1.8 %experts.11 = (bf16[64,2048]{1,0:T(8,128)(2,1)S(1)}, bf16[64,2048]{1,0:T(8,128)(2,1)S(1)}) custom-call(bf16[64,2048]{1,0:T(8,128)(2,1)S(1)} %collective-permute-done.26.refs_0_, bf16[64,2048]{1,0:T(8,128)(2,1)S(1)} %collective-permute-done.27.refs_1_, bf16[144,512]{1,0:T(8,128)(2,1)S(1)} %collective-permute-done.1.refs_4_.refs_2_, ...), custom_call_target="tpu_custom_call" | custom-call | flops 1207959552 | bytes 9437184 | tf_op jit(solution)/shard_map/experts/pallas_call | solution.py:283
  62.1 1.7 %collective-permute-done.24.refs_0_ = bf16[64,2048]{1,0:T(8,128)(2,1)S(1)} collective-permute-done((bf16[64,2048]{1,0:T(8,128)(2,1)S(1)}, bf16[64,2048]{1,0:T(8,128)(2,1)S(1)}, u32[]{:S(2)}, u32[]{:S(2)}) %collective-permute-start.24) | collective-permute-done | bytes 262176 | tf_op jit(solution)/shard_map/ppermute | solution.py:323
  64.2 1.8 %experts.12 = (bf16[64,2048]{1,0:T(8,128)(2,1)S(1)}, bf16[64,2048]{1,0:T(8,128)(2,1)S(1)}) custom-call(bf16[64,2048]{1,0:T(8,128)(2,1)S(1)} %collective-permute-done.24.refs_0_, bf16[64,2048]{1,0:T(8,128)(2,1)S(1)} %collective-permute-done.25.refs_1_, bf16[144,512]{1,0:T(8,128)(2,1)S(1)} %collective-permute-done.3.refs_5_.refs_2_, ...), custom_call_target="tpu_custom_call" | custom-call | flops 1207959552 | bytes 9437184 | tf_op jit(solution)/shard_map/experts/pallas_call | solution.py:283
  66.1 3.4 %collective-permute-done.29.refs_0_ = bf16[64,2048]{1,0:T(8,128)(2,1)S(1)} collective-permute-done((bf16[64,2048]{1,0:T(8,128)(2,1)S(1)}, bf16[64,2048]{1,0:T(8,128)(2,1)S(1)}, u32[]{:S(2)}, u32[]{:S(2)}) %collective-permute-start.29) | collective-permute-done | bytes 262176 | tf_op jit(solution)/shard_map/ppermute | solution.py:323
  69.5 1.6 %collective-permute-start.31 = (bf16[64,2048]{1,0:T(8,128)(2,1)S(1)}, bf16[64,2048]{1,0:T(8,128)(2,1)S(1)}, u32[]{:S(2)}, u32[]{:S(2)}) collective-permute-start(bf16[64,2048]{1,0:T(8,128)(2,1)S(1)} %collective-permute-done.30.refs_1_), channel_id=1, source_target_pairs={{4,0},{5,1},{8,4},{9,5},{12,8},{13,9},{14,12},{15,13},{10,14},{11,... | collective-permute-start | bytes 786440 | tf_op jit(solution)/shard_map/ppermute | solution.py:323
  71.0 1.8 %experts.13 = (bf16[64,2048]{1,0:T(8,128)(2,1)S(1)}, bf16[64,2048]{1,0:T(8,128)(2,1)S(1)}) custom-call(bf16[64,2048]{1,0:T(8,128)(2,1)S(1)} %collective-permute-done.29.refs_0_, bf16[64,2048]{1,0:T(8,128)(2,1)S(1)} %collective-permute-done.30.refs_1_, bf16[144,512]{1,0:T(8,128)(2,1)S(1)} %collective-permute-done.3.refs_5_.refs_2_, ...), custom_call_target="tpu_custom_call" | custom-call | flops 1207959552 | bytes 9437184 | tf_op jit(solution)/shard_map/experts/pallas_call | solution.py:283
  73.4 1.6 %collective-permute-start.33 = (bf16[64,2048]{1,0:T(8,128)(2,1)S(1)}, bf16[64,2048]{1,0:T(8,128)(2,1)S(1)}, u32[]{:S(2)}, u32[]{:S(2)}) collective-permute-start(bf16[64,2048]{1,0:T(8,128)(2,1)S(1)} %get-tuple-element.219), channel_id=1, source_target_pairs={{4,0},{5,1},{8,4},{9,5},{12,8},{13,9},{14,12},{15,13},{10,14},{11,... | collective-permute-start | bytes 786440 | tf_op jit(solution)/shard_map/ppermute | solution.py:323
  75.0 3.2 %collective-permute-done.31.refs_1_ = bf16[64,2048]{1,0:T(8,128)(2,1)S(1)} collective-permute-done((bf16[64,2048]{1,0:T(8,128)(2,1)S(1)}, bf16[64,2048]{1,0:T(8,128)(2,1)S(1)}, u32[]{:S(2)}, u32[]{:S(2)}) %collective-permute-start.31) | collective-permute-done | bytes 262176 | tf_op jit(solution)/shard_map/ppermute | solution.py:323
  78.2 1.8 %experts.14 = (bf16[64,2048]{1,0:T(8,128)(2,1)S(1)}, bf16[64,2048]{1,0:T(8,128)(2,1)S(1)}) custom-call(bf16[64,2048]{1,0:T(8,128)(2,1)S(1)} %collective-permute-done.28.refs_0_, bf16[64,2048]{1,0:T(8,128)(2,1)S(1)} %collective-permute-done.31.refs_1_, bf16[144,512]{1,0:T(8,128)(2,1)S(1)} %collective-permute-done.11.refs_2_.refs_14_, ...), custom_call_target="tpu_custom_call" | custom-call | flops 1207959552 | bytes 9437184 | tf_op jit(solution)/shard_map/experts/pallas_call | solution.py:283
  80.9 1.5 %collective-permute-start.38 = (bf16[64,2048]{1,0:T(8,128)(2,1)S(1)}, bf16[64,2048]{1,0:T(8,128)(2,1)S(1)}, u32[]{:S(2)}, u32[]{:S(2)}) collective-permute-start(bf16[64,2048]{1,0:T(8,128)(2,1)S(1)} %get-tuple-element.218), channel_id=1, source_target_pairs={{4,0},{5,1},{8,4},{9,5},{12,8},{13,9},{14,12},{15,13},{10,14},{11,... | collective-permute-start | bytes 786440 | tf_op jit(solution)/shard_map/ppermute | solution.py:323
  82.3 1.5 %collective-permute-done.33 = bf16[64,2048]{1,0:T(8,128)(2,1)S(1)} collective-permute-done((bf16[64,2048]{1,0:T(8,128)(2,1)S(1)}, bf16[64,2048]{1,0:T(8,128)(2,1)S(1)}, u32[]{:S(2)}, u32[]{:S(2)}) %collective-permute-start.33) | collective-permute-done | bytes 262176 | tf_op jit(solution)/shard_map/ppermute | solution.py:323
  83.8 1.8 %experts.15 = (bf16[64,2048]{1,0:T(8,128)(2,1)S(1)}, bf16[64,2048]{1,0:T(8,128)(2,1)S(1)}) custom-call(bf16[64,2048]{1,0:T(8,128)(2,1)S(1)} %get-tuple-element.148.refs_0_, bf16[64,2048]{1,0:T(8,128)(2,1)S(1)} %get-tuple-element.168.refs_1_, bf16[144,512]{1,0:T(8,128)(2,1)S(1)} %copy-done.3, bf16[1,2048,384]{2,1,0:T(8,128)(2,1)S(1)} %copy-done, ...), custom_call_target="tpu_custom_call" | custom-call | flops 1207959552 | bytes 9437184 | tf_op jit(solution)/shard_map/experts/pallas_call | solution.py:283
  85.7 2.3 %collective-permute-done.34 = bf16[64,2048]{1,0:T(8,128)(2,1)S(1)} collective-permute-done((bf16[64,2048]{1,0:T(8,128)(2,1)S(1)}, bf16[64,2048]{1,0:T(8,128)(2,1)S(1)}, u32[]{:S(2)}, u32[]{:S(2)}) %collective-permute-start.34) | collective-permute-done | bytes 262176 | tf_op jit(solution)/shard_map/ppermute | solution.py:323
  88.9 1.3 %collective-permute-start.40 = (bf16[64,2048]{1,0:T(8,128)(2,1)S(1)}, bf16[64,2048]{1,0:T(8,128)(2,1)S(1)}, u32[]{:S(2)}, u32[]{:S(2)}) collective-permute-start(bf16[64,2048]{1,0:T(8,128)(2,1)S(1)} %add_convert_fusion.8), channel_id=1, source_target_pairs={{4,0},{5,1},{8,4},{9,5},{12,8},{13,9},{14,12},{15,13},{10,14},{11,... | collective-permute-start | bytes 786440 | tf_op jit(solution)/shard_map/ppermute | solution.py:323
  90.3 1.6 %collective-permute-start.39 = (bf16[64,2048]{1,0:T(8,128)(2,1)S(1)}, bf16[64,2048]{1,0:T(8,128)(2,1)S(1)}, u32[]{:S(2)}, u32[]{:S(2)}) collective-permute-start(bf16[64,2048]{1,0:T(8,128)(2,1)S(1)} %add_convert_fusion.7), channel_id=1, source_target_pairs={{4,0},{5,1},{8,4},{9,5},{12,8},{13,9},{14,12},{15,13},{10,14},{11,... | collective-permute-start | bytes 786440 | tf_op jit(solution)/shard_map/ppermute | solution.py:323
  92.5 4.8 %collective-permute-done.35 = bf16[64,2048]{1,0:T(8,128)(2,1)S(1)} collective-permute-done((bf16[64,2048]{1,0:T(8,128)(2,1)S(1)}, bf16[64,2048]{1,0:T(8,128)(2,1)S(1)}, u32[]{:S(2)}, u32[]{:S(2)}) %collective-permute-start.35) | collective-permute-done | bytes 262176 | tf_op jit(solution)/shard_map/ppermute | solution.py:323
  98.2 1.3 %collective-permute-start.44 = (bf16[64,2048]{1,0:T(8,128)(2,1)S(1)}, bf16[64,2048]{1,0:T(8,128)(2,1)S(1)}, u32[]{:S(2)}, u32[]{:S(2)}) collective-permute-start(bf16[64,2048]{1,0:T(8,128)(2,1)S(1)} %add_convert_fusion.6), channel_id=1, source_target_pairs={{4,0},{5,1},{8,4},{9,5},{12,8},{13,9},{14,12},{15,13},{10,14},{11,... | collective-permute-start | bytes 786440 | tf_op jit(solution)/shard_map/ppermute | solution.py:323
  99.6 3.3 %collective-permute-done.42 = bf16[64,2048]{1,0:T(8,128)(2,1)S(1)} collective-permute-done((bf16[64,2048]{1,0:T(8,128)(2,1)S(1)}, bf16[64,2048]{1,0:T(8,128)(2,1)S(1)}, u32[]{:S(2)}, u32[]{:S(2)}) %collective-permute-start.42) | collective-permute-done | bytes 262176 | tf_op jit(solution)/shard_map/ppermute | solution.py:323
  106.0 2.5 %collective-permute-done.36 = bf16[64,2048]{1,0:T(8,128)(2,1)S(1)} collective-permute-done((bf16[64,2048]{1,0:T(8,128)(2,1)S(1)}, bf16[64,2048]{1,0:T(8,128)(2,1)S(1)}, u32[]{:S(2)}, u32[]{:S(2)}) %collective-permute-start.36) | collective-permute-done | bytes 262176 | tf_op jit(solution)/shard_map/ppermute | solution.py:323
  109.5 1.3 %collective-permute-start.45 = (bf16[64,2048]{1,0:T(8,128)(2,1)S(1)}, bf16[64,2048]{1,0:T(8,128)(2,1)S(1)}, u32[]{:S(2)}, u32[]{:S(2)}) collective-permute-start(bf16[64,2048]{1,0:T(8,128)(2,1)S(1)} %add_convert_fusion.1), channel_id=1, source_target_pairs={{4,0},{5,1},{8,4},{9,5},{12,8},{13,9},{14,12},{15,13},{10,14},{11,... | collective-permute-start | bytes 786440 | tf_op jit(solution)/shard_map/ppermute | solution.py:323
  110.8 1.7 %collective-permute-done.41 = bf16[64,2048]{1,0:T(8,128)(2,1)S(1)} collective-permute-done((bf16[64,2048]{1,0:T(8,128)(2,1)S(1)}, bf16[64,2048]{1,0:T(8,128)(2,1)S(1)}, u32[]{:S(2)}, u32[]{:S(2)}) %collective-permute-start.41) | collective-permute-done | bytes 262176 | tf_op jit(solution)/shard_map/ppermute | solution.py:323
  112.5 2.7 %collective-permute-done.37 = bf16[64,2048]{1,0:T(8,128)(2,1)S(1)} collective-permute-done((bf16[64,2048]{1,0:T(8,128)(2,1)S(1)}, bf16[64,2048]{1,0:T(8,128)(2,1)S(1)}, u32[]{:S(2)}, u32[]{:S(2)}) %collective-permute-start.37) | collective-permute-done | bytes 262176 | tf_op jit(solution)/shard_map/ppermute | solution.py:323
  (84 shorter events, 17.7 us)
Async XLA Ops:
  2.3 21.9 %copy-start.3 = (bf16[144,512]{1,0:T(8,128)(2,1)S(1)}, bf16[144,512]{1,0:T(8,128)(2,1)}, u32[]{:S(2)}) copy-start(bf16[144,512]{1,0:T(8,128)(2,1)} %pack_message.1.refs_1_.refs_2_) | copy-start | bytes 442372
  2.3 7.2 %collective-permute-start.2 = (bf16[144,512]{1,0:T(8,128)(2,1)}, bf16[144,512]{1,0:T(8,128)(2,1)S(1)}, u32[]{:S(2)}, u32[]{:S(2)}) collective-permute-start(bf16[144,512]{1,0:T(8,128)(2,1)} %pack_message.1.refs_1_.refs_2_), channel_id=1, source_target_pairs={{4,0},{5,1},{8,4},{9,5},{12,8},{13,9},{14,12},{15,13},{10,14},{11,... | collective-permute-start | bytes 442376 | tf_op jit(solution)/shard_map/ppermute | solution.py:323
  5.2 5.5 %collective-permute-start = (bf16[144,512]{1,0:T(8,128)(2,1)}, bf16[144,512]{1,0:T(8,128)(2,1)S(1)}, u32[]{:S(2)}, u32[]{:S(2)}) collective-permute-start(bf16[144,512]{1,0:T(8,128)(2,1)} %pack_message.1.refs_1_.refs_2_), channel_id=1, source_target_pairs={{0,4},{1,5},{4,8},{5,9},{8,12},{9,13},{12,14},{13,15},{14,10},{15,... | collective-permute-start | bytes 442376 | tf_op jit(solution)/shard_map/ppermute | solution.py:323
  5.3 15.2 %collective-permute-start.6 = (bf16[144,512]{1,0:T(8,128)(2,1)}, bf16[144,512]{1,0:T(8,128)(2,1)S(1)}, u32[]{:S(2)}, u32[]{:S(2)}) collective-permute-start(bf16[144,512]{1,0:T(8,128)(2,1)} %pack_message.1.refs_1_.refs_2_), channel_id=1, source_target_pairs={{0,1},{1,0},{2,3},{3,2},{4,5},{5,4},{6,7},{7,6},{8,9},{9,8},{10,11... | collective-permute-start | bytes 442376 | tf_op jit(solution)/shard_map/ppermute | solution.py:323
  10.8 5.1 %collective-permute-start.1 = (bf16[144,512]{1,0:T(8,128)(2,1)S(1)}, bf16[144,512]{1,0:T(8,128)(2,1)S(1)}, u32[]{:S(2)}, u32[]{:S(2)}) collective-permute-start(bf16[144,512]{1,0:T(8,128)(2,1)S(1)} %collective-permute-done.refs_3_.refs_2_), channel_id=1, source_target_pairs={{0,4},{1,5},{4,8},{5,9},{8,12},{9,13},{12,14},{13,15},{14,10},{15,... | collective-permute-start | bytes 442376 | tf_op jit(solution)/shard_map/ppermute | solution.py:323
  11.1 17.7 %copy-start.2 = (bf16[1,384,2048]{2,1,0:T(8,128)(2,1)S(1)}, bf16[1,384,2048]{2,1,0:T(8,128)(2,1)}, u32[]{:S(2)}) copy-start(bf16[1,384,2048]{2,1,0:T(8,128)(2,1)} %refs_5_.15) | copy-start | bytes 4718596
  12.5 8.0 %collective-permute-start.9 = (bf16[144,512]{1,0:T(8,128)(2,1)S(1)}, bf16[144,512]{1,0:T(8,128)(2,1)S(1)}, u32[]{:S(2)}, u32[]{:S(2)}) collective-permute-start(bf16[144,512]{1,0:T(8,128)(2,1)S(1)} %collective-permute-done.2.refs_6_.refs_3_), channel_id=1, source_target_pairs={{0,1},{1,0},{2,3},{3,2},{4,5},{5,4},{6,7},{7,6},{8,9},{9,8},{10,11... | collective-permute-start | bytes 442376 | tf_op jit(solution)/shard_map/ppermute | solution.py:323
  12.5 6.2 %collective-permute-start.4 = (bf16[144,512]{1,0:T(8,128)(2,1)S(1)}, bf16[144,512]{1,0:T(8,128)(2,1)S(1)}, u32[]{:S(2)}, u32[]{:S(2)}) collective-permute-start(bf16[144,512]{1,0:T(8,128)(2,1)S(1)} %collective-permute-done.2.refs_6_.refs_3_), channel_id=1, source_target_pairs={{4,0},{5,1},{8,4},{9,5},{12,8},{13,9},{14,12},{15,13},{10,14},{11,... | collective-permute-start | bytes 442376 | tf_op jit(solution)/shard_map/ppermute | solution.py:323
  15.9 5.2 %collective-permute-start.3 = (bf16[144,512]{1,0:T(8,128)(2,1)S(1)}, bf16[144,512]{1,0:T(8,128)(2,1)S(1)}, u32[]{:S(2)}, u32[]{:S(2)}) collective-permute-start(bf16[144,512]{1,0:T(8,128)(2,1)S(1)} %collective-permute-done.1.refs_4_.refs_2_), channel_id=1, source_target_pairs={{0,4},{1,5},{4,8},{5,9},{8,12},{9,13},{12,14},{13,15},{14,10},{15,... | collective-permute-start | bytes 442376 | tf_op jit(solution)/shard_map/ppermute | solution.py:323
  16.3 5.1 %collective-permute-start.7 = (bf16[144,512]{1,0:T(8,128)(2,1)S(1)}, bf16[144,512]{1,0:T(8,128)(2,1)S(1)}, u32[]{:S(2)}, u32[]{:S(2)}) collective-permute-start(bf16[144,512]{1,0:T(8,128)(2,1)S(1)} %collective-permute-done.refs_3_.refs_2_), channel_id=1, source_target_pairs={{0,1},{1,0},{2,3},{3,2},{4,5},{5,4},{6,7},{7,6},{8,9},{9,8},{10,11... | collective-permute-start | bytes 442376 | tf_op jit(solution)/shard_map/ppermute | solution.py:323
  18.8 5.4 %collective-permute-start.5 = (bf16[144,512]{1,0:T(8,128)(2,1)S(1)}, bf16[144,512]{1,0:T(8,128)(2,1)S(1)}, u32[]{:S(2)}, u32[]{:S(2)}) collective-permute-start(bf16[144,512]{1,0:T(8,128)(2,1)S(1)} %collective-permute-done.4.refs_7_.refs_3_), channel_id=1, source_target_pairs={{4,0},{5,1},{8,4},{9,5},{12,8},{13,9},{14,12},{15,13},{10,14},{11,... | collective-permute-start | bytes 442376 | tf_op jit(solution)/shard_map/ppermute | solution.py:323
  20.5 3.7 %collective-permute-start.10 = (bf16[144,512]{1,0:T(8,128)(2,1)S(1)}, bf16[144,512]{1,0:T(8,128)(2,1)S(1)}, u32[]{:S(2)}, u32[]{:S(2)}) collective-permute-start(bf16[144,512]{1,0:T(8,128)(2,1)S(1)} %collective-permute-done.4.refs_7_.refs_3_), channel_id=1, source_target_pairs={{0,1},{1,0},{2,3},{3,2},{4,5},{5,4},{6,7},{7,6},{8,9},{9,8},{10,11... | collective-permute-start | bytes 442376 | tf_op jit(solution)/shard_map/ppermute | solution.py:323
  20.5 3.7 %collective-permute-start.8 = (bf16[144,512]{1,0:T(8,128)(2,1)S(1)}, bf16[144,512]{1,0:T(8,128)(2,1)S(1)}, u32[]{:S(2)}, u32[]{:S(2)}) collective-permute-start(bf16[144,512]{1,0:T(8,128)(2,1)S(1)} %collective-permute-done.1.refs_4_.refs_2_), channel_id=1, source_target_pairs={{0,1},{1,0},{2,3},{3,2},{4,5},{5,4},{6,7},{7,6},{8,9},{9,8},{10,11... | collective-permute-start | bytes 442376 | tf_op jit(solution)/shard_map/ppermute | solution.py:323
  21.1 5.7 %collective-permute-start.11 = (bf16[144,512]{1,0:T(8,128)(2,1)S(1)}, bf16[144,512]{1,0:T(8,128)(2,1)S(1)}, u32[]{:S(2)}, u32[]{:S(2)}) collective-permute-start(bf16[144,512]{1,0:T(8,128)(2,1)S(1)} %collective-permute-done.3.refs_5_.refs_2_), channel_id=1, source_target_pairs={{0,4},{1,5},{4,8},{5,9},{8,12},{9,13},{12,14},{13,15},{14,10},{15,... | collective-permute-start | bytes 442376 | tf_op jit(solution)/shard_map/ppermute | solution.py:323
  21.5 5.8 %collective-permute-start.12 = (bf16[144,512]{1,0:T(8,128)(2,1)S(1)}, bf16[144,512]{1,0:T(8,128)(2,1)S(1)}, u32[]{:S(2)}, u32[]{:S(2)}) collective-permute-start(bf16[144,512]{1,0:T(8,128)(2,1)S(1)} %collective-permute-done.3.refs_5_.refs_2_), channel_id=1, source_target_pairs={{0,1},{1,0},{2,3},{3,2},{4,5},{5,4},{6,7},{7,6},{8,9},{9,8},{10,11... | collective-permute-start | bytes 442376 | tf_op jit(solution)/shard_map/ppermute | solution.py:323
  24.2 3.1 %collective-permute-start.13 = (bf16[144,512]{1,0:T(8,128)(2,1)S(1)}, bf16[144,512]{1,0:T(8,128)(2,1)S(1)}, u32[]{:S(2)}, u32[]{:S(2)}) collective-permute-start(bf16[144,512]{1,0:T(8,128)(2,1)S(1)} %collective-permute-done.5.refs_8_.refs_3_), channel_id=1, source_target_pairs={{0,1},{1,0},{2,3},{3,2},{4,5},{5,4},{6,7},{7,6},{8,9},{9,8},{10,11... | collective-permute-start | bytes 442376 | tf_op jit(solution)/shard_map/ppermute | solution.py:323
  26.8 1.5 %collective-permute-start.14 = (bf16[144,512]{1,0:T(8,128)(2,1)S(1)}, bf16[144,512]{1,0:T(8,128)(2,1)S(1)}, u32[]{:S(2)}, u32[]{:S(2)}) collective-permute-start(bf16[144,512]{1,0:T(8,128)(2,1)S(1)} %collective-permute-done.11.refs_2_.refs_14_), channel_id=1, source_target_pairs={{0,1},{1,0},{2,3},{3,2},{4,5},{5,4},{6,7},{7,6},{8,9},{9,8},{10,11... | collective-permute-start | bytes 442376 | tf_op jit(solution)/shard_map/ppermute | solution.py:323
  28.3 7.7 %collective-permute-start.15 = (bf16[1,2048,384]{2,1,0:T(8,128)(2,1)S(1)}, bf16[1,2048,384]{2,1,0:T(8,128)(2,1)S(1)}, u32[]{:S(2)}, u32[]{:S(2)}) collective-permute-start(bf16[1,2048,384]{2,1,0:T(8,128)(2,1)S(1)} %copy-done), channel_id=1, source_target_pairs={{0,1},{1,0},{2,3},{3,2},{4,5},{5,4},{6,7},{7,6},{8,9},{9,8},{10,11... | collective-permute-start | bytes 4718600 | tf_op jit(solution)/shard_map/ppermute | solution.py:323
  28.7 7.4 %collective-permute-start.16 = (bf16[1,2048,384]{2,1,0:T(8,128)(2,1)S(1)}, bf16[1,2048,384]{2,1,0:T(8,128)(2,1)S(1)}, u32[]{:S(2)}, u32[]{:S(2)}) collective-permute-start(bf16[1,2048,384]{2,1,0:T(8,128)(2,1)S(1)} %copy-done.1), channel_id=1, source_target_pairs={{0,1},{1,0},{2,3},{3,2},{4,5},{5,4},{6,7},{7,6},{8,9},{9,8},{10,11... | collective-permute-start | bytes 4718600 | tf_op jit(solution)/shard_map/ppermute | solution.py:323
  28.8 12.9 %collective-permute-start.23 = (bf16[1,384,2048]{2,1,0:T(8,128)(2,1)S(1)}, bf16[1,384,2048]{2,1,0:T(8,128)(2,1)S(1)}, u32[]{:S(2)}, u32[]{:S(2)}) collective-permute-start(bf16[1,384,2048]{2,1,0:T(8,128)(2,1)S(1)} %copy-done.2), channel_id=1, source_target_pairs={{0,1},{1,0},{2,3},{3,2},{4,5},{5,4},{6,7},{7,6},{8,9},{9,8},{10,11... | collective-permute-start | bytes 4718600 | tf_op jit(solution)/shard_map/ppermute | solution.py:323
  30.6 9.1 %collective-permute-start.19 = (bf16[64,2048]{1,0:T(8,128)(2,1)S(1)}, bf16[64,2048]{1,0:T(8,128)(2,1)S(1)}, u32[]{:S(2)}, u32[]{:S(2)}) collective-permute-start(bf16[64,2048]{1,0:T(8,128)(2,1)S(1)} %get-tuple-element.148.refs_0_), channel_id=1, source_target_pairs={{4,0},{5,1},{8,4},{9,5},{12,8},{13,9},{14,12},{15,13},{10,14},{11,... | collective-permute-start | bytes 786440 | tf_op jit(solution)/shard_map/ppermute | solution.py:323
  32.3 9.0 %collective-permute-start.17 = (bf16[64,2048]{1,0:T(8,128)(2,1)S(1)}, bf16[64,2048]{1,0:T(8,128)(2,1)S(1)}, u32[]{:S(2)}, u32[]{:S(2)}) collective-permute-start(bf16[64,2048]{1,0:T(8,128)(2,1)S(1)} %get-tuple-element.148.refs_0_), channel_id=1, source_target_pairs={{0,4},{1,5},{4,8},{5,9},{8,12},{9,13},{12,14},{13,15},{14,10},{15,... | collective-permute-start | bytes 786440 | tf_op jit(solution)/shard_map/ppermute | solution.py:323
  36.0 9.2 %collective-permute-start.22 = (bf16[64,2048]{1,0:T(8,128)(2,1)S(1)}, bf16[64,2048]{1,0:T(8,128)(2,1)S(1)}, u32[]{:S(2)}, u32[]{:S(2)}) collective-permute-start(bf16[64,2048]{1,0:T(8,128)(2,1)S(1)} %get-tuple-element.168.refs_1_), channel_id=1, source_target_pairs={{4,0},{5,1},{8,4},{9,5},{12,8},{13,9},{14,12},{15,13},{10,14},{11,... | collective-permute-start | bytes 786440 | tf_op jit(solution)/shard_map/ppermute | solution.py:323
  37.8 9.2 %collective-permute-start.21 = (bf16[64,2048]{1,0:T(8,128)(2,1)S(1)}, bf16[64,2048]{1,0:T(8,128)(2,1)S(1)}, u32[]{:S(2)}, u32[]{:S(2)}) collective-permute-start(bf16[64,2048]{1,0:T(8,128)(2,1)S(1)} %get-tuple-element.168.refs_1_), channel_id=1, source_target_pairs={{0,4},{1,5},{4,8},{5,9},{8,12},{9,13},{12,14},{13,15},{14,10},{15,... | collective-permute-start | bytes 786440 | tf_op jit(solution)/shard_map/ppermute | solution.py:323
  39.7 11.2 %collective-permute-start.20 = (bf16[64,2048]{1,0:T(8,128)(2,1)S(1)}, bf16[64,2048]{1,0:T(8,128)(2,1)S(1)}, u32[]{:S(2)}, u32[]{:S(2)}) collective-permute-start(bf16[64,2048]{1,0:T(8,128)(2,1)S(1)} %collective-permute-done.19.refs_1_), channel_id=1, source_target_pairs={{4,0},{5,1},{8,4},{9,5},{12,8},{13,9},{14,12},{15,13},{10,14},{11,... | collective-permute-start | bytes 786440 | tf_op jit(solution)/shard_map/ppermute | solution.py:323
  41.4 11.3 %collective-permute-start.18 = (bf16[64,2048]{1,0:T(8,128)(2,1)S(1)}, bf16[64,2048]{1,0:T(8,128)(2,1)S(1)}, u32[]{:S(2)}, u32[]{:S(2)}) collective-permute-start(bf16[64,2048]{1,0:T(8,128)(2,1)S(1)} %collective-permute-done.17.refs_0_), channel_id=1, source_target_pairs={{0,4},{1,5},{4,8},{5,9},{8,12},{9,13},{12,14},{13,15},{14,10},{15,... | collective-permute-start | bytes 786440 | tf_op jit(solution)/shard_map/ppermute | solution.py:323
  47.0 11.2 %collective-permute-start.26 = (bf16[64,2048]{1,0:T(8,128)(2,1)S(1)}, bf16[64,2048]{1,0:T(8,128)(2,1)S(1)}, u32[]{:S(2)}, u32[]{:S(2)}) collective-permute-start(bf16[64,2048]{1,0:T(8,128)(2,1)S(1)} %collective-permute-done.21.refs_0_), channel_id=1, source_target_pairs={{0,4},{1,5},{4,8},{5,9},{8,12},{9,13},{12,14},{13,15},{14,10},{15,... | collective-permute-start | bytes 786440 | tf_op jit(solution)/shard_map/ppermute | solution.py:323
  47.4 10.9 %collective-permute-start.27 = (bf16[64,2048]{1,0:T(8,128)(2,1)S(1)}, bf16[64,2048]{1,0:T(8,128)(2,1)S(1)}, u32[]{:S(2)}, u32[]{:S(2)}) collective-permute-start(bf16[64,2048]{1,0:T(8,128)(2,1)S(1)} %collective-permute-done.22.refs_1_), channel_id=1, source_target_pairs={{4,0},{5,1},{8,4},{9,5},{12,8},{13,9},{14,12},{15,13},{10,14},{11,... | collective-permute-start | bytes 786440 | tf_op jit(solution)/shard_map/ppermute | solution.py:323
  52.6 11.2 %collective-permute-start.24 = (bf16[64,2048]{1,0:T(8,128)(2,1)S(1)}, bf16[64,2048]{1,0:T(8,128)(2,1)S(1)}, u32[]{:S(2)}, u32[]{:S(2)}) collective-permute-start(bf16[64,2048]{1,0:T(8,128)(2,1)S(1)} %collective-permute-done.18.refs_0_), channel_id=1, source_target_pairs={{0,4},{1,5},{4,8},{5,9},{8,12},{9,13},{12,14},{13,15},{14,10},{15,... | collective-permute-start | bytes 786440 | tf_op jit(solution)/shard_map/ppermute | solution.py:323
  53.0 10.9 %collective-permute-start.25 = (bf16[64,2048]{1,0:T(8,128)(2,1)S(1)}, bf16[64,2048]{1,0:T(8,128)(2,1)S(1)}, u32[]{:S(2)}, u32[]{:S(2)}) collective-permute-start(bf16[64,2048]{1,0:T(8,128)(2,1)S(1)} %collective-permute-done.20.refs_1_), channel_id=1, source_target_pairs={{4,0},{5,1},{8,4},{9,5},{12,8},{13,9},{14,12},{15,13},{10,14},{11,... | collective-permute-start | bytes 786440 | tf_op jit(solution)/shard_map/ppermute | solution.py:323
  58.2 11.2 %collective-permute-start.29 = (bf16[64,2048]{1,0:T(8,128)(2,1)S(1)}, bf16[64,2048]{1,0:T(8,128)(2,1)S(1)}, u32[]{:S(2)}, u32[]{:S(2)}) collective-permute-start(bf16[64,2048]{1,0:T(8,128)(2,1)S(1)} %collective-permute-done.26.refs_0_), channel_id=1, source_target_pairs={{0,4},{1,5},{4,8},{5,9},{8,12},{9,13},{12,14},{13,15},{14,10},{15,... | collective-permute-start | bytes 786440 | tf_op jit(solution)/shard_map/ppermute | solution.py:323
  58.6 10.9 %collective-permute-start.30 = (bf16[64,2048]{1,0:T(8,128)(2,1)S(1)}, bf16[64,2048]{1,0:T(8,128)(2,1)S(1)}, u32[]{:S(2)}, u32[]{:S(2)}) collective-permute-start(bf16[64,2048]{1,0:T(8,128)(2,1)S(1)} %collective-permute-done.27.refs_1_), channel_id=1, source_target_pairs={{4,0},{5,1},{8,4},{9,5},{12,8},{13,9},{14,12},{15,13},{10,14},{11,... | collective-permute-start | bytes 786440 | tf_op jit(solution)/shard_map/ppermute | solution.py:323
  63.9 11.1 %collective-permute-start.28 = (bf16[64,2048]{1,0:T(8,128)(2,1)S(1)}, bf16[64,2048]{1,0:T(8,128)(2,1)S(1)}, u32[]{:S(2)}, u32[]{:S(2)}) collective-permute-start(bf16[64,2048]{1,0:T(8,128)(2,1)S(1)} %collective-permute-done.24.refs_0_), channel_id=1, source_target_pairs={{0,4},{1,5},{4,8},{5,9},{8,12},{9,13},{12,14},{13,15},{14,10},{15,... | collective-permute-start | bytes 786440 | tf_op jit(solution)/shard_map/ppermute | solution.py:323
  69.5 8.7 %collective-permute-start.31 = (bf16[64,2048]{1,0:T(8,128)(2,1)S(1)}, bf16[64,2048]{1,0:T(8,128)(2,1)S(1)}, u32[]{:S(2)}, u32[]{:S(2)}) collective-permute-start(bf16[64,2048]{1,0:T(8,128)(2,1)S(1)} %collective-permute-done.30.refs_1_), channel_id=1, source_target_pairs={{4,0},{5,1},{8,4},{9,5},{12,8},{13,9},{14,12},{15,13},{10,14},{11,... | collective-permute-start | bytes 786440 | tf_op jit(solution)/shard_map/ppermute | solution.py:323
  72.9 10.9 %collective-permute-start.32 = (bf16[64,2048]{1,0:T(8,128)(2,1)S(1)}, bf16[64,2048]{1,0:T(8,128)(2,1)S(1)}, u32[]{:S(2)}, u32[]{:S(2)}) collective-permute-start(bf16[64,2048]{1,0:T(8,128)(2,1)S(1)} %get-tuple-element.215), channel_id=1, source_target_pairs={{0,4},{1,5},{4,8},{5,9},{8,12},{9,13},{12,14},{13,15},{14,10},{15,... | collective-permute-start | bytes 786440 | tf_op jit(solution)/shard_map/ppermute | solution.py:323
  73.4 10.4 %collective-permute-start.33 = (bf16[64,2048]{1,0:T(8,128)(2,1)S(1)}, bf16[64,2048]{1,0:T(8,128)(2,1)S(1)}, u32[]{:S(2)}, u32[]{:S(2)}) collective-permute-start(bf16[64,2048]{1,0:T(8,128)(2,1)S(1)} %get-tuple-element.219), channel_id=1, source_target_pairs={{4,0},{5,1},{8,4},{9,5},{12,8},{13,9},{14,12},{15,13},{10,14},{11,... | collective-permute-start | bytes 786440 | tf_op jit(solution)/shard_map/ppermute | solution.py:323
  80.0 7.9 %collective-permute-start.34 = (bf16[64,2048]{1,0:T(8,128)(2,1)S(1)}, bf16[64,2048]{1,0:T(8,128)(2,1)S(1)}, u32[]{:S(2)}, u32[]{:S(2)}) collective-permute-start(bf16[64,2048]{1,0:T(8,128)(2,1)S(1)} %get-tuple-element.217), channel_id=1, source_target_pairs={{0,4},{1,5},{4,8},{5,9},{8,12},{9,13},{12,14},{13,15},{14,10},{15,... | collective-permute-start | bytes 786440 | tf_op jit(solution)/shard_map/ppermute | solution.py:323
  80.9 7.9 %collective-permute-start.38 = (bf16[64,2048]{1,0:T(8,128)(2,1)S(1)}, bf16[64,2048]{1,0:T(8,128)(2,1)S(1)}, u32[]{:S(2)}, u32[]{:S(2)}) collective-permute-start(bf16[64,2048]{1,0:T(8,128)(2,1)S(1)} %get-tuple-element.218), channel_id=1, source_target_pairs={{4,0},{5,1},{8,4},{9,5},{12,8},{13,9},{14,12},{15,13},{10,14},{11,... | collective-permute-start | bytes 786440 | tf_op jit(solution)/shard_map/ppermute | solution.py:323
  88.0 9.3 %collective-permute-start.35 = (bf16[64,2048]{1,0:T(8,128)(2,1)S(1)}, bf16[64,2048]{1,0:T(8,128)(2,1)S(1)}, u32[]{:S(2)}, u32[]{:S(2)}) collective-permute-start(bf16[64,2048]{1,0:T(8,128)(2,1)S(1)} %add_convert_fusion.11), channel_id=1, source_target_pairs={{0,4},{1,5},{4,8},{5,9},{8,12},{9,13},{12,14},{13,15},{14,10},{15,... | collective-permute-start | bytes 786440 | tf_op jit(solution)/shard_map/ppermute | solution.py:323
  88.9 9.3 %collective-permute-start.40 = (bf16[64,2048]{1,0:T(8,128)(2,1)S(1)}, bf16[64,2048]{1,0:T(8,128)(2,1)S(1)}, u32[]{:S(2)}, u32[]{:S(2)}) collective-permute-start(bf16[64,2048]{1,0:T(8,128)(2,1)S(1)} %add_convert_fusion.8), channel_id=1, source_target_pairs={{4,0},{5,1},{8,4},{9,5},{12,8},{13,9},{14,12},{15,13},{10,14},{11,... | collective-permute-start | bytes 786440 | tf_op jit(solution)/shard_map/ppermute | solution.py:323
  90.3 13.5 %collective-permute-start.39 = (bf16[64,2048]{1,0:T(8,128)(2,1)S(1)}, bf16[64,2048]{1,0:T(8,128)(2,1)S(1)}, u32[]{:S(2)}, u32[]{:S(2)}) collective-permute-start(bf16[64,2048]{1,0:T(8,128)(2,1)S(1)} %add_convert_fusion.7), channel_id=1, source_target_pairs={{4,0},{5,1},{8,4},{9,5},{12,8},{13,9},{14,12},{15,13},{10,14},{11,... | collective-permute-start | bytes 786440 | tf_op jit(solution)/shard_map/ppermute | solution.py:323
  91.9 11.0 %collective-permute-start.42 = (bf16[64,2048]{1,0:T(8,128)(2,1)S(1)}, bf16[64,2048]{1,0:T(8,128)(2,1)S(1)}, u32[]{:S(2)}, u32[]{:S(2)}) collective-permute-start(bf16[64,2048]{1,0:T(8,128)(2,1)S(1)} %add_convert_fusion.3), channel_id=1, source_target_pairs={{0,4},{1,5},{4,8},{5,9},{8,12},{9,13},{12,14},{13,15},{14,10},{15,... | collective-permute-start | bytes 786440 | tf_op jit(solution)/shard_map/ppermute | solution.py:323
  97.4 11.2 %collective-permute-start.36 = (bf16[64,2048]{1,0:T(8,128)(2,1)S(1)}, bf16[64,2048]{1,0:T(8,128)(2,1)S(1)}, u32[]{:S(2)}, u32[]{:S(2)}) collective-permute-start(bf16[64,2048]{1,0:T(8,128)(2,1)S(1)} %add_convert_fusion.10), channel_id=1, source_target_pairs={{0,4},{1,5},{4,8},{5,9},{8,12},{9,13},{12,14},{13,15},{14,10},{15,... | collective-permute-start | bytes 786440 | tf_op jit(solution)/shard_map/ppermute | solution.py:323
  98.2 11.2 %collective-permute-start.44 = (bf16[64,2048]{1,0:T(8,128)(2,1)S(1)}, bf16[64,2048]{1,0:T(8,128)(2,1)S(1)}, u32[]{:S(2)}, u32[]{:S(2)}) collective-permute-start(bf16[64,2048]{1,0:T(8,128)(2,1)S(1)} %add_convert_fusion.6), channel_id=1, source_target_pairs={{4,0},{5,1},{8,4},{9,5},{12,8},{13,9},{14,12},{15,13},{10,14},{11,... | collective-permute-start | bytes 786440 | tf_op jit(solution)/shard_map/ppermute | solution.py:323
  103.8 8.7 %collective-permute-start.41 = (bf16[64,2048]{1,0:T(8,128)(2,1)S(1)}, bf16[64,2048]{1,0:T(8,128)(2,1)S(1)}, u32[]{:S(2)}, u32[]{:S(2)}) collective-permute-start(bf16[64,2048]{1,0:T(8,128)(2,1)S(1)} %add_convert_fusion.5), channel_id=1, source_target_pairs={{4,0},{5,1},{8,4},{9,5},{12,8},{13,9},{14,12},{15,13},{10,14},{11,... | collective-permute-start | bytes 786440 | tf_op jit(solution)/shard_map/ppermute | solution.py:323
  105.2 10.1 %collective-permute-start.43 = (bf16[64,2048]{1,0:T(8,128)(2,1)S(1)}, bf16[64,2048]{1,0:T(8,128)(2,1)S(1)}, u32[]{:S(2)}, u32[]{:S(2)}) collective-permute-start(bf16[64,2048]{1,0:T(8,128)(2,1)S(1)} %add_convert_fusion.2), channel_id=1, source_target_pairs={{0,4},{1,5},{4,8},{5,9},{8,12},{9,13},{12,14},{13,15},{14,10},{15,... | collective-permute-start | bytes 786440 | tf_op jit(solution)/shard_map/ppermute | solution.py:323
  108.6 6.6 %collective-permute-start.37 = (bf16[64,2048]{1,0:T(8,128)(2,1)S(1)}, bf16[64,2048]{1,0:T(8,128)(2,1)S(1)}, u32[]{:S(2)}, u32[]{:S(2)}) collective-permute-start(bf16[64,2048]{1,0:T(8,128)(2,1)S(1)} %add_convert_fusion.9), channel_id=1, source_target_pairs={{0,4},{1,5},{4,8},{5,9},{8,12},{9,13},{12,14},{13,15},{14,10},{15,... | collective-permute-start | bytes 786440 | tf_op jit(solution)/shard_map/ppermute | solution.py:323
  109.5 6.4 %collective-permute-start.45 = (bf16[64,2048]{1,0:T(8,128)(2,1)S(1)}, bf16[64,2048]{1,0:T(8,128)(2,1)S(1)}, u32[]{:S(2)}, u32[]{:S(2)}) collective-permute-start(bf16[64,2048]{1,0:T(8,128)(2,1)S(1)} %add_convert_fusion.1), channel_id=1, source_target_pairs={{4,0},{5,1},{8,4},{9,5},{12,8},{13,9},{14,12},{15,13},{10,14},{11,... | collective-permute-start | bytes 786440 | tf_op jit(solution)/shard_map/ppermute | solution.py:323
  (4 other events, 60.4 us)

commit v11 on v10

--- a/solution.py
+++ b/solution.py
@@ -389,14 +389,14 @@
     out_right = {key: pair[1] for key, pair in outs.items()}
 
     sums_on = {1: send(out_right[far - 1, 1], onward)}
-    sums_back = {0: send(out_left[far - 1, 0], back)}
+    sums_back = {0: send(later(out_left[far - 1, 0], from_right[far, 1]), back)}
     (far_upper, far_lower), unused = experts_on(
         [(from_left[far, 0], 0, 0), (from_right[far, 1], 0, 1)], [left[far]], outs[far - 1, 1]
     )
     sums_on[0] = send(far_upper, onward)
     sums_back[1] = send(far_lower, back)
     own_out, unused = experts_on(
-        [(upper, 0, 0), (lower, 0, 1)], [message], (far_upper, far_lower, sums_on[1], sums_back[0])
+        [(upper, 0, 0), (lower, 0, 1)], [message], (far_upper, far_lower, sums_on[1])
     )
     for hop in range(far - 1, 0, -1):
         onto, backto = sums_on[0], sums_back[1]

time: 117 us -> 119 us (1.017)
  waiting for transfers between devices: 50.6 us -> 53.4 us
    ppermute x46, waiting for transfers between devices: 50.6 us -> 53.4 us  [send(): return lax.ppermute(array, 'ctx', pairs)]
  transfers between devices with their start and end apart: 46 -> 46, of which waited for: 25 -> 28; matrix products, arithmetic and copies ran while one was open for 2% -> 2% of each run, Pallas kernels for 19% -> 19%
where the time goes in v11:
time: 119 us
  waiting for transfers between devices  53.4 us (45%)
  starting transfers between devices  37.7 us (32%)
  Pallas kernels  23.5 us (20%)
  other arithmetic  3.02 us (3%)
    ppermute x46, waiting for transfers between devices, send(): return lax.ppermute(array, 'ctx', pairs)  53.4 us
    ppermute x46, starting transfers between devices, send(): return lax.ppermute(array, 'ctx', pairs)  37.7 us
    pallas_call x8, Pallas kernels, run_experts(): pl.pallas_call(functools.partial(expert_kernel, [piece[1:] for piece in p...  14.7 us
    pallas_call x3, Pallas kernels, attend_call(): pl.pallas_call(functools.partial(attend_kernel, count, half, begun, ended...  7.23 us
  transfers between devices with their start and end apart: 46, of which 28 were waited for; matrix products, arithmetic and copies ran while one was open for 2% of the time, Pallas kernels for 19%

profile of v11, /device:TPU:0, one launch (start us, length us, event | category | flops | bytes accessed | tf_op | source)
XLA Modules:
  0.0 118.6 jit_solution(5333176892654892617)
XLA Ops:
  0.7 1.6 %pack_message.1.refs_1_.refs_2_ = bf16[144,512]{1,0:T(8,128)(2,1)} custom-call(s32[1]{0:T(128)S(6)} %copy.12.pos_ref, bf16[128,256]{1,0:T(8,128)(2,1)} %key_ref.1, bf16[128,256]{1,0:T(8,128)(2,1)} %value_ref.1, s32[8,128]{1,0:T(8,128)} %bitcast.2, f32[8,128]{1,0:T(8,128)} %bitcast.3), custom_call_target="tpu_custom_call" | custom-call | tf_op jit(solution)/shard_map/pack_message/pallas_call | solution.py:54
  2.3 3.0 %collective-permute-start.2 = (bf16[144,512]{1,0:T(8,128)(2,1)}, bf16[144,512]{1,0:T(8,128)(2,1)S(1)}, u32[]{:S(2)}, u32[]{:S(2)}) collective-permute-start(bf16[144,512]{1,0:T(8,128)(2,1)} %pack_message.1.refs_1_.refs_2_), channel_id=1, source_target_pairs={{4,0},{5,1},{8,4},{9,5},{12,8},{13,9},{14,12},{15,13},{10,14},{11,... | collective-permute-start | bytes 442376 | tf_op jit(solution)/shard_map/ppermute | solution.py:323
  5.3 4.1 %collective-permute-done.2.refs_6_.refs_3_ = bf16[144,512]{1,0:T(8,128)(2,1)S(1)} collective-permute-done((bf16[144,512]{1,0:T(8,128)(2,1)}, bf16[144,512]{1,0:T(8,128)(2,1)S(1)}, u32[]{:S(2)}, u32[]{:S(2)}) %collective-permute-start.2) | collective-permute-done | bytes 147488 | tf_op jit(solution)/shard_map/ppermute | solution.py:323
  9.4 1.3 %collective-permute-done.refs_3_.refs_2_ = bf16[144,512]{1,0:T(8,128)(2,1)S(1)} collective-permute-done((bf16[144,512]{1,0:T(8,128)(2,1)}, bf16[144,512]{1,0:T(8,128)(2,1)S(1)}, u32[]{:S(2)}, u32[]{:S(2)}) %collective-permute-start) | collective-permute-done | bytes 147488 | tf_op jit(solution)/shard_map/ppermute | solution.py:323
  12.5 1.7 %collective-permute-start.4 = (bf16[144,512]{1,0:T(8,128)(2,1)S(1)}, bf16[144,512]{1,0:T(8,128)(2,1)S(1)}, u32[]{:S(2)}, u32[]{:S(2)}) collective-permute-start(bf16[144,512]{1,0:T(8,128)(2,1)S(1)} %collective-permute-done.2.refs_6_.refs_3_), channel_id=1, source_target_pairs={{4,0},{5,1},{8,4},{9,5},{12,8},{13,9},{14,12},{15,13},{10,14},{11,... | collective-permute-start | bytes 442376 | tf_op jit(solution)/shard_map/ppermute | solution.py:323
  14.3 1.6 %collective-permute-done.1.refs_4_.refs_2_ = bf16[144,512]{1,0:T(8,128)(2,1)S(1)} collective-permute-done((bf16[144,512]{1,0:T(8,128)(2,1)S(1)}, bf16[144,512]{1,0:T(8,128)(2,1)S(1)}, u32[]{:S(2)}, u32[]{:S(2)}) %collective-permute-start.1) | collective-permute-done | bytes 147488 | tf_op jit(solution)/shard_map/ppermute | solution.py:323
  16.3 2.5 %collective-permute-done.4.refs_7_.refs_3_ = bf16[144,512]{1,0:T(8,128)(2,1)S(1)} collective-permute-done((bf16[144,512]{1,0:T(8,128)(2,1)S(1)}, bf16[144,512]{1,0:T(8,128)(2,1)S(1)}, u32[]{:S(2)}, u32[]{:S(2)}) %collective-permute-start.4) | collective-permute-done | bytes 147488 | tf_op jit(solution)/shard_map/ppermute | solution.py:323
  18.8 1.7 %collective-permute-start.5 = (bf16[144,512]{1,0:T(8,128)(2,1)S(1)}, bf16[144,512]{1,0:T(8,128)(2,1)S(1)}, u32[]{:S(2)}, u32[]{:S(2)}) collective-permute-start(bf16[144,512]{1,0:T(8,128)(2,1)S(1)} %collective-permute-done.4.refs_7_.refs_3_), channel_id=1, source_target_pairs={{4,0},{5,1},{8,4},{9,5},{12,8},{13,9},{14,12},{15,13},{10,14},{11,... | collective-permute-start | bytes 442376 | tf_op jit(solution)/shard_map/ppermute | solution.py:323
  21.5 2.7 %collective-permute-done.5.refs_8_.refs_3_ = bf16[144,512]{1,0:T(8,128)(2,1)S(1)} collective-permute-done((bf16[144,512]{1,0:T(8,128)(2,1)S(1)}, bf16[144,512]{1,0:T(8,128)(2,1)S(1)}, u32[]{:S(2)}, u32[]{:S(2)}) %collective-permute-start.5) | collective-permute-done | bytes 147488 | tf_op jit(solution)/shard_map/ppermute | solution.py:323
  24.2 2.5 %attend.3 = (f32[1024,256]{1,0:T(8,128)S(1)}, f32[1024,128]{1,0:T(8,128)S(1)}) custom-call(bf16[128,2048]{1,0:T(8,128)(2,1)S(1)} %broadcast_multiply_fusion.refs_0_, bf16[144,512]{1,0:T(8,128)(2,1)S(1)} %copy-done.3, bf16[144,512]{1,0:T(8,128)(2,1)S(1)} %copy-done.3, bf16[144,512]{1,0:T(8,128)(2,1)S(1)} %collective-permute-done.refs_3_.refs_2_, ...), custom_call_target="tpu_custom_call" | custom-call | bytes 1024 | tf_op jit(solution)/shard_map/attend/pallas_call | solution.py:182
  29.2 1.4 %attend.4 = (f32[64,2048]{1,0:T(8,128)S(1)}, bf16[64,2048]{1,0:T(8,128)(2,1)S(1)}) custom-call(bf16[128,2048]{1,0:T(8,128)(2,1)S(1)} %broadcast_multiply_fusion.refs_0_, bf16[144,512]{1,0:T(8,128)(2,1)S(1)} %copy-done.3, bf16[144,512]{1,0:T(8,128)(2,1)S(1)} %collective-permute-done.11.refs_2_.refs_14_, ...), custom_call_target="tpu_custom_call" | custom-call | flops 536870912 | bytes 4194304 | tf_op jit(solution)/shard_map/attend/pallas_call | solution.py:182
  30.6 1.7 %collective-permute-start.19 = (bf16[64,2048]{1,0:T(8,128)(2,1)S(1)}, bf16[64,2048]{1,0:T(8,128)(2,1)S(1)}, u32[]{:S(2)}, u32[]{:S(2)}) collective-permute-start(bf16[64,2048]{1,0:T(8,128)(2,1)S(1)} %get-tuple-element.149.refs_0_), channel_id=1, source_target_pairs={{4,0},{5,1},{8,4},{9,5},{12,8},{13,9},{14,12},{15,13},{10,14},{11,... | collective-permute-start | bytes 786440 | tf_op jit(solution)/shard_map/ppermute | solution.py:323
  32.7 3.3 %attend.5 = (f32[64,2048]{1,0:T(8,128)S(1)}, bf16[64,2048]{1,0:T(8,128)(2,1)S(1)}) custom-call(bf16[128,2048]{1,0:T(8,128)(2,1)S(1)} %broadcast_multiply_fusion.refs_0_, bf16[144,512]{1,0:T(8,128)(2,1)S(1)} %copy-done.3, bf16[144,512]{1,0:T(8,128)(2,1)S(1)} %copy-done.3, bf16[144,512]{1,0:T(8,128)(2,1)S(1)} %collective-permute-done.refs_3_.refs_2_, ...), custom_call_target="tpu_custom_call" | custom-call | flops 2147483648 | bytes 4194304 | tf_op jit(solution)/shard_map/attend/pallas_call | solution.py:182
  36.0 1.7 %collective-permute-start.22 = (bf16[64,2048]{1,0:T(8,128)(2,1)S(1)}, bf16[64,2048]{1,0:T(8,128)(2,1)S(1)}, u32[]{:S(2)}, u32[]{:S(2)}) collective-permute-start(bf16[64,2048]{1,0:T(8,128)(2,1)S(1)} %get-tuple-element.169.refs_1_), channel_id=1, source_target_pairs={{4,0},{5,1},{8,4},{9,5},{12,8},{13,9},{14,12},{15,13},{10,14},{11,... | collective-permute-start | bytes 786440 | tf_op jit(solution)/shard_map/ppermute | solution.py:323
  38.1 1.5 %collective-permute-done.19.refs_1_ = bf16[64,2048]{1,0:T(8,128)(2,1)S(1)} collective-permute-done((bf16[64,2048]{1,0:T(8,128)(2,1)S(1)}, bf16[64,2048]{1,0:T(8,128)(2,1)S(1)}, u32[]{:S(2)}, u32[]{:S(2)}) %collective-permute-start.19) | collective-permute-done | bytes 262176 | tf_op jit(solution)/shard_map/ppermute | solution.py:323
  39.7 1.7 %collective-permute-start.20 = (bf16[64,2048]{1,0:T(8,128)(2,1)S(1)}, bf16[64,2048]{1,0:T(8,128)(2,1)S(1)}, u32[]{:S(2)}, u32[]{:S(2)}) collective-permute-start(bf16[64,2048]{1,0:T(8,128)(2,1)S(1)} %collective-permute-done.19.refs_1_), channel_id=1, source_target_pairs={{4,0},{5,1},{8,4},{9,5},{12,8},{13,9},{14,12},{15,13},{10,14},{11,... | collective-permute-start | bytes 786440 | tf_op jit(solution)/shard_map/ppermute | solution.py:323
  41.7 1.8 %experts.8 = (bf16[64,2048]{1,0:T(8,128)(2,1)S(1)}, bf16[64,2048]{1,0:T(8,128)(2,1)S(1)}) custom-call(bf16[64,2048]{1,0:T(8,128)(2,1)S(1)} %collective-permute-done.17.refs_0_, bf16[64,2048]{1,0:T(8,128)(2,1)S(1)} %collective-permute-done.19.refs_1_, bf16[144,512]{1,0:T(8,128)(2,1)S(1)} %collective-permute-done.refs_3_.refs_2_, ...), custom_call_target="tpu_custom_call" | custom-call | flops 1207959552 | bytes 9437184 | tf_op jit(solution)/shard_map/experts/pallas_call | solution.py:283
  43.5 1.7 %collective-permute-done.22.refs_1_ = bf16[64,2048]{1,0:T(8,128)(2,1)S(1)} collective-permute-done((bf16[64,2048]{1,0:T(8,128)(2,1)S(1)}, bf16[64,2048]{1,0:T(8,128)(2,1)S(1)}, u32[]{:S(2)}, u32[]{:S(2)}) %collective-permute-start.22) | collective-permute-done | bytes 262176 | tf_op jit(solution)/shard_map/ppermute | solution.py:323
  45.3 1.7 %collective-permute-done.21.refs_0_ = bf16[64,2048]{1,0:T(8,128)(2,1)S(1)} collective-permute-done((bf16[64,2048]{1,0:T(8,128)(2,1)S(1)}, bf16[64,2048]{1,0:T(8,128)(2,1)S(1)}, u32[]{:S(2)}, u32[]{:S(2)}) %collective-permute-start.21) | collective-permute-done | bytes 262176 | tf_op jit(solution)/shard_map/ppermute | solution.py:323
  47.4 1.7 %collective-permute-start.27 = (bf16[64,2048]{1,0:T(8,128)(2,1)S(1)}, bf16[64,2048]{1,0:T(8,128)(2,1)S(1)}, u32[]{:S(2)}, u32[]{:S(2)}) collective-permute-start(bf16[64,2048]{1,0:T(8,128)(2,1)S(1)} %collective-permute-done.22.refs_1_), channel_id=1, source_target_pairs={{4,0},{5,1},{8,4},{9,5},{12,8},{13,9},{14,12},{15,13},{10,14},{11,... | collective-permute-start | bytes 786440 | tf_op jit(solution)/shard_map/ppermute | solution.py:323
  49.0 1.8 %experts.9 = (bf16[64,2048]{1,0:T(8,128)(2,1)S(1)}, bf16[64,2048]{1,0:T(8,128)(2,1)S(1)}) custom-call(bf16[64,2048]{1,0:T(8,128)(2,1)S(1)} %collective-permute-done.21.refs_0_, bf16[64,2048]{1,0:T(8,128)(2,1)S(1)} %collective-permute-done.22.refs_1_, bf16[144,512]{1,0:T(8,128)(2,1)S(1)} %collective-permute-done.refs_3_.refs_2_, ...), custom_call_target="tpu_custom_call" | custom-call | flops 1207959552 | bytes 9437184 | tf_op jit(solution)/shard_map/experts/pallas_call | solution.py:283
  50.9 1.7 %collective-permute-done.18.refs_0_ = bf16[64,2048]{1,0:T(8,128)(2,1)S(1)} collective-permute-done((bf16[64,2048]{1,0:T(8,128)(2,1)S(1)}, bf16[64,2048]{1,0:T(8,128)(2,1)S(1)}, u32[]{:S(2)}, u32[]{:S(2)}) %collective-permute-start.18) | collective-permute-done | bytes 262176 | tf_op jit(solution)/shard_map/ppermute | solution.py:323
  53.0 1.7 %collective-permute-start.25 = (bf16[64,2048]{1,0:T(8,128)(2,1)S(1)}, bf16[64,2048]{1,0:T(8,128)(2,1)S(1)}, u32[]{:S(2)}, u32[]{:S(2)}) collective-permute-start(bf16[64,2048]{1,0:T(8,128)(2,1)S(1)} %collective-permute-done.20.refs_1_), channel_id=1, source_target_pairs={{4,0},{5,1},{8,4},{9,5},{12,8},{13,9},{14,12},{15,13},{10,14},{11,... | collective-permute-start | bytes 786440 | tf_op jit(solution)/shard_map/ppermute | solution.py:323
  54.7 1.8 %experts.10 = (bf16[64,2048]{1,0:T(8,128)(2,1)S(1)}, bf16[64,2048]{1,0:T(8,128)(2,1)S(1)}) custom-call(bf16[64,2048]{1,0:T(8,128)(2,1)S(1)} %collective-permute-done.18.refs_0_, bf16[64,2048]{1,0:T(8,128)(2,1)S(1)} %collective-permute-done.20.refs_1_, bf16[144,512]{1,0:T(8,128)(2,1)S(1)} %collective-permute-done.1.refs_4_.refs_2_, ...), custom_call_target="tpu_custom_call" | custom-call | flops 1207959552 | bytes 9437184 | tf_op jit(solution)/shard_map/experts/pallas_call | solution.py:283
  56.5 1.7 %collective-permute-done.26.refs_0_ = bf16[64,2048]{1,0:T(8,128)(2,1)S(1)} collective-permute-done((bf16[64,2048]{1,0:T(8,128)(2,1)S(1)}, bf16[64,2048]{1,0:T(8,128)(2,1)S(1)}, u32[]{:S(2)}, u32[]{:S(2)}) %collective-permute-start.26) | collective-permute-done | bytes 262176 | tf_op jit(solution)/shard_map/ppermute | solution.py:323
  58.6 1.7 %collective-permute-start.30 = (bf16[64,2048]{1,0:T(8,128)(2,1)S(1)}, bf16[64,2048]{1,0:T(8,128)(2,1)S(1)}, u32[]{:S(2)}, u32[]{:S(2)}) collective-permute-start(bf16[64,2048]{1,0:T(8,128)(2,1)S(1)} %collective-permute-done.27.refs_1_), channel_id=1, source_target_pairs={{4,0},{5,1},{8,4},{9,5},{12,8},{13,9},{14,12},{15,13},{10,14},{11,... | collective-permute-start | bytes 786440 | tf_op jit(solution)/shard_map/ppermute | solution.py:323
  60.3 1.8 %experts.11 = (bf16[64,2048]{1,0:T(8,128)(2,1)S(1)}, bf16[64,2048]{1,0:T(8,128)(2,1)S(1)}) custom-call(bf16[64,2048]{1,0:T(8,128)(2,1)S(1)} %collective-permute-done.26.refs_0_, bf16[64,2048]{1,0:T(8,128)(2,1)S(1)} %collective-permute-done.27.refs_1_, bf16[144,512]{1,0:T(8,128)(2,1)S(1)} %collective-permute-done.1.refs_4_.refs_2_, ...), custom_call_target="tpu_custom_call" | custom-call | flops 1207959552 | bytes 9437184 | tf_op jit(solution)/shard_map/experts/pallas_call | solution.py:283
  62.1 1.7 %collective-permute-done.24.refs_0_ = bf16[64,2048]{1,0:T(8,128)(2,1)S(1)} collective-permute-done((bf16[64,2048]{1,0:T(8,128)(2,1)S(1)}, bf16[64,2048]{1,0:T(8,128)(2,1)S(1)}, u32[]{:S(2)}, u32[]{:S(2)}) %collective-permute-start.24) | collective-permute-done | bytes 262176 | tf_op jit(solution)/shard_map/ppermute | solution.py:323
  64.2 1.8 %experts.12 = (bf16[64,2048]{1,0:T(8,128)(2,1)S(1)}, bf16[64,2048]{1,0:T(8,128)(2,1)S(1)}) custom-call(bf16[64,2048]{1,0:T(8,128)(2,1)S(1)} %collective-permute-done.24.refs_0_, bf16[64,2048]{1,0:T(8,128)(2,1)S(1)} %collective-permute-done.25.refs_1_, bf16[144,512]{1,0:T(8,128)(2,1)S(1)} %collective-permute-done.3.refs_5_.refs_2_, ...), custom_call_target="tpu_custom_call" | custom-call | flops 1207959552 | bytes 9437184 | tf_op jit(solution)/shard_map/experts/pallas_call | solution.py:283
  66.1 3.4 %collective-permute-done.29.refs_0_ = bf16[64,2048]{1,0:T(8,128)(2,1)S(1)} collective-permute-done((bf16[64,2048]{1,0:T(8,128)(2,1)S(1)}, bf16[64,2048]{1,0:T(8,128)(2,1)S(1)}, u32[]{:S(2)}, u32[]{:S(2)}) %collective-permute-start.29) | collective-permute-done | bytes 262176 | tf_op jit(solution)/shard_map/ppermute | solution.py:323
  69.5 1.6 %collective-permute-start.31 = (bf16[64,2048]{1,0:T(8,128)(2,1)S(1)}, bf16[64,2048]{1,0:T(8,128)(2,1)S(1)}, u32[]{:S(2)}, u32[]{:S(2)}) collective-permute-start(bf16[64,2048]{1,0:T(8,128)(2,1)S(1)} %collective-permute-done.30.refs_1_), channel_id=1, source_target_pairs={{4,0},{5,1},{8,4},{9,5},{12,8},{13,9},{14,12},{15,13},{10,14},{11,... | collective-permute-start | bytes 786440 | tf_op jit(solution)/shard_map/ppermute | solution.py:323
  71.0 1.8 %experts.13 = (bf16[64,2048]{1,0:T(8,128)(2,1)S(1)}, bf16[64,2048]{1,0:T(8,128)(2,1)S(1)}) custom-call(bf16[64,2048]{1,0:T(8,128)(2,1)S(1)} %collective-permute-done.29.refs_0_, bf16[64,2048]{1,0:T(8,128)(2,1)S(1)} %collective-permute-done.30.refs_1_, bf16[144,512]{1,0:T(8,128)(2,1)S(1)} %collective-permute-done.3.refs_5_.refs_2_, ...), custom_call_target="tpu_custom_call" | custom-call | flops 1207959552 | bytes 9437184 | tf_op jit(solution)/shard_map/experts/pallas_call | solution.py:283
  73.4 1.3 %collective-permute-done.28.refs_0_ = bf16[64,2048]{1,0:T(8,128)(2,1)S(1)} collective-permute-done((bf16[64,2048]{1,0:T(8,128)(2,1)S(1)}, bf16[64,2048]{1,0:T(8,128)(2,1)S(1)}, u32[]{:S(2)}, u32[]{:S(2)}) %collective-permute-start.28) | collective-permute-done | bytes 262176 | tf_op jit(solution)/shard_map/ppermute | solution.py:323
  75.9 1.8 %experts.14 = (bf16[64,2048]{1,0:T(8,128)(2,1)S(1)}, bf16[64,2048]{1,0:T(8,128)(2,1)S(1)}) custom-call(bf16[64,2048]{1,0:T(8,128)(2,1)S(1)} %collective-permute-done.28.refs_0_, bf16[64,2048]{1,0:T(8,128)(2,1)S(1)} %collective-permute-done.31.refs_1_, bf16[144,512]{1,0:T(8,128)(2,1)S(1)} %collective-permute-done.11.refs_2_.refs_14_, ...), custom_call_target="tpu_custom_call" | custom-call | flops 1207959552 | bytes 9437184 | tf_op jit(solution)/shard_map/experts/pallas_call | solution.py:283
  78.4 1.4 %collective-permute-start.38 = (bf16[64,2048]{1,0:T(8,128)(2,1)S(1)}, bf16[64,2048]{1,0:T(8,128)(2,1)S(1)}, u32[]{:S(2)}, u32[]{:S(2)}) collective-permute-start(bf16[64,2048]{1,0:T(8,128)(2,1)S(1)} %get-tuple-element.219), channel_id=1, source_target_pairs={{4,0},{5,1},{8,4},{9,5},{12,8},{13,9},{14,12},{15,13},{10,14},{11,... | collective-permute-start | bytes 786440 | tf_op jit(solution)/shard_map/ppermute | solution.py:323
  79.8 1.9 %collective-permute-done.32 = bf16[64,2048]{1,0:T(8,128)(2,1)S(1)} collective-permute-done((bf16[64,2048]{1,0:T(8,128)(2,1)S(1)}, bf16[64,2048]{1,0:T(8,128)(2,1)S(1)}, u32[]{:S(2)}, u32[]{:S(2)}) %collective-permute-start.32) | collective-permute-done | bytes 262176 | tf_op jit(solution)/shard_map/ppermute | solution.py:323
  81.7 1.6 %collective-permute-start.37 = (bf16[64,2048]{1,0:T(8,128)(2,1)S(1)}, bf16[64,2048]{1,0:T(8,128)(2,1)S(1)}, u32[]{:S(2)}, u32[]{:S(2)}) collective-permute-start(bf16[64,2048]{1,0:T(8,128)(2,1)S(1)} %get-tuple-element.226), channel_id=1, source_target_pairs={{4,0},{5,1},{8,4},{9,5},{12,8},{13,9},{14,12},{15,13},{10,14},{11,... | collective-permute-start | bytes 786440 | tf_op jit(solution)/shard_map/ppermute | solution.py:323
  83.2 1.8 %experts.15 = (bf16[64,2048]{1,0:T(8,128)(2,1)S(1)}, bf16[64,2048]{1,0:T(8,128)(2,1)S(1)}) custom-call(bf16[64,2048]{1,0:T(8,128)(2,1)S(1)} %get-tuple-element.149.refs_0_, bf16[64,2048]{1,0:T(8,128)(2,1)S(1)} %get-tuple-element.169.refs_1_, bf16[144,512]{1,0:T(8,128)(2,1)S(1)} %copy-done.3, bf16[1,2048,384]{2,1,0:T(8,128)(2,1)S(1)} %copy-done, ...), custom_call_target="tpu_custom_call" | custom-call | flops 1207959552 | bytes 9437184 | tf_op jit(solution)/shard_map/experts/pallas_call | solution.py:283
  86.7 1.5 %collective-permute-start.40 = (bf16[64,2048]{1,0:T(8,128)(2,1)S(1)}, bf16[64,2048]{1,0:T(8,128)(2,1)S(1)}, u32[]{:S(2)}, u32[]{:S(2)}) collective-permute-start(bf16[64,2048]{1,0:T(8,128)(2,1)S(1)} %add_convert_fusion.8), channel_id=1, source_target_pairs={{4,0},{5,1},{8,4},{9,5},{12,8},{13,9},{14,12},{15,13},{10,14},{11,... | collective-permute-start | bytes 786440 | tf_op jit(solution)/shard_map/ppermute | solution.py:323
  88.9 3.3 %collective-permute-done.37 = bf16[64,2048]{1,0:T(8,128)(2,1)S(1)} collective-permute-done((bf16[64,2048]{1,0:T(8,128)(2,1)S(1)}, bf16[64,2048]{1,0:T(8,128)(2,1)S(1)}, u32[]{:S(2)}, u32[]{:S(2)}) %collective-permute-start.37) | collective-permute-done | bytes 262176 | tf_op jit(solution)/shard_map/ppermute | solution.py:323
  92.3 1.4 %collective-permute-start.39 = (bf16[64,2048]{1,0:T(8,128)(2,1)S(1)}, bf16[64,2048]{1,0:T(8,128)(2,1)S(1)}, u32[]{:S(2)}, u32[]{:S(2)}) collective-permute-start(bf16[64,2048]{1,0:T(8,128)(2,1)S(1)} %add_convert_fusion.7), channel_id=1, source_target_pairs={{4,0},{5,1},{8,4},{9,5},{12,8},{13,9},{14,12},{15,13},{10,14},{11,... | collective-permute-start | bytes 786440 | tf_op jit(solution)/shard_map/ppermute | solution.py:323
  95.2 2.6 %collective-permute-done.40 = bf16[64,2048]{1,0:T(8,128)(2,1)S(1)} collective-permute-done((bf16[64,2048]{1,0:T(8,128)(2,1)S(1)}, bf16[64,2048]{1,0:T(8,128)(2,1)S(1)}, u32[]{:S(2)}, u32[]{:S(2)}) %collective-permute-start.40) | collective-permute-done | bytes 262176 | tf_op jit(solution)/shard_map/ppermute | solution.py:323
  97.9 1.4 %collective-permute-start.44 = (bf16[64,2048]{1,0:T(8,128)(2,1)S(1)}, bf16[64,2048]{1,0:T(8,128)(2,1)S(1)}, u32[]{:S(2)}, u32[]{:S(2)}) collective-permute-start(bf16[64,2048]{1,0:T(8,128)(2,1)S(1)} %add_convert_fusion.6), channel_id=1, source_target_pairs={{4,0},{5,1},{8,4},{9,5},{12,8},{13,9},{14,12},{15,13},{10,14},{11,... | collective-permute-start | bytes 786440 | tf_op jit(solution)/shard_map/ppermute | solution.py:323
  100.9 2.6 %collective-permute-done.39 = bf16[64,2048]{1,0:T(8,128)(2,1)S(1)} collective-permute-done((bf16[64,2048]{1,0:T(8,128)(2,1)S(1)}, bf16[64,2048]{1,0:T(8,128)(2,1)S(1)}, u32[]{:S(2)}, u32[]{:S(2)}) %collective-permute-start.39) | collective-permute-done | bytes 262176 | tf_op jit(solution)/shard_map/ppermute | solution.py:323
  103.5 1.4 %collective-permute-start.41 = (bf16[64,2048]{1,0:T(8,128)(2,1)S(1)}, bf16[64,2048]{1,0:T(8,128)(2,1)S(1)}, u32[]{:S(2)}, u32[]{:S(2)}) collective-permute-start(bf16[64,2048]{1,0:T(8,128)(2,1)S(1)} %add_convert_fusion.5), channel_id=1, source_target_pairs={{4,0},{5,1},{8,4},{9,5},{12,8},{13,9},{14,12},{15,13},{10,14},{11,... | collective-permute-start | bytes 786440 | tf_op jit(solution)/shard_map/ppermute | solution.py:323
  105.9 3.2 %collective-permute-done.44 = bf16[64,2048]{1,0:T(8,128)(2,1)S(1)} collective-permute-done((bf16[64,2048]{1,0:T(8,128)(2,1)S(1)}, bf16[64,2048]{1,0:T(8,128)(2,1)S(1)}, u32[]{:S(2)}, u32[]{:S(2)}) %collective-permute-start.44) | collective-permute-done | bytes 262176 | tf_op jit(solution)/shard_map/ppermute | solution.py:323
  109.1 1.4 %collective-permute-start.45 = (bf16[64,2048]{1,0:T(8,128)(2,1)S(1)}, bf16[64,2048]{1,0:T(8,128)(2,1)S(1)}, u32[]{:S(2)}, u32[]{:S(2)}) collective-permute-start(bf16[64,2048]{1,0:T(8,128)(2,1)S(1)} %add_convert_fusion.1), channel_id=1, source_target_pairs={{4,0},{5,1},{8,4},{9,5},{12,8},{13,9},{14,12},{15,13},{10,14},{11,... | collective-permute-start | bytes 786440 | tf_op jit(solution)/shard_map/ppermute | solution.py:323
  111.3 6.2 %collective-permute-done.45 = bf16[64,2048]{1,0:T(8,128)(2,1)S(1)} collective-permute-done((bf16[64,2048]{1,0:T(8,128)(2,1)S(1)}, bf16[64,2048]{1,0:T(8,128)(2,1)S(1)}, u32[]{:S(2)}, u32[]{:S(2)}) %collective-permute-start.45) | collective-permute-done | bytes 262176 | tf_op jit(solution)/shard_map/ppermute | solution.py:323
  (84 shorter events, 18.9 us)
Async XLA Ops:
  2.3 21.9 %copy-start.3 = (bf16[144,512]{1,0:T(8,128)(2,1)S(1)}, bf16[144,512]{1,0:T(8,128)(2,1)}, u32[]{:S(2)}) copy-start(bf16[144,512]{1,0:T(8,128)(2,1)} %pack_message.1.refs_1_.refs_2_) | copy-start | bytes 442372
  2.3 7.2 %collective-permute-start.2 = (bf16[144,512]{1,0:T(8,128)(2,1)}, bf16[144,512]{1,0:T(8,128)(2,1)S(1)}, u32[]{:S(2)}, u32[]{:S(2)}) collective-permute-start(bf16[144,512]{1,0:T(8,128)(2,1)} %pack_message.1.refs_1_.refs_2_), channel_id=1, source_target_pairs={{4,0},{5,1},{8,4},{9,5},{12,8},{13,9},{14,12},{15,13},{10,14},{11,... | collective-permute-start | bytes 442376 | tf_op jit(solution)/shard_map/ppermute | solution.py:323
  5.2 5.5 %collective-permute-start = (bf16[144,512]{1,0:T(8,128)(2,1)}, bf16[144,512]{1,0:T(8,128)(2,1)S(1)}, u32[]{:S(2)}, u32[]{:S(2)}) collective-permute-start(bf16[144,512]{1,0:T(8,128)(2,1)} %pack_message.1.refs_1_.refs_2_), channel_id=1, source_target_pairs={{0,4},{1,5},{4,8},{5,9},{8,12},{9,13},{12,14},{13,15},{14,10},{15,... | collective-permute-start | bytes 442376 | tf_op jit(solution)/shard_map/ppermute | solution.py:323
  5.3 15.2 %collective-permute-start.6 = (bf16[144,512]{1,0:T(8,128)(2,1)}, bf16[144,512]{1,0:T(8,128)(2,1)S(1)}, u32[]{:S(2)}, u32[]{:S(2)}) collective-permute-start(bf16[144,512]{1,0:T(8,128)(2,1)} %pack_message.1.refs_1_.refs_2_), channel_id=1, source_target_pairs={{0,1},{1,0},{2,3},{3,2},{4,5},{5,4},{6,7},{7,6},{8,9},{9,8},{10,11... | collective-permute-start | bytes 442376 | tf_op jit(solution)/shard_map/ppermute | solution.py:323
  10.8 5.1 %collective-permute-start.1 = (bf16[144,512]{1,0:T(8,128)(2,1)S(1)}, bf16[144,512]{1,0:T(8,128)(2,1)S(1)}, u32[]{:S(2)}, u32[]{:S(2)}) collective-permute-start(bf16[144,512]{1,0:T(8,128)(2,1)S(1)} %collective-permute-done.refs_3_.refs_2_), channel_id=1, source_target_pairs={{0,4},{1,5},{4,8},{5,9},{8,12},{9,13},{12,14},{13,15},{14,10},{15,... | collective-permute-start | bytes 442376 | tf_op jit(solution)/shard_map/ppermute | solution.py:323
  11.1 17.7 %copy-start.2 = (bf16[1,384,2048]{2,1,0:T(8,128)(2,1)S(1)}, bf16[1,384,2048]{2,1,0:T(8,128)(2,1)}, u32[]{:S(2)}) copy-start(bf16[1,384,2048]{2,1,0:T(8,128)(2,1)} %refs_5_.15) | copy-start | bytes 4718596
  12.5 8.0 %collective-permute-start.9 = (bf16[144,512]{1,0:T(8,128)(2,1)S(1)}, bf16[144,512]{1,0:T(8,128)(2,1)S(1)}, u32[]{:S(2)}, u32[]{:S(2)}) collective-permute-start(bf16[144,512]{1,0:T(8,128)(2,1)S(1)} %collective-permute-done.2.refs_6_.refs_3_), channel_id=1, source_target_pairs={{0,1},{1,0},{2,3},{3,2},{4,5},{5,4},{6,7},{7,6},{8,9},{9,8},{10,11... | collective-permute-start | bytes 442376 | tf_op jit(solution)/shard_map/ppermute | solution.py:323
  12.5 6.2 %collective-permute-start.4 = (bf16[144,512]{1,0:T(8,128)(2,1)S(1)}, bf16[144,512]{1,0:T(8,128)(2,1)S(1)}, u32[]{:S(2)}, u32[]{:S(2)}) collective-permute-start(bf16[144,512]{1,0:T(8,128)(2,1)S(1)} %collective-permute-done.2.refs_6_.refs_3_), channel_id=1, source_target_pairs={{4,0},{5,1},{8,4},{9,5},{12,8},{13,9},{14,12},{15,13},{10,14},{11,... | collective-permute-start | bytes 442376 | tf_op jit(solution)/shard_map/ppermute | solution.py:323
  15.9 5.2 %collective-permute-start.3 = (bf16[144,512]{1,0:T(8,128)(2,1)S(1)}, bf16[144,512]{1,0:T(8,128)(2,1)S(1)}, u32[]{:S(2)}, u32[]{:S(2)}) collective-permute-start(bf16[144,512]{1,0:T(8,128)(2,1)S(1)} %collective-permute-done.1.refs_4_.refs_2_), channel_id=1, source_target_pairs={{0,4},{1,5},{4,8},{5,9},{8,12},{9,13},{12,14},{13,15},{14,10},{15,... | collective-permute-start | bytes 442376 | tf_op jit(solution)/shard_map/ppermute | solution.py:323
  16.3 5.1 %collective-permute-start.7 = (bf16[144,512]{1,0:T(8,128)(2,1)S(1)}, bf16[144,512]{1,0:T(8,128)(2,1)S(1)}, u32[]{:S(2)}, u32[]{:S(2)}) collective-permute-start(bf16[144,512]{1,0:T(8,128)(2,1)S(1)} %collective-permute-done.refs_3_.refs_2_), channel_id=1, source_target_pairs={{0,1},{1,0},{2,3},{3,2},{4,5},{5,4},{6,7},{7,6},{8,9},{9,8},{10,11... | collective-permute-start | bytes 442376 | tf_op jit(solution)/shard_map/ppermute | solution.py:323
  18.8 5.4 %collective-permute-start.5 = (bf16[144,512]{1,0:T(8,128)(2,1)S(1)}, bf16[144,512]{1,0:T(8,128)(2,1)S(1)}, u32[]{:S(2)}, u32[]{:S(2)}) collective-permute-start(bf16[144,512]{1,0:T(8,128)(2,1)S(1)} %collective-permute-done.4.refs_7_.refs_3_), channel_id=1, source_target_pairs={{4,0},{5,1},{8,4},{9,5},{12,8},{13,9},{14,12},{15,13},{10,14},{11,... | collective-permute-start | bytes 442376 | tf_op jit(solution)/shard_map/ppermute | solution.py:323
  20.5 3.7 %collective-permute-start.10 = (bf16[144,512]{1,0:T(8,128)(2,1)S(1)}, bf16[144,512]{1,0:T(8,128)(2,1)S(1)}, u32[]{:S(2)}, u32[]{:S(2)}) collective-permute-start(bf16[144,512]{1,0:T(8,128)(2,1)S(1)} %collective-permute-done.4.refs_7_.refs_3_), channel_id=1, source_target_pairs={{0,1},{1,0},{2,3},{3,2},{4,5},{5,4},{6,7},{7,6},{8,9},{9,8},{10,11... | collective-permute-start | bytes 442376 | tf_op jit(solution)/shard_map/ppermute | solution.py:323
  20.5 3.7 %collective-permute-start.8 = (bf16[144,512]{1,0:T(8,128)(2,1)S(1)}, bf16[144,512]{1,0:T(8,128)(2,1)S(1)}, u32[]{:S(2)}, u32[]{:S(2)}) collective-permute-start(bf16[144,512]{1,0:T(8,128)(2,1)S(1)} %collective-permute-done.1.refs_4_.refs_2_), channel_id=1, source_target_pairs={{0,1},{1,0},{2,3},{3,2},{4,5},{5,4},{6,7},{7,6},{8,9},{9,8},{10,11... | collective-permute-start | bytes 442376 | tf_op jit(solution)/shard_map/ppermute | solution.py:323
  21.1 5.7 %collective-permute-start.11 = (bf16[144,512]{1,0:T(8,128)(2,1)S(1)}, bf16[144,512]{1,0:T(8,128)(2,1)S(1)}, u32[]{:S(2)}, u32[]{:S(2)}) collective-permute-start(bf16[144,512]{1,0:T(8,128)(2,1)S(1)} %collective-permute-done.3.refs_5_.refs_2_), channel_id=1, source_target_pairs={{0,4},{1,5},{4,8},{5,9},{8,12},{9,13},{12,14},{13,15},{14,10},{15,... | collective-permute-start | bytes 442376 | tf_op jit(solution)/shard_map/ppermute | solution.py:323
  21.5 5.8 %collective-permute-start.12 = (bf16[144,512]{1,0:T(8,128)(2,1)S(1)}, bf16[144,512]{1,0:T(8,128)(2,1)S(1)}, u32[]{:S(2)}, u32[]{:S(2)}) collective-permute-start(bf16[144,512]{1,0:T(8,128)(2,1)S(1)} %collective-permute-done.3.refs_5_.refs_2_), channel_id=1, source_target_pairs={{0,1},{1,0},{2,3},{3,2},{4,5},{5,4},{6,7},{7,6},{8,9},{9,8},{10,11... | collective-permute-start | bytes 442376 | tf_op jit(solution)/shard_map/ppermute | solution.py:323
  24.2 3.1 %collective-permute-start.13 = (bf16[144,512]{1,0:T(8,128)(2,1)S(1)}, bf16[144,512]{1,0:T(8,128)(2,1)S(1)}, u32[]{:S(2)}, u32[]{:S(2)}) collective-permute-start(bf16[144,512]{1,0:T(8,128)(2,1)S(1)} %collective-permute-done.5.refs_8_.refs_3_), channel_id=1, source_target_pairs={{0,1},{1,0},{2,3},{3,2},{4,5},{5,4},{6,7},{7,6},{8,9},{9,8},{10,11... | collective-permute-start | bytes 442376 | tf_op jit(solution)/shard_map/ppermute | solution.py:323
  26.8 1.5 %collective-permute-start.14 = (bf16[144,512]{1,0:T(8,128)(2,1)S(1)}, bf16[144,512]{1,0:T(8,128)(2,1)S(1)}, u32[]{:S(2)}, u32[]{:S(2)}) collective-permute-start(bf16[144,512]{1,0:T(8,128)(2,1)S(1)} %collective-permute-done.11.refs_2_.refs_14_), channel_id=1, source_target_pairs={{0,1},{1,0},{2,3},{3,2},{4,5},{5,4},{6,7},{7,6},{8,9},{9,8},{10,11... | collective-permute-start | bytes 442376 | tf_op jit(solution)/shard_map/ppermute | solution.py:323
  28.3 7.7 %collective-permute-start.15 = (bf16[1,2048,384]{2,1,0:T(8,128)(2,1)S(1)}, bf16[1,2048,384]{2,1,0:T(8,128)(2,1)S(1)}, u32[]{:S(2)}, u32[]{:S(2)}) collective-permute-start(bf16[1,2048,384]{2,1,0:T(8,128)(2,1)S(1)} %copy-done), channel_id=1, source_target_pairs={{0,1},{1,0},{2,3},{3,2},{4,5},{5,4},{6,7},{7,6},{8,9},{9,8},{10,11... | collective-permute-start | bytes 4718600 | tf_op jit(solution)/shard_map/ppermute | solution.py:323
  28.7 7.4 %collective-permute-start.16 = (bf16[1,2048,384]{2,1,0:T(8,128)(2,1)S(1)}, bf16[1,2048,384]{2,1,0:T(8,128)(2,1)S(1)}, u32[]{:S(2)}, u32[]{:S(2)}) collective-permute-start(bf16[1,2048,384]{2,1,0:T(8,128)(2,1)S(1)} %copy-done.1), channel_id=1, source_target_pairs={{0,1},{1,0},{2,3},{3,2},{4,5},{5,4},{6,7},{7,6},{8,9},{9,8},{10,11... | collective-permute-start | bytes 4718600 | tf_op jit(solution)/shard_map/ppermute | solution.py:323
  28.8 12.9 %collective-permute-start.23 = (bf16[1,384,2048]{2,1,0:T(8,128)(2,1)S(1)}, bf16[1,384,2048]{2,1,0:T(8,128)(2,1)S(1)}, u32[]{:S(2)}, u32[]{:S(2)}) collective-permute-start(bf16[1,384,2048]{2,1,0:T(8,128)(2,1)S(1)} %copy-done.2), channel_id=1, source_target_pairs={{0,1},{1,0},{2,3},{3,2},{4,5},{5,4},{6,7},{7,6},{8,9},{9,8},{10,11... | collective-permute-start | bytes 4718600 | tf_op jit(solution)/shard_map/ppermute | solution.py:323
  30.6 9.1 %collective-permute-start.19 = (bf16[64,2048]{1,0:T(8,128)(2,1)S(1)}, bf16[64,2048]{1,0:T(8,128)(2,1)S(1)}, u32[]{:S(2)}, u32[]{:S(2)}) collective-permute-start(bf16[64,2048]{1,0:T(8,128)(2,1)S(1)} %get-tuple-element.149.refs_0_), channel_id=1, source_target_pairs={{4,0},{5,1},{8,4},{9,5},{12,8},{13,9},{14,12},{15,13},{10,14},{11,... | collective-permute-start | bytes 786440 | tf_op jit(solution)/shard_map/ppermute | solution.py:323
  32.3 9.0 %collective-permute-start.17 = (bf16[64,2048]{1,0:T(8,128)(2,1)S(1)}, bf16[64,2048]{1,0:T(8,128)(2,1)S(1)}, u32[]{:S(2)}, u32[]{:S(2)}) collective-permute-start(bf16[64,2048]{1,0:T(8,128)(2,1)S(1)} %get-tuple-element.149.refs_0_), channel_id=1, source_target_pairs={{0,4},{1,5},{4,8},{5,9},{8,12},{9,13},{12,14},{13,15},{14,10},{15,... | collective-permute-start | bytes 786440 | tf_op jit(solution)/shard_map/ppermute | solution.py:323
  36.0 9.2 %collective-permute-start.22 = (bf16[64,2048]{1,0:T(8,128)(2,1)S(1)}, bf16[64,2048]{1,0:T(8,128)(2,1)S(1)}, u32[]{:S(2)}, u32[]{:S(2)}) collective-permute-start(bf16[64,2048]{1,0:T(8,128)(2,1)S(1)} %get-tuple-element.169.refs_1_), channel_id=1, source_target_pairs={{4,0},{5,1},{8,4},{9,5},{12,8},{13,9},{14,12},{15,13},{10,14},{11,... | collective-permute-start | bytes 786440 | tf_op jit(solution)/shard_map/ppermute | solution.py:323
  37.8 9.2 %collective-permute-start.21 = (bf16[64,2048]{1,0:T(8,128)(2,1)S(1)}, bf16[64,2048]{1,0:T(8,128)(2,1)S(1)}, u32[]{:S(2)}, u32[]{:S(2)}) collective-permute-start(bf16[64,2048]{1,0:T(8,128)(2,1)S(1)} %get-tuple-element.169.refs_1_), channel_id=1, source_target_pairs={{0,4},{1,5},{4,8},{5,9},{8,12},{9,13},{12,14},{13,15},{14,10},{15,... | collective-permute-start | bytes 786440 | tf_op jit(solution)/shard_map/ppermute | solution.py:323
  39.7 11.2 %collective-permute-start.20 = (bf16[64,2048]{1,0:T(8,128)(2,1)S(1)}, bf16[64,2048]{1,0:T(8,128)(2,1)S(1)}, u32[]{:S(2)}, u32[]{:S(2)}) collective-permute-start(bf16[64,2048]{1,0:T(8,128)(2,1)S(1)} %collective-permute-done.19.refs_1_), channel_id=1, source_target_pairs={{4,0},{5,1},{8,4},{9,5},{12,8},{13,9},{14,12},{15,13},{10,14},{11,... | collective-permute-start | bytes 786440 | tf_op jit(solution)/shard_map/ppermute | solution.py:323
  41.4 11.3 %collective-permute-start.18 = (bf16[64,2048]{1,0:T(8,128)(2,1)S(1)}, bf16[64,2048]{1,0:T(8,128)(2,1)S(1)}, u32[]{:S(2)}, u32[]{:S(2)}) collective-permute-start(bf16[64,2048]{1,0:T(8,128)(2,1)S(1)} %collective-permute-done.17.refs_0_), channel_id=1, source_target_pairs={{0,4},{1,5},{4,8},{5,9},{8,12},{9,13},{12,14},{13,15},{14,10},{15,... | collective-permute-start | bytes 786440 | tf_op jit(solution)/shard_map/ppermute | solution.py:323
  47.0 11.2 %collective-permute-start.26 = (bf16[64,2048]{1,0:T(8,128)(2,1)S(1)}, bf16[64,2048]{1,0:T(8,128)(2,1)S(1)}, u32[]{:S(2)}, u32[]{:S(2)}) collective-permute-start(bf16[64,2048]{1,0:T(8,128)(2,1)S(1)} %collective-permute-done.21.refs_0_), channel_id=1, source_target_pairs={{0,4},{1,5},{4,8},{5,9},{8,12},{9,13},{12,14},{13,15},{14,10},{15,... | collective-permute-start | bytes 786440 | tf_op jit(solution)/shard_map/ppermute | solution.py:323
  47.4 10.9 %collective-permute-start.27 = (bf16[64,2048]{1,0:T(8,128)(2,1)S(1)}, bf16[64,2048]{1,0:T(8,128)(2,1)S(1)}, u32[]{:S(2)}, u32[]{:S(2)}) collective-permute-start(bf16[64,2048]{1,0:T(8,128)(2,1)S(1)} %collective-permute-done.22.refs_1_), channel_id=1, source_target_pairs={{4,0},{5,1},{8,4},{9,5},{12,8},{13,9},{14,12},{15,13},{10,14},{11,... | collective-permute-start | bytes 786440 | tf_op jit(solution)/shard_map/ppermute | solution.py:323
  52.6 11.2 %collective-permute-start.24 = (bf16[64,2048]{1,0:T(8,128)(2,1)S(1)}, bf16[64,2048]{1,0:T(8,128)(2,1)S(1)}, u32[]{:S(2)}, u32[]{:S(2)}) collective-permute-start(bf16[64,2048]{1,0:T(8,128)(2,1)S(1)} %collective-permute-done.18.refs_0_), channel_id=1, source_target_pairs={{0,4},{1,5},{4,8},{5,9},{8,12},{9,13},{12,14},{13,15},{14,10},{15,... | collective-permute-start | bytes 786440 | tf_op jit(solution)/shard_map/ppermute | solution.py:323
  53.0 10.9 %collective-permute-start.25 = (bf16[64,2048]{1,0:T(8,128)(2,1)S(1)}, bf16[64,2048]{1,0:T(8,128)(2,1)S(1)}, u32[]{:S(2)}, u32[]{:S(2)}) collective-permute-start(bf16[64,2048]{1,0:T(8,128)(2,1)S(1)} %collective-permute-done.20.refs_1_), channel_id=1, source_target_pairs={{4,0},{5,1},{8,4},{9,5},{12,8},{13,9},{14,12},{15,13},{10,14},{11,... | collective-permute-start | bytes 786440 | tf_op jit(solution)/shard_map/ppermute | solution.py:323
  58.2 11.2 %collective-permute-start.29 = (bf16[64,2048]{1,0:T(8,128)(2,1)S(1)}, bf16[64,2048]{1,0:T(8,128)(2,1)S(1)}, u32[]{:S(2)}, u32[]{:S(2)}) collective-permute-start(bf16[64,2048]{1,0:T(8,128)(2,1)S(1)} %collective-permute-done.26.refs_0_), channel_id=1, source_target_pairs={{0,4},{1,5},{4,8},{5,9},{8,12},{9,13},{12,14},{13,15},{14,10},{15,... | collective-permute-start | bytes 786440 | tf_op jit(solution)/shard_map/ppermute | solution.py:323
  58.6 10.9 %collective-permute-start.30 = (bf16[64,2048]{1,0:T(8,128)(2,1)S(1)}, bf16[64,2048]{1,0:T(8,128)(2,1)S(1)}, u32[]{:S(2)}, u32[]{:S(2)}) collective-permute-start(bf16[64,2048]{1,0:T(8,128)(2,1)S(1)} %collective-permute-done.27.refs_1_), channel_id=1, source_target_pairs={{4,0},{5,1},{8,4},{9,5},{12,8},{13,9},{14,12},{15,13},{10,14},{11,... | collective-permute-start | bytes 786440 | tf_op jit(solution)/shard_map/ppermute | solution.py:323
  63.9 10.9 %collective-permute-start.28 = (bf16[64,2048]{1,0:T(8,128)(2,1)S(1)}, bf16[64,2048]{1,0:T(8,128)(2,1)S(1)}, u32[]{:S(2)}, u32[]{:S(2)}) collective-permute-start(bf16[64,2048]{1,0:T(8,128)(2,1)S(1)} %collective-permute-done.24.refs_0_), channel_id=1, source_target_pairs={{0,4},{1,5},{4,8},{5,9},{8,12},{9,13},{12,14},{13,15},{14,10},{15,... | collective-permute-start | bytes 786440 | tf_op jit(solution)/shard_map/ppermute | solution.py:323
  69.5 6.4 %collective-permute-start.31 = (bf16[64,2048]{1,0:T(8,128)(2,1)S(1)}, bf16[64,2048]{1,0:T(8,128)(2,1)S(1)}, u32[]{:S(2)}, u32[]{:S(2)}) collective-permute-start(bf16[64,2048]{1,0:T(8,128)(2,1)S(1)} %collective-permute-done.30.refs_1_), channel_id=1, source_target_pairs={{4,0},{5,1},{8,4},{9,5},{12,8},{13,9},{14,12},{15,13},{10,14},{11,... | collective-permute-start | bytes 786440 | tf_op jit(solution)/shard_map/ppermute | solution.py:323
  72.9 8.8 %collective-permute-start.32 = (bf16[64,2048]{1,0:T(8,128)(2,1)S(1)}, bf16[64,2048]{1,0:T(8,128)(2,1)S(1)}, u32[]{:S(2)}, u32[]{:S(2)}) collective-permute-start(bf16[64,2048]{1,0:T(8,128)(2,1)S(1)} %get-tuple-element.216), channel_id=1, source_target_pairs={{0,4},{1,5},{4,8},{5,9},{8,12},{9,13},{12,14},{13,15},{14,10},{15,... | collective-permute-start | bytes 786440 | tf_op jit(solution)/shard_map/ppermute | solution.py:323
  77.7 7.6 %collective-permute-start.33 = (bf16[64,2048]{1,0:T(8,128)(2,1)S(1)}, bf16[64,2048]{1,0:T(8,128)(2,1)S(1)}, u32[]{:S(2)}, u32[]{:S(2)}) collective-permute-start(bf16[64,2048]{1,0:T(8,128)(2,1)S(1)} %get-tuple-element.218), channel_id=1, source_target_pairs={{0,4},{1,5},{4,8},{5,9},{8,12},{9,13},{12,14},{13,15},{14,10},{15,... | collective-permute-start | bytes 786440 | tf_op jit(solution)/shard_map/ppermute | solution.py:323
  78.4 8.2 %collective-permute-start.38 = (bf16[64,2048]{1,0:T(8,128)(2,1)S(1)}, bf16[64,2048]{1,0:T(8,128)(2,1)S(1)}, u32[]{:S(2)}, u32[]{:S(2)}) collective-permute-start(bf16[64,2048]{1,0:T(8,128)(2,1)S(1)} %get-tuple-element.219), channel_id=1, source_target_pairs={{4,0},{5,1},{8,4},{9,5},{12,8},{13,9},{14,12},{15,13},{10,14},{11,... | collective-permute-start | bytes 786440 | tf_op jit(solution)/shard_map/ppermute | solution.py:323
  81.7 10.5 %collective-permute-start.37 = (bf16[64,2048]{1,0:T(8,128)(2,1)S(1)}, bf16[64,2048]{1,0:T(8,128)(2,1)S(1)}, u32[]{:S(2)}, u32[]{:S(2)}) collective-permute-start(bf16[64,2048]{1,0:T(8,128)(2,1)S(1)} %get-tuple-element.226), channel_id=1, source_target_pairs={{4,0},{5,1},{8,4},{9,5},{12,8},{13,9},{14,12},{15,13},{10,14},{11,... | collective-permute-start | bytes 786440 | tf_op jit(solution)/shard_map/ppermute | solution.py:323
  85.4 9.3 %collective-permute-start.34 = (bf16[64,2048]{1,0:T(8,128)(2,1)S(1)}, bf16[64,2048]{1,0:T(8,128)(2,1)S(1)}, u32[]{:S(2)}, u32[]{:S(2)}) collective-permute-start(bf16[64,2048]{1,0:T(8,128)(2,1)S(1)} %add_convert_fusion.11), channel_id=1, source_target_pairs={{0,4},{1,5},{4,8},{5,9},{8,12},{9,13},{12,14},{13,15},{14,10},{15,... | collective-permute-start | bytes 786440 | tf_op jit(solution)/shard_map/ppermute | solution.py:323
  86.7 11.1 %collective-permute-start.40 = (bf16[64,2048]{1,0:T(8,128)(2,1)S(1)}, bf16[64,2048]{1,0:T(8,128)(2,1)S(1)}, u32[]{:S(2)}, u32[]{:S(2)}) collective-permute-start(bf16[64,2048]{1,0:T(8,128)(2,1)S(1)} %add_convert_fusion.8), channel_id=1, source_target_pairs={{4,0},{5,1},{8,4},{9,5},{12,8},{13,9},{14,12},{15,13},{10,14},{11,... | collective-permute-start | bytes 786440 | tf_op jit(solution)/shard_map/ppermute | solution.py:323
  88.2 12.1 %collective-permute-start.42 = (bf16[64,2048]{1,0:T(8,128)(2,1)S(1)}, bf16[64,2048]{1,0:T(8,128)(2,1)S(1)}, u32[]{:S(2)}, u32[]{:S(2)}) collective-permute-start(bf16[64,2048]{1,0:T(8,128)(2,1)S(1)} %add_convert_fusion.3), channel_id=1, source_target_pairs={{0,4},{1,5},{4,8},{5,9},{8,12},{9,13},{12,14},{13,15},{14,10},{15,... | collective-permute-start | bytes 786440 | tf_op jit(solution)/shard_map/ppermute | solution.py:323
  92.3 11.2 %collective-permute-start.39 = (bf16[64,2048]{1,0:T(8,128)(2,1)S(1)}, bf16[64,2048]{1,0:T(8,128)(2,1)S(1)}, u32[]{:S(2)}, u32[]{:S(2)}) collective-permute-start(bf16[64,2048]{1,0:T(8,128)(2,1)S(1)} %add_convert_fusion.7), channel_id=1, source_target_pairs={{4,0},{5,1},{8,4},{9,5},{12,8},{13,9},{14,12},{15,13},{10,14},{11,... | collective-permute-start | bytes 786440 | tf_op jit(solution)/shard_map/ppermute | solution.py:323
  94.8 11.1 %collective-permute-start.35 = (bf16[64,2048]{1,0:T(8,128)(2,1)S(1)}, bf16[64,2048]{1,0:T(8,128)(2,1)S(1)}, u32[]{:S(2)}, u32[]{:S(2)}) collective-permute-start(bf16[64,2048]{1,0:T(8,128)(2,1)S(1)} %add_convert_fusion.10), channel_id=1, source_target_pairs={{0,4},{1,5},{4,8},{5,9},{8,12},{9,13},{12,14},{13,15},{14,10},{15,... | collective-permute-start | bytes 786440 | tf_op jit(solution)/shard_map/ppermute | solution.py:323
  97.9 11.2 %collective-permute-start.44 = (bf16[64,2048]{1,0:T(8,128)(2,1)S(1)}, bf16[64,2048]{1,0:T(8,128)(2,1)S(1)}, u32[]{:S(2)}, u32[]{:S(2)}) collective-permute-start(bf16[64,2048]{1,0:T(8,128)(2,1)S(1)} %add_convert_fusion.6), channel_id=1, source_target_pairs={{4,0},{5,1},{8,4},{9,5},{12,8},{13,9},{14,12},{15,13},{10,14},{11,... | collective-permute-start | bytes 786440 | tf_op jit(solution)/shard_map/ppermute | solution.py:323
  100.4 10.9 %collective-permute-start.43 = (bf16[64,2048]{1,0:T(8,128)(2,1)S(1)}, bf16[64,2048]{1,0:T(8,128)(2,1)S(1)}, u32[]{:S(2)}, u32[]{:S(2)}) collective-permute-start(bf16[64,2048]{1,0:T(8,128)(2,1)S(1)} %add_convert_fusion.2), channel_id=1, source_target_pairs={{0,4},{1,5},{4,8},{5,9},{8,12},{9,13},{12,14},{13,15},{14,10},{15,... | collective-permute-start | bytes 786440 | tf_op jit(solution)/shard_map/ppermute | solution.py:323
  103.5 14.1 %collective-permute-start.41 = (bf16[64,2048]{1,0:T(8,128)(2,1)S(1)}, bf16[64,2048]{1,0:T(8,128)(2,1)S(1)}, u32[]{:S(2)}, u32[]{:S(2)}) collective-permute-start(bf16[64,2048]{1,0:T(8,128)(2,1)S(1)} %add_convert_fusion.5), channel_id=1, source_target_pairs={{4,0},{5,1},{8,4},{9,5},{12,8},{13,9},{14,12},{15,13},{10,14},{11,... | collective-permute-start | bytes 786440 | tf_op jit(solution)/shard_map/ppermute | solution.py:323
  109.1 8.4 %collective-permute-start.45 = (bf16[64,2048]{1,0:T(8,128)(2,1)S(1)}, bf16[64,2048]{1,0:T(8,128)(2,1)S(1)}, u32[]{:S(2)}, u32[]{:S(2)}) collective-permute-start(bf16[64,2048]{1,0:T(8,128)(2,1)S(1)} %add_convert_fusion.1), channel_id=1, source_target_pairs={{4,0},{5,1},{8,4},{9,5},{12,8},{13,9},{14,12},{15,13},{10,14},{11,... | collective-permute-start | bytes 786440 | tf_op jit(solution)/shard_map/ppermute | solution.py:323
  110.6 7.0 %collective-permute-start.36 = (bf16[64,2048]{1,0:T(8,128)(2,1)S(1)}, bf16[64,2048]{1,0:T(8,128)(2,1)S(1)}, u32[]{:S(2)}, u32[]{:S(2)}) collective-permute-start(bf16[64,2048]{1,0:T(8,128)(2,1)S(1)} %add_convert_fusion.9), channel_id=1, source_target_pairs={{0,4},{1,5},{4,8},{5,9},{8,12},{9,13},{12,14},{13,15},{14,10},{15,... | collective-permute-start | bytes 786440 | tf_op jit(solution)/shard_map/ppermute | solution.py:323
  (4 other events, 60.4 us)
